TPU v7x, 32 devices: a whole 2x2x4 slice. The times are simulated.
32 devices in a mesh: grp: 2 (over y), lvl: 4 (over x, core), col: 4 (over z).
Axes of the slice: x: 2, y: 2, z: 4, core: 2. Of those that a mesh axis runs over, the one named last changes fastest.
Arguments:
- inverse_diag: float32 [64, 256, 256], P(('grp', 'lvl')), parts along dimension 0, may hold values from 0 to 2, as said below
- down_block: float32 [64, 256, 256], P(('grp', 'lvl')), parts along dimension 0, may hold values from 0 to 2, as said below
- up_block: float32 [64, 256, 256], P(('grp', 'lvl')), parts along dimension 0, may hold values from 0 to 1, as said below
- reward: float32 [64, 64, 256], P(('grp', 'lvl'), 'col'), parts along dimension 0, may hold values from -6 to 6
Outputs:
- values: float32 [64, 64, 256], P(('grp', 'lvl'), 'col'), parts along dimension 0
There are 2 independent parts, one for each index of `grp`. A program takes and returns all parts, laid end to end along the dimension named above; each array names one. Nothing has to cross between parts.
Inputs may be any that keep to these rules, and one draw needn't show every extreme that they name: `inverse_diag`: Nonnegative. `down_block`: Nonnegative. `up_block`: Nonnegative.
All inputs are finite; a program needn't handle non-finite values.
Results may differ from a plain program's by a relative error of at most 0.00011.
Values sent between devices are 32-bit elements; how exact they have to be, the bound alone decides.
No kernel may reach another device: no remote copies, remote signals or barrier semaphores. Data moves between devices by JAX's collectives and lax.ppermute only.
A program may use at most 64 MiB of HBM per device.

v0:
```python
import jax
import jax.numpy as jnp
from jax import lax
from jax.sharding import PartitionSpec as P

SWEEPS = 8


PRECISE = lax.Precision.HIGHEST


def from_behind(value, axis, steps):
    count = lax.axis_size(axis)
    first, last = (max(0, -steps), min(count, count - steps))
    return lax.ppermute(value, axis, [(source, source + steps) for source in range(first, last)])


def entering_2(part, axis, combine, identity):
    place = lax.axis_index(axis)
    gathered = jax.tree.map(lambda a: lax.all_gather(a, axis), part)
    state = jax.tree.map(lambda a, e: jnp.zeros_like(a) + jnp.asarray(e, a.dtype), part, identity)

    def one(step, state):
        return combine(
            state, jax.tree.map(lambda a: lax.dynamic_index_in_dim(a, step, 0, False), gathered)
        )

    return lax.fori_loop(0, place, one, state)


def apply_right(vector, matrix):
    return jnp.einsum("km,pm->kp", vector, matrix, precision=PRECISE)


def local_sweep(entering, inverse_diag, down_block, base_terms):

    def level_step(carried, inputs):
        inv_here, down_here, base_here = inputs
        updated = apply_right(base_here + apply_right(carried, down_here), inv_here)
        return (updated, updated)

    return lax.scan(level_step, entering, (inverse_diag, down_block, base_terms))


def transfer_full(inverse_diag, down_block):
    identity_mat = jnp.eye(inverse_diag.shape[1], dtype=jnp.float32)

    def compose(product, inputs):
        inv_here, down_here = inputs
        return (
            jnp.matmul(
                inv_here, jnp.matmul(down_here, product, precision=PRECISE), precision=PRECISE
            ),
            None,
        )

    result, _ = lax.scan(compose, identity_mat, (inverse_diag, down_block))
    return result


def local(inverse_diag, down_block, up_block, reward):
    phases = reward.shape[2]
    identity_mat = jnp.eye(phases, dtype=jnp.float32)
    transfer = transfer_full(inverse_diag, down_block)
    estimate = jnp.zeros_like(reward)
    for repeat in range(SWEEPS):
        rim_values = from_behind(estimate[0], "lvl", -1)
        beyond = jnp.concatenate([estimate[1:], rim_values[None]], axis=0)
        base_terms = reward + jnp.einsum("lkm,lpm->lkp", beyond, up_block, precision=PRECISE)
        outgoing, _ = local_sweep(jnp.zeros_like(reward[0]), inverse_diag, down_block, base_terms)

        def compose_maps(earlier, later):
            joined = jnp.matmul(later[0], earlier[0], precision=PRECISE)
            return (joined, apply_right(earlier[1], later[0]) + later[1])

        prefix = entering_2(
            (transfer, outgoing), "lvl", compose_maps, (identity_mat, jnp.zeros_like(outgoing))
        )
        entering = prefix[1]
        _, estimate = local_sweep(entering, inverse_diag, down_block, base_terms)
    return estimate


def solution(mesh):
    placed = (
        P(("grp", "lvl"), None, None),
        P(("grp", "lvl"), None, None),
        P(("grp", "lvl"), None, None),
        P(("grp", "lvl"), "col", None),
    )
    return jax.shard_map(
        local, mesh=mesh, in_specs=placed, out_specs=P(("grp", "lvl"), "col", None), check_vma=False
    )
```

profile of v0, /device:TPU:11, one launch (start us, length us, event | category | flops | bytes accessed | tf_op | source)
XLA Modules:
  0.0 493.3 jit_solution(10380933580429825770)
XLA Ops:
  6.5 2.7 collective-permute-start
  9.3 21.6 %while.282 = (s32[]{:T(128)}, f32[256,256]{1,0:T(8,128)S(1)}, f32[8,256,256]{2,1,0:T(8,128)}, f32[8,256,256]{2,1,0:T(8,128)}, s32[]{:T(128)}) while((s32[]{:T(128)}, f32[256,256]{1,0:T(8,128)S(1)}, f32[8,256,256]{2,1,0:T(8,128)}, f32[8,256,256]{2,1,0:T(8,128)}, s32[]{:T(128)}) %tuple.378), condition=%wide.region_1.2_spmd, body=%wide.region_0.1_spmd.sunk | while | flops 402653184 | bytes 1573949 | solution.py:57
  33.5 20.4 %while.283 = (s32[]{:T(128)}, f32[16,256]{1,0:T(8,128)S(1)}, f32[8,16,256]{2,1,0:T(8,128)S(1)}, f32[8,256,256]{2,1,0:T(8,128)}, f32[8,256,256]{2,1,0:T(8,128)}, /*index=5*/s32[]{:T(128)}) while((s32[]{:T(128)}, f32[16,256]{1,0:T(8,128)S(1)}, f32[8,16,256]{2,1,0:T(8,128)S(1)}, f32[8,256,256]{2,1,0:T(8,128)}, f32[8,256,256]{2,1,0:T(8,128)}, ...), condition=%wide.region_3.4_spmd, body=%wide.region_2.3_spmd.sunk | while | flops 25169920 | bytes 607813 | solution.py:42
  53.9 5.1 %all-gather.1 = f32[64,256]{1,0:T(8,128)S(1)} all-gather(f32[16,256]{1,0:T(8,128)S(1)} %get-tuple-element.852), channel_id=3, replica_groups=mesh['grp'=2,'lvl'=4,'col'=4] {'lvl'}, dimensions={0}, use_global_device_ids=true | all-gather | bytes 81920 | tf_op jit(solution)/shard_map/all_gather | solution.py:20
  59.1 3.9 while.284
  63.0 20.4 %while.285 = (s32[]{:T(128)}, f32[16,256]{1,0:T(8,128)S(1)}, f32[8,16,256]{2,1,0:T(8,128)S(1)}, f32[8,16,256]{2,1,0:T(8,128)S(1)}, f32[8,256,256]{2,1,0:T(8,128)}, /*index=5*/f32[8,256,256]{2,1,0:T(8,128)}, s32[]{:T(128)}) while((s32[]{:T(128)}, f32[16,256]{1,0:T(8,128)S(1)}, f32[8,16,256]{2,1,0:T(8,128)S(1)}, f32[8,16,256]{2,1,0:T(8,128)S(1)}, ...), condition=%wide.region_7.8_spmd, body=%wide.region_6.7_spmd.sunk | while | flops 25169920 | bytes 624717 | solution.py:42
  87.4 20.4 %while.286 = (s32[]{:T(128)}, f32[16,256]{1,0:T(8,128)S(1)}, f32[8,16,256]{2,1,0:T(8,128)S(1)}, f32[8,256,256]{2,1,0:T(8,128)}, f32[8,256,256]{2,1,0:T(8,128)}, /*index=5*/s32[]{:T(128)}) while((s32[]{:T(128)}, f32[16,256]{1,0:T(8,128)S(1)}, f32[8,16,256]{2,1,0:T(8,128)S(1)}, f32[8,256,256]{2,1,0:T(8,128)}, f32[8,256,256]{2,1,0:T(8,128)}, ...), condition=%wide.region_9.10_spmd, body=%wide.region_8.9_spmd.sunk | while | flops 25169920 | bytes 607813 | solution.py:42
  107.9 5.5 %all-gather.2 = f32[64,256]{1,0:T(8,128)S(1)} all-gather(f32[16,256]{1,0:T(8,128)S(1)} %get-tuple-element.855), channel_id=4, replica_groups=mesh['grp'=2,'lvl'=4,'col'=4] {'lvl'}, dimensions={0}, use_global_device_ids=true | all-gather | bytes 81920 | tf_op jit(solution)/shard_map/all_gather | solution.py:20
  115.0 25.3 %while.288 = (s32[]{:T(128)}, f32[16,256]{1,0:T(8,128)S(1)}, f32[8,16,256]{2,1,0:T(8,128)}, f32[8,16,256]{2,1,0:T(8,128)S(1)}, f32[8,256,256]{2,1,0:T(8,128)}, /*index=5*/f32[8,256,256]{2,1,0:T(8,128)}, s32[]{:T(128)}) while((s32[]{:T(128)}, f32[16,256]{1,0:T(8,128)S(1)}, f32[8,16,256]{2,1,0:T(8,128)}, f32[8,16,256]{2,1,0:T(8,128)S(1)}, ...), condition=%wide.region_13.14_spmd, body=%wide.region_12.13_spmd.sunk | while | flops 25169920 | bytes 624717 | solution.py:42
  122.6 1.9 bitcast_dynamic-update-slice_fusion.17
  125.8 1.9 bitcast_dynamic-update-slice_fusion.17
  129.0 1.9 bitcast_dynamic-update-slice_fusion.17
  132.1 1.9 bitcast_dynamic-update-slice_fusion.17
  135.3 1.9 bitcast_dynamic-update-slice_fusion.17
  138.4 1.9 bitcast_dynamic-update-slice_fusion.17
  145.5 20.4 %while.289 = (s32[]{:T(128)}, f32[16,256]{1,0:T(8,128)S(1)}, f32[8,16,256]{2,1,0:T(8,128)S(1)}, f32[8,256,256]{2,1,0:T(8,128)}, f32[8,256,256]{2,1,0:T(8,128)}, /*index=5*/s32[]{:T(128)}) while((s32[]{:T(128)}, f32[16,256]{1,0:T(8,128)S(1)}, f32[8,16,256]{2,1,0:T(8,128)S(1)}, f32[8,256,256]{2,1,0:T(8,128)}, f32[8,256,256]{2,1,0:T(8,128)}, ...), condition=%wide.region_15.16_spmd, body=%wide.region_14.15_spmd.sunk | while | flops 25169920 | bytes 607813 | solution.py:42
  166.0 5.7 %all-gather.3 = f32[64,256]{1,0:T(8,128)S(1)} all-gather(f32[16,256]{1,0:T(8,128)S(1)} %get-tuple-element.858), channel_id=5, replica_groups=mesh['grp'=2,'lvl'=4,'col'=4] {'lvl'}, dimensions={0}, use_global_device_ids=true | all-gather | bytes 81920 | tf_op jit(solution)/shard_map/all_gather | solution.py:20
  173.4 25.3 %while.291 = (s32[]{:T(128)}, f32[16,256]{1,0:T(8,128)S(1)}, f32[8,16,256]{2,1,0:T(8,128)}, f32[8,16,256]{2,1,0:T(8,128)S(1)}, f32[8,256,256]{2,1,0:T(8,128)}, /*index=5*/f32[8,256,256]{2,1,0:T(8,128)}, s32[]{:T(128)}) while((s32[]{:T(128)}, f32[16,256]{1,0:T(8,128)S(1)}, f32[8,16,256]{2,1,0:T(8,128)}, f32[8,16,256]{2,1,0:T(8,128)S(1)}, ...), condition=%wide.region_19.20_spmd, body=%wide.region_18.19_spmd.sunk | while | flops 25169920 | bytes 624717 | solution.py:42
  174.6 1.9 bitcast_dynamic-update-slice_fusion.18
  177.8 1.9 bitcast_dynamic-update-slice_fusion.18
  181.0 1.9 bitcast_dynamic-update-slice_fusion.18
  184.1 1.9 bitcast_dynamic-update-slice_fusion.18
  187.3 1.9 bitcast_dynamic-update-slice_fusion.18
  190.4 1.9 bitcast_dynamic-update-slice_fusion.18
  203.9 20.4 %while.292 = (s32[]{:T(128)}, f32[16,256]{1,0:T(8,128)S(1)}, f32[8,16,256]{2,1,0:T(8,128)S(1)}, f32[8,256,256]{2,1,0:T(8,128)}, f32[8,256,256]{2,1,0:T(8,128)}, /*index=5*/s32[]{:T(128)}) while((s32[]{:T(128)}, f32[16,256]{1,0:T(8,128)S(1)}, f32[8,16,256]{2,1,0:T(8,128)S(1)}, f32[8,256,256]{2,1,0:T(8,128)}, f32[8,256,256]{2,1,0:T(8,128)}, ...), condition=%wide.region_21.22_spmd, body=%wide.region_20.21_spmd.sunk | while | flops 25169920 | bytes 607813 | solution.py:42
  224.3 5.8 %all-gather.4 = f32[64,256]{1,0:T(8,128)S(1)} all-gather(f32[16,256]{1,0:T(8,128)S(1)} %get-tuple-element.861), channel_id=6, replica_groups=mesh['grp'=2,'lvl'=4,'col'=4] {'lvl'}, dimensions={0}, use_global_device_ids=true | all-gather | bytes 81920 | tf_op jit(solution)/shard_map/all_gather | solution.py:20
  232.0 25.3 %while.294 = (s32[]{:T(128)}, f32[16,256]{1,0:T(8,128)S(1)}, f32[8,16,256]{2,1,0:T(8,128)}, f32[8,16,256]{2,1,0:T(8,128)S(1)}, f32[8,256,256]{2,1,0:T(8,128)}, /*index=5*/f32[8,256,256]{2,1,0:T(8,128)}, s32[]{:T(128)}) while((s32[]{:T(128)}, f32[16,256]{1,0:T(8,128)S(1)}, f32[8,16,256]{2,1,0:T(8,128)}, f32[8,16,256]{2,1,0:T(8,128)S(1)}, ...), condition=%wide.region_25.26_spmd, body=%wide.region_24.25_spmd.sunk | while | flops 25169920 | bytes 624717 | solution.py:42
  233.3 1.9 bitcast_dynamic-update-slice_fusion.19
  236.4 1.9 bitcast_dynamic-update-slice_fusion.19
  249.1 1.9 bitcast_dynamic-update-slice_fusion.19
  252.2 1.9 bitcast_dynamic-update-slice_fusion.19
  255.4 1.9 bitcast_dynamic-update-slice_fusion.19
  262.5 20.4 %while.295 = (s32[]{:T(128)}, f32[16,256]{1,0:T(8,128)S(1)}, f32[8,16,256]{2,1,0:T(8,128)S(1)}, f32[8,256,256]{2,1,0:T(8,128)}, f32[8,256,256]{2,1,0:T(8,128)}, /*index=5*/s32[]{:T(128)}) while((s32[]{:T(128)}, f32[16,256]{1,0:T(8,128)S(1)}, f32[8,16,256]{2,1,0:T(8,128)S(1)}, f32[8,256,256]{2,1,0:T(8,128)}, f32[8,256,256]{2,1,0:T(8,128)}, ...), condition=%wide.region_27.28_spmd, body=%wide.region_26.27_spmd.sunk | while | flops 25169920 | bytes 607813 | solution.py:42
  282.9 5.8 %all-gather.5 = f32[64,256]{1,0:T(8,128)S(1)} all-gather(f32[16,256]{1,0:T(8,128)S(1)} %get-tuple-element.864), channel_id=7, replica_groups=mesh['grp'=2,'lvl'=4,'col'=4] {'lvl'}, dimensions={0}, use_global_device_ids=true | all-gather | bytes 81920 | tf_op jit(solution)/shard_map/all_gather | solution.py:20
  290.5 25.3 %while.297 = (s32[]{:T(128)}, f32[16,256]{1,0:T(8,128)S(1)}, f32[8,16,256]{2,1,0:T(8,128)}, f32[8,16,256]{2,1,0:T(8,128)S(1)}, f32[8,256,256]{2,1,0:T(8,128)}, /*index=5*/f32[8,256,256]{2,1,0:T(8,128)}, s32[]{:T(128)}) while((s32[]{:T(128)}, f32[16,256]{1,0:T(8,128)S(1)}, f32[8,16,256]{2,1,0:T(8,128)}, f32[8,16,256]{2,1,0:T(8,128)S(1)}, ...), condition=%wide.region_31.32_spmd, body=%wide.region_30.31_spmd.sunk | while | flops 25169920 | bytes 624717 | solution.py:42
  291.8 1.9 bitcast_dynamic-update-slice_fusion.20
  294.9 1.9 bitcast_dynamic-update-slice_fusion.20
  298.1 1.9 bitcast_dynamic-update-slice_fusion.20
  301.2 1.9 bitcast_dynamic-update-slice_fusion.20
  321.0 20.4 %while.298 = (s32[]{:T(128)}, f32[16,256]{1,0:T(8,128)S(1)}, f32[8,16,256]{2,1,0:T(8,128)S(1)}, f32[8,256,256]{2,1,0:T(8,128)}, f32[8,256,256]{2,1,0:T(8,128)}, /*index=5*/s32[]{:T(128)}) while((s32[]{:T(128)}, f32[16,256]{1,0:T(8,128)S(1)}, f32[8,16,256]{2,1,0:T(8,128)S(1)}, f32[8,256,256]{2,1,0:T(8,128)}, f32[8,256,256]{2,1,0:T(8,128)}, ...), condition=%wide.region_33.34_spmd, body=%wide.region_32.33_spmd.sunk | while | flops 25169920 | bytes 607813 | solution.py:42
  341.4 5.8 %all-gather.6 = f32[64,256]{1,0:T(8,128)S(1)} all-gather(f32[16,256]{1,0:T(8,128)S(1)} %get-tuple-element.867), channel_id=8, replica_groups=mesh['grp'=2,'lvl'=4,'col'=4] {'lvl'}, dimensions={0}, use_global_device_ids=true | all-gather | bytes 81920 | tf_op jit(solution)/shard_map/all_gather | solution.py:20
  349.0 25.3 %while.300 = (s32[]{:T(128)}, f32[16,256]{1,0:T(8,128)S(1)}, f32[8,16,256]{2,1,0:T(8,128)}, f32[8,16,256]{2,1,0:T(8,128)S(1)}, f32[8,256,256]{2,1,0:T(8,128)}, /*index=5*/f32[8,256,256]{2,1,0:T(8,128)}, s32[]{:T(128)}) while((s32[]{:T(128)}, f32[16,256]{1,0:T(8,128)S(1)}, f32[8,16,256]{2,1,0:T(8,128)}, f32[8,16,256]{2,1,0:T(8,128)S(1)}, ...), condition=%wide.region_37.38_spmd, body=%wide.region_36.37_spmd.sunk | while | flops 25169920 | bytes 624717 | solution.py:42
  379.5 20.4 %while.301 = (s32[]{:T(128)}, f32[16,256]{1,0:T(8,128)S(1)}, f32[8,16,256]{2,1,0:T(8,128)S(1)}, f32[8,256,256]{2,1,0:T(8,128)}, f32[8,256,256]{2,1,0:T(8,128)}, /*index=5*/s32[]{:T(128)}) while((s32[]{:T(128)}, f32[16,256]{1,0:T(8,128)S(1)}, f32[8,16,256]{2,1,0:T(8,128)S(1)}, f32[8,256,256]{2,1,0:T(8,128)}, f32[8,256,256]{2,1,0:T(8,128)}, ...), condition=%wide.region_39.40_spmd, body=%wide.region_38.39_spmd.sunk | while | flops 25169920 | bytes 607813 | solution.py:42
  399.9 5.8 %all-gather.7 = f32[64,256]{1,0:T(8,128)S(1)} all-gather(f32[16,256]{1,0:T(8,128)S(1)} %get-tuple-element.870), channel_id=9, replica_groups=mesh['grp'=2,'lvl'=4,'col'=4] {'lvl'}, dimensions={0}, use_global_device_ids=true | all-gather | bytes 81920 | tf_op jit(solution)/shard_map/all_gather | solution.py:20
  407.4 25.3 %while.303 = (s32[]{:T(128)}, f32[16,256]{1,0:T(8,128)S(1)}, f32[8,16,256]{2,1,0:T(8,128)}, f32[8,16,256]{2,1,0:T(8,128)S(1)}, f32[8,256,256]{2,1,0:T(8,128)}, /*index=5*/f32[8,256,256]{2,1,0:T(8,128)}, s32[]{:T(128)}) while((s32[]{:T(128)}, f32[16,256]{1,0:T(8,128)S(1)}, f32[8,16,256]{2,1,0:T(8,128)}, f32[8,16,256]{2,1,0:T(8,128)S(1)}, ...), condition=%wide.region_43.44_spmd, body=%wide.region_42.43_spmd.sunk | while | flops 25169920 | bytes 624717 | solution.py:42
  438.0 20.4 %while.304 = (s32[]{:T(128)}, f32[16,256]{1,0:T(8,128)S(1)}, f32[8,16,256]{2,1,0:T(8,128)S(1)}, f32[8,256,256]{2,1,0:T(8,128)}, f32[8,256,256]{2,1,0:T(8,128)}, /*index=5*/s32[]{:T(128)}) while((s32[]{:T(128)}, f32[16,256]{1,0:T(8,128)S(1)}, f32[8,16,256]{2,1,0:T(8,128)S(1)}, f32[8,256,256]{2,1,0:T(8,128)}, f32[8,256,256]{2,1,0:T(8,128)}, ...), condition=%wide.region_45.46_spmd, body=%wide.region_44.45_spmd.sunk | while | flops 25169920 | bytes 607813 | solution.py:42
  458.4 5.8 %all-gather.8 = f32[64,256]{1,0:T(8,128)S(1)} all-gather(f32[16,256]{1,0:T(8,128)S(1)} %get-tuple-element.873), channel_id=10, replica_groups=mesh['grp'=2,'lvl'=4,'col'=4] {'lvl'}, dimensions={0}, use_global_device_ids=true | all-gather | bytes 81920 | tf_op jit(solution)/shard_map/all_gather | solution.py:20
  465.3 20.4 %while.306 = (s32[]{:T(128)}, f32[16,256]{1,0:T(8,128)S(1)}, f32[8,16,256]{2,1,0:T(8,128)S(1)}, f32[8,16,256]{2,1,0:T(8,128)S(1)}, f32[8,256,256]{2,1,0:T(8,128)}, /*index=5*/f32[8,256,256]{2,1,0:T(8,128)}, s32[]{:T(128)}) while((s32[]{:T(128)}, f32[16,256]{1,0:T(8,128)S(1)}, f32[8,16,256]{2,1,0:T(8,128)S(1)}, ...), condition=%wide.region_49.50_spmd, body=%wide.region_48.49_spmd.sunk | while | flops 25169920 | bytes 624717 | solution.py:42
  (381 shorter events, 389.9 us)
Async XLA Ops:
  6.5 25.1 %copy-start = (f32[8,256,256]{2,1,0:T(8,128)S(1)}, f32[8,256,256]{2,1,0:T(8,128)}, u32[]{:S(2)}) copy-start(f32[8,256,256]{2,1,0:T(8,128)} %param.56) | copy-start | bytes 6291460
  6.5 52.5 %all-gather.11.cloned.1.call-start = ((), (), s32[]{:S(2)}) async-start(), calls=%async_computation | async-start | bytes 1310720 | tf_op jit(solution)/shard_map/all_gather | solution.py:20
  6.5 25.1 %collective-permute-start = (f32[16,256]{1,0:T(8,128)S(1)}, f32[16,256]{1,0:T(8,128)S(1)}, u32[]{:S(2)}, u32[]{:S(2)}) collective-permute-start(f32[16,256]{1,0:T(8,128)S(1)} %broadcast.8), channel_id=1, source_target_pairs={{4,0},{8,4},{12,8},{5,1},{9,5},{13,9},{6,2},{10,6},{14,10},{7,3},{... | collective-permute-start | bytes 49160 | tf_op jit(solution)/shard_map/ppermute | solution.py:15
  9.3 22.4 %copy-start.3 = (f32[8,16,256]{2,1,0:T(8,128)S(1)}, f32[8,16,256]{2,1,0:T(8,128)}, u32[]{:S(2)}) copy-start(f32[8,16,256]{2,1,0:T(8,128)} %param.57) | copy-start | bytes 393220
  30.9 0.7 copy-start.2
  83.5 2.1 collective-permute-start.1
  85.6 27.7 %copy-start.1 = (f32[4,256,256]{2,1,0:T(8,128)S(1)}, f32[4,256,256]{2,1,0:T(8,128)}, u32[]{:S(2)}) copy-start(f32[4,256,256]{2,1,0:T(8,128)} %get-tuple-element.2566) | copy-start | bytes 3145732
  141.1 2.6 collective-permute-start.2
  199.4 2.6 collective-permute-start.3
  258.0 2.6 collective-permute-start.4
  316.5 2.6 collective-permute-start.5
  375.0 2.6 collective-permute-start.6
  433.5 2.6 collective-permute-start.7
  485.7 0.7 copy-start.4
Sparse Core Ops, SparseCore 0:
  31.7 16.8 all-gather.10
where the time goes:
time: 503 us; the launch traced here: 493 us
  matrix products  394 us (78%)
  blocking collectives  45.5 us (9%)
  local copies, waits for them, and re-layouts  16 us (3%)
  starting transfers between devices  14.3 us (3%)
  between operations  13.8 us (3%)
  loops' own time  8.79 us (2%)
    dot_general x280, matrix products, apply_right(): return jnp.einsum('km,pm->kp', vector, matrix, precision=PRECISE)  358 us
    all_gather x8, blocking collectives, entering_2(): gathered = jax.tree.map(lambda a: lax.all_gather(a, axis), part)  45.5 us
    dot_general x8, matrix products, local(): jnp.einsum('lkm,lpm->lkp', beyond, up_block, precision=PRECISE)  14.7 us
    ppermute x8, starting transfers between devices, from_behind(): lax.ppermute(value, axis, [(source, source + steps) for source in range(f...  14.3 us
    dot_general x8, matrix products, compose(): jnp.matmul(down_here, product, precision=PRECISE)  10.7 us
    dot_general x8, matrix products, compose(): jnp.matmul(inv_here, jnp.matmul(down_here, product, precision=PRECISE), p...  10.7 us
  transfers between devices with their start and end apart: 9, of which 1 were waited for; matrix products, arithmetic and copies ran while one was open for 10% of the time, Pallas kernels for 0%

commit v1 on v0

v1 whole, which is shorter than its diff:
```python
import functools

import jax
import jax.numpy as jnp
from jax import lax
from jax.experimental import pallas as pl
from jax.experimental.pallas import tpu as pltpu
from jax.sharding import PartitionSpec as P

SWEEPS = 8
CHUNK = 4
CHUNKS = SWEEPS // CHUNK
AHEAD = SWEEPS - 1
F32 = jnp.float32
BF16 = jnp.bfloat16


def resident(shape, dtype):
    return pltpu.VMEM(shape, dtype)


def pin(x, memory=pltpu.VMEM):
    return pltpu.with_memory_space_constraint(x, memory)


def split(x):
    high = x.astype(BF16)
    return high, (x - high.astype(F32)).astype(BF16)


def dot(a, b):
    return jnp.dot(a, b, preferred_element_type=F32)


def dot_parts(a, b):
    return dot(a[0], b[0]) + (dot(a[0], b[1]) + dot(a[1], b[0]))


def prepare_kernel(
    inv_hbm, down_hbm, up_hbm, reward,
    a_high, a_low, b_high, b_low, base, kept,
    inv, down, up, x_high, x_low, sems,
):
    levels = inv.shape[0]
    phases = inv.shape[1]
    columns = reward.shape[1]

    def copies(i):
        return [
            pltpu.make_async_copy(source.at[i], target.at[i], sems.at[n, i])
            for n, (source, target) in enumerate(((inv_hbm, inv), (down_hbm, down), (up_hbm, up)))
        ]

    for i in range(levels):
        for copy in copies(i):
            copy.start()

    def products(i, _):
        for copy in copies(i):
            copy.wait()
        here = split(inv[i])
        a_high[i], a_low[i] = split(dot_parts(here, split(down[i])).T)
        b_high[i], b_low[i] = split(dot_parts(here, split(up[i])).T)
        pay = split(reward[i])
        base[i] = dot_nt(pay[0], here[0]) + (dot_nt(pay[0], here[1]) + dot_nt(pay[1], here[0]))
        return 0

    lax.fori_loop(0, levels, products, 0)

    rows = lax.broadcasted_iota(jnp.int32, (phases, phases), 0)
    lanes = lax.broadcasted_iota(jnp.int32, (phases, phases), 1)
    x_high[...] = jnp.zeros_like(x_high)
    x_low[...] = jnp.zeros_like(x_low)
    x_high[0, 0:phases] = jnp.where(rows == lanes, 1.0, 0.0).astype(BF16)

    def sweep(n, _):
        def level(i, _):
            below = (x_high[i], x_low[i])
            above = (x_high[i + 2], x_low[i + 2])
            new = dot_parts(below, (a_high[i], a_low[i])) + dot_parts(above, (b_high[i], b_low[i]))
            first = new[0:phases]
            second = new[phases : phases + columns] + base[i]
            x_high[i + 1, 0:phases], x_low[i + 1, 0:phases] = split(first)
            x_high[i + 1, phases : phases + columns], x_low[i + 1, phases : phases + columns] = split(second)

            @pl.when(i == 0)
            def _():
                kept[n, 0:phases] = first
                kept[n, phases : phases + columns] = second

            return 0

        lax.fori_loop(0, AHEAD - n, level, 0)

        @pl.when(n == 0)
        def _():
            x_high[0] = jnp.zeros_like(x_high[0])

        return 0

    lax.fori_loop(0, AHEAD, sweep, 0)


def dot_nt(a, b):
    return lax.dot_general(a, b, (((1,), (1,)), ((), ())), preferred_element_type=F32)


def prepare(inverse_diag, down_block, up_block, reward):
    levels, phases, _ = inverse_diag.shape
    columns = reward.shape[1]
    matrix = (levels, phases, phases)
    assert levels >= AHEAD
    vmem = pl.BlockSpec(memory_space=pltpu.VMEM)
    return pl.pallas_call(
        prepare_kernel,
        out_shape=[resident(matrix, BF16)] * 4
        + [
            resident((levels, columns, phases), F32),
            jax.ShapeDtypeStruct((AHEAD, phases + columns, phases), F32),
        ],
        in_specs=[pl.BlockSpec(memory_space=pltpu.HBM)] * 3 + [vmem],
        out_specs=[vmem] * 6,
        scratch_shapes=[pltpu.VMEM(matrix, F32)] * 3
        + [pltpu.VMEM((levels + 2, phases + columns, phases), BF16)] * 2
        + [pltpu.SemaphoreType.DMA((3, levels))],
        compiler_params=pltpu.CompilerParams(vmem_limit_bytes=30 * 2**20),
        name="prepare",
    )(*[pin(x, pltpu.HBM) for x in (inverse_diag, down_block, up_block)], reward)


def stack(x):
    high = x.astype(BF16).astype(F32)
    return jnp.concatenate([high, x - high], axis=0).astype(BF16)


def fold(total):
    half = total.shape[0] // 2
    return total[:half] + total[half:]


def stage_kernel(choices, place, a_high, a_low, b_high, b_low, base, kept, state, entering, earlier, new_state, leaving):
    levels, columns, phases = state.shape

    def apply(x, high, low):
        return dot(x, high) + dot(x, low)

    def chunk_of(chunk):
        first = chunk * CHUNK
        feedback = {j: split(kept[j, 0:phases]) for j in range(first + CHUNK - 1)}
        above = {}
        for n in range(first, first + CHUNK):
            above[n] = jnp.zeros((columns, phases), F32) if n == 0 else kept[n - 1, phases : phases + columns]
        past = {n: stack(earlier[n - first + CHUNK - 1]) for n in range(1, first + 1)}
        for j in range(first + CHUNK - 1) if first else ():
            pairs = [(n, n - j) for n in above if n - j in past]
            if pairs:
                total = apply(jnp.concatenate([past[m] for _, m in pairs], axis=0), *feedback[j])
                for p, (n, _) in enumerate(pairs):
                    above[n] += fold(total[p * 2 * columns : (p + 1) * 2 * columns])

        now = {}
        for i in range(levels):
            now[i, first] = stack(state[i]) if first else None
        for k in range(CHUNK):
            now[-1, first + 1 + k] = stack(entering[k])
        for step in range(levels + 2 * (CHUNK - 1)):
            for k in range(CHUNK):
                i = step - 2 * k
                if not 0 <= i < levels:
                    continue
                n = first + 1 + k
                total = apply(now[i - 1, n], a_high[i], a_low[i])
                if n > 1:
                    over = stack(above[n - 1]) if i == levels - 1 else now[i + 1, n - 1]
                    total += apply(over, b_high[i], b_low[i])
                value = base[i] + fold(total)
                now[i, n] = stack(value)
                if k == CHUNK - 1:
                    new_state[i] = value
                if i == levels - 1:
                    leaving[k] = value
                    for later in range(n, first + CHUNK):
                        above[later] += fold(apply(now[i, n], *feedback[later - n]))

    chunk = place[0]
    for choice in choices:
        pl.when(chunk == choice)(functools.partial(chunk_of, choice))

    @pl.when(functools.reduce(jnp.logical_and, [chunk != choice for choice in choices]))
    def _():
        new_state[...] = state[...]
        leaving[...] = jnp.zeros_like(leaving)


def stage(choices, chunk, weights, kept, state, entering, earlier):
    vmem = pl.BlockSpec(memory_space=pltpu.VMEM)
    weights = [pin(w) for w in weights]
    return pl.pallas_call(
        functools.partial(stage_kernel, choices),
        out_shape=[
            jax.ShapeDtypeStruct(state.shape, F32),
            jax.ShapeDtypeStruct(entering.shape, F32),
        ],
        in_specs=[pl.BlockSpec(memory_space=pltpu.SMEM)] + [vmem] * 9,
        out_specs=[vmem] * 2,
        compiler_params=pltpu.CompilerParams(vmem_limit_bytes=24 * 2**20),
        name="stage",
    )(chunk, *weights, kept, state, entering, earlier)


def local(inverse_diag, down_block, up_block, reward):
    levels, given, phases = reward.shape
    columns = -(-given // 16) * 16
    reward = jnp.pad(reward, ((0, 0), (0, columns - given), (0, 0)))
    count = lax.axis_size("lvl")
    place = lax.axis_index("lvl")
    *weights, kept = prepare(inverse_diag, down_block, up_block, reward)
    kept = lax.ppermute(kept, "lvl", [(d + 1, d) for d in range(count - 1)])
    state = jnp.zeros_like(reward)
    entering = jnp.zeros((CHUNK, columns, phases), F32)
    leaving = entering
    stages = count + CHUNKS - 1
    for step in range(stages):
        choices = [c for c in range(CHUNKS) if 0 <= step - c < count]
        chunk = jnp.reshape(step - place, (1,)).astype(jnp.int32)
        state, leaving_now = stage(choices, chunk, weights, kept, state, entering, leaving)
        leaving = leaving_now
        if step < stages - 1:
            entering = lax.ppermute(leaving, "lvl", [(d, d + 1) for d in range(count - 1)])
    return state[:, :given]


def solution(mesh):
    placed = (
        P(("grp", "lvl"), None, None),
        P(("grp", "lvl"), None, None),
        P(("grp", "lvl"), None, None),
        P(("grp", "lvl"), "col", None),
    )
    return jax.shard_map(
        local, mesh=mesh, in_specs=placed, out_specs=P(("grp", "lvl"), "col", None), check_vma=False
    )
```

time: 503 us -> 104 us (0.21); the launches traced: 493 us -> 103 us
  matrix products: 394 us -> 0 us
  blocking collectives: 45.5 us -> 0 us
  waiting for transfers between devices: 0.84 us -> 41.9 us
  Pallas kernels: 0 us -> 26.5 us
  between operations: 13.8 us -> 0.13 us
  local copies, waits for them, and re-layouts: 16 us -> 26.6 us
  loops' own time: 8.79 us -> 0 us
  starting transfers between devices: 14.3 us -> 7.87 us
    dot_general x304 -> x0, matrix products: 394 us -> none  [the longest x280 358 us: apply_right(): return jnp.einsum('km,pm->kp', vector, matrix, precision=PRECISE)]
    all_gather x8 -> x0, blocking collectives: 45.5 us -> none  [entering_2(): gathered = jax.tree.map(lambda a: lax.all_gather(a, axis), part)]
    ppermute x8 -> x5, waiting for transfers between devices: 0.82 us -> 41.9 us  [the longest x4 38.3 us: local(): lax.ppermute(leaving, 'lvl', [(d, d + 1) for d in range(count - 1)])]
    pallas_call x0 -> x6, Pallas kernels: none -> 26.5 us  [the longest x1 18 us: prepare(): pl.pallas_call(prepare_kernel, out_shape=[resident(matrix, BF16)] * 4 + [...]
    unnamed x10 -> x50, local copies, waits for them, and re-layouts: 1.41 us -> 26.6 us
    another operation x25 -> x0, loops' own time: 8.79 us -> none  [the longest x16 7.71 us: local_sweep(): lax.scan(level_step, entering, (inverse_diag, down_block, base_terms))]
    ppermute x8 -> x5, starting transfers between devices: 14.3 us -> 7.87 us  [the longest x4 5.18 us: local(): lax.ppermute(leaving, 'lvl', [(d, d + 1) for d in range(count - 1)])]
    slice x7 -> x0, local copies, waits for them, and re-layouts: 5.47 us -> none  [local(): beyond = jnp.concatenate([estimate[1:], rim_values[None]], axis=0)]
  transfers between devices with their start and end apart: 9 -> 5, of which waited for: 1 -> 5; matrix products, arithmetic and copies ran while one was open for 10% -> 0% of each run, Pallas kernels for 0% -> 0%
where the time goes in v1:
time: 104 us; the launch traced here: 103 us
  waiting for transfers between devices  41.9 us (40%)
  local copies, waits for them, and re-layouts  26.6 us (26%)
  Pallas kernels  26.5 us (25%)
  starting transfers between devices  7.87 us (8%)
    ppermute x4, waiting for transfers between devices, local(): lax.ppermute(leaving, 'lvl', [(d, d + 1) for d in range(count - 1)])  38.3 us
    unnamed x50, local copies, waits for them, and re-layouts  26.6 us
    pallas_call x1, Pallas kernels, prepare(): pl.pallas_call(prepare_kernel, out_shape=[resident(matrix, BF16)] * 4 + [...  18 us
    pallas_call x5, Pallas kernels, stage(): pl.pallas_call(functools.partial(stage_kernel, choices), out_shape=[jax.S...  8.5 us
    ppermute x4, starting transfers between devices, local(): lax.ppermute(leaving, 'lvl', [(d, d + 1) for d in range(count - 1)])  5.18 us
    ppermute x1, waiting for transfers between devices, local(): kept = lax.ppermute(kept, 'lvl', [(d + 1, d) for d in range(count - 1)])  3.64 us
    ppermute x1, starting transfers between devices, local(): kept = lax.ppermute(kept, 'lvl', [(d + 1, d) for d in range(count - 1)])  2.69 us
  transfers between devices with their start and end apart: 5, of which 5 were waited for; matrix products, arithmetic and copies ran while one was open for 0% of the time, Pallas kernels for 0%

profile of v1, /device:TPU:11, one launch (start us, length us, event | category | flops | bytes accessed | tf_op | source)
XLA Modules:
  0.0 103.0 jit_solution(14182499981187282237)
XLA Ops:
  0.0 0.0 copy-start.18
  0.0 0.9 copy-done.18
  0.9 18.0 %prepare.1 = (bf16[8,256,256]{2,1,0:T(8,128)(2,1)S(1)}, bf16[8,256,256]{2,1,0:T(8,128)(2,1)S(1)}, bf16[8,256,256]{2,1,0:T(8,128)(2,1)S(1)}, bf16[8,256,256]{2,1,...) custom-call(f32[8,256,256]{2,1,0:T(8,128)} %inv_hbm.1, f32[8,256,256]{2,1,0:T(8,128)} %down_hbm.1, ...), custom_call_target="tpu_custom_call" | custom-call | tf_op jit(solution)/shard_map/prepare/pallas_call | solution.py:114
  18.9 0.0 copy-start
  18.9 1.0 copy-done
  19.9 0.0 copy-start.6
  19.9 1.0 copy-done.6
  20.9 0.0 copy-start.12
  20.9 1.0 copy-done.12
  21.9 2.7 %collective-permute-start = (f32[7,272,256]{2,1,0:T(8,128)}, f32[7,272,256]{2,1,0:T(8,128)S(1)}, u32[]{:S(2)}, u32[]{:S(2)}) collective-permute-start(f32[7,272,256]{2,1,0:T(8,128)} %get-tuple-element.25), channel_id=1, source_target_pairs={{4,0},{8,4},{12,8},{5,1},{9,5},{13,9},{6,2},{10,6},{14,10},{7,3},{... | collective-permute-start | bytes 5849096 | tf_op jit(solution)/shard_map/ppermute | solution.py:218
  24.6 3.6 %collective-permute-done.kept = f32[7,272,256]{2,1,0:T(8,128)S(1)} collective-permute-done((f32[7,272,256]{2,1,0:T(8,128)}, f32[7,272,256]{2,1,0:T(8,128)S(1)}, u32[]{:S(2)}, u32[]{:S(2)}) %collective-permute-start) | collective-permute-done | bytes 1949728 | tf_op jit(solution)/shard_map/ppermute | solution.py:218
  28.2 0.0 copy-start.1
  28.2 1.2 %copy-done.1 = bf16[8,256,256]{2,1,0:T(8,128)(2,1)S(1)} copy-done((bf16[8,256,256]{2,1,0:T(8,128)(2,1)S(1)}, bf16[8,256,256]{2,1,0:T(8,128)(2,1)}, u32[]{:S(2)}) %copy-start.1) | copy-done | bytes 1048600
  29.5 0.0 copy-start.7
  29.5 1.2 %copy-done.7 = bf16[8,256,256]{2,1,0:T(8,128)(2,1)S(1)} copy-done((bf16[8,256,256]{2,1,0:T(8,128)(2,1)S(1)}, bf16[8,256,256]{2,1,0:T(8,128)(2,1)}, u32[]{:S(2)}) %copy-start.7) | copy-done | bytes 1048600
  30.7 0.0 copy-start.13
  30.7 1.2 %copy-done.13 = bf16[8,256,256]{2,1,0:T(8,128)(2,1)S(1)} copy-done((bf16[8,256,256]{2,1,0:T(8,128)(2,1)S(1)}, bf16[8,256,256]{2,1,0:T(8,128)(2,1)}, u32[]{:S(2)}) %copy-start.13) | copy-done | bytes 1048600
  31.9 1.3 %collective-permute-start.1 = (f32[4,16,256]{2,1,0:T(8,128)S(1)}, f32[4,16,256]{2,1,0:T(8,128)S(1)}, u32[]{:S(2)}, u32[]{:S(2)}) collective-permute-start(f32[4,16,256]{2,1,0:T(8,128)S(1)} %get-tuple-element.27.earlier), channel_id=1, source_target_pairs={{0,4},{4,8},{8,12},{1,5},{5,9},{9,13},{2,6},{6,10},{10,14},{3,7},{... | collective-permute-start | bytes 196616 | tf_op jit(solution)/shard_map/ppermute | solution.py:229
  33.2 19.9 %collective-permute-done.1.entering = f32[4,16,256]{2,1,0:T(8,128)S(1)} collective-permute-done((f32[4,16,256]{2,1,0:T(8,128)S(1)}, f32[4,16,256]{2,1,0:T(8,128)S(1)}, u32[]{:S(2)}, u32[]{:S(2)}) %collective-permute-start.1) | collective-permute-done | bytes 65568 | tf_op jit(solution)/shard_map/ppermute | solution.py:229
  53.1 0.0 copy-start.19
  53.1 0.6 copy-done.19
  53.7 0.0 copy-start.2
  53.7 1.2 %copy-done.2 = bf16[8,256,256]{2,1,0:T(8,128)(2,1)S(1)} copy-done((bf16[8,256,256]{2,1,0:T(8,128)(2,1)S(1)}, bf16[8,256,256]{2,1,0:T(8,128)(2,1)}, u32[]{:S(2)}) %copy-start.2) | copy-done | bytes 1048600
  54.9 0.0 copy-start.8
  54.9 1.2 %copy-done.8 = bf16[8,256,256]{2,1,0:T(8,128)(2,1)S(1)} copy-done((bf16[8,256,256]{2,1,0:T(8,128)(2,1)S(1)}, bf16[8,256,256]{2,1,0:T(8,128)(2,1)}, u32[]{:S(2)}) %copy-start.8) | copy-done | bytes 1048600
  56.2 1.2 %copy-done.14 = bf16[8,256,256]{2,1,0:T(8,128)(2,1)S(1)} copy-done((bf16[8,256,256]{2,1,0:T(8,128)(2,1)S(1)}, bf16[8,256,256]{2,1,0:T(8,128)(2,1)}, u32[]{:S(2)}) %copy-start.14) | copy-done | bytes 1048600
  57.4 0.8 copy-done.20
  58.2 1.3 %collective-permute-start.2 = (f32[4,16,256]{2,1,0:T(8,128)S(1)}, f32[4,16,256]{2,1,0:T(8,128)S(1)}, u32[]{:S(2)}, u32[]{:S(2)}) collective-permute-start(f32[4,16,256]{2,1,0:T(8,128)S(1)} %get-tuple-element.29.earlier), channel_id=1, source_target_pairs={{0,4},{4,8},{8,12},{1,5},{5,9},{9,13},{2,6},{6,10},{10,14},{3,7},{... | collective-permute-start | bytes 196616 | tf_op jit(solution)/shard_map/ppermute | solution.py:229
  59.6 4.3 %collective-permute-done.2.entering = f32[4,16,256]{2,1,0:T(8,128)S(1)} collective-permute-done((f32[4,16,256]{2,1,0:T(8,128)S(1)}, f32[4,16,256]{2,1,0:T(8,128)S(1)}, u32[]{:S(2)}, u32[]{:S(2)}) %collective-permute-start.2) | collective-permute-done | bytes 65568 | tf_op jit(solution)/shard_map/ppermute | solution.py:229
  63.9 0.6 copy-done.21
  64.5 1.2 %copy-done.3 = bf16[8,256,256]{2,1,0:T(8,128)(2,1)S(1)} copy-done((bf16[8,256,256]{2,1,0:T(8,128)(2,1)S(1)}, bf16[8,256,256]{2,1,0:T(8,128)(2,1)}, u32[]{:S(2)}) %copy-start.3) | copy-done | bytes 1048600
  65.8 1.2 %copy-done.9 = bf16[8,256,256]{2,1,0:T(8,128)(2,1)S(1)} copy-done((bf16[8,256,256]{2,1,0:T(8,128)(2,1)S(1)}, bf16[8,256,256]{2,1,0:T(8,128)(2,1)}, u32[]{:S(2)}) %copy-start.9) | copy-done | bytes 1048600
  67.0 1.2 %copy-done.15 = bf16[8,256,256]{2,1,0:T(8,128)(2,1)S(1)} copy-done((bf16[8,256,256]{2,1,0:T(8,128)(2,1)S(1)}, bf16[8,256,256]{2,1,0:T(8,128)(2,1)}, u32[]{:S(2)}) %copy-start.15) | copy-done | bytes 1048600
  68.2 0.8 copy-done.22
  69.1 1.3 %collective-permute-start.3 = (f32[4,16,256]{2,1,0:T(8,128)S(1)}, f32[4,16,256]{2,1,0:T(8,128)S(1)}, u32[]{:S(2)}, u32[]{:S(2)}) collective-permute-start(f32[4,16,256]{2,1,0:T(8,128)S(1)} %get-tuple-element.31.earlier), channel_id=1, source_target_pairs={{0,4},{4,8},{8,12},{1,5},{5,9},{9,13},{2,6},{6,10},{10,14},{3,7},{... | collective-permute-start | bytes 196616 | tf_op jit(solution)/shard_map/ppermute | solution.py:229
  70.4 9.6 %collective-permute-done.3.entering = f32[4,16,256]{2,1,0:T(8,128)S(1)} collective-permute-done((f32[4,16,256]{2,1,0:T(8,128)S(1)}, f32[4,16,256]{2,1,0:T(8,128)S(1)}, u32[]{:S(2)}, u32[]{:S(2)}) %collective-permute-start.3) | collective-permute-done | bytes 65568 | tf_op jit(solution)/shard_map/ppermute | solution.py:229
  79.9 0.6 copy-done.23
  80.6 1.2 %copy-done.4 = bf16[8,256,256]{2,1,0:T(8,128)(2,1)S(1)} copy-done((bf16[8,256,256]{2,1,0:T(8,128)(2,1)S(1)}, bf16[8,256,256]{2,1,0:T(8,128)(2,1)}, u32[]{:S(2)}) %copy-start.4) | copy-done | bytes 1048600
  81.8 1.2 %copy-done.10 = bf16[8,256,256]{2,1,0:T(8,128)(2,1)S(1)} copy-done((bf16[8,256,256]{2,1,0:T(8,128)(2,1)S(1)}, bf16[8,256,256]{2,1,0:T(8,128)(2,1)}, u32[]{:S(2)}) %copy-start.10) | copy-done | bytes 1048600
  83.0 1.2 %copy-done.16 = bf16[8,256,256]{2,1,0:T(8,128)(2,1)S(1)} copy-done((bf16[8,256,256]{2,1,0:T(8,128)(2,1)S(1)}, bf16[8,256,256]{2,1,0:T(8,128)(2,1)}, u32[]{:S(2)}) %copy-start.16) | copy-done | bytes 1048600
  84.2 0.8 copy-done.24
  85.1 3.8 %stage.8 = (f32[8,16,256]{2,1,0:T(8,128)S(1)}, f32[4,16,256]{2,1,0:T(8,128)S(1)}) custom-call(s32[1]{0:T(128)} %bitcast.1.place, bf16[8,256,256]{2,1,0:T(8,128)(2,1)S(1)} %get-tuple-element.20.a_high, bf16[8,256,256]{2,1,0:T(8,128)(2,1)S(1)} %copy-done.4, bf16[8,256,256]{2,1,0:T(8,128)(2,1)S(1)} %copy-done.10, bf16[8,256,256]{2,1,0:T(8,128)(2,1)S(1)} %copy-done.16, ...), custom_call_target="tpu_custom_call" | custom-call | tf_op jit(solution)/shard_map/stage/pallas_call | solution.py:198
  88.9 1.3 %collective-permute-start.4 = (f32[4,16,256]{2,1,0:T(8,128)S(1)}, f32[4,16,256]{2,1,0:T(8,128)S(1)}, u32[]{:S(2)}, u32[]{:S(2)}) collective-permute-start(f32[4,16,256]{2,1,0:T(8,128)S(1)} %get-tuple-element.33.earlier), channel_id=1, source_target_pairs={{0,4},{4,8},{8,12},{1,5},{5,9},{9,13},{2,6},{6,10},{10,14},{3,7},{... | collective-permute-start | bytes 196616 | tf_op jit(solution)/shard_map/ppermute | solution.py:229
  90.2 4.5 %collective-permute-done.4.entering = f32[4,16,256]{2,1,0:T(8,128)S(1)} collective-permute-done((f32[4,16,256]{2,1,0:T(8,128)S(1)}, f32[4,16,256]{2,1,0:T(8,128)S(1)}, u32[]{:S(2)}, u32[]{:S(2)}) %collective-permute-start.4) | collective-permute-done | bytes 65568 | tf_op jit(solution)/shard_map/ppermute | solution.py:229
  94.7 1.2 %copy-done.5 = bf16[8,256,256]{2,1,0:T(8,128)(2,1)S(1)} copy-done((bf16[8,256,256]{2,1,0:T(8,128)(2,1)S(1)}, bf16[8,256,256]{2,1,0:T(8,128)(2,1)}, u32[]{:S(2)}) %copy-start.5) | copy-done | bytes 1048600
  95.9 1.2 %copy-done.11 = bf16[8,256,256]{2,1,0:T(8,128)(2,1)S(1)} copy-done((bf16[8,256,256]{2,1,0:T(8,128)(2,1)S(1)}, bf16[8,256,256]{2,1,0:T(8,128)(2,1)}, u32[]{:S(2)}) %copy-start.11) | copy-done | bytes 1048600
  97.1 1.2 %copy-done.17 = bf16[8,256,256]{2,1,0:T(8,128)(2,1)S(1)} copy-done((bf16[8,256,256]{2,1,0:T(8,128)(2,1)S(1)}, bf16[8,256,256]{2,1,0:T(8,128)(2,1)}, u32[]{:S(2)}) %copy-start.17) | copy-done | bytes 1048600
  98.3 4.7 %stage.9 = (f32[8,16,256]{2,1,0:T(8,128)}, f32[4,16,256]{2,1,0:T(8,128)}) custom-call(s32[1]{0:T(128)} %bitcast.place, bf16[8,256,256]{2,1,0:T(8,128)(2,1)S(1)} %get-tuple-element.20.a_high, bf16[8,256,256]{2,1,0:T(8,128)(2,1)S(1)} %copy-done.5, bf16[8,256,256]{2,1,0:T(8,128)(2,1)S(1)} %copy-done.11, bf16[8,256,256]{2,1,0:T(8,128)(2,1)S(1)} %copy-done.17, ...), custom_call_target="tpu_custom_call" | custom-call | tf_op jit(solution)/shard_map/stage/pallas_call | solution.py:198
  (20 shorter events, 0.1 us)
Async XLA Ops:
  0.0 0.9 copy-start.18
  18.9 1.0 copy-start
  19.9 1.0 copy-start.6
  20.9 1.0 copy-start.12
  21.9 6.3 %collective-permute-start = (f32[7,272,256]{2,1,0:T(8,128)}, f32[7,272,256]{2,1,0:T(8,128)S(1)}, u32[]{:S(2)}, u32[]{:S(2)}) collective-permute-start(f32[7,272,256]{2,1,0:T(8,128)} %get-tuple-element.25), channel_id=1, source_target_pairs={{4,0},{8,4},{12,8},{5,1},{9,5},{13,9},{6,2},{10,6},{14,10},{7,3},{... | collective-permute-start | bytes 5849096 | tf_op jit(solution)/shard_map/ppermute | solution.py:218
  28.2 1.2 %copy-start.1 = (bf16[8,256,256]{2,1,0:T(8,128)(2,1)S(1)}, bf16[8,256,256]{2,1,0:T(8,128)(2,1)}, u32[]{:S(2)}) copy-start(bf16[8,256,256]{2,1,0:T(8,128)(2,1)} %copy-done) | copy-start | bytes 3145732
  29.5 1.2 %copy-start.7 = (bf16[8,256,256]{2,1,0:T(8,128)(2,1)S(1)}, bf16[8,256,256]{2,1,0:T(8,128)(2,1)}, u32[]{:S(2)}) copy-start(bf16[8,256,256]{2,1,0:T(8,128)(2,1)} %copy-done.6) | copy-start | bytes 3145732
  30.7 1.2 %copy-start.13 = (bf16[8,256,256]{2,1,0:T(8,128)(2,1)S(1)}, bf16[8,256,256]{2,1,0:T(8,128)(2,1)}, u32[]{:S(2)}) copy-start(bf16[8,256,256]{2,1,0:T(8,128)(2,1)} %copy-done.12) | copy-start | bytes 3145732
  31.9 21.2 %collective-permute-start.1 = (f32[4,16,256]{2,1,0:T(8,128)S(1)}, f32[4,16,256]{2,1,0:T(8,128)S(1)}, u32[]{:S(2)}, u32[]{:S(2)}) collective-permute-start(f32[4,16,256]{2,1,0:T(8,128)S(1)} %get-tuple-element.27.earlier), channel_id=1, source_target_pairs={{0,4},{4,8},{8,12},{1,5},{5,9},{9,13},{2,6},{6,10},{10,14},{3,7},{... | collective-permute-start | bytes 196616 | tf_op jit(solution)/shard_map/ppermute | solution.py:229
  53.1 0.6 copy-start.19
  53.7 1.2 %copy-start.2 = (bf16[8,256,256]{2,1,0:T(8,128)(2,1)S(1)}, bf16[8,256,256]{2,1,0:T(8,128)(2,1)}, u32[]{:S(2)}) copy-start(bf16[8,256,256]{2,1,0:T(8,128)(2,1)} %copy-done) | copy-start | bytes 3145732
  54.9 1.2 %copy-start.8 = (bf16[8,256,256]{2,1,0:T(8,128)(2,1)S(1)}, bf16[8,256,256]{2,1,0:T(8,128)(2,1)}, u32[]{:S(2)}) copy-start(bf16[8,256,256]{2,1,0:T(8,128)(2,1)} %copy-done.6) | copy-start | bytes 3145732
  56.2 1.2 %copy-start.14 = (bf16[8,256,256]{2,1,0:T(8,128)(2,1)S(1)}, bf16[8,256,256]{2,1,0:T(8,128)(2,1)}, u32[]{:S(2)}) copy-start(bf16[8,256,256]{2,1,0:T(8,128)(2,1)} %copy-done.12) | copy-start | bytes 3145732
  57.4 0.8 copy-start.20
  58.2 5.7 %collective-permute-start.2 = (f32[4,16,256]{2,1,0:T(8,128)S(1)}, f32[4,16,256]{2,1,0:T(8,128)S(1)}, u32[]{:S(2)}, u32[]{:S(2)}) collective-permute-start(f32[4,16,256]{2,1,0:T(8,128)S(1)} %get-tuple-element.29.earlier), channel_id=1, source_target_pairs={{0,4},{4,8},{8,12},{1,5},{5,9},{9,13},{2,6},{6,10},{10,14},{3,7},{... | collective-permute-start | bytes 196616 | tf_op jit(solution)/shard_map/ppermute | solution.py:229
  63.9 0.6 copy-start.21
  64.5 1.2 %copy-start.3 = (bf16[8,256,256]{2,1,0:T(8,128)(2,1)S(1)}, bf16[8,256,256]{2,1,0:T(8,128)(2,1)}, u32[]{:S(2)}) copy-start(bf16[8,256,256]{2,1,0:T(8,128)(2,1)} %copy-done) | copy-start | bytes 3145732
  65.8 1.2 %copy-start.9 = (bf16[8,256,256]{2,1,0:T(8,128)(2,1)S(1)}, bf16[8,256,256]{2,1,0:T(8,128)(2,1)}, u32[]{:S(2)}) copy-start(bf16[8,256,256]{2,1,0:T(8,128)(2,1)} %copy-done.6) | copy-start | bytes 3145732
  67.0 1.2 %copy-start.15 = (bf16[8,256,256]{2,1,0:T(8,128)(2,1)S(1)}, bf16[8,256,256]{2,1,0:T(8,128)(2,1)}, u32[]{:S(2)}) copy-start(bf16[8,256,256]{2,1,0:T(8,128)(2,1)} %copy-done.12) | copy-start | bytes 3145732
  68.2 0.8 copy-start.22
  69.1 10.9 %collective-permute-start.3 = (f32[4,16,256]{2,1,0:T(8,128)S(1)}, f32[4,16,256]{2,1,0:T(8,128)S(1)}, u32[]{:S(2)}, u32[]{:S(2)}) collective-permute-start(f32[4,16,256]{2,1,0:T(8,128)S(1)} %get-tuple-element.31.earlier), channel_id=1, source_target_pairs={{0,4},{4,8},{8,12},{1,5},{5,9},{9,13},{2,6},{6,10},{10,14},{3,7},{... | collective-permute-start | bytes 196616 | tf_op jit(solution)/shard_map/ppermute | solution.py:229
  79.9 0.6 copy-start.23
  80.6 1.2 %copy-start.4 = (bf16[8,256,256]{2,1,0:T(8,128)(2,1)S(1)}, bf16[8,256,256]{2,1,0:T(8,128)(2,1)}, u32[]{:S(2)}) copy-start(bf16[8,256,256]{2,1,0:T(8,128)(2,1)} %copy-done) | copy-start | bytes 3145732
  81.8 1.2 %copy-start.10 = (bf16[8,256,256]{2,1,0:T(8,128)(2,1)S(1)}, bf16[8,256,256]{2,1,0:T(8,128)(2,1)}, u32[]{:S(2)}) copy-start(bf16[8,256,256]{2,1,0:T(8,128)(2,1)} %copy-done.6) | copy-start | bytes 3145732
  83.0 1.2 %copy-start.16 = (bf16[8,256,256]{2,1,0:T(8,128)(2,1)S(1)}, bf16[8,256,256]{2,1,0:T(8,128)(2,1)}, u32[]{:S(2)}) copy-start(bf16[8,256,256]{2,1,0:T(8,128)(2,1)} %copy-done.12) | copy-start | bytes 3145732
  84.2 0.8 copy-start.24
  88.9 5.8 %collective-permute-start.4 = (f32[4,16,256]{2,1,0:T(8,128)S(1)}, f32[4,16,256]{2,1,0:T(8,128)S(1)}, u32[]{:S(2)}, u32[]{:S(2)}) collective-permute-start(f32[4,16,256]{2,1,0:T(8,128)S(1)} %get-tuple-element.33.earlier), channel_id=1, source_target_pairs={{0,4},{4,8},{8,12},{1,5},{5,9},{9,13},{2,6},{6,10},{10,14},{3,7},{... | collective-permute-start | bytes 196616 | tf_op jit(solution)/shard_map/ppermute | solution.py:229
  94.7 1.2 %copy-start.5 = (bf16[8,256,256]{2,1,0:T(8,128)(2,1)S(1)}, bf16[8,256,256]{2,1,0:T(8,128)(2,1)}, u32[]{:S(2)}) copy-start(bf16[8,256,256]{2,1,0:T(8,128)(2,1)} %copy-done) | copy-start | bytes 3145732
  95.9 1.2 %copy-start.11 = (bf16[8,256,256]{2,1,0:T(8,128)(2,1)S(1)}, bf16[8,256,256]{2,1,0:T(8,128)(2,1)}, u32[]{:S(2)}) copy-start(bf16[8,256,256]{2,1,0:T(8,128)(2,1)} %copy-done.6) | copy-start | bytes 3145732
  97.1 1.2 %copy-start.17 = (bf16[8,256,256]{2,1,0:T(8,128)(2,1)S(1)}, bf16[8,256,256]{2,1,0:T(8,128)(2,1)}, u32[]{:S(2)}) copy-start(bf16[8,256,256]{2,1,0:T(8,128)(2,1)} %copy-done.12) | copy-start | bytes 3145732

commit v2 on v1

v2 whole, which is shorter than its diff:
```python
import functools

import jax
import jax.numpy as jnp
from jax import lax
from jax.experimental import pallas as pl
from jax.experimental.pallas import tpu as pltpu
from jax.sharding import PartitionSpec as P

SWEEPS = 8
CHUNK = 4
CHUNKS = SWEEPS // CHUNK
AHEAD = SWEEPS - 1
SOON = CHUNK - 1
F32 = jnp.float32
BF16 = jnp.bfloat16


def resident(shape, dtype):
    return pltpu.VMEM(shape, dtype)


def pin(x, memory=pltpu.VMEM):
    return pltpu.with_memory_space_constraint(x, memory)


def split(x):
    high = x.astype(BF16)
    return high, (x - high.astype(F32)).astype(BF16)


def dot(a, b):
    return jnp.dot(a, b, preferred_element_type=F32)


def dot_nt(a, b):
    return lax.dot_general(a, b, (((1,), (1,)), ((), ())), preferred_element_type=F32)


def dot_parts(a, b, dot=dot):
    return dot(a[0], b[0]) + (dot(a[0], b[1]) + dot(a[1], b[0]))


def response(first, last, x_high, x_low, a_high, a_low, b_high, b_low, base, kept):
    phases = base.shape[2]
    columns = base.shape[1]
    rows = phases + columns

    def store(i, new):
        top = new[0:phases]
        end = new[phases:rows] + base[i]
        x_high[i, 0:phases], x_low[i, 0:phases] = split(top)
        x_high[i, phases:rows], x_low[i, phases:rows] = split(end)
        return top, end

    def from_below(i):
        return dot_parts((x_high[i - 1], x_low[i - 1]), (a_high[i], a_low[i]))

    def from_above(i):
        return dot_parts((x_high[i + 1], x_low[i + 1]), (b_high[i], b_low[i]))

    for n in range(first, last):
        if n == 0:
            x_high[0, 0:phases], x_low[0, 0:phases] = a_high[0], a_low[0]
            x_high[0, phases:rows], x_low[0, phases:rows] = split(base[0])
            kept[0, 0:phases] = a_high[0].astype(F32) + a_low[0].astype(F32)
            kept[0, phases:rows] = base[0]
        else:
            kept[n - first, 0:phases], kept[n - first, phases:rows] = store(0, from_above(0))

        def level(i, _, n=n):
            store(i, from_below(i) if n == 0 else from_below(i) + from_above(i))
            return 0

        lax.fori_loop(1, AHEAD - n, level, 0)


def prepare_kernel(
    inv_hbm, down_hbm, up_hbm, reward,
    a_high, a_low, b_high, b_low, base, x_high, x_low, kept,
    inv, down, up, sems,
):
    levels = inv.shape[0]

    def copies(i):
        return [
            pltpu.make_async_copy(source.at[i], target.at[i], sems.at[n, i])
            for n, (source, target) in enumerate(((inv_hbm, inv), (down_hbm, down), (up_hbm, up)))
        ]

    for i in range(levels):
        for copy in copies(i):
            copy.start()

    def products(i, _):
        for copy in copies(i):
            copy.wait()
        here = split(inv[i])
        a_high[i], a_low[i] = split(dot_parts(here, split(down[i])).T)
        b_high[i], b_low[i] = split(dot_parts(here, split(up[i])).T)
        base[i] = dot_parts(split(reward[i]), here, dot_nt)
        return 0

    lax.fori_loop(0, levels, products, 0, unroll=2)
    response(0, SOON, x_high, x_low, a_high, a_low, b_high, b_low, base, kept)


VMEM = pl.BlockSpec(memory_space=pltpu.VMEM)


def prepare(inverse_diag, down_block, up_block, reward):
    levels, phases, _ = inverse_diag.shape
    columns = reward.shape[1]
    matrix = (levels, phases, phases)
    assert levels >= AHEAD
    return pl.pallas_call(
        prepare_kernel,
        out_shape=[resident(matrix, BF16)] * 4
        + [resident((levels, columns, phases), F32)]
        + [resident((AHEAD, phases + columns, phases), BF16)] * 2
        + [resident((SOON, phases + columns, phases), F32)],
        in_specs=[pl.BlockSpec(memory_space=pltpu.HBM)] * 3 + [VMEM],
        out_specs=[VMEM] * 8,
        scratch_shapes=[pltpu.VMEM(matrix, F32)] * 3 + [pltpu.SemaphoreType.DMA((3, levels))],
        compiler_params=pltpu.CompilerParams(vmem_limit_bytes=24 * 2**20),
        name="prepare",
    )(*[pin(x, pltpu.HBM) for x in (inverse_diag, down_block, up_block)], reward)


def prepare_rest_kernel(a_high, a_low, b_high, b_low, base, given_high, given_low, kept, x_high, x_low):
    x_high[...] = given_high[...]
    x_low[...] = given_low[...]
    response(SOON, AHEAD, x_high, x_low, a_high, a_low, b_high, b_low, base, kept)


def prepare_rest(weights, x_high, x_low):
    _, rows, phases = x_high.shape
    return pl.pallas_call(
        prepare_rest_kernel,
        out_shape=resident((AHEAD - SOON, rows, phases), F32),
        in_specs=[VMEM] * 7,
        out_specs=VMEM,
        scratch_shapes=[pltpu.VMEM(x_high.shape, BF16)] * 2,
        compiler_params=pltpu.CompilerParams(vmem_limit_bytes=16 * 2**20),
        cost_estimate=pl.CostEstimate(flops=10**10, bytes_accessed=2**24, transcendentals=0),
        name="prepare_rest",
    )(*[pin(w) for w in (*weights, x_high, x_low)])


def stack(x):
    high = x.astype(BF16).astype(F32)
    return jnp.concatenate([high, x - high], axis=0).astype(BF16)


def fold(total):
    half = total.shape[0] // 2
    return total[:half] + total[half:]


def apply(x, high, low):
    return dot(x, high) + dot(x, low)


def stage_kernel(step, choices, has_past, has_soon, has_late, *refs):
    a_high, a_low, b_high, b_low, base, kept_soon = refs[:6]
    rest = list(refs[6:])
    kept_late = rest.pop(0) if has_late else None
    state, earlier = (rest.pop(0), rest.pop(0)) if has_past else (None, None)
    entering = rest.pop(0) if has_soon else None
    new_state, leaving = rest
    levels, columns, phases = base.shape

    def kept(j):
        return kept_soon.at[j] if j < SOON else kept_late.at[j - SOON]

    def chunk_of(chunk):
        first = chunk * CHUNK
        feedback = {j: split(kept(j)[0:phases]) for j in range(first + CHUNK - 1)}
        above = {}
        for n in range(max(first, 1), first + CHUNK):
            above[n] = kept(n - 1)[phases : phases + columns]
        past = {n: stack(earlier[n - first + CHUNK - 1]) for n in range(1, first + 1)}
        for j in range(first + CHUNK - 1) if first else ():
            pairs = [(n, n - j) for n in above if n - j in past]
            if pairs:
                total = apply(jnp.concatenate([past[m] for _, m in pairs], axis=0), *feedback[j])
                for p, (n, _) in enumerate(pairs):
                    above[n] += fold(total[p * 2 * columns : (p + 1) * 2 * columns])

        now = {}
        if first:
            for i in range(levels):
                now[i, first] = stack(state[i])
        if has_soon:
            for k in range(CHUNK):
                now[-1, first + 1 + k] = stack(entering[k])
        for turn in range(levels + 2 * (CHUNK - 1)):
            for k in range(CHUNK):
                i = turn - 2 * k
                if not 0 <= i < levels:
                    continue
                n = first + 1 + k
                value = base[i]
                if (i - 1, n) in now:
                    value += fold(apply(now[i - 1, n], a_high[i], a_low[i]))
                if n > 1:
                    over = stack(above[n - 1]) if i == levels - 1 else now[i + 1, n - 1]
                    value += fold(apply(over, b_high[i], b_low[i]))
                now[i, n] = stack(value)
                if k == CHUNK - 1:
                    new_state[i] = value
                if i == levels - 1:
                    leaving[k] = value
                    for later in range(n, first + CHUNK):
                        above[later] += fold(apply(now[i, n], *feedback[later - n]))

    chunk = step - lax.axis_index("lvl")
    for choice in choices:
        pl.when(chunk == choice)(functools.partial(chunk_of, choice))

    @pl.when(functools.reduce(jnp.logical_and, [chunk != choice for choice in choices]))
    def _():
        new_state[...] = state[...] if has_past else jnp.zeros_like(new_state)
        leaving[...] = jnp.zeros_like(leaving)


def stage(step, choices, weights, kept_soon, kept_late, past, entering, last):
    levels, columns, phases = weights[-1].shape
    operands = [*weights, kept_soon]
    if kept_late is not None:
        operands.append(kept_late)
    if past is not None:
        operands.extend(past)
    if entering is not None:
        operands.append(entering)
    return pl.pallas_call(
        functools.partial(
            stage_kernel, step, choices, past is not None, entering is not None, kept_late is not None
        ),
        out_shape=[
            (jax.ShapeDtypeStruct if last else resident)((levels, columns, phases), F32),
            resident((CHUNK, columns, phases), F32),
        ],
        in_specs=[VMEM] * len(operands),
        out_specs=[VMEM] * 2,
        compiler_params=pltpu.CompilerParams(vmem_limit_bytes=16 * 2**20),
        name="stage",
    )(*[pin(x) for x in operands])


def local(inverse_diag, down_block, up_block, reward):
    given = reward.shape[1]
    columns = -(-given // 16) * 16
    if columns != given:
        reward = jnp.pad(reward, ((0, 0), (0, columns - given), (0, 0)))
    count = lax.axis_size("lvl")
    downward = [(d + 1, d) for d in range(count - 1)]
    upward = [(d, d + 1) for d in range(count - 1)]
    *weights, x_high, x_low, kept_soon = prepare(inverse_diag, down_block, up_block, reward)
    kept_soon = lax.ppermute(kept_soon, "lvl", downward)
    late_here = prepare_rest(weights, x_high, x_low)
    kept_soon, late_here = lax.optimization_barrier((kept_soon, late_here))
    kept_late = lax.ppermute(late_here, "lvl", downward)
    past = entering = None
    stages = count + CHUNKS - 1
    for step in range(stages):
        choices = [c for c in range(CHUNKS) if 0 <= step - c < count]
        late = kept_late if step else None
        state, leaving = past = stage(step, choices, weights, kept_soon, late, past, entering, step == stages - 1)
        if step < stages - 1:
            entering = lax.ppermute(leaving, "lvl", upward)
    return state[:, :given] if columns != given else state


def solution(mesh):
    placed = (
        P(("grp", "lvl"), None, None),
        P(("grp", "lvl"), None, None),
        P(("grp", "lvl"), None, None),
        P(("grp", "lvl"), "col", None),
    )
    return jax.shard_map(
        local, mesh=mesh, in_specs=placed, out_specs=P(("grp", "lvl"), "col", None), check_vma=False
    )
```

time: 104 us -> 72.1 us (0.69)
  local copies, waits for them, and re-layouts: 26.6 us -> 0.9 us
  waiting for transfers between devices: 41.9 us -> 31.3 us
  starting transfers between devices: 7.87 us -> 16 us
  Pallas kernels: 26.5 us -> 23.5 us
    unnamed x50 -> x2, local copies, waits for them, and re-layouts: 26.6 us -> 0.9 us
    ppermute x5 -> x6, waiting for transfers between devices: 41.9 us -> 31.3 us  [the longest x4 31.3 us: local(): entering = lax.ppermute(leaving, 'lvl', upward)]
    ppermute x5 -> x6, starting transfers between devices: 7.87 us -> 16 us  [the longest x1 8.23 us: local(): kept_late = lax.ppermute(late_here, 'lvl', downward)]
    pallas_call x1, Pallas kernels: 18 us -> 11.3 us  [prepare(): pl.pallas_call(prepare_kernel, out_shape=[resident(matrix, BF16)] * 4 + [...]
    pallas_call x5 -> x6, Pallas kernels: 8.5 us -> 12.2 us  [the longest x5 8.54 us: stage(): pl.pallas_call(functools.partial(stage_kernel, step, choices, past is not...]
  transfers between devices with their start and end apart: 5 -> 6, of which waited for: 5 -> 4; matrix products, arithmetic and copies ran while one was open for 0% -> 0% of each run, Pallas kernels for 0% -> 5%
where the time goes in v2:
time: 72.1 us; the launch traced here: 71.9 us
  waiting for transfers between devices  31.3 us (43%)
  Pallas kernels  23.5 us (33%)
  starting transfers between devices  16 us (22%)
  local copies, waits for them, and re-layouts  0.9 us (1%)
    ppermute x4, waiting for transfers between devices, local(): entering = lax.ppermute(leaving, 'lvl', upward)  31.3 us
    pallas_call x1, Pallas kernels, prepare(): pl.pallas_call(prepare_kernel, out_shape=[resident(matrix, BF16)] * 4 + [...  11.3 us
    pallas_call x5, Pallas kernels, stage(): pl.pallas_call(functools.partial(stage_kernel, step, choices, past is not...  8.54 us
    ppermute x1, starting transfers between devices, local(): kept_late = lax.ppermute(late_here, 'lvl', downward)  8.23 us
    ppermute x4, starting transfers between devices, local(): entering = lax.ppermute(leaving, 'lvl', upward)  5.18 us
    pallas_call x1, Pallas kernels, prepare_rest(): pl.pallas_call(prepare_rest_kernel, out_shape=resident((AHEAD - SOON, row...  3.69 us
    ppermute x1, starting transfers between devices, local(): kept_soon = lax.ppermute(kept_soon, 'lvl', downward)  2.64 us
  transfers between devices with their start and end apart: 6, of which 4 were waited for; matrix products, arithmetic and copies ran while one was open for 0% of the time, Pallas kernels for 5%

profile of v2, /device:TPU:11, one launch (start us, length us, event | category | flops | bytes accessed | tf_op | source)
XLA Modules:
  0.0 71.9 jit_solution(7451898532102400435)
XLA Ops:
  0.0 0.0 copy-start
  0.0 0.9 %copy-done = f32[8,16,256]{2,1,0:T(8,128)S(1)} copy-done((f32[8,16,256]{2,1,0:T(8,128)S(1)}, f32[8,16,256]{2,1,0:T(8,128)}, u32[]{:S(2)}) %copy-start) | copy-done | bytes 131096
  0.9 11.3 %prepare.1 = (bf16[8,256,256]{2,1,0:T(8,128)(2,1)S(1)}, bf16[8,256,256]{2,1,0:T(8,128)(2,1)S(1)}, bf16[8,256,256]{2,1,0:T(8,128)(2,1)S(1)}, bf16[8,256,256]{2,1,...) custom-call(f32[8,256,256]{2,1,0:T(8,128)} %inv_hbm.1, ...), custom_call_target="tpu_custom_call" | custom-call | tf_op jit(solution)/shard_map/prepare/pallas_call | solution.py:116
  12.2 2.6 %collective-permute-start = (f32[3,272,256]{2,1,0:T(8,128)S(1)}, f32[3,272,256]{2,1,0:T(8,128)S(1)}, u32[]{:S(2)}, u32[]{:S(2)}) collective-permute-start(f32[3,272,256]{2,1,0:T(8,128)S(1)} %get-tuple-element.29), channel_id=1, source_target_pairs={{4,0},{8,4},{12,8},{5,1},{9,5},{13,9},{6,2},{10,6},{14,10},{7,3},{... | collective-permute-start | bytes 2506760 | tf_op jit(solution)/shard_map/ppermute | solution.py:260
  14.8 3.7 %prepare_rest.1 = f32[4,272,256]{2,1,0:T(8,128)S(1)} custom-call(bf16[8,256,256]{2,1,0:T(8,128)(2,1)S(1)} %get-tuple-element.24.a_high.refs_0_, bf16[8,256,256]{2,1,0:T(8,128)(2,1)S(1)} %get-tuple-element.25.a_low.refs_1_, bf16[8,256,256]{2,1,0:T(8,128)(2,1)S(1)} %get-tuple-element.26.b_high.refs_2_, ...), custom_call_target="tpu_custom_call" | custom-call | flops 10000000000 | bytes 16777216 | tf_op jit(solution)/shard_map/prepare_rest/pallas_call | solution.py:138
  18.5 0.0 collective-permute-done.refs_5_
  18.5 8.2 %collective-permute-start.1 = (f32[4,272,256]{2,1,0:T(8,128)S(1)}, f32[4,272,256]{2,1,0:T(8,128)S(1)}, u32[]{:S(2)}, u32[]{:S(2)}) collective-permute-start(f32[4,272,256]{2,1,0:T(8,128)S(1)} %prepare_rest.1), channel_id=1, source_target_pairs={{4,0},{8,4},{12,8},{5,1},{9,5},{13,9},{6,2},{10,6},{14,10},{7,3},{... | collective-permute-start | bytes 3342344 | tf_op jit(solution)/shard_map/ppermute | solution.py:263
  26.8 1.3 %collective-permute-start.2 = (f32[4,16,256]{2,1,0:T(8,128)S(1)}, f32[4,16,256]{2,1,0:T(8,128)S(1)}, u32[]{:S(2)}, u32[]{:S(2)}) collective-permute-start(f32[4,16,256]{2,1,0:T(8,128)S(1)} %get-tuple-element.35.refs_8_), channel_id=1, source_target_pairs={{0,4},{4,8},{8,12},{1,5},{5,9},{9,13},{2,6},{6,10},{10,14},{3,7},{... | collective-permute-start | bytes 196616 | tf_op jit(solution)/shard_map/ppermute | solution.py:271
  28.1 3.2 %collective-permute-done.2.refs_9_ = f32[4,16,256]{2,1,0:T(8,128)S(1)} collective-permute-done((f32[4,16,256]{2,1,0:T(8,128)S(1)}, f32[4,16,256]{2,1,0:T(8,128)S(1)}, u32[]{:S(2)}, u32[]{:S(2)}) %collective-permute-start.2) | collective-permute-done | bytes 65568 | tf_op jit(solution)/shard_map/ppermute | solution.py:271
  31.3 0.0 collective-permute-done.1.refs_6_
  31.3 1.3 %collective-permute-start.3 = (f32[4,16,256]{2,1,0:T(8,128)S(1)}, f32[4,16,256]{2,1,0:T(8,128)S(1)}, u32[]{:S(2)}, u32[]{:S(2)}) collective-permute-start(f32[4,16,256]{2,1,0:T(8,128)S(1)} %get-tuple-element.37.refs_8_), channel_id=1, source_target_pairs={{0,4},{4,8},{8,12},{1,5},{5,9},{9,13},{2,6},{6,10},{10,14},{3,7},{... | collective-permute-start | bytes 196616 | tf_op jit(solution)/shard_map/ppermute | solution.py:271
  32.6 11.7 %collective-permute-done.3.refs_9_ = f32[4,16,256]{2,1,0:T(8,128)S(1)} collective-permute-done((f32[4,16,256]{2,1,0:T(8,128)S(1)}, f32[4,16,256]{2,1,0:T(8,128)S(1)}, u32[]{:S(2)}, u32[]{:S(2)}) %collective-permute-start.3) | collective-permute-done | bytes 65568 | tf_op jit(solution)/shard_map/ppermute | solution.py:271
  44.3 1.3 %collective-permute-start.4 = (f32[4,16,256]{2,1,0:T(8,128)S(1)}, f32[4,16,256]{2,1,0:T(8,128)S(1)}, u32[]{:S(2)}, u32[]{:S(2)}) collective-permute-start(f32[4,16,256]{2,1,0:T(8,128)S(1)} %get-tuple-element.39.refs_8_), channel_id=1, source_target_pairs={{0,4},{4,8},{8,12},{1,5},{5,9},{9,13},{2,6},{6,10},{10,14},{3,7},{... | collective-permute-start | bytes 196616 | tf_op jit(solution)/shard_map/ppermute | solution.py:271
  45.6 12.0 %collective-permute-done.4.refs_9_ = f32[4,16,256]{2,1,0:T(8,128)S(1)} collective-permute-done((f32[4,16,256]{2,1,0:T(8,128)S(1)}, f32[4,16,256]{2,1,0:T(8,128)S(1)}, u32[]{:S(2)}, u32[]{:S(2)}) %collective-permute-start.4) | collective-permute-done | bytes 65568 | tf_op jit(solution)/shard_map/ppermute | solution.py:271
  57.6 3.8 %stage.8 = (f32[8,16,256]{2,1,0:T(8,128)S(1)}, f32[4,16,256]{2,1,0:T(8,128)S(1)}) custom-call(bf16[8,256,256]{2,1,0:T(8,128)(2,1)S(1)} %get-tuple-element.24.a_high.refs_0_, bf16[8,256,256]{2,1,0:T(8,128)(2,1)S(1)} %get-tuple-element.25.a_low.refs_1_, bf16[8,256,256]{2,1,0:T(8,128)(2,1)S(1)} %get-tuple-element.26.b_high.refs_2_, ...), custom_call_target="tpu_custom_call" | custom-call | tf_op jit(solution)/shard_map/stage/pallas_call | solution.py:236
  61.4 1.3 %collective-permute-start.5 = (f32[4,16,256]{2,1,0:T(8,128)S(1)}, f32[4,16,256]{2,1,0:T(8,128)S(1)}, u32[]{:S(2)}, u32[]{:S(2)}) collective-permute-start(f32[4,16,256]{2,1,0:T(8,128)S(1)} %get-tuple-element.41.refs_8_), channel_id=1, source_target_pairs={{0,4},{4,8},{8,12},{1,5},{5,9},{9,13},{2,6},{6,10},{10,14},{3,7},{... | collective-permute-start | bytes 196616 | tf_op jit(solution)/shard_map/ppermute | solution.py:271
  62.7 4.5 %collective-permute-done.5.refs_9_ = f32[4,16,256]{2,1,0:T(8,128)S(1)} collective-permute-done((f32[4,16,256]{2,1,0:T(8,128)S(1)}, f32[4,16,256]{2,1,0:T(8,128)S(1)}, u32[]{:S(2)}, u32[]{:S(2)}) %collective-permute-start.5) | collective-permute-done | bytes 65568 | tf_op jit(solution)/shard_map/ppermute | solution.py:271
  67.2 4.7 %stage.9 = (f32[8,16,256]{2,1,0:T(8,128)}, f32[4,16,256]{2,1,0:T(8,128)}) custom-call(bf16[8,256,256]{2,1,0:T(8,128)(2,1)S(1)} %get-tuple-element.24.a_high.refs_0_, bf16[8,256,256]{2,1,0:T(8,128)(2,1)S(1)} %get-tuple-element.25.a_low.refs_1_, bf16[8,256,256]{2,1,0:T(8,128)(2,1)S(1)} %get-tuple-element.26.b_high.refs_2_, ...), custom_call_target="tpu_custom_call" | custom-call | tf_op jit(solution)/shard_map/stage/pallas_call | solution.py:236
  (3 shorter events, 0.1 us)
Async XLA Ops:
  0.0 0.9 %copy-start = (f32[8,16,256]{2,1,0:T(8,128)S(1)}, f32[8,16,256]{2,1,0:T(8,128)}, u32[]{:S(2)}) copy-start(f32[8,16,256]{2,1,0:T(8,128)} %reward.1) | copy-start | bytes 393220
  12.2 6.3 %collective-permute-start = (f32[3,272,256]{2,1,0:T(8,128)S(1)}, f32[3,272,256]{2,1,0:T(8,128)S(1)}, u32[]{:S(2)}, u32[]{:S(2)}) collective-permute-start(f32[3,272,256]{2,1,0:T(8,128)S(1)} %get-tuple-element.29), channel_id=1, source_target_pairs={{4,0},{8,4},{12,8},{5,1},{9,5},{13,9},{6,2},{10,6},{14,10},{7,3},{... | collective-permute-start | bytes 2506760 | tf_op jit(solution)/shard_map/ppermute | solution.py:260
  18.5 12.8 %collective-permute-start.1 = (f32[4,272,256]{2,1,0:T(8,128)S(1)}, f32[4,272,256]{2,1,0:T(8,128)S(1)}, u32[]{:S(2)}, u32[]{:S(2)}) collective-permute-start(f32[4,272,256]{2,1,0:T(8,128)S(1)} %prepare_rest.1), channel_id=1, source_target_pairs={{4,0},{8,4},{12,8},{5,1},{9,5},{13,9},{6,2},{10,6},{14,10},{7,3},{... | collective-permute-start | bytes 3342344 | tf_op jit(solution)/shard_map/ppermute | solution.py:263
  26.8 4.5 %collective-permute-start.2 = (f32[4,16,256]{2,1,0:T(8,128)S(1)}, f32[4,16,256]{2,1,0:T(8,128)S(1)}, u32[]{:S(2)}, u32[]{:S(2)}) collective-permute-start(f32[4,16,256]{2,1,0:T(8,128)S(1)} %get-tuple-element.35.refs_8_), channel_id=1, source_target_pairs={{0,4},{4,8},{8,12},{1,5},{5,9},{9,13},{2,6},{6,10},{10,14},{3,7},{... | collective-permute-start | bytes 196616 | tf_op jit(solution)/shard_map/ppermute | solution.py:271
  31.3 13.0 %collective-permute-start.3 = (f32[4,16,256]{2,1,0:T(8,128)S(1)}, f32[4,16,256]{2,1,0:T(8,128)S(1)}, u32[]{:S(2)}, u32[]{:S(2)}) collective-permute-start(f32[4,16,256]{2,1,0:T(8,128)S(1)} %get-tuple-element.37.refs_8_), channel_id=1, source_target_pairs={{0,4},{4,8},{8,12},{1,5},{5,9},{9,13},{2,6},{6,10},{10,14},{3,7},{... | collective-permute-start | bytes 196616 | tf_op jit(solution)/shard_map/ppermute | solution.py:271
  44.3 13.3 %collective-permute-start.4 = (f32[4,16,256]{2,1,0:T(8,128)S(1)}, f32[4,16,256]{2,1,0:T(8,128)S(1)}, u32[]{:S(2)}, u32[]{:S(2)}) collective-permute-start(f32[4,16,256]{2,1,0:T(8,128)S(1)} %get-tuple-element.39.refs_8_), channel_id=1, source_target_pairs={{0,4},{4,8},{8,12},{1,5},{5,9},{9,13},{2,6},{6,10},{10,14},{3,7},{... | collective-permute-start | bytes 196616 | tf_op jit(solution)/shard_map/ppermute | solution.py:271
  61.4 5.8 %collective-permute-start.5 = (f32[4,16,256]{2,1,0:T(8,128)S(1)}, f32[4,16,256]{2,1,0:T(8,128)S(1)}, u32[]{:S(2)}, u32[]{:S(2)}) collective-permute-start(f32[4,16,256]{2,1,0:T(8,128)S(1)} %get-tuple-element.41.refs_8_), channel_id=1, source_target_pairs={{0,4},{4,8},{8,12},{1,5},{5,9},{9,13},{2,6},{6,10},{10,14},{3,7},{... | collective-permute-start | bytes 196616 | tf_op jit(solution)/shard_map/ppermute | solution.py:271

commit v3 on v2

v3 whole, which is shorter than its diff:
```python
import functools

import jax
import jax.numpy as jnp
from jax import lax
from jax.experimental import pallas as pl
from jax.experimental.pallas import tpu as pltpu
from jax.sharding import PartitionSpec as P

SWEEPS = 8
CHUNK = 4
CHUNKS = SWEEPS // CHUNK
AHEAD = SWEEPS - 1
SOON = CHUNK - 1
F32 = jnp.float32
BF16 = jnp.bfloat16


def resident(shape, dtype):
    return pltpu.VMEM(shape, dtype)


def pin(x, memory=pltpu.VMEM):
    return pltpu.with_memory_space_constraint(x, memory)


def split(x):
    high = x.astype(BF16)
    return high, (x - high.astype(F32)).astype(BF16)


def dot(a, b):
    return jnp.dot(a, b, preferred_element_type=F32)


def dot_nt(a, b):
    return lax.dot_general(a, b, (((1,), (1,)), ((), ())), preferred_element_type=F32)


def dot_parts(a, b, dot=dot):
    return dot(a[0], b[0]) + (dot(a[0], b[1]) + dot(a[1], b[0]))


def response(first, last, x_high, x_low, a_high, a_low, b_high, b_low, base, kept):
    _, columns, phases = base.shape
    rows = phases + columns

    def store(i, new):
        top = new[0:phases]
        end = new[phases:rows] + base[i]
        x_high[i, 0:phases], x_low[i, 0:phases] = split(top)
        x_high[i, phases:rows], x_low[i, phases:rows] = split(end)
        return top, end

    def from_below(i):
        return dot_parts((x_high[i - 1], x_low[i - 1]), (a_high[i], a_low[i]))

    def from_above(i):
        return dot_parts((x_high[i + 1], x_low[i + 1]), (b_high[i], b_low[i]))

    for d in range(first, last):
        if d == 0:
            x_high[0, 0:phases], x_low[0, 0:phases] = a_high[0], a_low[0]
            x_high[0, phases:rows], x_low[0, phases:rows] = split(base[0])
            kept[0, 0:phases] = a_high[0].astype(F32) + a_low[0].astype(F32)
            kept[0, phases:rows] = base[0]
            continue
        store(d, from_below(d))

        def level(k, _, d=d):
            i = d - k
            store(i, from_below(i) + from_above(i))
            return 0

        lax.fori_loop(1, d, level, 0)
        kept[d - first, 0:phases], kept[d - first, phases:rows] = store(0, from_above(0))


def products(levels, hbm, reward, a_high, a_low, b_high, b_low, base, buffers, sems):
    def copies(i):
        return [
            pltpu.make_async_copy(source.at[i], target.at[i - levels[0]], sems.at[n, i - levels[0]])
            for n, (source, target) in enumerate(zip(hbm, buffers))
        ]

    for i in levels:
        for copy in copies(i):
            copy.start()

    inv, down, up = buffers
    for i in levels:
        for copy in copies(i):
            copy.wait()
        at = i - levels[0]
        here = split(inv[at])
        a_high[i], a_low[i] = split(dot_parts(here, split(down[at])).T)
        b_high[i], b_low[i] = split(dot_parts(here, split(up[at])).T)
        base[i] = dot_parts(split(reward[i]), here, dot_nt)


def prepare_kernel(
    inv, down, up, reward, a_high, a_low, b_high, b_low, base, x_high, x_low, kept, *scratch
):
    *buffers, sems = scratch
    products(range(SOON), (inv, down, up), reward, a_high, a_low, b_high, b_low, base, buffers, sems)
    response(0, SOON, x_high, x_low, a_high, a_low, b_high, b_low, base, kept)


def prepare_rest_kernel(
    inv, down, up, reward, a_high_soon, a_low_soon, b_high_soon, b_low_soon, base_soon, x_high_soon, x_low_soon,
    a_high, a_low, b_high, b_low, base, kept, x_high, x_low, *scratch
):
    *buffers, sems = scratch
    levels = reward.shape[0]
    for target, source in (
        (a_high, a_high_soon), (a_low, a_low_soon), (b_high, b_high_soon), (b_low, b_low_soon),
        (base, base_soon), (x_high, x_high_soon), (x_low, x_low_soon),
    ):
        target[0:SOON] = source[...]
    products(range(SOON, levels), (inv, down, up), reward, a_high, a_low, b_high, b_low, base, buffers, sems)
    response(SOON, AHEAD, x_high, x_low, a_high, a_low, b_high, b_low, base, kept)


VMEM = pl.BlockSpec(memory_space=pltpu.VMEM)
HBM = pl.BlockSpec(memory_space=pltpu.HBM)


def operators(levels, columns, phases):
    matrix = (levels, phases, phases)
    return [resident(matrix, BF16)] * 4 + [resident((levels, columns, phases), F32)]


def buffers(levels, phases):
    return [pltpu.VMEM((levels, phases, phases), F32)] * 3 + [pltpu.SemaphoreType.DMA((3, levels))]


def prepare(inverse_diag, down_block, up_block, reward):
    levels, columns, phases = reward.shape
    assert levels >= AHEAD
    rows = phases + columns
    given = [pin(x, pltpu.HBM) for x in (inverse_diag, down_block, up_block)] + [pin(reward)]
    *soon, kept_soon = pl.pallas_call(
        prepare_kernel,
        out_shape=operators(SOON, columns, phases)
        + [resident((SOON, rows, phases), BF16)] * 2
        + [resident((SOON, rows, phases), F32)],
        in_specs=[HBM] * 3 + [VMEM],
        out_specs=[VMEM] * 8,
        scratch_shapes=buffers(SOON, phases),
        compiler_params=pltpu.CompilerParams(vmem_limit_bytes=16 * 2**20),
        name="prepare",
    )(*given)
    *weights, kept_late = pl.pallas_call(
        prepare_rest_kernel,
        out_shape=operators(levels, columns, phases) + [resident((AHEAD - SOON, rows, phases), F32)],
        in_specs=[HBM] * 3 + [VMEM] * 8,
        out_specs=[VMEM] * 6,
        scratch_shapes=[pltpu.VMEM((AHEAD, rows, phases), BF16)] * 2 + buffers(levels - SOON, phases),
        compiler_params=pltpu.CompilerParams(vmem_limit_bytes=24 * 2**20),
        cost_estimate=pl.CostEstimate(flops=10**10, bytes_accessed=2**24, transcendentals=0),
        name="prepare_rest",
    )(*given, *[pin(x) for x in soon])
    return weights, kept_soon, kept_late


def stack(x):
    high = x.astype(BF16).astype(F32)
    return jnp.concatenate([high, x - high], axis=0).astype(BF16)


def fold(total):
    half = total.shape[0] // 2
    return total[:half] + total[half:]


def apply(x, high, low):
    return dot(x, high) + dot(x, low)


def kept_at(soon, late, j):
    return soon[j] if j < SOON else late[j - SOON]


def carried(soon, late, past, first, last):
    phases = soon.shape[2]
    above = {n: kept_at(soon, late, n - 1)[phases:] for n in range(max(first, 1), last + 1)}
    columns = soon.shape[1] - phases
    for j in range(last) if past else ():
        pairs = [(n, n - j) for n in above if n - j in past]
        if pairs:
            total = apply(
                jnp.concatenate([past[m] for _, m in pairs], axis=0), *split(kept_at(soon, late, j)[0:phases])
            )
            for p, (n, _) in enumerate(pairs):
                above[n] += fold(total[p * 2 * columns : (p + 1) * 2 * columns])
    return above


def stage_kernel(step, choices, names, *refs):
    a_high, a_low, b_high, b_low, base = refs[:5]
    given = dict(zip(names, refs[5:]))
    new_state, leaving = refs[5 + len(names) :]
    levels, columns, phases = base.shape
    soon = given["soon"]

    def chunk_of(chunk):
        first = chunk * CHUNK
        feedback = [split(soon[j, 0:phases]) for j in range(SOON)]
        if not first:
            above = carried(soon, None, {}, first, first + CHUNK - 1)
        elif "late" in given:
            past = {n + 1: stack(given["earlier"][n]) for n in range(first)}
            above = carried(soon, given["late"], past, first, first + CHUNK - 1)
        else:
            above = {first + k: given["returned"][k] if "returned" in given else 0.0 for k in range(CHUNK)}

        now = {}
        if first:
            for i in range(levels):
                now[i, first] = stack(given["state"][i])
        if "entering" in given:
            for k in range(CHUNK):
                now[-1, first + 1 + k] = stack(given["entering"][k])
        for turn in range(levels + 2 * (CHUNK - 1)):
            for k in range(CHUNK):
                i = turn - 2 * k
                if not 0 <= i < levels:
                    continue
                n = first + 1 + k
                value = base[i]
                if (i - 1, n) in now:
                    value += fold(apply(now[i - 1, n], a_high[i], a_low[i]))
                if n > 1:
                    over = stack(above[n - 1] + jnp.zeros_like(value)) if i == levels - 1 else now[i + 1, n - 1]
                    value += fold(apply(over, b_high[i], b_low[i]))
                now[i, n] = stack(value)
                if k == CHUNK - 1:
                    new_state[i] = value
                if i == levels - 1:
                    leaving[k] = value
                    for later in range(n, first + CHUNK):
                        above[later] += fold(apply(now[i, n], *feedback[later - n]))

    chunk = step - lax.axis_index("lvl")
    for choice in choices:
        pl.when(chunk == choice)(functools.partial(chunk_of, choice))

    @pl.when(functools.reduce(jnp.logical_and, [chunk != choice for choice in choices]))
    def _():
        new_state[...] = given["state"][...] if "state" in given else jnp.zeros_like(new_state)
        leaving[...] = jnp.zeros_like(leaving)


def stage(step, choices, weights, given, last):
    levels, columns, phases = weights[-1].shape
    given = {name: x for name, x in given.items() if x is not None}
    return pl.pallas_call(
        functools.partial(stage_kernel, step, choices, tuple(given)),
        out_shape=[
            (jax.ShapeDtypeStruct if last else resident)((levels, columns, phases), F32),
            resident((CHUNK, columns, phases), F32),
        ],
        in_specs=[VMEM] * (len(weights) + len(given)),
        out_specs=[VMEM] * 2,
        compiler_params=pltpu.CompilerParams(vmem_limit_bytes=16 * 2**20),
        name="stage",
    )(*[pin(x) for x in (*weights, *given.values())])


def answer_kernel(step, soon, late, entering, returned):
    @pl.when(lax.axis_index("lvl") == step)
    def _():
        past = {n + 1: stack(entering[n]) for n in range(CHUNK)}
        above = carried(soon, late, past, CHUNK, 2 * CHUNK - 1)
        for k in range(CHUNK):
            returned[k] = above[CHUNK + k]

    @pl.when(lax.axis_index("lvl") != step)
    def _():
        returned[...] = jnp.zeros_like(returned)


def answer(step, soon, late, entering):
    return pl.pallas_call(
        functools.partial(answer_kernel, step),
        out_shape=resident(entering.shape, F32),
        in_specs=[VMEM] * 3,
        out_specs=VMEM,
        compiler_params=pltpu.CompilerParams(vmem_limit_bytes=8 * 2**20),
        name="answer",
    )(*[pin(x) for x in (soon, late, entering)])


def local(inverse_diag, down_block, up_block, reward):
    given = reward.shape[1]
    columns = -(-given // 16) * 16
    if columns != given:
        reward = jnp.pad(reward, ((0, 0), (0, columns - given), (0, 0)))
    count = lax.axis_size("lvl")
    assert CHUNKS == 2
    weights, soon_here, late_here = prepare(inverse_diag, down_block, up_block, reward)
    soon = lax.ppermute(soon_here, "lvl", [(d + 1, d) for d in range(count - 1)])
    soon, late_sent = lax.optimization_barrier((soon, late_here))
    late = lax.ppermute(late_sent, "lvl", [(d + 1, d) for d in range(0, count - 1, 2)])
    state = leaving = entering = None
    stages = count + CHUNKS - 1
    for step in range(stages):
        returned = None
        if step % 2 == 0 and 0 < step < count:
            returned = lax.ppermute(answer(step, soon_here, late_here, entering), "lvl", [(step, step - 1)])
        choices = [c for c in range(CHUNKS) if 0 <= step - c < count]
        state, leaving = stage(
            step,
            choices,
            weights,
            {
                "soon": soon,
                "late": late if step % 2 else None,
                "returned": returned,
                "state": state,
                "earlier": leaving if step % 2 else None,
                "entering": entering,
            },
            step == stages - 1,
        )
        if step < stages - 1:
            entering = lax.ppermute(leaving, "lvl", [(d, d + 1) for d in range(count - 1)])
    return state[:, :given] if columns != given else state


def solution(mesh):
    placed = (
        P(("grp", "lvl"), None, None),
        P(("grp", "lvl"), None, None),
        P(("grp", "lvl"), None, None),
        P(("grp", "lvl"), "col", None),
    )
    return jax.shard_map(
        local, mesh=mesh, in_specs=placed, out_specs=P(("grp", "lvl"), "col", None), check_vma=False
    )
```

time: 72.1 us -> 58.3 us (0.81)
  waiting for transfers between devices: 31.3 us -> 22.9 us
  starting transfers between devices: 16 us -> 10.4 us
    ppermute x6 -> x7, waiting for transfers between devices: 31.3 us -> 22.9 us  [the longest x4 22.9 us: local(): lax.ppermute(leaving, 'lvl', [(d, d + 1) for d in range(count - 1)])]
    ppermute x6 -> x7, starting transfers between devices: 16 us -> 10.4 us  [the longest x4 5.17 us: local(): lax.ppermute(leaving, 'lvl', [(d, d + 1) for d in range(count - 1)])]
    pallas_call x7 -> x8, Pallas kernels: 23.5 us -> 23.7 us  [the longest x1 10.9 us: prepare(): pl.pallas_call(prepare_rest_kernel, out_shape=operators(levels, columns,...]
  transfers between devices with their start and end apart: 6 -> 7, of which waited for: 4 -> 4; matrix products, arithmetic and copies ran while one was open for 0% -> 0% of each run, Pallas kernels for 5% -> 19%
where the time goes in v3:
time: 58.3 us; the launch traced here: 58 us
  Pallas kernels  23.7 us (41%)
  waiting for transfers between devices  22.9 us (39%)
  starting transfers between devices  10.4 us (18%)
  local copies, waits for them, and re-layouts  0.91 us (2%)
    ppermute x4, waiting for transfers between devices, local(): lax.ppermute(leaving, 'lvl', [(d, d + 1) for d in range(count - 1)])  22.9 us
    pallas_call x1, Pallas kernels, prepare(): pl.pallas_call(prepare_rest_kernel, out_shape=operators(levels, columns,...  10.9 us
    pallas_call x5, Pallas kernels, stage(): pl.pallas_call(functools.partial(stage_kernel, step, choices, tuple(given...  8.85 us
    ppermute x4, starting transfers between devices, local(): lax.ppermute(leaving, 'lvl', [(d, d + 1) for d in range(count - 1)])  5.17 us
    pallas_call x1, Pallas kernels, prepare(): pl.pallas_call(prepare_kernel, out_shape=operators(SOON, columns, phases)...  3.87 us
    ppermute x1, starting transfers between devices, local(): lax.ppermute(soon_here, 'lvl', [(d + 1, d) for d in range(count - 1)])  2.63 us
    ppermute x1, starting transfers between devices, local(): lax.ppermute(late_sent, 'lvl', [(d + 1, d) for d in range(0, count - 1, 2)])  1.92 us
  transfers between devices with their start and end apart: 7, of which 4 were waited for; matrix products, arithmetic and copies ran while one was open for 0% of the time, Pallas kernels for 19%

profile of v3, /device:TPU:11, one launch (start us, length us, event | category | flops | bytes accessed | tf_op | source)
XLA Modules:
  0.0 58.0 jit_solution(7272868168936534046)
XLA Ops:
  0.0 0.0 copy-start
  0.0 0.9 %copy-done = f32[8,16,256]{2,1,0:T(8,128)S(1)} copy-done((f32[8,16,256]{2,1,0:T(8,128)S(1)}, f32[8,16,256]{2,1,0:T(8,128)}, u32[]{:S(2)}) %copy-start) | copy-done | bytes 131096
  0.9 0.0 copy-start.1
  0.9 3.9 %prepare.1 = (bf16[3,256,256]{2,1,0:T(8,128)(2,1)S(1)}, bf16[3,256,256]{2,1,0:T(8,128)(2,1)S(1)}, bf16[3,256,256]{2,1,0:T(8,128)(2,1)S(1)}, bf16[3,256,256]{2,1,...) custom-call(f32[8,256,256]{2,1,0:T(8,128)} %inv.3, ...), custom_call_target="tpu_custom_call" | custom-call | tf_op jit(solution)/shard_map/prepare/pallas_call | solution.py:142
  4.8 2.6 %collective-permute-start = (f32[3,272,256]{2,1,0:T(8,128)S(1)}, f32[3,272,256]{2,1,0:T(8,128)S(1)}, u32[]{:S(2)}, u32[]{:S(2)}) collective-permute-start(f32[3,272,256]{2,1,0:T(8,128)S(1)} %get-tuple-element.42.soon), channel_id=1, source_target_pairs={{4,0},{8,4},{12,8},{5,1},{9,5},{13,9},{6,2},{10,6},{14,10},{7,3},{... | collective-permute-start | bytes 2506760 | tf_op jit(solution)/shard_map/ppermute | solution.py:302
  7.4 0.0 copy-done.1
  7.4 10.9 %prepare_rest.1 = (bf16[8,256,256]{2,1,0:T(8,128)(2,1)S(1)}, bf16[8,256,256]{2,1,0:T(8,128)(2,1)S(1)}, bf16[8,256,256]{2,1,0:T(8,128)(2,1)S(1)}, bf16[8,256,256]...) custom-call(f32[8,256,256]{2,1,0:T(8,128)} %inv.3, f32[8,256,256]{2,1,0:T(8,128)} %down.3, ...), custom_call_target="tpu_custom_call" | custom-call | flops 10000000000 | bytes 16777216 | tf_op jit(solution)/shard_map/prepare_rest/pallas_call | solution.py:153
  18.4 0.0 collective-permute-done.refs_5_
  18.4 1.9 %collective-permute-start.1 = (f32[4,272,256]{2,1,0:T(8,128)S(1)}, f32[4,272,256]{2,1,0:T(8,128)S(1)}, u32[]{:S(2)}, u32[]{:S(2)}) collective-permute-start(f32[4,272,256]{2,1,0:T(8,128)S(1)} %get-tuple-element.45.late), channel_id=1, source_target_pairs={{4,0},{12,8},{5,1},{13,9},{6,2},{14,10},{7,3},{15,11},{20,16},{28,... | collective-permute-start | bytes 3342344 | tf_op jit(solution)/shard_map/ppermute | solution.py:304
  20.4 1.3 %collective-permute-start.2 = (f32[4,16,256]{2,1,0:T(8,128)S(1)}, f32[4,16,256]{2,1,0:T(8,128)S(1)}, u32[]{:S(2)}, u32[]{:S(2)}) collective-permute-start(f32[4,16,256]{2,1,0:T(8,128)S(1)} %get-tuple-element.47.refs_8_), channel_id=1, source_target_pairs={{0,4},{4,8},{8,12},{1,5},{5,9},{9,13},{2,6},{6,10},{10,14},{3,7},{... | collective-permute-start | bytes 196616 | tf_op jit(solution)/shard_map/ppermute | solution.py:327
  21.7 1.8 %collective-permute-done.2.refs_9_ = f32[4,16,256]{2,1,0:T(8,128)S(1)} collective-permute-done((f32[4,16,256]{2,1,0:T(8,128)S(1)}, f32[4,16,256]{2,1,0:T(8,128)S(1)}, u32[]{:S(2)}, u32[]{:S(2)}) %collective-permute-start.2) | collective-permute-done | bytes 65568 | tf_op jit(solution)/shard_map/ppermute | solution.py:327
  23.5 0.0 collective-permute-done.1.refs_6_
  23.5 1.3 %collective-permute-start.3 = (f32[4,16,256]{2,1,0:T(8,128)S(1)}, f32[4,16,256]{2,1,0:T(8,128)S(1)}, u32[]{:S(2)}, u32[]{:S(2)}) collective-permute-start(f32[4,16,256]{2,1,0:T(8,128)S(1)} %get-tuple-element.48), channel_id=1, source_target_pairs={{0,4},{4,8},{8,12},{1,5},{5,9},{9,13},{2,6},{6,10},{10,14},{3,7},{... | collective-permute-start | bytes 196616 | tf_op jit(solution)/shard_map/ppermute | solution.py:327
  24.8 3.1 %collective-permute-done.3.entering.refs_8_ = f32[4,16,256]{2,1,0:T(8,128)S(1)} collective-permute-done((f32[4,16,256]{2,1,0:T(8,128)S(1)}, f32[4,16,256]{2,1,0:T(8,128)S(1)}, u32[]{:S(2)}, u32[]{:S(2)}) %collective-permute-start.3) | collective-permute-done | bytes 65568 | tf_op jit(solution)/shard_map/ppermute | solution.py:327
  27.9 0.7 %collective-permute-start.4 = (f32[4,16,256]{2,1,0:T(8,128)S(1)}, f32[4,16,256]{2,1,0:T(8,128)S(1)}, u32[]{:S(2)}, u32[]{:S(2)}) collective-permute-start(f32[4,16,256]{2,1,0:T(8,128)S(1)} %answer.1), channel_id=1, source_target_pairs={{8,4},{9,5},{10,6},{11,7},{24,20},{25,21},{26,22},{27,23}} | collective-permute-start | bytes 196616 | tf_op jit(solution)/shard_map/ppermute | solution.py:310
  28.6 0.0 collective-permute-done.4.refs_6_
  28.7 1.3 %collective-permute-start.5 = (f32[4,16,256]{2,1,0:T(8,128)S(1)}, f32[4,16,256]{2,1,0:T(8,128)S(1)}, u32[]{:S(2)}, u32[]{:S(2)}) collective-permute-start(f32[4,16,256]{2,1,0:T(8,128)S(1)} %get-tuple-element.51.refs_8_), channel_id=1, source_target_pairs={{0,4},{4,8},{8,12},{1,5},{5,9},{9,13},{2,6},{6,10},{10,14},{3,7},{... | collective-permute-start | bytes 196616 | tf_op jit(solution)/shard_map/ppermute | solution.py:327
  30.0 13.1 %collective-permute-done.5.refs_9_ = f32[4,16,256]{2,1,0:T(8,128)S(1)} collective-permute-done((f32[4,16,256]{2,1,0:T(8,128)S(1)}, f32[4,16,256]{2,1,0:T(8,128)S(1)}, u32[]{:S(2)}, u32[]{:S(2)}) %collective-permute-start.5) | collective-permute-done | bytes 65568 | tf_op jit(solution)/shard_map/ppermute | solution.py:327
  43.1 3.9 %stage.8 = (f32[8,16,256]{2,1,0:T(8,128)S(1)}, f32[4,16,256]{2,1,0:T(8,128)S(1)}) custom-call(bf16[8,256,256]{2,1,0:T(8,128)(2,1)S(1)} %get-tuple-element.37.refs_0_, bf16[8,256,256]{2,1,0:T(8,128)(2,1)S(1)} %get-tuple-element.38.refs_1_, bf16[8,256,256]{2,1,0:T(8,128)(2,1)S(1)} %get-tuple-element.39.refs_2_, ...), custom_call_target="tpu_custom_call" | custom-call | tf_op jit(solution)/shard_map/stage/pallas_call | solution.py:257
  47.0 1.3 %collective-permute-start.6 = (f32[4,16,256]{2,1,0:T(8,128)S(1)}, f32[4,16,256]{2,1,0:T(8,128)S(1)}, u32[]{:S(2)}, u32[]{:S(2)}) collective-permute-start(f32[4,16,256]{2,1,0:T(8,128)S(1)} %get-tuple-element.53), channel_id=1, source_target_pairs={{0,4},{4,8},{8,12},{1,5},{5,9},{9,13},{2,6},{6,10},{10,14},{3,7},{... | collective-permute-start | bytes 196616 | tf_op jit(solution)/shard_map/ppermute | solution.py:327
  48.3 4.8 %collective-permute-done.6.refs_7_ = f32[4,16,256]{2,1,0:T(8,128)S(1)} collective-permute-done((f32[4,16,256]{2,1,0:T(8,128)S(1)}, f32[4,16,256]{2,1,0:T(8,128)S(1)}, u32[]{:S(2)}, u32[]{:S(2)}) %collective-permute-start.6) | collective-permute-done | bytes 65568 | tf_op jit(solution)/shard_map/ppermute | solution.py:327
  53.1 4.9 %stage.9 = (f32[8,16,256]{2,1,0:T(8,128)}, f32[4,16,256]{2,1,0:T(8,128)}) custom-call(bf16[8,256,256]{2,1,0:T(8,128)(2,1)S(1)} %get-tuple-element.37.refs_0_, bf16[8,256,256]{2,1,0:T(8,128)(2,1)S(1)} %get-tuple-element.38.refs_1_, bf16[8,256,256]{2,1,0:T(8,128)(2,1)S(1)} %get-tuple-element.39.refs_2_, bf16[8,256,256]{2,1,0:T(8,128)(2,1)S(1)} %get-tuple-element.40.refs_3_, ...), custom_call_target="tpu_custom_call" | custom-call | tf_op jit(solution)/shard_map/stage/pallas_call | solution.py:257
  (4 shorter events, 0.1 us)
Async XLA Ops:
  0.0 0.9 %copy-start = (f32[8,16,256]{2,1,0:T(8,128)S(1)}, f32[8,16,256]{2,1,0:T(8,128)}, u32[]{:S(2)}) copy-start(f32[8,16,256]{2,1,0:T(8,128)} %reward.3) | copy-start | bytes 393220
  0.9 6.5 %copy-start.1 = (f32[8,16,256]{2,1,0:T(8,128)S(1)}, f32[8,16,256]{2,1,0:T(8,128)}, u32[]{:S(2)}) copy-start(f32[8,16,256]{2,1,0:T(8,128)} %reward.3) | copy-start | bytes 393220
  4.8 13.6 %collective-permute-start = (f32[3,272,256]{2,1,0:T(8,128)S(1)}, f32[3,272,256]{2,1,0:T(8,128)S(1)}, u32[]{:S(2)}, u32[]{:S(2)}) collective-permute-start(f32[3,272,256]{2,1,0:T(8,128)S(1)} %get-tuple-element.42.soon), channel_id=1, source_target_pairs={{4,0},{8,4},{12,8},{5,1},{9,5},{13,9},{6,2},{10,6},{14,10},{7,3},{... | collective-permute-start | bytes 2506760 | tf_op jit(solution)/shard_map/ppermute | solution.py:302
  18.4 5.1 %collective-permute-start.1 = (f32[4,272,256]{2,1,0:T(8,128)S(1)}, f32[4,272,256]{2,1,0:T(8,128)S(1)}, u32[]{:S(2)}, u32[]{:S(2)}) collective-permute-start(f32[4,272,256]{2,1,0:T(8,128)S(1)} %get-tuple-element.45.late), channel_id=1, source_target_pairs={{4,0},{12,8},{5,1},{13,9},{6,2},{14,10},{7,3},{15,11},{20,16},{28,... | collective-permute-start | bytes 3342344 | tf_op jit(solution)/shard_map/ppermute | solution.py:304
  20.4 3.1 %collective-permute-start.2 = (f32[4,16,256]{2,1,0:T(8,128)S(1)}, f32[4,16,256]{2,1,0:T(8,128)S(1)}, u32[]{:S(2)}, u32[]{:S(2)}) collective-permute-start(f32[4,16,256]{2,1,0:T(8,128)S(1)} %get-tuple-element.47.refs_8_), channel_id=1, source_target_pairs={{0,4},{4,8},{8,12},{1,5},{5,9},{9,13},{2,6},{6,10},{10,14},{3,7},{... | collective-permute-start | bytes 196616 | tf_op jit(solution)/shard_map/ppermute | solution.py:327
  23.5 4.4 %collective-permute-start.3 = (f32[4,16,256]{2,1,0:T(8,128)S(1)}, f32[4,16,256]{2,1,0:T(8,128)S(1)}, u32[]{:S(2)}, u32[]{:S(2)}) collective-permute-start(f32[4,16,256]{2,1,0:T(8,128)S(1)} %get-tuple-element.48), channel_id=1, source_target_pairs={{0,4},{4,8},{8,12},{1,5},{5,9},{9,13},{2,6},{6,10},{10,14},{3,7},{... | collective-permute-start | bytes 196616 | tf_op jit(solution)/shard_map/ppermute | solution.py:327
  27.9 0.7 %collective-permute-start.4 = (f32[4,16,256]{2,1,0:T(8,128)S(1)}, f32[4,16,256]{2,1,0:T(8,128)S(1)}, u32[]{:S(2)}, u32[]{:S(2)}) collective-permute-start(f32[4,16,256]{2,1,0:T(8,128)S(1)} %answer.1), channel_id=1, source_target_pairs={{8,4},{9,5},{10,6},{11,7},{24,20},{25,21},{26,22},{27,23}} | collective-permute-start | bytes 196616 | tf_op jit(solution)/shard_map/ppermute | solution.py:310
  28.7 14.4 %collective-permute-start.5 = (f32[4,16,256]{2,1,0:T(8,128)S(1)}, f32[4,16,256]{2,1,0:T(8,128)S(1)}, u32[]{:S(2)}, u32[]{:S(2)}) collective-permute-start(f32[4,16,256]{2,1,0:T(8,128)S(1)} %get-tuple-element.51.refs_8_), channel_id=1, source_target_pairs={{0,4},{4,8},{8,12},{1,5},{5,9},{9,13},{2,6},{6,10},{10,14},{3,7},{... | collective-permute-start | bytes 196616 | tf_op jit(solution)/shard_map/ppermute | solution.py:327
  47.0 6.1 %collective-permute-start.6 = (f32[4,16,256]{2,1,0:T(8,128)S(1)}, f32[4,16,256]{2,1,0:T(8,128)S(1)}, u32[]{:S(2)}, u32[]{:S(2)}) collective-permute-start(f32[4,16,256]{2,1,0:T(8,128)S(1)} %get-tuple-element.53), channel_id=1, source_target_pairs={{0,4},{4,8},{8,12},{1,5},{5,9},{9,13},{2,6},{6,10},{10,14},{3,7},{... | collective-permute-start | bytes 196616 | tf_op jit(solution)/shard_map/ppermute | solution.py:327

commit v4 on v3

v4 whole, which is shorter than its diff:
```python
import functools

import jax
import jax.numpy as jnp
from jax import lax
from jax.experimental import pallas as pl
from jax.experimental.pallas import tpu as pltpu
from jax.sharding import PartitionSpec as P

SWEEPS = 8
CHUNK = 4
CHUNKS = SWEEPS // CHUNK
AHEAD = SWEEPS - 1
SOON = CHUNK - 1
F32 = jnp.float32
BF16 = jnp.bfloat16


def resident(shape, dtype):
    return pltpu.VMEM(shape, dtype)


def pin(x, memory=pltpu.VMEM):
    return pltpu.with_memory_space_constraint(x, memory)


def split(x):
    high = x.astype(BF16)
    return high, (x - high.astype(F32)).astype(BF16)


def dot(a, b):
    return jnp.dot(a, b, preferred_element_type=F32)


def dot_nt(a, b):
    return lax.dot_general(a, b, (((1,), (1,)), ((), ())), preferred_element_type=F32)


def dot_parts(a, b):
    return dot(jnp.concatenate([a[0], a[0], a[1]], axis=1), jnp.concatenate([b[0], b[1], b[0]], axis=0))


def place_operators(weight, i, down, up):
    phases = down.shape[0]
    for k, part in enumerate((*split(down.T), *split(up.T))):
        weight[i, k * phases : (k + 1) * phases] = part


def response(first, last, x_high, x_low, weight, base, kept):
    _, columns, phases = base.shape
    rows = phases + columns

    def store(i, new):
        top = new[0:phases]
        end = new[phases:rows] + base[i]
        x_high[i, 0:phases], x_low[i, 0:phases] = split(top)
        x_high[i, phases:rows], x_low[i, phases:rows] = split(end)
        return top, end

    def operator(i, k):
        high = weight[i, 2 * k * phases : (2 * k + 1) * phases]
        low = weight[i, (2 * k + 1) * phases : (2 * k + 2) * phases]
        return [high, low, high]

    def value(i):
        return [x_high[i], x_high[i], x_low[i]]

    def product(values, operators):
        return dot(jnp.concatenate(values, axis=1), jnp.concatenate(operators, axis=0))

    for d in range(first, last):
        if d == 0:
            high, low = weight[0, 0:phases], weight[0, phases : 2 * phases]
            x_high[0, 0:phases], x_low[0, 0:phases] = high, low
            x_high[0, phases:rows], x_low[0, phases:rows] = split(base[0])
            kept[0, 0:phases] = high.astype(F32) + low.astype(F32)
            kept[0, phases:rows] = base[0]
            continue
        store(d, product(value(d - 1), operator(d, 0)))

        def level(k, _, d=d):
            i = d - k
            store(i, product(value(i - 1) + value(i + 1), operator(i, 0) + operator(i, 1)))
            return 0

        lax.fori_loop(1, d, level, 0)
        kept[d - first, 0:phases], kept[d - first, phases:rows] = store(0, product(value(1), operator(0, 1)))


def products(levels, given, weight, base, buffers, sems):
    first = levels[0]

    def copies(i):
        return [
            pltpu.make_async_copy(source.at[i], target.at[i - first], sems.at[n, i - first])
            for n, (source, target) in enumerate(zip(given, buffers))
        ]

    for i in levels:
        for copy in copies(i):
            copy.start()

    inv, down, up, pay = buffers
    for i in levels:
        for copy in copies(i):
            copy.wait()
        at = i - first
        here = split(inv[at])
        place_operators(weight, i, dot_parts(here, split(down[at])), dot_parts(here, split(up[at])))
        high, low = split(pay[at])
        base[i] = dot_nt(high, here[0]) + (dot_nt(high, here[1]) + dot_nt(low, here[0]))


def prepare_kernel(inv, down, up, reward, weight, base, x_high, x_low, kept, *scratch):
    *buffers, sems = scratch
    products(range(SOON), (inv, down, up, reward), weight, base, buffers, sems)
    response(0, SOON, x_high, x_low, weight, base, kept)


def prepare_rest_kernel(inv, down, up, reward, weight_soon, base_soon, weight, base, *scratch):
    *buffers, sems = scratch
    levels = reward.shape[0]
    weight[0:SOON] = weight_soon[...]
    base[0:SOON] = base_soon[...]
    products(range(SOON, levels), (inv, down, up, reward), weight, base, buffers, sems)


def respond_kernel(weight, base, x_high_soon, x_low_soon, kept, x_high, x_low):
    @pl.when(lax.axis_index("lvl") > 0)
    def _():
        x_high[0:SOON] = x_high_soon[...]
        x_low[0:SOON] = x_low_soon[...]
        response(SOON, AHEAD, x_high, x_low, weight, base, kept)


VMEM = pl.BlockSpec(memory_space=pltpu.VMEM)
HBM = pl.BlockSpec(memory_space=pltpu.HBM)


def operators(levels, columns, phases):
    return [resident((levels, 4 * phases, phases), BF16), resident((levels, columns, phases), F32)]


def buffers(levels, columns, phases):
    return (
        [pltpu.VMEM((levels, phases, phases), F32)] * 3
        + [pltpu.VMEM((levels, columns, phases), F32)]
        + [pltpu.SemaphoreType.DMA((4, levels))]
    )


def prepare(inverse_diag, down_block, up_block, reward):
    levels, columns, phases = reward.shape
    assert levels >= AHEAD
    rows = phases + columns
    given = [pin(x, pltpu.HBM) for x in (inverse_diag, down_block, up_block, reward)]
    *soon, kept_soon = pl.pallas_call(
        prepare_kernel,
        out_shape=operators(SOON, columns, phases)
        + [resident((SOON, rows, phases), BF16)] * 2
        + [resident((SOON, rows, phases), F32)],
        in_specs=[HBM] * 4,
        out_specs=[VMEM] * 5,
        scratch_shapes=buffers(SOON, columns, phases),
        compiler_params=pltpu.CompilerParams(vmem_limit_bytes=16 * 2**20),
        name="prepare",
    )(*given)
    weights = pl.pallas_call(
        prepare_rest_kernel,
        out_shape=operators(levels, columns, phases),
        in_specs=[HBM] * 4 + [VMEM] * 2,
        out_specs=[VMEM] * 2,
        scratch_shapes=buffers(levels - SOON, columns, phases),
        compiler_params=pltpu.CompilerParams(vmem_limit_bytes=16 * 2**20),
        name="prepare_rest",
    )(*given, *[pin(x) for x in soon[:2]])
    return weights, soon[2:], kept_soon


def respond(weights, started):
    _, rows, phases = started[0].shape
    return pl.pallas_call(
        respond_kernel,
        out_shape=resident((AHEAD - SOON, rows, phases), F32),
        in_specs=[VMEM] * 4,
        out_specs=VMEM,
        scratch_shapes=[pltpu.VMEM((AHEAD, rows, phases), BF16)] * 2,
        compiler_params=pltpu.CompilerParams(vmem_limit_bytes=16 * 2**20),
        name="respond",
    )(*[pin(x) for x in (*weights, *started)])


def stack(x):
    high = x.astype(BF16).astype(F32)
    return jnp.concatenate([high, x - high], axis=0).astype(BF16)


def fold(total):
    half = total.shape[0] // 2
    return total[:half] + total[half:]


def apply(terms):
    values = jnp.concatenate([x for x, _ in terms for _ in range(2)], axis=1)
    return fold(dot(values, jnp.concatenate([operator for _, operator in terms], axis=0)))


def whole(operator):
    return jnp.concatenate(split(operator), axis=0)


def kept_at(soon, late, j):
    return soon[j] if j < SOON else late[j - SOON]


def carried(soon, late, past, first, last):
    phases = soon.shape[2]
    above = {n: kept_at(soon, late, n - 1)[phases:] for n in range(max(first, 1), last + 1)}
    for j in range(last) if past else ():
        pairs = [(n, n - j) for n in above if n - j in past]
        for n, m in pairs:
            above[n] += apply([(past[m], whole(kept_at(soon, late, j)[0:phases]))])
    return above


def chunk_kernel(chunk, place, names, *refs):
    given = dict(zip(names, refs))
    new_state, leaving = refs[len(names) :]
    weight, base, soon = given["weight"], given["base"], given["soon"]
    levels, columns, phases = base.shape
    first = chunk * CHUNK

    @pl.when(lax.axis_index("lvl") != place)
    def _():
        for name, target in (("state", new_state), ("leaving", leaving)):
            target[...] = given[name][...] if name in given else jnp.zeros_like(target)

    @pl.when(lax.axis_index("lvl") == place)
    def _():
        feedback = [whole(soon[j, 0:phases]) for j in range(SOON)]
        if not first:
            above = carried(soon, None, {}, first, first + CHUNK - 1)
        elif "late" in given:
            past = {n + 1: stack(given["earlier"][n]) for n in range(first)}
            above = carried(soon, given["late"], past, first, first + CHUNK - 1)
        else:
            zero = jnp.zeros((columns, phases), F32)
            above = {first + k: given["returned"][k] if "returned" in given else zero for k in range(CHUNK)}

        now = {}
        if first:
            for i in range(levels):
                now[i, first] = stack(given["state"][i])
        if "entering" in given:
            for k in range(CHUNK):
                now[-1, first + 1 + k] = stack(given["entering"][k])
        for turn in range(levels + 2 * (CHUNK - 1)):
            for k in range(CHUNK):
                i = turn - 2 * k
                if not 0 <= i < levels:
                    continue
                n = first + 1 + k
                terms = []
                if (i - 1, n) in now:
                    terms.append((now[i - 1, n], weight[i, 0 : 2 * phases]))
                if n > 1:
                    over = stack(above[n - 1]) if i == levels - 1 else now[i + 1, n - 1]
                    terms.append((over, weight[i, 2 * phases : 4 * phases]))
                value = base[i] + apply(terms) if terms else base[i]
                now[i, n] = stack(value)
                if k == CHUNK - 1:
                    new_state[i] = value
                if i == levels - 1:
                    leaving[k] = value
                    for later in range(n, first + CHUNK):
                        above[later] += apply([(now[i, n], feedback[later - n])])


def run_chunk(chunk, place, given, last=False):
    given = {name: x for name, x in given.items() if x is not None}
    names = tuple(given)
    levels, columns, phases = given["base"].shape
    return pl.pallas_call(
        functools.partial(chunk_kernel, chunk, place, names),
        out_shape=[
            (jax.ShapeDtypeStruct if last else resident)((levels, columns, phases), F32),
            resident((CHUNK, columns, phases), F32),
        ],
        in_specs=[VMEM] * len(given),
        out_specs=[VMEM] * 2,
        compiler_params=pltpu.CompilerParams(vmem_limit_bytes=16 * 2**20),
        name="chunk",
    )(*[pin(x) for x in given.values()])


def answer_kernel(step, soon, late, entering, returned):
    @pl.when(lax.axis_index("lvl") == step)
    def _():
        past = {n + 1: stack(entering[n]) for n in range(CHUNK)}
        above = carried(soon, late, past, CHUNK, 2 * CHUNK - 1)
        for k in range(CHUNK):
            returned[k] = above[CHUNK + k]


def answer(step, soon, late, entering):
    return pl.pallas_call(
        functools.partial(answer_kernel, step),
        out_shape=resident(entering.shape, F32),
        in_specs=[VMEM] * 3,
        out_specs=VMEM,
        compiler_params=pltpu.CompilerParams(vmem_limit_bytes=8 * 2**20),
        name="answer",
    )(*[pin(x) for x in (soon, late, entering)])


def local(inverse_diag, down_block, up_block, reward):
    given = reward.shape[1]
    columns = -(-given // 16) * 16
    if columns != given:
        reward = jnp.pad(reward, ((0, 0), (0, columns - given), (0, 0)))
    count = lax.axis_size("lvl")
    assert CHUNKS == 2
    weights, started, soon_here = prepare(inverse_diag, down_block, up_block, reward)
    late_here = respond(weights, started)
    upward = [(d, d + 1) for d in range(count - 1)]
    from_odd = [(d + 1, d) for d in range(0, count - 1, 2)]
    soon = lax.ppermute(soon_here, "lvl", [(d + 1, d) for d in range(count - 1)])
    soon, late_here = lax.optimization_barrier((soon, late_here))
    late = returned = entering = leaving = state = None
    for step in range(count + 1):
        earlier = leaving
        shared = {"weight": weights[0], "base": weights[1], "entering": entering}
        if step % 2 == 0 and 0 < step < count:
            returned = lax.ppermute(answer(step, soon_here, late_here, entering), "lvl", [(step, step - 1)])
        if step < count:
            own = {**shared, "soon": soon, "state": state}
            state, leaving = run_chunk(0, step, own)
        if step == 1:
            late_sent, entering = lax.optimization_barrier((late_here, entering))
            late = lax.ppermute(late_sent, "lvl", from_odd)
        if step > 0:
            own = {**shared, "soon": soon, "state": state, "leaving": leaving}
            if step % 2:
                own.update(late=late, earlier=earlier)
            elif step < count:
                own.update(returned=returned)
            state, leaving = run_chunk(1, step - 1, own, last=step == count)
        if step < count:
            entering = lax.ppermute(leaving, "lvl", upward)
    return state[:, :given] if columns != given else state


def solution(mesh):
    placed = (
        P(("grp", "lvl"), None, None),
        P(("grp", "lvl"), None, None),
        P(("grp", "lvl"), None, None),
        P(("grp", "lvl"), "col", None),
    )
    return jax.shard_map(
        local, mesh=mesh, in_specs=placed, out_specs=P(("grp", "lvl"), "col", None), check_vma=False
    )
```

time: 58.3 us -> 60.3 us (1.034)
  starting transfers between devices: 10.4 us -> 12.8 us
  local copies, waits for them, and re-layouts: 0.91 us -> 0 us
    pallas_call x5 -> x9, Pallas kernels: 8.85 us -> 16.4 us  [the longest x8 9.22 us: run_chunk(): pl.pallas_call(functools.partial(chunk_kernel, chunk, place, names), out_...]
    pallas_call x1, Pallas kernels: 10.9 us -> 3.92 us  [prepare(): pl.pallas_call(prepare_rest_kernel, out_shape=operators(levels, columns,...]
    ppermute x5, starting transfers between devices: 7.08 us -> 9.54 us  [the longest x4 5.17 us: local(): entering = lax.ppermute(leaving, 'lvl', upward)]
    unnamed x4 -> x0, local copies, waits for them, and re-layouts: 0.91 us -> none
  transfers between devices with their start and end apart: 7 -> 7, of which waited for: 4 -> 5; matrix products, arithmetic and copies ran while one was open for 0% -> 0% of each run, Pallas kernels for 19% -> 19%
where the time goes in v4:
time: 60.3 us; the launch traced here: 60 us
  Pallas kernels  24.2 us (40%)
  waiting for transfers between devices  22.8 us (38%)
  starting transfers between devices  12.8 us (21%)
    ppermute x4, waiting for transfers between devices, local(): entering = lax.ppermute(leaving, 'lvl', upward)  20.6 us
    pallas_call x8, Pallas kernels, run_chunk(): pl.pallas_call(functools.partial(chunk_kernel, chunk, place, names), out_...  9.22 us
    pallas_call x1, Pallas kernels, respond(): pl.pallas_call(respond_kernel, out_shape=resident((AHEAD - SOON, rows, ph...  7.23 us
    ppermute x4, starting transfers between devices, local(): entering = lax.ppermute(leaving, 'lvl', upward)  5.17 us
    ppermute x1, starting transfers between devices, local(): late = lax.ppermute(late_sent, 'lvl', from_odd)  4.37 us
    pallas_call x1, Pallas kernels, prepare(): pl.pallas_call(prepare_rest_kernel, out_shape=operators(levels, columns,...  3.92 us
    pallas_call x1, Pallas kernels, prepare(): pl.pallas_call(prepare_kernel, out_shape=operators(SOON, columns, phases)...  3.84 us
    ppermute x1, starting transfers between devices, local(): lax.ppermute(soon_here, 'lvl', [(d + 1, d) for d in range(count - 1)])  2.63 us
  transfers between devices with their start and end apart: 7, of which 5 were waited for; matrix products, arithmetic and copies ran while one was open for 0% of the time, Pallas kernels for 19%

profile of v4, /device:TPU:11, one launch (start us, length us, event | category | flops | bytes accessed | tf_op | source)
XLA Modules:
  0.0 60.0 jit_solution(3094431493091712785)
XLA Ops:
  0.0 3.8 %prepare.1 = (bf16[3,1024,256]{2,1,0:T(8,128)(2,1)S(1)}, f32[3,16,256]{2,1,0:T(8,128)S(1)}, bf16[3,272,256]{2,1,0:T(8,128)(2,1)S(1)}, bf16[3,272,256]{2,1,0:T(8,128)(2,1)S(1)}, f32[3,272,256]{2,1,0:T(8,128)S(1)}) custom-call(f32[8,256,256]{2,1,0:T(8,128)} %inv.3, f32[8,256,256]{2,1,0:T(8,128)} %down.3, f32[8,256,256]{2,1,0:T(8,128)} %up.3, f32[8,16,256]{2,1,0:T(8,128)} %reward.3), custom_call_target="tpu_custom_call" | custom-call | tf_op jit(solution)/shard_map/prepare/pallas_call | solution.py:158
  3.8 2.6 %collective-permute-start = (f32[3,272,256]{2,1,0:T(8,128)S(1)}, f32[3,272,256]{2,1,0:T(8,128)S(1)}, u32[]{:S(2)}, u32[]{:S(2)}) collective-permute-start(f32[3,272,256]{2,1,0:T(8,128)S(1)} %get-tuple-element.34.soon), channel_id=1, source_target_pairs={{4,0},{8,4},{12,8},{5,1},{9,5},{13,9},{6,2},{10,6},{14,10},{7,3},{... | collective-permute-start | bytes 2506760 | tf_op jit(solution)/shard_map/ppermute | solution.py:328
  6.5 3.9 %prepare_rest.1 = (bf16[8,1024,256]{2,1,0:T(8,128)(2,1)S(1)}, f32[8,16,256]{2,1,0:T(8,128)S(1)}) custom-call(f32[8,256,256]{2,1,0:T(8,128)} %inv.3, f32[8,256,256]{2,1,0:T(8,128)} %down.3, f32[8,256,256]{2,1,0:T(8,128)} %up.3, f32[8,16,256]{2,1,0:T(8,128)} %reward.3, bf16[3,1024,256]{2,1,0:T(8,128)(2,1)S(1)} %get-tuple-element.30.weight_soon, ...), custom_call_target="tpu_custom_call" | custom-call | tf_op jit(solution)/shard_map/prepare_rest/pallas_call | solution.py:169
  10.4 7.2 %respond.1.late = f32[4,272,256]{2,1,0:T(8,128)S(1)} custom-call(bf16[8,1024,256]{2,1,0:T(8,128)(2,1)S(1)} %get-tuple-element.32.weight.refs_0_, f32[8,16,256]{2,1,0:T(8,128)S(1)} %get-tuple-element.33.base.refs_1_, bf16[3,272,256]{2,1,0:T(8,128)(2,1)S(1)} %get-tuple-element.35.x_high_soon, bf16[3,272,256]{2,1,0:T(8,128)(2,1)S(1)} %get-tuple-element.36.x_low_soon), custom_call_target="tpu_custom_call" | custom-call | tf_op jit(solution)/shard_map/respond/pallas_call | solution.py:183
  17.6 0.0 collective-permute-done.refs_2_.refs_3_
  17.7 1.3 %collective-permute-start.1 = (f32[4,16,256]{2,1,0:T(8,128)S(1)}, f32[4,16,256]{2,1,0:T(8,128)S(1)}, u32[]{:S(2)}, u32[]{:S(2)}) collective-permute-start(f32[4,16,256]{2,1,0:T(8,128)S(1)} %get-tuple-element.38.refs_7_), channel_id=1, source_target_pairs={{0,4},{4,8},{8,12},{1,5},{5,9},{9,13},{2,6},{6,10},{10,14},{3,7},{... | collective-permute-start | bytes 196616 | tf_op jit(solution)/shard_map/ppermute | solution.py:350
  19.0 1.8 %collective-permute-done.1.refs_2_ = f32[4,16,256]{2,1,0:T(8,128)S(1)} collective-permute-done((f32[4,16,256]{2,1,0:T(8,128)S(1)}, f32[4,16,256]{2,1,0:T(8,128)S(1)}, u32[]{:S(2)}, u32[]{:S(2)}) %collective-permute-start.1) | collective-permute-done | bytes 65568 | tf_op jit(solution)/shard_map/ppermute | solution.py:350
  20.8 4.4 %collective-permute-start.2 = (f32[4,272,256]{2,1,0:T(8,128)S(1)}, f32[4,272,256]{2,1,0:T(8,128)S(1)}, u32[]{:S(2)}, u32[]{:S(2)}) collective-permute-start(f32[4,272,256]{2,1,0:T(8,128)S(1)} %respond.1.late), channel_id=1, source_target_pairs={{4,0},{12,8},{5,1},{13,9},{6,2},{14,10},{7,3},{15,11},{20,16},{28,... | collective-permute-start | bytes 3342344 | tf_op jit(solution)/shard_map/ppermute | solution.py:341
  25.3 2.3 %collective-permute-done.2.refs_6_ = f32[4,272,256]{2,1,0:T(8,128)S(1)} collective-permute-done((f32[4,272,256]{2,1,0:T(8,128)S(1)}, f32[4,272,256]{2,1,0:T(8,128)S(1)}, u32[]{:S(2)}, u32[]{:S(2)}) %collective-permute-start.2) | collective-permute-done | bytes 1114144 | tf_op jit(solution)/shard_map/ppermute | solution.py:341
  27.5 0.2 chunk.10
  27.7 1.3 %collective-permute-start.3 = (f32[4,16,256]{2,1,0:T(8,128)S(1)}, f32[4,16,256]{2,1,0:T(8,128)S(1)}, u32[]{:S(2)}, u32[]{:S(2)}) collective-permute-start(f32[4,16,256]{2,1,0:T(8,128)S(1)} %get-tuple-element.44), channel_id=1, source_target_pairs={{0,4},{4,8},{8,12},{1,5},{5,9},{9,13},{2,6},{6,10},{10,14},{3,7},{... | collective-permute-start | bytes 196616 | tf_op jit(solution)/shard_map/ppermute | solution.py:350
  29.0 1.8 %collective-permute-done.3.refs_2_.entering = f32[4,16,256]{2,1,0:T(8,128)S(1)} collective-permute-done((f32[4,16,256]{2,1,0:T(8,128)S(1)}, f32[4,16,256]{2,1,0:T(8,128)S(1)}, u32[]{:S(2)}, u32[]{:S(2)}) %collective-permute-start.3) | collective-permute-done | bytes 65568 | tf_op jit(solution)/shard_map/ppermute | solution.py:350
  30.9 0.7 %collective-permute-start.4 = (f32[4,16,256]{2,1,0:T(8,128)S(1)}, f32[4,16,256]{2,1,0:T(8,128)S(1)}, u32[]{:S(2)}, u32[]{:S(2)}) collective-permute-start(f32[4,16,256]{2,1,0:T(8,128)S(1)} %answer.1), channel_id=1, source_target_pairs={{8,4},{9,5},{10,6},{11,7},{24,20},{25,21},{26,22},{27,23}} | collective-permute-start | bytes 196616 | tf_op jit(solution)/shard_map/ppermute | solution.py:335
  31.6 0.0 collective-permute-done.4.refs_6_
  31.6 1.3 %collective-permute-start.5 = (f32[4,16,256]{2,1,0:T(8,128)S(1)}, f32[4,16,256]{2,1,0:T(8,128)S(1)}, u32[]{:S(2)}, u32[]{:S(2)}) collective-permute-start(f32[4,16,256]{2,1,0:T(8,128)S(1)} %get-tuple-element.48.refs_7_), channel_id=1, source_target_pairs={{0,4},{4,8},{8,12},{1,5},{5,9},{9,13},{2,6},{6,10},{10,14},{3,7},{... | collective-permute-start | bytes 196616 | tf_op jit(solution)/shard_map/ppermute | solution.py:350
  32.9 9.3 %collective-permute-done.5.refs_2_ = f32[4,16,256]{2,1,0:T(8,128)S(1)} collective-permute-done((f32[4,16,256]{2,1,0:T(8,128)S(1)}, f32[4,16,256]{2,1,0:T(8,128)S(1)}, u32[]{:S(2)}, u32[]{:S(2)}) %collective-permute-start.5) | collective-permute-done | bytes 65568 | tf_op jit(solution)/shard_map/ppermute | solution.py:350
  42.2 3.8 %chunk.13 = (f32[8,16,256]{2,1,0:T(8,128)S(1)}, f32[4,16,256]{2,1,0:T(8,128)S(1)}) custom-call(bf16[8,1024,256]{2,1,0:T(8,128)(2,1)S(1)} %get-tuple-element.32.weight.refs_0_, f32[8,16,256]{2,1,0:T(8,128)S(1)} %get-tuple-element.33.base.refs_1_, f32[4,16,256]{2,1,0:T(8,128)S(1)} %collective-permute-done.5.refs_2_, ...), custom_call_target="tpu_custom_call" | custom-call | tf_op jit(solution)/shard_map/chunk/pallas_call | solution.py:284
  46.0 0.3 chunk.14
  46.3 1.3 %collective-permute-start.6 = (f32[4,16,256]{2,1,0:T(8,128)S(1)}, f32[4,16,256]{2,1,0:T(8,128)S(1)}, u32[]{:S(2)}, u32[]{:S(2)}) collective-permute-start(f32[4,16,256]{2,1,0:T(8,128)S(1)} %get-tuple-element.52.refs_5_), channel_id=1, source_target_pairs={{0,4},{4,8},{8,12},{1,5},{5,9},{9,13},{2,6},{6,10},{10,14},{3,7},{... | collective-permute-start | bytes 196616 | tf_op jit(solution)/shard_map/ppermute | solution.py:350
  47.6 7.5 %collective-permute-done.6.refs_2_ = f32[4,16,256]{2,1,0:T(8,128)S(1)} collective-permute-done((f32[4,16,256]{2,1,0:T(8,128)S(1)}, f32[4,16,256]{2,1,0:T(8,128)S(1)}, u32[]{:S(2)}, u32[]{:S(2)}) %collective-permute-start.6) | collective-permute-done | bytes 65568 | tf_op jit(solution)/shard_map/ppermute | solution.py:350
  55.1 4.9 %chunk.15 = (f32[8,16,256]{2,1,0:T(8,128)}, f32[4,16,256]{2,1,0:T(8,128)}) custom-call(bf16[8,1024,256]{2,1,0:T(8,128)(2,1)S(1)} %get-tuple-element.32.weight.refs_0_, f32[8,16,256]{2,1,0:T(8,128)S(1)} %get-tuple-element.33.base.refs_1_, f32[4,16,256]{2,1,0:T(8,128)S(1)} %collective-permute-done.6.refs_2_, ...), custom_call_target="tpu_custom_call" | custom-call | tf_op jit(solution)/shard_map/chunk/pallas_call | solution.py:284
  (5 shorter events, 0.1 us)
Async XLA Ops:
  3.8 13.8 %collective-permute-start = (f32[3,272,256]{2,1,0:T(8,128)S(1)}, f32[3,272,256]{2,1,0:T(8,128)S(1)}, u32[]{:S(2)}, u32[]{:S(2)}) collective-permute-start(f32[3,272,256]{2,1,0:T(8,128)S(1)} %get-tuple-element.34.soon), channel_id=1, source_target_pairs={{4,0},{8,4},{12,8},{5,1},{9,5},{13,9},{6,2},{10,6},{14,10},{7,3},{... | collective-permute-start | bytes 2506760 | tf_op jit(solution)/shard_map/ppermute | solution.py:328
  17.7 3.1 %collective-permute-start.1 = (f32[4,16,256]{2,1,0:T(8,128)S(1)}, f32[4,16,256]{2,1,0:T(8,128)S(1)}, u32[]{:S(2)}, u32[]{:S(2)}) collective-permute-start(f32[4,16,256]{2,1,0:T(8,128)S(1)} %get-tuple-element.38.refs_7_), channel_id=1, source_target_pairs={{0,4},{4,8},{8,12},{1,5},{5,9},{9,13},{2,6},{6,10},{10,14},{3,7},{... | collective-permute-start | bytes 196616 | tf_op jit(solution)/shard_map/ppermute | solution.py:350
  20.8 6.7 %collective-permute-start.2 = (f32[4,272,256]{2,1,0:T(8,128)S(1)}, f32[4,272,256]{2,1,0:T(8,128)S(1)}, u32[]{:S(2)}, u32[]{:S(2)}) collective-permute-start(f32[4,272,256]{2,1,0:T(8,128)S(1)} %respond.1.late), channel_id=1, source_target_pairs={{4,0},{12,8},{5,1},{13,9},{6,2},{14,10},{7,3},{15,11},{20,16},{28,... | collective-permute-start | bytes 3342344 | tf_op jit(solution)/shard_map/ppermute | solution.py:341
  27.7 3.1 %collective-permute-start.3 = (f32[4,16,256]{2,1,0:T(8,128)S(1)}, f32[4,16,256]{2,1,0:T(8,128)S(1)}, u32[]{:S(2)}, u32[]{:S(2)}) collective-permute-start(f32[4,16,256]{2,1,0:T(8,128)S(1)} %get-tuple-element.44), channel_id=1, source_target_pairs={{0,4},{4,8},{8,12},{1,5},{5,9},{9,13},{2,6},{6,10},{10,14},{3,7},{... | collective-permute-start | bytes 196616 | tf_op jit(solution)/shard_map/ppermute | solution.py:350
  30.9 0.7 %collective-permute-start.4 = (f32[4,16,256]{2,1,0:T(8,128)S(1)}, f32[4,16,256]{2,1,0:T(8,128)S(1)}, u32[]{:S(2)}, u32[]{:S(2)}) collective-permute-start(f32[4,16,256]{2,1,0:T(8,128)S(1)} %answer.1), channel_id=1, source_target_pairs={{8,4},{9,5},{10,6},{11,7},{24,20},{25,21},{26,22},{27,23}} | collective-permute-start | bytes 196616 | tf_op jit(solution)/shard_map/ppermute | solution.py:335
  31.6 10.6 %collective-permute-start.5 = (f32[4,16,256]{2,1,0:T(8,128)S(1)}, f32[4,16,256]{2,1,0:T(8,128)S(1)}, u32[]{:S(2)}, u32[]{:S(2)}) collective-permute-start(f32[4,16,256]{2,1,0:T(8,128)S(1)} %get-tuple-element.48.refs_7_), channel_id=1, source_target_pairs={{0,4},{4,8},{8,12},{1,5},{5,9},{9,13},{2,6},{6,10},{10,14},{3,7},{... | collective-permute-start | bytes 196616 | tf_op jit(solution)/shard_map/ppermute | solution.py:350
  46.3 8.8 %collective-permute-start.6 = (f32[4,16,256]{2,1,0:T(8,128)S(1)}, f32[4,16,256]{2,1,0:T(8,128)S(1)}, u32[]{:S(2)}, u32[]{:S(2)}) collective-permute-start(f32[4,16,256]{2,1,0:T(8,128)S(1)} %get-tuple-element.52.refs_5_), channel_id=1, source_target_pairs={{0,4},{4,8},{8,12},{1,5},{5,9},{9,13},{2,6},{6,10},{10,14},{3,7},{... | collective-permute-start | bytes 196616 | tf_op jit(solution)/shard_map/ppermute | solution.py:350

commit v5 on v4

--- a/solution.py
+++ b/solution.py
@@ -37,14 +37,20 @@
     return lax.dot_general(a, b, (((1,), (1,)), ((), ())), preferred_element_type=F32)
 
 
-def dot_parts(a, b):
-    return dot(jnp.concatenate([a[0], a[0], a[1]], axis=1), jnp.concatenate([b[0], b[1], b[0]], axis=0))
+def dot_parts(a, b, dot=dot):
+    return dot(a[0], b[0]) + (dot(a[0], b[1]) + dot(a[1], b[0]))
 
 
 def place_operators(weight, i, down, up):
     phases = down.shape[0]
     for k, part in enumerate((*split(down.T), *split(up.T))):
         weight[i, k * phases : (k + 1) * phases] = part
+
+
+def operator(weight, i, k):
+    phases = weight.shape[2]
+    at = 2 * k * phases
+    return weight[i, at : at + phases], weight[i, at + phases : at + 2 * phases]
 
 
 def response(first, last, x_high, x_low, weight, base, kept):
@@ -58,16 +64,11 @@
         x_high[i, phases:rows], x_low[i, phases:rows] = split(end)
         return top, end
 
-    def operator(i, k):
-        high = weight[i, 2 * k * phases : (2 * k + 1) * phases]
-        low = weight[i, (2 * k + 1) * phases : (2 * k + 2) * phases]
-        return [high, low, high]
-
-    def value(i):
-        return [x_high[i], x_high[i], x_low[i]]
-
-    def product(values, operators):
-        return dot(jnp.concatenate(values, axis=1), jnp.concatenate(operators, axis=0))
+    def from_below(i):
+        return dot_parts((x_high[i - 1], x_low[i - 1]), operator(weight, i, 0))
+
+    def from_above(i):
+        return dot_parts((x_high[i + 1], x_low[i + 1]), operator(weight, i, 1))
 
     for d in range(first, last):
         if d == 0:
@@ -77,15 +78,15 @@
             kept[0, 0:phases] = high.astype(F32) + low.astype(F32)
             kept[0, phases:rows] = base[0]
             continue
-        store(d, product(value(d - 1), operator(d, 0)))
+        store(d, from_below(d))
 
         def level(k, _, d=d):
             i = d - k
-            store(i, product(value(i - 1) + value(i + 1), operator(i, 0) + operator(i, 1)))
+            store(i, from_below(i) + from_above(i))
             return 0
 
         lax.fori_loop(1, d, level, 0)
-        kept[d - first, 0:phases], kept[d - first, phases:rows] = store(0, product(value(1), operator(0, 1)))
+        kept[d - first, 0:phases], kept[d - first, phases:rows] = store(0, from_above(0))
 
 
 def products(levels, given, weight, base, buffers, sems):
@@ -108,8 +109,7 @@
         at = i - first
         here = split(inv[at])
         place_operators(weight, i, dot_parts(here, split(down[at])), dot_parts(here, split(up[at])))
-        high, low = split(pay[at])
-        base[i] = dot_nt(high, here[0]) + (dot_nt(high, here[1]) + dot_nt(low, here[0]))
+        base[i] = dot_parts(split(pay[at]), here, dot_nt)
 
 
 def prepare_kernel(inv, down, up, reward, weight, base, x_high, x_low, kept, *scratch):
@@ -206,6 +206,13 @@
     return fold(dot(values, jnp.concatenate([operator for _, operator in terms], axis=0)))
 
 
+def apply_each(values, operator, columns):
+    phases = operator.shape[1]
+    values = jnp.concatenate(values, axis=0) if len(values) > 1 else values[0]
+    total = dot(values, operator[0:phases]) + dot(values, operator[phases:])
+    return [fold(total[at : at + 2 * columns]) for at in range(0, total.shape[0], 2 * columns)]
+
+
 def whole(operator):
     return jnp.concatenate(split(operator), axis=0)
 
@@ -217,17 +224,46 @@
 def carried(soon, late, past, first, last):
     phases = soon.shape[2]
     above = {n: kept_at(soon, late, n - 1)[phases:] for n in range(max(first, 1), last + 1)}
+    columns = soon.shape[1] - phases
     for j in range(last) if past else ():
         pairs = [(n, n - j) for n in above if n - j in past]
-        for n, m in pairs:
-            above[n] += apply([(past[m], whole(kept_at(soon, late, j)[0:phases]))])
+        if pairs:
+            terms = [past[m] for _, m in pairs]
+            for (n, _), term in zip(pairs, apply_each(terms, whole(kept_at(soon, late, j)[0:phases]), columns)):
+                above[n] += term
     return above
 
 
-def chunk_kernel(chunk, place, names, *refs):
+def wave(first, weight, base, now, above, feedback, due, emit):
+    levels, _, phases = base.shape
+    for turn in range(levels + 2 * (CHUNK - 1)):
+        for k in range(CHUNK):
+            i = turn - 2 * k
+            if not (0 <= i < levels and due(i, k)):
+                continue
+            n = first + 1 + k
+            terms = []
+            if (i - 1, n) in now:
+                terms.append((now[i - 1, n], weight[i, 0 : 2 * phases]))
+            if n > 1:
+                over = stack(above[n - 1]) if i == levels - 1 else now[i + 1, n - 1]
+                terms.append((over, weight[i, 2 * phases : 4 * phases]))
+            value = base[i] + apply(terms) if terms else base[i]
+            now[i, n] = stack(value)
+            emit(i, k, value)
+            if i == levels - 1:
+                for later in range(n, first + CHUNK):
+                    above[later] += apply([(now[i, n], feedback[later - n])])
+
+
+def edge_level(levels, k):
+    return levels - 2 - k
+
+
+def chunk_kernel(chunk, place, part, names, *refs):
     given = dict(zip(names, refs))
     new_state, leaving = refs[len(names) :]
-    weight, base, soon = given["weight"], given["base"], given["soon"]
+    weight, base = given["weight"], given["base"]
     levels, columns, phases = base.shape
     first = chunk * CHUNK
 
@@ -238,60 +274,160 @@
 
     @pl.when(lax.axis_index("lvl") == place)
     def _():
-        feedback = [whole(soon[j, 0:phases]) for j in range(SOON)]
-        if not first:
-            above = carried(soon, None, {}, first, first + CHUNK - 1)
-        elif "late" in given:
-            past = {n + 1: stack(given["earlier"][n]) for n in range(first)}
-            above = carried(soon, given["late"], past, first, first + CHUNK - 1)
-        else:
-            zero = jnp.zeros((columns, phases), F32)
-            above = {first + k: given["returned"][k] if "returned" in given else zero for k in range(CHUNK)}
+        zero = jnp.zeros((columns, phases), F32)
+        above, feedback = {first + k: zero for k in range(CHUNK)}, []
+        if part != "early":
+            soon = given["soon"]
+            feedback = [whole(soon[j, 0:phases]) for j in range(SOON)]
+            if not first:
+                above = carried(soon, None, {}, first, first + CHUNK - 1)
+            elif "late" in given:
+                past = {n + 1: stack(given["earlier"][n]) for n in range(first)}
+                above = carried(soon, given["late"], past, first, first + CHUNK - 1)
+            elif "returned" in given:
+                above = {first + k: given["returned"][k] for k in range(CHUNK)}
 
         now = {}
-        if first:
+        if part == "late":
+            for k in range(CHUNK):
+                now[edge_level(levels, k), first + 1 + k] = stack(given["edge"][k])
+            new_state[...] = given["state"][...]
+        elif first:
             for i in range(levels):
                 now[i, first] = stack(given["state"][i])
-        if "entering" in given:
+        if part != "late" and "entering" in given:
             for k in range(CHUNK):
                 now[-1, first + 1 + k] = stack(given["entering"][k])
-        for turn in range(levels + 2 * (CHUNK - 1)):
-            for k in range(CHUNK):
-                i = turn - 2 * k
-                if not 0 <= i < levels:
-                    continue
-                n = first + 1 + k
-                terms = []
-                if (i - 1, n) in now:
-                    terms.append((now[i - 1, n], weight[i, 0 : 2 * phases]))
-                if n > 1:
-                    over = stack(above[n - 1]) if i == levels - 1 else now[i + 1, n - 1]
-                    terms.append((over, weight[i, 2 * phases : 4 * phases]))
-                value = base[i] + apply(terms) if terms else base[i]
-                now[i, n] = stack(value)
-                if k == CHUNK - 1:
-                    new_state[i] = value
-                if i == levels - 1:
-                    leaving[k] = value
-                    for later in range(n, first + CHUNK):
-                        above[later] += apply([(now[i, n], feedback[later - n])])
-
-
-def run_chunk(chunk, place, given, last=False):
+
+        def due(i, k):
+            return part == "all" or (i <= edge_level(levels, k)) == (part == "early")
+
+        def emit(i, k, value):
+            if k == CHUNK - 1:
+                new_state[i] = value
+            if i == (edge_level(levels, k) if part == "early" else levels - 1):
+                leaving[k] = value
+
+        wave(first, weight, base, now, above, feedback, due, emit)
+
+
+def run_chunk(chunk, place, given, part="all"):
     given = {name: x for name, x in given.items() if x is not None}
-    names = tuple(given)
     levels, columns, phases = given["base"].shape
     return pl.pallas_call(
-        functools.partial(chunk_kernel, chunk, place, names),
-        out_shape=[
-            (jax.ShapeDtypeStruct if last else resident)((levels, columns, phases), F32),
-            resident((CHUNK, columns, phases), F32),
-        ],
+        functools.partial(chunk_kernel, chunk, place, part, tuple(given)),
+        out_shape=[resident((levels, columns, phases), F32), resident((CHUNK, columns, phases), F32)],
         in_specs=[VMEM] * len(given),
         out_specs=[VMEM] * 2,
         compiler_params=pltpu.CompilerParams(vmem_limit_bytes=16 * 2**20),
         name="chunk",
     )(*[pin(x) for x in given.values()])
+
+
+def among(places):
+    return functools.reduce(jnp.logical_or, [lax.axis_index("lvl") == place for place in places])
+
+
+def spread_kernel(places, weight, soon, out):
+    levels, _, phases = weight.shape
+
+    def get(at):
+        return out[at, 0:phases], out[at, phases : 2 * phases]
+
+    def put(at, value):
+        out[at, 0:phases], out[at, phases : 2 * phases] = split(value)
+
+    @pl.when(among(places))
+    def _():
+        out[0] = weight[0, 0 : 2 * phases]
+
+        def up(i, _):
+            put(i, dot_parts(get(i - 1), operator(weight, i, 0)))
+            return 0
+
+        lax.fori_loop(1, levels, up, 0)
+        feedback = [split(soon[j, 0:phases]) for j in range(CHUNK - 1)]
+        for a in range(1, CHUNK):
+            at, old = a * levels, (a - 1) * levels
+            put(at, dot_parts(get(old + 1), operator(weight, 0, 1)))
+
+            def both(i, _, at=at, old=old):
+                below = dot_parts(get(at + i - 1), operator(weight, i, 0))
+                put(at + i, below + dot_parts(get(old + i + 1), operator(weight, i, 1)))
+                return 0
+
+            lax.fori_loop(1, levels - 1, both, 0)
+            back = sum(dot_parts(get((a - 1 - j) * levels + levels - 1), feedback[j]) for j in range(a))
+            top = levels - 1
+            below = dot_parts(get(at + top - 1), operator(weight, top, 0))
+            put(at + top, below + dot_parts(split(back), operator(weight, top, 1)))
+
+
+def spread(places, weight, soon):
+    levels, _, phases = weight.shape
+    return pl.pallas_call(
+        functools.partial(spread_kernel, places),
+        out_shape=resident((CHUNK * levels, 2 * phases, phases), BF16),
+        in_specs=[VMEM] * 2,
+        out_specs=VMEM,
+        compiler_params=pltpu.CompilerParams(vmem_limit_bytes=16 * 2**20),
+        name="spread",
+    )(*[pin(x) for x in (weight, soon)])
+
+
+def finish_leaving_kernel(place, ways, entering, leaving, before, new):
+    levels = ways.shape[0] // CHUNK
+    columns = entering.shape[1]
+
+    @pl.when(lax.axis_index("lvl") != place)
+    def _():
+        new[...] = before[...]
+
+    @pl.when(lax.axis_index("lvl") == place)
+    def _():
+        values = [stack(entering[k]) for k in range(CHUNK)]
+        total = [leaving[k] for k in range(CHUNK)]
+        for a in range(CHUNK):
+            for k, term in enumerate(apply_each(values[: CHUNK - a], ways[a * levels + levels - 1], columns)):
+                total[a + k] += term
+        for k in range(CHUNK):
+            new[k] = total[k]
+
+
+def finish_leaving(place, ways, entering, leaving, before):
+    return pl.pallas_call(
+        functools.partial(finish_leaving_kernel, place),
+        out_shape=resident(leaving.shape, F32),
+        in_specs=[VMEM] * 4,
+        out_specs=VMEM,
+        compiler_params=pltpu.CompilerParams(vmem_limit_bytes=8 * 2**20),
+        name="finish_leaving",
+    )(*[pin(x) for x in (ways, entering, leaving, before)])
+
+
+def finish_state_kernel(place, ways, entering, state, new):
+    levels = state.shape[0]
+
+    @pl.when(lax.axis_index("lvl") != place)
+    def _():
+        new[...] = state[...]
+
+    @pl.when(lax.axis_index("lvl") == place)
+    def _():
+        values = [stack(entering[CHUNK - 1 - a]) for a in range(CHUNK)]
+        for i in range(levels):
+            new[i] = state[i] + apply([(values[a], ways[a * levels + i]) for a in range(CHUNK)])
+
+
+def finish_state(place, ways, entering, state, last):
+    return pl.pallas_call(
+        functools.partial(finish_state_kernel, place),
+        out_shape=(jax.ShapeDtypeStruct if last else resident)(state.shape, F32),
+        in_specs=[VMEM] * 3,
+        out_specs=VMEM,
+        compiler_params=pltpu.CompilerParams(vmem_limit_bytes=8 * 2**20),
+        name="finish_state",
+    )(*[pin(x) for x in (ways, entering, state)])
 
 
 def answer_kernel(step, soon, late, entering, returned):
@@ -320,34 +456,51 @@
     if columns != given:
         reward = jnp.pad(reward, ((0, 0), (0, columns - given), (0, 0)))
     count = lax.axis_size("lvl")
-    assert CHUNKS == 2
     weights, started, soon_here = prepare(inverse_diag, down_block, up_block, reward)
     late_here = respond(weights, started)
-    upward = [(d, d + 1) for d in range(count - 1)]
-    from_odd = [(d + 1, d) for d in range(0, count - 1, 2)]
-    soon = lax.ppermute(soon_here, "lvl", [(d + 1, d) for d in range(count - 1)])
+    assert CHUNKS == 2 and count > 1
+    top = count - 1
+    from_odd = [(d + 1, d) for d in range(0, top, 2)]
+    soon = lax.ppermute(soon_here, "lvl", [(d + 1, d) for d in range(top)])
     soon, late_here = lax.optimization_barrier((soon, late_here))
-    late = returned = entering = leaving = state = None
+    weight, base = weights
+    own = {"weight": weight, "base": base, "soon": soon}
+    ready = [d for d in range(1, count) if d % 2 == 0 or d == top]
+    state = leaving = entering = late = ways = parted = None
     for step in range(count + 1):
+        place = step - 1
         earlier = leaving
-        shared = {"weight": weights[0], "base": weights[1], "entering": entering}
+        returned = edge = None
         if step % 2 == 0 and 0 < step < count:
-            returned = lax.ppermute(answer(step, soon_here, late_here, entering), "lvl", [(step, step - 1)])
+            returned = lax.ppermute(answer(step, soon_here, late_here, entering), "lvl", [(step, place)])
+            state, edge = run_chunk(
+                1, place, {"weight": weight, "base": base, "entering": entering, "state": state}, "early"
+            )
+        if place in ready and place < top:
+            leaving = finish_leaving(place, ways, entering, parted, leaving)
         if step < count:
-            own = {**shared, "soon": soon, "state": state}
-            state, leaving = run_chunk(0, step, own)
+            state, leaving = run_chunk(0, step, {**own, "entering": entering, "state": state, "leaving": leaving})
         if step == 1:
             late_sent, entering = lax.optimization_barrier((late_here, entering))
             late = lax.ppermute(late_sent, "lvl", from_odd)
-        if step > 0:
-            own = {**shared, "soon": soon, "state": state, "leaving": leaving}
-            if step % 2:
-                own.update(late=late, earlier=earlier)
-            elif step < count:
-                own.update(returned=returned)
-            state, leaving = run_chunk(1, step - 1, own, last=step == count)
+            state, leaving = run_chunk(
+                1, 0, {**own, "late": late, "earlier": earlier, "state": state, "leaving": leaving}
+            )
+        if returned is not None:
+            state, leaving = run_chunk(
+                1, place, {**own, "returned": returned, "edge": edge, "state": state, "leaving": leaving}, "late"
+            )
+        came = entering
         if step < count:
-            entering = lax.ppermute(leaving, "lvl", upward)
+            pairs = [(d, d + 1) for d in (place, step) if 0 <= d < top]
+            entering = lax.ppermute(leaving, "lvl", pairs) if pairs else None
+        if step == 0:
+            ways, entering = lax.optimization_barrier((spread(ready, weight, soon), entering))
+        if place in ready:
+            state = finish_state(place, ways, came, state, step == count)
+        if step in ready:
+            extra = {} if step == top else {"late": late, "earlier": leaving}
+            state, parted = run_chunk(1, step, {**own, **extra, "state": state})
     return state[:, :given] if columns != given else state
 
 

time: 60.3 us -> 60.4 us (level)
  Pallas kernels: 24.2 us -> 37.6 us
  waiting for transfers between devices: 22.8 us -> 13.2 us
  starting transfers between devices: 12.8 us -> 9.16 us
    pallas_call x8 -> x13, Pallas kernels: 9.22 us -> 22.6 us  [the longest x1 11.3 us: spread(): pl.pallas_call(functools.partial(spread_kernel, places), out_shape=reside...]
    ppermute x5, waiting for transfers between devices: 20.6 us -> 11.1 us  [the longest x4 11.1 us: local(): entering = lax.ppermute(leaving, 'lvl', pairs) if pairs else None]
    ppermute x1, starting transfers between devices: 4.37 us -> 1.94 us  [local(): late = lax.ppermute(late_sent, 'lvl', from_odd)]
    ppermute x5, starting transfers between devices: 7.8 us -> 6.55 us  [the longest x4 3.92 us: local(): entering = lax.ppermute(leaving, 'lvl', pairs) if pairs else None]
  transfers between devices with their start and end apart: 7 -> 7, of which waited for: 5 -> 2; matrix products, arithmetic and copies ran while one was open for 0% -> 0% of each run, Pallas kernels for 19% -> 46%
where the time goes in v5:
time: 60.4 us; the launch traced here: 60.2 us
  Pallas kernels  37.6 us (62%)
  waiting for transfers between devices  13.2 us (22%)
  starting transfers between devices  9.16 us (15%)
    pallas_call x1, Pallas kernels, spread(): pl.pallas_call(functools.partial(spread_kernel, places), out_shape=reside...  11.3 us
    ppermute x4, waiting for transfers between devices, local(): entering = lax.ppermute(leaving, 'lvl', pairs) if pairs else None  11.1 us
    pallas_call x9, Pallas kernels, run_chunk(): pl.pallas_call(functools.partial(chunk_kernel, chunk, place, part, tuple(...  9.16 us
    pallas_call x1, Pallas kernels, respond(): pl.pallas_call(respond_kernel, out_shape=resident((AHEAD - SOON, rows, ph...  7.22 us
    ppermute x4, starting transfers between devices, local(): entering = lax.ppermute(leaving, 'lvl', pairs) if pairs else None  3.92 us
    pallas_call x1, Pallas kernels, prepare(): pl.pallas_call(prepare_rest_kernel, out_shape=operators(levels, columns,...  3.9 us
    pallas_call x1, Pallas kernels, prepare(): pl.pallas_call(prepare_kernel, out_shape=operators(SOON, columns, phases)...  3.82 us
    ppermute x1, starting transfers between devices, local(): soon = lax.ppermute(soon_here, 'lvl', [(d + 1, d) for d in range(top)])  2.63 us
  transfers between devices with their start and end apart: 7, of which 2 were waited for; matrix products, arithmetic and copies ran while one was open for 0% of the time, Pallas kernels for 46%

profile of v5, /device:TPU:11, one launch (start us, length us, event | category | flops | bytes accessed | tf_op | source)
XLA Modules:
  0.0 60.2 jit_solution(15141700481258691663)
XLA Ops:
  0.0 3.8 %prepare.1 = (bf16[3,1024,256]{2,1,0:T(8,128)(2,1)S(1)}, f32[3,16,256]{2,1,0:T(8,128)S(1)}, bf16[3,272,256]{2,1,0:T(8,128)(2,1)S(1)}, bf16[3,272,256]{2,1,0:T(8,128)(2,1)S(1)}, f32[3,272,256]{2,1,0:T(8,128)S(1)}) custom-call(f32[8,256,256]{2,1,0:T(8,128)} %inv.3, f32[8,256,256]{2,1,0:T(8,128)} %down.3, f32[8,256,256]{2,1,0:T(8,128)} %up.3, f32[8,16,256]{2,1,0:T(8,128)} %reward.3), custom_call_target="tpu_custom_call" | custom-call | tf_op jit(solution)/shard_map/prepare/pallas_call | solution.py:158
  3.8 2.6 %collective-permute-start = (f32[3,272,256]{2,1,0:T(8,128)S(1)}, f32[3,272,256]{2,1,0:T(8,128)S(1)}, u32[]{:S(2)}, u32[]{:S(2)}) collective-permute-start(f32[3,272,256]{2,1,0:T(8,128)S(1)} %get-tuple-element.37.soon), channel_id=1, source_target_pairs={{4,0},{8,4},{12,8},{5,1},{9,5},{13,9},{6,2},{10,6},{14,10},{7,3},{... | collective-permute-start | bytes 2506760 | tf_op jit(solution)/shard_map/ppermute | solution.py:464
  6.5 3.9 %prepare_rest.1 = (bf16[8,1024,256]{2,1,0:T(8,128)(2,1)S(1)}, f32[8,16,256]{2,1,0:T(8,128)S(1)}) custom-call(f32[8,256,256]{2,1,0:T(8,128)} %inv.3, f32[8,256,256]{2,1,0:T(8,128)} %down.3, f32[8,256,256]{2,1,0:T(8,128)} %up.3, f32[8,16,256]{2,1,0:T(8,128)} %reward.3, bf16[3,1024,256]{2,1,0:T(8,128)(2,1)S(1)} %get-tuple-element.34.weight_soon, ...), custom_call_target="tpu_custom_call" | custom-call | tf_op jit(solution)/shard_map/prepare_rest/pallas_call | solution.py:169
  10.4 7.2 %respond.1.late = f32[4,272,256]{2,1,0:T(8,128)S(1)} custom-call(bf16[8,1024,256]{2,1,0:T(8,128)(2,1)S(1)} %get-tuple-element.36.weight.refs_0_, f32[8,16,256]{2,1,0:T(8,128)S(1)} %get-tuple-element.38.base.refs_1_, bf16[3,272,256]{2,1,0:T(8,128)(2,1)S(1)} %get-tuple-element.39.x_high_soon, bf16[3,272,256]{2,1,0:T(8,128)(2,1)S(1)} %get-tuple-element.40.x_low_soon), custom_call_target="tpu_custom_call" | custom-call | tf_op jit(solution)/shard_map/respond/pallas_call | solution.py:183
  17.6 0.0 collective-permute-done.soon.refs_2_
  17.7 0.7 %collective-permute-start.1 = (f32[4,16,256]{2,1,0:T(8,128)S(1)}, f32[4,16,256]{2,1,0:T(8,128)S(1)}, u32[]{:S(2)}, u32[]{:S(2)}) collective-permute-start(f32[4,16,256]{2,1,0:T(8,128)S(1)} %get-tuple-element.42.refs_5_.refs_4_), channel_id=1, source_target_pairs={{0,4},{1,5},{2,6},{3,7},{16,20},{17,21},{18,22},{19,23}} | collective-permute-start | bytes 196616 | tf_op jit(solution)/shard_map/ppermute | solution.py:496
  18.3 11.3 %spread.1.ways = bf16[32,512,256]{2,1,0:T(8,128)(2,1)S(1)} custom-call(bf16[8,1024,256]{2,1,0:T(8,128)(2,1)S(1)} %get-tuple-element.36.weight.refs_0_, f32[3,272,256]{2,1,0:T(8,128)S(1)} %collective-permute-done.soon.refs_2_), custom_call_target="tpu_custom_call" | custom-call | tf_op jit(solution)/shard_map/spread/pallas_call | solution.py:368
  29.7 0.0 collective-permute-done.1.refs_3_
  29.7 1.9 %collective-permute-start.2 = (f32[4,272,256]{2,1,0:T(8,128)S(1)}, f32[4,272,256]{2,1,0:T(8,128)S(1)}, u32[]{:S(2)}, u32[]{:S(2)}) collective-permute-start(f32[4,272,256]{2,1,0:T(8,128)S(1)} %respond.1.late), channel_id=1, source_target_pairs={{4,0},{12,8},{5,1},{13,9},{6,2},{14,10},{7,3},{15,11},{20,16},{28,... | collective-permute-start | bytes 3342344 | tf_op jit(solution)/shard_map/ppermute | solution.py:485
  31.6 0.2 chunk.10
  31.9 2.1 %collective-permute-done.2.refs_3_ = f32[4,272,256]{2,1,0:T(8,128)S(1)} collective-permute-done((f32[4,272,256]{2,1,0:T(8,128)S(1)}, f32[4,272,256]{2,1,0:T(8,128)S(1)}, u32[]{:S(2)}, u32[]{:S(2)}) %collective-permute-start.2) | collective-permute-done | bytes 1114144 | tf_op jit(solution)/shard_map/ppermute | solution.py:485
  33.9 0.7 %collective-permute-start.3 = (f32[4,16,256]{2,1,0:T(8,128)S(1)}, f32[4,16,256]{2,1,0:T(8,128)S(1)}, u32[]{:S(2)}, u32[]{:S(2)}) collective-permute-start(f32[4,16,256]{2,1,0:T(8,128)S(1)} %get-tuple-element.50.refs_5_), channel_id=1, source_target_pairs={{0,4},{4,8},{1,5},{5,9},{2,6},{6,10},{3,7},{7,11},{16,20},{20,24},... | collective-permute-start | bytes 196616 | tf_op jit(solution)/shard_map/ppermute | solution.py:496
  34.6 0.0 collective-permute-done.3.entering.refs_2_.refs_3_
  34.7 0.7 %collective-permute-start.4 = (f32[4,16,256]{2,1,0:T(8,128)S(1)}, f32[4,16,256]{2,1,0:T(8,128)S(1)}, u32[]{:S(2)}, u32[]{:S(2)}) collective-permute-start(f32[4,16,256]{2,1,0:T(8,128)S(1)} %answer.1), channel_id=1, source_target_pairs={{8,4},{9,5},{10,6},{11,7},{24,20},{25,21},{26,22},{27,23}} | collective-permute-start | bytes 196616 | tf_op jit(solution)/shard_map/ppermute | solution.py:475
  35.4 0.0 collective-permute-done.4.refs_3_
  35.5 1.3 %collective-permute-start.5 = (f32[4,16,256]{2,1,0:T(8,128)S(1)}, f32[4,16,256]{2,1,0:T(8,128)S(1)}, u32[]{:S(2)}, u32[]{:S(2)}) collective-permute-start(f32[4,16,256]{2,1,0:T(8,128)S(1)} %get-tuple-element.56.refs_4_.before), channel_id=1, source_target_pairs={{4,8},{8,12},{5,9},{9,13},{6,10},{10,14},{7,11},{11,15},{20,24},{2... | collective-permute-start | bytes 196616 | tf_op jit(solution)/shard_map/ppermute | solution.py:496
  36.8 0.3 chunk.15
  37.0 11.1 %collective-permute-done.5.entering.refs_3_ = f32[4,16,256]{2,1,0:T(8,128)S(1)} collective-permute-done((f32[4,16,256]{2,1,0:T(8,128)S(1)}, f32[4,16,256]{2,1,0:T(8,128)S(1)}, u32[]{:S(2)}, u32[]{:S(2)}) %collective-permute-start.5) | collective-permute-done | bytes 65568 | tf_op jit(solution)/shard_map/ppermute | solution.py:496
  48.2 3.8 %chunk.16 = (f32[8,16,256]{2,1,0:T(8,128)S(1)}, f32[4,16,256]{2,1,0:T(8,128)S(1)}) custom-call(bf16[8,1024,256]{2,1,0:T(8,128)(2,1)S(1)} %get-tuple-element.36.weight.refs_0_, f32[8,16,256]{2,1,0:T(8,128)S(1)} %get-tuple-element.38.base.refs_1_, f32[3,272,256]{2,1,0:T(8,128)S(1)} %collective-permute-done.soon.refs_2_, ...), custom_call_target="tpu_custom_call" | custom-call | tf_op jit(solution)/shard_map/chunk/pallas_call | solution.py:317
  51.9 1.3 %collective-permute-start.6 = (f32[4,16,256]{2,1,0:T(8,128)S(1)}, f32[4,16,256]{2,1,0:T(8,128)S(1)}, u32[]{:S(2)}, u32[]{:S(2)}) collective-permute-start(f32[4,16,256]{2,1,0:T(8,128)S(1)} %get-tuple-element.60), channel_id=1, source_target_pairs={{8,12},{9,13},{10,14},{11,15},{24,28},{25,29},{26,30},{27,31}} | collective-permute-start | bytes 196616 | tf_op jit(solution)/shard_map/ppermute | solution.py:496
  53.3 4.8 %chunk.17 = (f32[8,16,256]{2,1,0:T(8,128)S(1)}, f32[4,16,256]{2,1,0:T(8,128)}) custom-call(bf16[8,1024,256]{2,1,0:T(8,128)(2,1)S(1)} %get-tuple-element.36.weight.refs_0_, f32[8,16,256]{2,1,0:T(8,128)S(1)} %get-tuple-element.38.base.refs_1_, f32[3,272,256]{2,1,0:T(8,128)S(1)} %collective-permute-done.soon.refs_2_, f32[8,16,256]{2,1,0:T(8,128)S(1)} %finish_state.2.refs_3_), custom_call_target="tpu_custom_call" | custom-call | tf_op jit(solution)/shard_map/chunk/pallas_call | solution.py:317
  58.1 0.0 collective-permute-done.6.entering
  58.1 2.1 %finish_state.3 = f32[8,16,256]{2,1,0:T(8,128)} custom-call(bf16[32,512,256]{2,1,0:T(8,128)(2,1)S(1)} %spread.1.ways, f32[4,16,256]{2,1,0:T(8,128)S(1)} %collective-permute-done.6.entering, f32[8,16,256]{2,1,0:T(8,128)S(1)} %get-tuple-element.62.state), custom_call_target="tpu_custom_call" | custom-call | tf_op jit(solution)/shard_map/finish_state/pallas_call | solution.py:423
  (8 shorter events, 0.2 us)
Async XLA Ops:
  3.8 13.8 %collective-permute-start = (f32[3,272,256]{2,1,0:T(8,128)S(1)}, f32[3,272,256]{2,1,0:T(8,128)S(1)}, u32[]{:S(2)}, u32[]{:S(2)}) collective-permute-start(f32[3,272,256]{2,1,0:T(8,128)S(1)} %get-tuple-element.37.soon), channel_id=1, source_target_pairs={{4,0},{8,4},{12,8},{5,1},{9,5},{13,9},{6,2},{10,6},{14,10},{7,3},{... | collective-permute-start | bytes 2506760 | tf_op jit(solution)/shard_map/ppermute | solution.py:464
  17.7 12.0 %collective-permute-start.1 = (f32[4,16,256]{2,1,0:T(8,128)S(1)}, f32[4,16,256]{2,1,0:T(8,128)S(1)}, u32[]{:S(2)}, u32[]{:S(2)}) collective-permute-start(f32[4,16,256]{2,1,0:T(8,128)S(1)} %get-tuple-element.42.refs_5_.refs_4_), channel_id=1, source_target_pairs={{0,4},{1,5},{2,6},{3,7},{16,20},{17,21},{18,22},{19,23}} | collective-permute-start | bytes 196616 | tf_op jit(solution)/shard_map/ppermute | solution.py:496
  29.7 4.2 %collective-permute-start.2 = (f32[4,272,256]{2,1,0:T(8,128)S(1)}, f32[4,272,256]{2,1,0:T(8,128)S(1)}, u32[]{:S(2)}, u32[]{:S(2)}) collective-permute-start(f32[4,272,256]{2,1,0:T(8,128)S(1)} %respond.1.late), channel_id=1, source_target_pairs={{4,0},{12,8},{5,1},{13,9},{6,2},{14,10},{7,3},{15,11},{20,16},{28,... | collective-permute-start | bytes 3342344 | tf_op jit(solution)/shard_map/ppermute | solution.py:485
  33.9 0.7 %collective-permute-start.3 = (f32[4,16,256]{2,1,0:T(8,128)S(1)}, f32[4,16,256]{2,1,0:T(8,128)S(1)}, u32[]{:S(2)}, u32[]{:S(2)}) collective-permute-start(f32[4,16,256]{2,1,0:T(8,128)S(1)} %get-tuple-element.50.refs_5_), channel_id=1, source_target_pairs={{0,4},{4,8},{1,5},{5,9},{2,6},{6,10},{3,7},{7,11},{16,20},{20,24},... | collective-permute-start | bytes 196616 | tf_op jit(solution)/shard_map/ppermute | solution.py:496
  34.7 0.8 %collective-permute-start.4 = (f32[4,16,256]{2,1,0:T(8,128)S(1)}, f32[4,16,256]{2,1,0:T(8,128)S(1)}, u32[]{:S(2)}, u32[]{:S(2)}) collective-permute-start(f32[4,16,256]{2,1,0:T(8,128)S(1)} %answer.1), channel_id=1, source_target_pairs={{8,4},{9,5},{10,6},{11,7},{24,20},{25,21},{26,22},{27,23}} | collective-permute-start | bytes 196616 | tf_op jit(solution)/shard_map/ppermute | solution.py:475
  35.5 12.7 %collective-permute-start.5 = (f32[4,16,256]{2,1,0:T(8,128)S(1)}, f32[4,16,256]{2,1,0:T(8,128)S(1)}, u32[]{:S(2)}, u32[]{:S(2)}) collective-permute-start(f32[4,16,256]{2,1,0:T(8,128)S(1)} %get-tuple-element.56.refs_4_.before), channel_id=1, source_target_pairs={{4,8},{8,12},{5,9},{9,13},{6,10},{10,14},{7,11},{11,15},{20,24},{2... | collective-permute-start | bytes 196616 | tf_op jit(solution)/shard_map/ppermute | solution.py:496
  51.9 6.1 %collective-permute-start.6 = (f32[4,16,256]{2,1,0:T(8,128)S(1)}, f32[4,16,256]{2,1,0:T(8,128)S(1)}, u32[]{:S(2)}, u32[]{:S(2)}) collective-permute-start(f32[4,16,256]{2,1,0:T(8,128)S(1)} %get-tuple-element.60), channel_id=1, source_target_pairs={{8,12},{9,13},{10,14},{11,15},{24,28},{25,29},{26,30},{27,31}} | collective-permute-start | bytes 196616 | tf_op jit(solution)/shard_map/ppermute | solution.py:496

commit v6 on v5

--- a/solution.py
+++ b/solution.py
@@ -260,19 +260,19 @@
     return levels - 2 - k
 
 
-def chunk_kernel(chunk, place, part, names, *refs):
+def chunk_kernel(chunk, places, part, names, *refs):
     given = dict(zip(names, refs))
     new_state, leaving = refs[len(names) :]
     weight, base = given["weight"], given["base"]
     levels, columns, phases = base.shape
     first = chunk * CHUNK
 
-    @pl.when(lax.axis_index("lvl") != place)
+    @pl.when(jnp.logical_not(among(places)))
     def _():
         for name, target in (("state", new_state), ("leaving", leaving)):
             target[...] = given[name][...] if name in given else jnp.zeros_like(target)
 
-    @pl.when(lax.axis_index("lvl") == place)
+    @pl.when(among(places))
     def _():
         zero = jnp.zeros((columns, phases), F32)
         above, feedback = {first + k: zero for k in range(CHUNK)}, []
@@ -311,11 +311,11 @@
         wave(first, weight, base, now, above, feedback, due, emit)
 
 
-def run_chunk(chunk, place, given, part="all"):
+def run_chunk(chunk, places, given, part="all"):
     given = {name: x for name, x in given.items() if x is not None}
     levels, columns, phases = given["base"].shape
     return pl.pallas_call(
-        functools.partial(chunk_kernel, chunk, place, part, tuple(given)),
+        functools.partial(chunk_kernel, chunk, tuple(places), part, tuple(given)),
         out_shape=[resident((levels, columns, phases), F32), resident((CHUNK, columns, phases), F32)],
         in_specs=[VMEM] * len(given),
         out_specs=[VMEM] * 2,
@@ -465,42 +465,51 @@
     soon, late_here = lax.optimization_barrier((soon, late_here))
     weight, base = weights
     own = {"weight": weight, "base": base, "soon": soon}
+    assert count > 1
+    top = count - 1
+    soon = lax.ppermute(soon_here, "lvl", [(d + 1, d) for d in range(top)])
+    late = lax.ppermute(late_here, "lvl", [(d + 1, d) for d in range(0, top, 2)])
+    soon, late_here = lax.optimization_barrier((soon, late_here))
+    weight, base = weights
+    own = {"weight": weight, "base": base, "soon": soon}
     ready = [d for d in range(1, count) if d % 2 == 0 or d == top]
-    state = leaving = entering = late = ways = parted = None
+    state = leaving = entering = ways = parted = None
     for step in range(count + 1):
         place = step - 1
         earlier = leaving
         returned = edge = None
         if step % 2 == 0 and 0 < step < count:
             returned = lax.ppermute(answer(step, soon_here, late_here, entering), "lvl", [(step, place)])
-            state, edge = run_chunk(
-                1, place, {"weight": weight, "base": base, "entering": entering, "state": state}, "early"
-            )
+            given_early = {"weight": weight, "base": base, "entering": entering, "state": state}
+            state, edge = run_chunk(1, [place], given_early, "early")
         if place in ready and place < top:
             leaving = finish_leaving(place, ways, entering, parted, leaving)
-        if step < count:
-            state, leaving = run_chunk(0, step, {**own, "entering": entering, "state": state, "leaving": leaving})
+        if step == 0:
+            state, leaving = started = run_chunk(0, [0, *ready], own)
+        elif step in ready:
+            if step < top:
+                leaving = finish_leaving(step, ways, entering, started[1], leaving)
+        elif step < count:
+            state, leaving = run_chunk(0, [step], {**own, "entering": entering, "state": state, "leaving": leaving})
         if step == 1:
-            late_sent, entering = lax.optimization_barrier((late_here, entering))
-            late = lax.ppermute(late_sent, "lvl", from_odd)
-            state, leaving = run_chunk(
-                1, 0, {**own, "late": late, "earlier": earlier, "state": state, "leaving": leaving}
-            )
+            given_first = {**own, "late": late, "earlier": earlier, "state": state, "leaving": leaving}
+            state, leaving = run_chunk(1, [0], given_first)
         if returned is not None:
-            state, leaving = run_chunk(
-                1, place, {**own, "returned": returned, "edge": edge, "state": state, "leaving": leaving}, "late"
-            )
+            given_rest = {**own, "returned": returned, "edge": edge, "state": state, "leaving": leaving}
+            state, leaving = run_chunk(1, [place], given_rest, "late")
         came = entering
         if step < count:
             pairs = [(d, d + 1) for d in (place, step) if 0 <= d < top]
             entering = lax.ppermute(leaving, "lvl", pairs) if pairs else None
-        if step == 0:
-            ways, entering = lax.optimization_barrier((spread(ready, weight, soon), entering))
+        if step == 1:
+            soon_then, leaving = lax.optimization_barrier((soon, leaving))
+            ways, entering = lax.optimization_barrier((spread(ready, weight, soon_then), entering))
         if place in ready:
             state = finish_state(place, ways, came, state, step == count)
         if step in ready:
+            state = finish_state(step, ways, came, state, False)
             extra = {} if step == top else {"late": late, "earlier": leaving}
-            state, parted = run_chunk(1, step, {**own, **extra, "state": state})
+            state, parted = run_chunk(1, [step], {**own, **extra, "state": state})
     return state[:, :given] if columns != given else state
 
 

time: 60.4 us -> 52.6 us (0.87)
  waiting for transfers between devices: 13.2 us -> 4.05 us
  Pallas kernels: 37.6 us -> 38.9 us
    ppermute x4, waiting for transfers between devices: 11.1 us -> 4.04 us  [local(): entering = lax.ppermute(leaving, 'lvl', pairs) if pairs else None]
    ppermute x1, waiting for transfers between devices: 2.07 us -> 0.01 us  [local(): lax.ppermute(late_here, 'lvl', [(d + 1, d) for d in range(0, top, 2)])]
    pallas_call x2 -> x4, Pallas kernels: 2.14 us -> 3.62 us  [finish_state(): pl.pallas_call(functools.partial(finish_state_kernel, place), out_shape=(...]
    pallas_call x9 -> x7, Pallas kernels: 9.16 us -> 8.93 us  [run_chunk(): pl.pallas_call(functools.partial(chunk_kernel, chunk, tuple(places), part...]
  transfers between devices with their start and end apart: 7 -> 7, of which waited for: 2 -> 2; matrix products, arithmetic and copies ran while one was open for 0% -> 0% of each run, Pallas kernels for 46% -> 62%
where the time goes in v6:
time: 52.6 us; the launch traced here: 52.3 us
  Pallas kernels  38.9 us (74%)
  starting transfers between devices  9.15 us (17%)
  waiting for transfers between devices  4.05 us (8%)
    pallas_call x1, Pallas kernels, spread(): pl.pallas_call(functools.partial(spread_kernel, places), out_shape=reside...  11.3 us
    pallas_call x7, Pallas kernels, run_chunk(): pl.pallas_call(functools.partial(chunk_kernel, chunk, tuple(places), part...  8.93 us
    pallas_call x1, Pallas kernels, respond(): pl.pallas_call(respond_kernel, out_shape=resident((AHEAD - SOON, rows, ph...  7.22 us
    ppermute x4, waiting for transfers between devices, local(): entering = lax.ppermute(leaving, 'lvl', pairs) if pairs else None  4.04 us
    ppermute x4, starting transfers between devices, local(): entering = lax.ppermute(leaving, 'lvl', pairs) if pairs else None  3.91 us
    pallas_call x1, Pallas kernels, prepare(): pl.pallas_call(prepare_rest_kernel, out_shape=operators(levels, columns,...  3.9 us
    pallas_call x1, Pallas kernels, prepare(): pl.pallas_call(prepare_kernel, out_shape=operators(SOON, columns, phases)...  3.82 us
    pallas_call x4, Pallas kernels, finish_state(): pl.pallas_call(functools.partial(finish_state_kernel, place), out_shape=(...  3.62 us
  transfers between devices with their start and end apart: 7, of which 2 were waited for; matrix products, arithmetic and copies ran while one was open for 0% of the time, Pallas kernels for 62%

profile of v6, /device:TPU:11, one launch (start us, length us, event | category | flops | bytes accessed | tf_op | source)
XLA Modules:
  0.0 52.3 jit_solution(17196602223104647181)
XLA Ops:
  0.0 3.8 %prepare.1 = (bf16[3,1024,256]{2,1,0:T(8,128)(2,1)S(1)}, f32[3,16,256]{2,1,0:T(8,128)S(1)}, bf16[3,272,256]{2,1,0:T(8,128)(2,1)S(1)}, bf16[3,272,256]{2,1,0:T(8,128)(2,1)S(1)}, f32[3,272,256]{2,1,0:T(8,128)S(1)}) custom-call(f32[8,256,256]{2,1,0:T(8,128)} %inv.3, f32[8,256,256]{2,1,0:T(8,128)} %down.3, f32[8,256,256]{2,1,0:T(8,128)} %up.3, f32[8,16,256]{2,1,0:T(8,128)} %reward.3), custom_call_target="tpu_custom_call" | custom-call | tf_op jit(solution)/shard_map/prepare/pallas_call | solution.py:158
  3.8 2.6 %collective-permute-start = (f32[3,272,256]{2,1,0:T(8,128)S(1)}, f32[3,272,256]{2,1,0:T(8,128)S(1)}, u32[]{:S(2)}, u32[]{:S(2)}) collective-permute-start(f32[3,272,256]{2,1,0:T(8,128)S(1)} %get-tuple-element.35.soon), channel_id=1, source_target_pairs={{4,0},{8,4},{12,8},{5,1},{9,5},{13,9},{6,2},{10,6},{14,10},{7,3},{... | collective-permute-start | bytes 2506760 | tf_op jit(solution)/shard_map/ppermute | solution.py:470
  6.5 3.9 %prepare_rest.1 = (bf16[8,1024,256]{2,1,0:T(8,128)(2,1)S(1)}, f32[8,16,256]{2,1,0:T(8,128)S(1)}) custom-call(f32[8,256,256]{2,1,0:T(8,128)} %inv.3, f32[8,256,256]{2,1,0:T(8,128)} %down.3, f32[8,256,256]{2,1,0:T(8,128)} %up.3, f32[8,16,256]{2,1,0:T(8,128)} %reward.3, bf16[3,1024,256]{2,1,0:T(8,128)(2,1)S(1)} %get-tuple-element.32.weight_soon, ...), custom_call_target="tpu_custom_call" | custom-call | tf_op jit(solution)/shard_map/prepare_rest/pallas_call | solution.py:169
  10.4 7.2 %respond.1.late = f32[4,272,256]{2,1,0:T(8,128)S(1)} custom-call(bf16[8,1024,256]{2,1,0:T(8,128)(2,1)S(1)} %get-tuple-element.34.weight.refs_0_, f32[8,16,256]{2,1,0:T(8,128)S(1)} %get-tuple-element.36.base.refs_1_, bf16[3,272,256]{2,1,0:T(8,128)(2,1)S(1)} %get-tuple-element.37.x_high_soon, bf16[3,272,256]{2,1,0:T(8,128)(2,1)S(1)} %get-tuple-element.38.x_low_soon), custom_call_target="tpu_custom_call" | custom-call | tf_op jit(solution)/shard_map/respond/pallas_call | solution.py:183
  17.6 0.0 collective-permute-done.refs_2_.soon
  17.6 1.9 %collective-permute-start.1 = (f32[4,272,256]{2,1,0:T(8,128)S(1)}, f32[4,272,256]{2,1,0:T(8,128)S(1)}, u32[]{:S(2)}, u32[]{:S(2)}) collective-permute-start(f32[4,272,256]{2,1,0:T(8,128)S(1)} %respond.1.late), channel_id=1, source_target_pairs={{4,0},{12,8},{5,1},{13,9},{6,2},{14,10},{7,3},{15,11},{20,16},{28,... | collective-permute-start | bytes 3342344 | tf_op jit(solution)/shard_map/ppermute | solution.py:471
  19.6 3.6 %chunk.7 = (f32[8,16,256]{2,1,0:T(8,128)S(1)}, f32[4,16,256]{2,1,0:T(8,128)S(1)}) custom-call(bf16[8,1024,256]{2,1,0:T(8,128)(2,1)S(1)} %get-tuple-element.34.weight.refs_0_, f32[8,16,256]{2,1,0:T(8,128)S(1)} %get-tuple-element.36.base.refs_1_, f32[3,272,256]{2,1,0:T(8,128)S(1)} %collective-permute-done.refs_2_.soon), custom_call_target="tpu_custom_call" | custom-call | tf_op jit(solution)/shard_map/chunk/pallas_call | solution.py:317
  23.2 0.7 %collective-permute-start.2 = (f32[4,16,256]{2,1,0:T(8,128)S(1)}, f32[4,16,256]{2,1,0:T(8,128)S(1)}, u32[]{:S(2)}, u32[]{:S(2)}) collective-permute-start(f32[4,16,256]{2,1,0:T(8,128)S(1)} %get-tuple-element.41.refs_5_.refs_4_.leaving), channel_id=1, source_target_pairs={{0,4},{1,5},{2,6},{3,7},{16,20},{17,21},{18,22},{19,23}} | collective-permute-start | bytes 196616 | tf_op jit(solution)/shard_map/ppermute | solution.py:503
  23.9 0.0 collective-permute-done.2.refs_3_
  23.9 0.0 collective-permute-done.1.refs_3_
  23.9 0.2 chunk.9
  24.1 0.7 %collective-permute-start.3 = (f32[4,16,256]{2,1,0:T(8,128)S(1)}, f32[4,16,256]{2,1,0:T(8,128)S(1)}, u32[]{:S(2)}, u32[]{:S(2)}) collective-permute-start(f32[4,16,256]{2,1,0:T(8,128)S(1)} %get-tuple-element.53.before), channel_id=1, source_target_pairs={{0,4},{4,8},{1,5},{5,9},{2,6},{6,10},{3,7},{7,11},{16,20},{20,24},... | collective-permute-start | bytes 196616 | tf_op jit(solution)/shard_map/ppermute | solution.py:503
  24.8 11.3 %spread.1.ways = bf16[32,512,256]{2,1,0:T(8,128)(2,1)S(1)} custom-call(bf16[8,1024,256]{2,1,0:T(8,128)(2,1)S(1)} %get-tuple-element.34.weight.refs_0_, f32[3,272,256]{2,1,0:T(8,128)S(1)} %collective-permute-done.refs_2_.soon), custom_call_target="tpu_custom_call" | custom-call | tf_op jit(solution)/shard_map/spread/pallas_call | solution.py:368
  36.2 0.0 collective-permute-done.3.entering.refs_2_
  36.2 0.7 %collective-permute-start.4 = (f32[4,16,256]{2,1,0:T(8,128)S(1)}, f32[4,16,256]{2,1,0:T(8,128)S(1)}, u32[]{:S(2)}, u32[]{:S(2)}) collective-permute-start(f32[4,16,256]{2,1,0:T(8,128)S(1)} %answer.1), channel_id=1, source_target_pairs={{8,4},{9,5},{10,6},{11,7},{24,20},{25,21},{26,22},{27,23}} | collective-permute-start | bytes 196616 | tf_op jit(solution)/shard_map/ppermute | solution.py:482
  36.9 0.0 collective-permute-done.4.refs_3_
  37.0 1.3 %collective-permute-start.5 = (f32[4,16,256]{2,1,0:T(8,128)S(1)}, f32[4,16,256]{2,1,0:T(8,128)S(1)}, u32[]{:S(2)}, u32[]{:S(2)}) collective-permute-start(f32[4,16,256]{2,1,0:T(8,128)S(1)} %get-tuple-element.54.refs_4_.before), channel_id=1, source_target_pairs={{4,8},{8,12},{5,9},{9,13},{6,10},{10,14},{7,11},{11,15},{20,24},{2... | collective-permute-start | bytes 196616 | tf_op jit(solution)/shard_map/ppermute | solution.py:503
  38.3 0.3 chunk.12
  38.6 3.8 %collective-permute-done.5.entering = f32[4,16,256]{2,1,0:T(8,128)S(1)} collective-permute-done((f32[4,16,256]{2,1,0:T(8,128)S(1)}, f32[4,16,256]{2,1,0:T(8,128)S(1)}, u32[]{:S(2)}, u32[]{:S(2)}) %collective-permute-start.5) | collective-permute-done | bytes 65568 | tf_op jit(solution)/shard_map/ppermute | solution.py:503
  42.4 1.3 %collective-permute-start.6 = (f32[4,16,256]{2,1,0:T(8,128)S(1)}, f32[4,16,256]{2,1,0:T(8,128)S(1)}, u32[]{:S(2)}, u32[]{:S(2)}) collective-permute-start(f32[4,16,256]{2,1,0:T(8,128)S(1)} %finish_leaving.3), channel_id=1, source_target_pairs={{8,12},{9,13},{10,14},{11,15},{24,28},{25,29},{26,30},{27,31}} | collective-permute-start | bytes 196616 | tf_op jit(solution)/shard_map/ppermute | solution.py:503
  43.7 1.5 %finish_state.6.refs_3_ = f32[8,16,256]{2,1,0:T(8,128)S(1)} custom-call(bf16[32,512,256]{2,1,0:T(8,128)(2,1)S(1)} %spread.1.ways, f32[4,16,256]{2,1,0:T(8,128)S(1)} %collective-permute-done.5.entering, f32[8,16,256]{2,1,0:T(8,128)S(1)} %finish_state.5.state), custom_call_target="tpu_custom_call" | custom-call | tf_op jit(solution)/shard_map/finish_state/pallas_call | solution.py:423
  45.2 4.8 %chunk.13 = (f32[8,16,256]{2,1,0:T(8,128)S(1)}, f32[4,16,256]{2,1,0:T(8,128)}) custom-call(bf16[8,1024,256]{2,1,0:T(8,128)(2,1)S(1)} %get-tuple-element.34.weight.refs_0_, f32[8,16,256]{2,1,0:T(8,128)S(1)} %get-tuple-element.36.base.refs_1_, f32[3,272,256]{2,1,0:T(8,128)S(1)} %collective-permute-done.refs_2_.soon, f32[8,16,256]{2,1,0:T(8,128)S(1)} %finish_state.6.refs_3_), custom_call_target="tpu_custom_call" | custom-call | tf_op jit(solution)/shard_map/chunk/pallas_call | solution.py:317
  50.0 0.2 collective-permute-done.6.entering
  50.2 2.1 %finish_state.7 = f32[8,16,256]{2,1,0:T(8,128)} custom-call(bf16[32,512,256]{2,1,0:T(8,128)(2,1)S(1)} %spread.1.ways, f32[4,16,256]{2,1,0:T(8,128)S(1)} %collective-permute-done.6.entering, f32[8,16,256]{2,1,0:T(8,128)S(1)} %get-tuple-element.58.state), custom_call_target="tpu_custom_call" | custom-call | tf_op jit(solution)/shard_map/finish_state/pallas_call | solution.py:423
  (8 shorter events, 0.2 us)
Async XLA Ops:
  3.8 13.8 %collective-permute-start = (f32[3,272,256]{2,1,0:T(8,128)S(1)}, f32[3,272,256]{2,1,0:T(8,128)S(1)}, u32[]{:S(2)}, u32[]{:S(2)}) collective-permute-start(f32[3,272,256]{2,1,0:T(8,128)S(1)} %get-tuple-element.35.soon), channel_id=1, source_target_pairs={{4,0},{8,4},{12,8},{5,1},{9,5},{13,9},{6,2},{10,6},{14,10},{7,3},{... | collective-permute-start | bytes 2506760 | tf_op jit(solution)/shard_map/ppermute | solution.py:470
  17.6 6.3 %collective-permute-start.1 = (f32[4,272,256]{2,1,0:T(8,128)S(1)}, f32[4,272,256]{2,1,0:T(8,128)S(1)}, u32[]{:S(2)}, u32[]{:S(2)}) collective-permute-start(f32[4,272,256]{2,1,0:T(8,128)S(1)} %respond.1.late), channel_id=1, source_target_pairs={{4,0},{12,8},{5,1},{13,9},{6,2},{14,10},{7,3},{15,11},{20,16},{28,... | collective-permute-start | bytes 3342344 | tf_op jit(solution)/shard_map/ppermute | solution.py:471
  23.2 0.7 %collective-permute-start.2 = (f32[4,16,256]{2,1,0:T(8,128)S(1)}, f32[4,16,256]{2,1,0:T(8,128)S(1)}, u32[]{:S(2)}, u32[]{:S(2)}) collective-permute-start(f32[4,16,256]{2,1,0:T(8,128)S(1)} %get-tuple-element.41.refs_5_.refs_4_.leaving), channel_id=1, source_target_pairs={{0,4},{1,5},{2,6},{3,7},{16,20},{17,21},{18,22},{19,23}} | collective-permute-start | bytes 196616 | tf_op jit(solution)/shard_map/ppermute | solution.py:503
  24.1 12.0 %collective-permute-start.3 = (f32[4,16,256]{2,1,0:T(8,128)S(1)}, f32[4,16,256]{2,1,0:T(8,128)S(1)}, u32[]{:S(2)}, u32[]{:S(2)}) collective-permute-start(f32[4,16,256]{2,1,0:T(8,128)S(1)} %get-tuple-element.53.before), channel_id=1, source_target_pairs={{0,4},{4,8},{1,5},{5,9},{2,6},{6,10},{3,7},{7,11},{16,20},{20,24},... | collective-permute-start | bytes 196616 | tf_op jit(solution)/shard_map/ppermute | solution.py:503
  36.2 0.7 %collective-permute-start.4 = (f32[4,16,256]{2,1,0:T(8,128)S(1)}, f32[4,16,256]{2,1,0:T(8,128)S(1)}, u32[]{:S(2)}, u32[]{:S(2)}) collective-permute-start(f32[4,16,256]{2,1,0:T(8,128)S(1)} %answer.1), channel_id=1, source_target_pairs={{8,4},{9,5},{10,6},{11,7},{24,20},{25,21},{26,22},{27,23}} | collective-permute-start | bytes 196616 | tf_op jit(solution)/shard_map/ppermute | solution.py:482
  37.0 5.4 %collective-permute-start.5 = (f32[4,16,256]{2,1,0:T(8,128)S(1)}, f32[4,16,256]{2,1,0:T(8,128)S(1)}, u32[]{:S(2)}, u32[]{:S(2)}) collective-permute-start(f32[4,16,256]{2,1,0:T(8,128)S(1)} %get-tuple-element.54.refs_4_.before), channel_id=1, source_target_pairs={{4,8},{8,12},{5,9},{9,13},{6,10},{10,14},{7,11},{11,15},{20,24},{2... | collective-permute-start | bytes 196616 | tf_op jit(solution)/shard_map/ppermute | solution.py:503
  42.4 7.8 %collective-permute-start.6 = (f32[4,16,256]{2,1,0:T(8,128)S(1)}, f32[4,16,256]{2,1,0:T(8,128)S(1)}, u32[]{:S(2)}, u32[]{:S(2)}) collective-permute-start(f32[4,16,256]{2,1,0:T(8,128)S(1)} %finish_leaving.3), channel_id=1, source_target_pairs={{8,12},{9,13},{10,14},{11,15},{24,28},{25,29},{26,30},{27,31}} | collective-permute-start | bytes 196616 | tf_op jit(solution)/shard_map/ppermute | solution.py:503

commit v7 on v6

--- a/solution.py
+++ b/solution.py
@@ -41,10 +41,10 @@
     return dot(a[0], b[0]) + (dot(a[0], b[1]) + dot(a[1], b[0]))
 
 
-def place_operators(weight, i, down, up):
-    phases = down.shape[0]
-    for k, part in enumerate((*split(down.T), *split(up.T))):
-        weight[i, k * phases : (k + 1) * phases] = part
+def place_operator(weight, i, k, value):
+    phases = value.shape[0]
+    for n, part in enumerate(split(value.T)):
+        weight[i, (2 * k + n) * phases : (2 * k + n + 1) * phases] = part
 
 
 def operator(weight, i, k):
@@ -89,45 +89,52 @@
         kept[d - first, 0:phases], kept[d - first, phases:rows] = store(0, from_above(0))
 
 
-def products(levels, given, weight, base, buffers, sems):
-    first = levels[0]
+def products(wanted, given, weight, base, buffers, sems):
+    first = min(wanted)
+    names = {i: [0] + [n for n in (1, 2, 3) if n - 1 in wanted[i]] for i in wanted}
 
     def copies(i):
         return [
-            pltpu.make_async_copy(source.at[i], target.at[i - first], sems.at[n, i - first])
-            for n, (source, target) in enumerate(zip(given, buffers))
+            pltpu.make_async_copy(given[n].at[i], buffers[n].at[i - first], sems.at[n, i - first]) for n in names[i]
         ]
 
-    for i in levels:
+    for i in wanted:
         for copy in copies(i):
             copy.start()
 
     inv, down, up, pay = buffers
-    for i in levels:
+    for i in wanted:
         for copy in copies(i):
             copy.wait()
         at = i - first
         here = split(inv[at])
-        place_operators(weight, i, dot_parts(here, split(down[at])), dot_parts(here, split(up[at])))
-        base[i] = dot_parts(split(pay[at]), here, dot_nt)
+        for k, block in ((0, down), (1, up)):
+            if k in wanted[i]:
+                place_operator(weight, i, k, dot_parts(here, split(block[at])))
+        if 2 in wanted[i]:
+            base[i] = dot_parts(split(pay[at]), here, dot_nt)
 
 
 def prepare_kernel(inv, down, up, reward, weight, base, x_high, x_low, kept, *scratch):
     *buffers, sems = scratch
-    products(range(SOON), (inv, down, up, reward), weight, base, buffers, sems)
+    wanted = {i: (0, 1, 2) if i < SOON - 1 else (0, 2) for i in range(SOON)}
+    products(wanted, (inv, down, up, reward), weight, base, buffers, sems)
     response(0, SOON, x_high, x_low, weight, base, kept)
 
 
 def prepare_rest_kernel(inv, down, up, reward, weight_soon, base_soon, weight, base, *scratch):
     *buffers, sems = scratch
-    levels = reward.shape[0]
-    weight[0:SOON] = weight_soon[...]
+    levels, phases = reward.shape[0], reward.shape[2]
+    for i in range(SOON):
+        rows = (4 if i < SOON - 1 else 2) * phases
+        weight[i, 0:rows] = weight_soon[i, 0:rows]
     base[0:SOON] = base_soon[...]
-    products(range(SOON, levels), (inv, down, up, reward), weight, base, buffers, sems)
-
-
-def respond_kernel(weight, base, x_high_soon, x_low_soon, kept, x_high, x_low):
-    @pl.when(lax.axis_index("lvl") > 0)
+    wanted = {i: (0, 1, 2) if i >= SOON else (1,) for i in range(SOON - 1, levels)}
+    products(wanted, (inv, down, up, reward), weight, base, buffers, sems)
+
+
+def respond_kernel(places, weight, base, x_high_soon, x_low_soon, kept, x_high, x_low):
+    @pl.when(among(places))
     def _():
         x_high[0:SOON] = x_high_soon[...]
         x_low[0:SOON] = x_low_soon[...]
@@ -171,17 +178,17 @@
         out_shape=operators(levels, columns, phases),
         in_specs=[HBM] * 4 + [VMEM] * 2,
         out_specs=[VMEM] * 2,
-        scratch_shapes=buffers(levels - SOON, columns, phases),
+        scratch_shapes=buffers(levels - SOON + 1, columns, phases),
         compiler_params=pltpu.CompilerParams(vmem_limit_bytes=16 * 2**20),
         name="prepare_rest",
     )(*given, *[pin(x) for x in soon[:2]])
     return weights, soon[2:], kept_soon
 
 
-def respond(weights, started):
+def respond(places, weights, started):
     _, rows, phases = started[0].shape
     return pl.pallas_call(
-        respond_kernel,
+        functools.partial(respond_kernel, tuple(places)),
         out_shape=resident((AHEAD - SOON, rows, phases), F32),
         in_specs=[VMEM] * 4,
         out_specs=VMEM,
@@ -328,56 +335,89 @@
     return functools.reduce(jnp.logical_or, [lax.axis_index("lvl") == place for place in places])
 
 
-def spread_kernel(places, weight, soon, out):
-    levels, _, phases = weight.shape
-
-    def get(at):
-        return out[at, 0:phases], out[at, phases : 2 * phases]
-
-    def put(at, value):
-        out[at, 0:phases], out[at, phases : 2 * phases] = split(value)
+def slot_of(levels, a, i):
+    return a * levels + i if a < CHUNK else CHUNK * levels + sum(AHEAD - n for n in range(CHUNK, a)) + i
+
+
+def spread_kernel(places, weight, base, soon, high, low, kept, state, leaving, back_high, back_low, soon_high, soon_low):
+    levels, columns, phases = base.shape
+    rows = phases + columns
+    top = levels - 1
+
+    def step(a, i, terms, last=False):
+        new = sum(dot_parts(x, y) for x, y in terms)
+        unit, run = new[0:phases], new[phases:rows] + base[i]
+        at = slot_of(levels, a, i)
+        high[at, 0:phases], low[at, 0:phases] = split(unit)
+        high[at, phases:rows], low[at, phases:rows] = split(run)
+        if last and a >= SOON:
+            kept[a - SOON, 0:phases], kept[a - SOON, phases:rows] = unit, run
+        if a == CHUNK - 1:
+            state[i] = run
+        return run
+
+    def get(a, i):
+        at = slot_of(levels, a, i)
+        return high[at], low[at]
+
+    def below(a, i):
+        return get(a, i - 1), operator(weight, i, 0)
+
+    def above(a, i):
+        return get(a - 1, i + 1), operator(weight, i, 1)
 
     @pl.when(among(places))
     def _():
-        out[0] = weight[0, 0 : 2 * phases]
+        for j in range(CHUNK - 1):
+            soon_high[j], soon_low[j] = split(soon[j, 0:phases])
+        high[0, 0:phases], low[0, 0:phases] = operator(weight, 0, 0)
+        high[0, phases:rows], low[0, phases:rows] = split(base[0])
 
         def up(i, _):
-            put(i, dot_parts(get(i - 1), operator(weight, i, 0)))
+            step(0, i, [below(0, i)])
             return 0
 
         lax.fori_loop(1, levels, up, 0)
-        feedback = [split(soon[j, 0:phases]) for j in range(CHUNK - 1)]
-        for a in range(1, CHUNK):
-            at, old = a * levels, (a - 1) * levels
-            put(at, dot_parts(get(old + 1), operator(weight, 0, 1)))
-
-            def both(i, _, at=at, old=old):
-                below = dot_parts(get(at + i - 1), operator(weight, i, 0))
-                put(at + i, below + dot_parts(get(old + i + 1), operator(weight, i, 1)))
+        leaving[0] = get(0, top)[0][phases:rows].astype(F32) + get(0, top)[1][phases:rows].astype(F32)
+        for a in range(1, AHEAD):
+            step(a, 0, [above(a, 0)], True)
+
+            def both(i, _, a=a):
+                step(a, i, [below(a, i), above(a, i)])
                 return 0
 
-            lax.fori_loop(1, levels - 1, both, 0)
-            back = sum(dot_parts(get((a - 1 - j) * levels + levels - 1), feedback[j]) for j in range(a))
-            top = levels - 1
-            below = dot_parts(get(at + top - 1), operator(weight, top, 0))
-            put(at + top, below + dot_parts(split(back), operator(weight, top, 1)))
-
-
-def spread(places, weight, soon):
-    levels, _, phases = weight.shape
-    return pl.pallas_call(
-        functools.partial(spread_kernel, places),
-        out_shape=resident((CHUNK * levels, 2 * phases, phases), BF16),
-        in_specs=[VMEM] * 2,
-        out_specs=VMEM,
+            lax.fori_loop(1, top if a < CHUNK else AHEAD - a, both, 0)
+            if a < CHUNK:
+                back = sum(dot_parts(get(a - 1 - j, top), (soon_high[j], soon_low[j])) for j in range(a))
+                back_high[0:phases], back_low[0:phases] = split(back[0:phases])
+                back_high[phases:rows], back_low[phases:rows] = split(back[phases:rows] + soon[a - 1, phases:rows])
+                terms = [below(a, top), ((back_high[...], back_low[...]), operator(weight, top, 1))]
+                leaving[a] = step(a, top, terms)
+
+
+def spread(places, weight, base, soon):
+    levels, columns, phases = base.shape
+    rows = phases + columns
+    slots = slot_of(levels, AHEAD, 0)
+    *ways, kept, state, leaving = pl.pallas_call(
+        functools.partial(spread_kernel, tuple(places)),
+        out_shape=[resident((slots, rows, phases), BF16)] * 2
+        + [
+            resident((AHEAD - SOON, rows, phases), F32),
+            resident((levels, columns, phases), F32),
+            resident((CHUNK, columns, phases), F32),
+        ],
+        in_specs=[VMEM] * 3,
+        out_specs=[VMEM] * 5,
+        scratch_shapes=[pltpu.VMEM((rows, phases), BF16)] * 2 + [pltpu.VMEM((CHUNK - 1, phases, phases), BF16)] * 2,
         compiler_params=pltpu.CompilerParams(vmem_limit_bytes=16 * 2**20),
         name="spread",
-    )(*[pin(x) for x in (weight, soon)])
-
-
-def finish_leaving_kernel(place, ways, entering, leaving, before, new):
-    levels = ways.shape[0] // CHUNK
-    columns = entering.shape[1]
+    )(*[pin(x) for x in (weight, base, soon)])
+    return ways, kept, state, leaving
+
+
+def finish_leaving_kernel(place, high, low, entering, leaving, before, new, *, levels):
+    columns, phases = entering.shape[1:]
 
     @pl.when(lax.axis_index("lvl") != place)
     def _():
@@ -388,25 +428,27 @@
         values = [stack(entering[k]) for k in range(CHUNK)]
         total = [leaving[k] for k in range(CHUNK)]
         for a in range(CHUNK):
-            for k, term in enumerate(apply_each(values[: CHUNK - a], ways[a * levels + levels - 1], columns)):
+            at = slot_of(levels, a, levels - 1)
+            pair = jnp.concatenate([high[at, 0:phases], low[at, 0:phases]], axis=0)
+            for k, term in enumerate(apply_each(values[: CHUNK - a], pair, columns)):
                 total[a + k] += term
         for k in range(CHUNK):
             new[k] = total[k]
 
 
-def finish_leaving(place, ways, entering, leaving, before):
+def finish_leaving(place, ways, entering, leaving, before, levels):
     return pl.pallas_call(
-        functools.partial(finish_leaving_kernel, place),
+        functools.partial(finish_leaving_kernel, place, levels=levels),
         out_shape=resident(leaving.shape, F32),
-        in_specs=[VMEM] * 4,
+        in_specs=[VMEM] * 5,
         out_specs=VMEM,
         compiler_params=pltpu.CompilerParams(vmem_limit_bytes=8 * 2**20),
         name="finish_leaving",
-    )(*[pin(x) for x in (ways, entering, leaving, before)])
-
-
-def finish_state_kernel(place, ways, entering, state, new):
-    levels = state.shape[0]
+    )(*[pin(x) for x in (*ways, entering, leaving, before)])
+
+
+def finish_state_kernel(place, high, low, entering, state, new):
+    levels, _, phases = state.shape
 
     @pl.when(lax.axis_index("lvl") != place)
     def _():
@@ -416,18 +458,22 @@
     def _():
         values = [stack(entering[CHUNK - 1 - a]) for a in range(CHUNK)]
         for i in range(levels):
-            new[i] = state[i] + apply([(values[a], ways[a * levels + i]) for a in range(CHUNK)])
+            terms = []
+            for a in range(CHUNK):
+                at = slot_of(levels, a, i)
+                terms.append((values[a], jnp.concatenate([high[at, 0:phases], low[at, 0:phases]], axis=0)))
+            new[i] = state[i] + apply(terms)
 
 
 def finish_state(place, ways, entering, state, last):
     return pl.pallas_call(
         functools.partial(finish_state_kernel, place),
         out_shape=(jax.ShapeDtypeStruct if last else resident)(state.shape, F32),
-        in_specs=[VMEM] * 3,
+        in_specs=[VMEM] * 4,
         out_specs=VMEM,
         compiler_params=pltpu.CompilerParams(vmem_limit_bytes=8 * 2**20),
         name="finish_state",
-    )(*[pin(x) for x in (ways, entering, state)])
+    )(*[pin(x) for x in (*ways, entering, state)])
 
 
 def answer_kernel(step, soon, late, entering, returned):
@@ -456,24 +502,21 @@
     if columns != given:
         reward = jnp.pad(reward, ((0, 0), (0, columns - given), (0, 0)))
     count = lax.axis_size("lvl")
-    weights, started, soon_here = prepare(inverse_diag, down_block, up_block, reward)
-    late_here = respond(weights, started)
     assert CHUNKS == 2 and count > 1
     top = count - 1
-    from_odd = [(d + 1, d) for d in range(0, top, 2)]
+    ready = [d for d in range(1, count) if d % 2 == 0 or d == top]
+    odd = [d for d in range(1, top, 2)]
+    weights, begun, soon_here = prepare(inverse_diag, down_block, up_block, reward)
+    weight, base = weights
+    late_odd = respond(odd, weights, begun) if odd else None
     soon = lax.ppermute(soon_here, "lvl", [(d + 1, d) for d in range(top)])
-    soon, late_here = lax.optimization_barrier((soon, late_here))
-    weight, base = weights
+    if odd:
+        late = lax.ppermute(late_odd, "lvl", [(d, d - 1) for d in odd])
+        soon, late_odd = lax.optimization_barrier((soon, late_odd))
+    ways, late_here, state, parted_first = spread(ready, weight, base, soon)
+    late_top = lax.ppermute(late_here, "lvl", [(top, top - 1)]) if top % 2 else None
     own = {"weight": weight, "base": base, "soon": soon}
-    assert count > 1
-    top = count - 1
-    soon = lax.ppermute(soon_here, "lvl", [(d + 1, d) for d in range(top)])
-    late = lax.ppermute(late_here, "lvl", [(d + 1, d) for d in range(0, top, 2)])
-    soon, late_here = lax.optimization_barrier((soon, late_here))
-    weight, base = weights
-    own = {"weight": weight, "base": base, "soon": soon}
-    ready = [d for d in range(1, count) if d % 2 == 0 or d == top]
-    state = leaving = entering = ways = parted = None
+    leaving = entering = parted = None
     for step in range(count + 1):
         place = step - 1
         earlier = leaving
@@ -483,16 +526,17 @@
             given_early = {"weight": weight, "base": base, "entering": entering, "state": state}
             state, edge = run_chunk(1, [place], given_early, "early")
         if place in ready and place < top:
-            leaving = finish_leaving(place, ways, entering, parted, leaving)
-        if step == 0:
-            state, leaving = started = run_chunk(0, [0, *ready], own)
-        elif step in ready:
+            leaving = finish_leaving(place, ways, entering, parted, leaving, base.shape[0])
+        if step in ready:
             if step < top:
-                leaving = finish_leaving(step, ways, entering, started[1], leaving)
+                leaving = finish_leaving(step, ways, entering, parted_first, leaving, base.shape[0])
         elif step < count:
-            state, leaving = run_chunk(0, [step], {**own, "entering": entering, "state": state, "leaving": leaving})
+            state, leaving = run_chunk(
+                0, [step], {**own, "entering": entering, "state": state, "leaving": leaving}
+            )
         if step == 1:
-            given_first = {**own, "late": late, "earlier": earlier, "state": state, "leaving": leaving}
+            first_late = late if odd else late_top
+            given_first = {**own, "late": first_late, "earlier": earlier, "state": state, "leaving": leaving}
             state, leaving = run_chunk(1, [0], given_first)
         if returned is not None:
             given_rest = {**own, "returned": returned, "edge": edge, "state": state, "leaving": leaving}
@@ -501,14 +545,11 @@
         if step < count:
             pairs = [(d, d + 1) for d in (place, step) if 0 <= d < top]
             entering = lax.ppermute(leaving, "lvl", pairs) if pairs else None
-        if step == 1:
-            soon_then, leaving = lax.optimization_barrier((soon, leaving))
-            ways, entering = lax.optimization_barrier((spread(ready, weight, soon_then), entering))
         if place in ready:
             state = finish_state(place, ways, came, state, step == count)
         if step in ready:
             state = finish_state(step, ways, came, state, False)
-            extra = {} if step == top else {"late": late, "earlier": leaving}
+            extra = {} if step == top else {"late": late_top if step == top - 1 else late, "earlier": leaving}
             state, parted = run_chunk(1, [step], {**own, **extra, "state": state})
     return state[:, :given] if columns != given else state
 

time: 52.6 us -> 54.8 us (1.042)
  Pallas kernels: 38.9 us -> 31.2 us
  starting transfers between devices: 9.15 us -> 14.8 us
  waiting for transfers between devices: 4.05 us -> 8.29 us
    ppermute x1 -> x2, starting transfers between devices: 1.94 us -> 7.61 us  [the longest x1 6.88 us: local(): lax.ppermute(late_here, 'lvl', [(top, top - 1)])]
    pallas_call x4, Pallas kernels: 18.6 us -> 14.1 us  [the longest x1 14.1 us: spread(): pl.pallas_call(functools.partial(spread_kernel, tuple(places)), out_shape...]
    ppermute x4, waiting for transfers between devices: 4.04 us -> 8.28 us  [local(): entering = lax.ppermute(leaving, 'lvl', pairs) if pairs else None]
    pallas_call x7, Pallas kernels: 8.93 us -> 5.37 us  [run_chunk(): pl.pallas_call(functools.partial(chunk_kernel, chunk, tuple(places), part...]
  transfers between devices with their start and end apart: 7 -> 8, of which waited for: 2 -> 2; matrix products, arithmetic and copies ran while one was open for 0% -> 0% of each run, Pallas kernels for 62% -> 46%
where the time goes in v7:
time: 54.8 us; the launch traced here: 54.6 us
  Pallas kernels  31.2 us (57%)
  starting transfers between devices  14.8 us (27%)
  waiting for transfers between devices  8.29 us (15%)
    pallas_call x1, Pallas kernels, spread(): pl.pallas_call(functools.partial(spread_kernel, tuple(places)), out_shape...  14.1 us
    ppermute x4, waiting for transfers between devices, local(): entering = lax.ppermute(leaving, 'lvl', pairs) if pairs else None  8.28 us
    ppermute x1, starting transfers between devices, local(): lax.ppermute(late_here, 'lvl', [(top, top - 1)])  6.88 us
    pallas_call x7, Pallas kernels, run_chunk(): pl.pallas_call(functools.partial(chunk_kernel, chunk, tuple(places), part...  5.37 us
    pallas_call x1, Pallas kernels, prepare(): pl.pallas_call(prepare_rest_kernel, out_shape=operators(levels, columns,...  4.28 us
    ppermute x4, starting transfers between devices, local(): entering = lax.ppermute(leaving, 'lvl', pairs) if pairs else None  3.9 us
    pallas_call x1, Pallas kernels, prepare(): pl.pallas_call(prepare_kernel, out_shape=operators(SOON, columns, phases)...  3.88 us
    pallas_call x4, Pallas kernels, finish_state(): pl.pallas_call(functools.partial(finish_state_kernel, place), out_shape=(...  3.57 us
  transfers between devices with their start and end apart: 8, of which 2 were waited for; matrix products, arithmetic and copies ran while one was open for 0% of the time, Pallas kernels for 46%

profile of v7, /device:TPU:11, one launch (start us, length us, event | category | flops | bytes accessed | tf_op | source)
XLA Modules:
  0.0 54.6 jit_solution(12493352813956166780)
XLA Ops:
  0.0 3.9 %prepare.1 = (bf16[3,1024,256]{2,1,0:T(8,128)(2,1)S(1)}, f32[3,16,256]{2,1,0:T(8,128)S(1)}, bf16[3,272,256]{2,1,0:T(8,128)(2,1)S(1)}, bf16[3,272,256]{2,1,0:T(8,128)(2,1)S(1)}, f32[3,272,256]{2,1,0:T(8,128)S(1)}) custom-call(f32[8,256,256]{2,1,0:T(8,128)} %inv.3, f32[8,256,256]{2,1,0:T(8,128)} %down.3, f32[8,256,256]{2,1,0:T(8,128)} %up.3, f32[8,16,256]{2,1,0:T(8,128)} %reward.3), custom_call_target="tpu_custom_call" | custom-call | tf_op jit(solution)/shard_map/prepare/pallas_call | solution.py:165
  3.9 2.6 %collective-permute-start = (f32[3,272,256]{2,1,0:T(8,128)S(1)}, f32[3,272,256]{2,1,0:T(8,128)S(1)}, u32[]{:S(2)}, u32[]{:S(2)}) collective-permute-start(f32[3,272,256]{2,1,0:T(8,128)S(1)} %get-tuple-element.35.soon), channel_id=1, source_target_pairs={{4,0},{8,4},{12,8},{5,1},{9,5},{13,9},{6,2},{10,6},{14,10},{7,3},{... | collective-permute-start | bytes 2506760 | tf_op jit(solution)/shard_map/ppermute | solution.py:512
  6.5 4.3 %prepare_rest.1 = (bf16[8,1024,256]{2,1,0:T(8,128)(2,1)S(1)}, f32[8,16,256]{2,1,0:T(8,128)S(1)}) custom-call(f32[8,256,256]{2,1,0:T(8,128)} %inv.3, f32[8,256,256]{2,1,0:T(8,128)} %down.3, f32[8,256,256]{2,1,0:T(8,128)} %up.3, f32[8,16,256]{2,1,0:T(8,128)} %reward.3, bf16[3,1024,256]{2,1,0:T(8,128)(2,1)S(1)} %get-tuple-element.31.weight_soon, ...), custom_call_target="tpu_custom_call" | custom-call | tf_op jit(solution)/shard_map/prepare_rest/pallas_call | solution.py:176
  10.8 0.7 %collective-permute-start.1 = (f32[4,272,256]{2,1,0:T(8,128)S(1)}, f32[4,272,256]{2,1,0:T(8,128)S(1)}, u32[]{:S(2)}, u32[]{:S(2)}) collective-permute-start(f32[4,272,256]{2,1,0:T(8,128)S(1)} %respond.1), channel_id=1, source_target_pairs={{4,0},{5,1},{6,2},{7,3},{20,16},{21,17},{22,18},{23,19}} | collective-permute-start | bytes 3342344 | tf_op jit(solution)/shard_map/ppermute | solution.py:514
  11.6 0.0 collective-permute-done.soon.refs_2_
  11.6 14.1 %spread.1 = (bf16[38,272,256]{2,1,0:T(8,128)(2,1)S(1)}, bf16[38,272,256]{2,1,0:T(8,128)(2,1)S(1)}, f32[4,272,256]{2,1,0:T(8,128)S(1)}, f32[8,16,256]{2,1,0:T(8,128)S(1)}, f32[4,16,256]{2,1,0:T(8,128)S(1)}) custom-call(bf16[8,1024,256]{2,1,0:T(8,128)(2,1)S(1)} %get-tuple-element.33.weight.refs_0_, f32[8,16,256]{2,1,0:T(8,128)S(1)} %get-tuple-element.34.base.refs_1_, ...), custom_call_target="tpu_custom_call" | custom-call | tf_op jit(solution)/shard_map/spread/pallas_call | solution.py:402
  25.7 6.9 %collective-permute-start.6 = (f32[4,272,256]{2,1,0:T(8,128)S(1)}, f32[4,272,256]{2,1,0:T(8,128)S(1)}, u32[]{:S(2)}, u32[]{:S(2)}) collective-permute-start(f32[4,272,256]{2,1,0:T(8,128)S(1)} %get-tuple-element.41.late), channel_id=1, source_target_pairs={{12,8},{13,9},{14,10},{15,11},{28,24},{29,25},{30,26},{31,27}} | collective-permute-start | bytes 3342344 | tf_op jit(solution)/shard_map/ppermute | solution.py:517
  32.6 0.2 chunk.7
  32.8 0.7 %collective-permute-start.2 = (f32[4,16,256]{2,1,0:T(8,128)S(1)}, f32[4,16,256]{2,1,0:T(8,128)S(1)}, u32[]{:S(2)}, u32[]{:S(2)}) collective-permute-start(f32[4,16,256]{2,1,0:T(8,128)S(1)} %get-tuple-element.43.refs_5_.refs_4_), channel_id=1, source_target_pairs={{0,4},{1,5},{2,6},{3,7},{16,20},{17,21},{18,22},{19,23}} | collective-permute-start | bytes 196616 | tf_op jit(solution)/shard_map/ppermute | solution.py:547
  33.5 0.0 collective-permute-done.2.refs_3_
  33.5 0.0 collective-permute-done.1.refs_3_
  33.6 0.7 %collective-permute-start.3 = (f32[4,16,256]{2,1,0:T(8,128)S(1)}, f32[4,16,256]{2,1,0:T(8,128)S(1)}, u32[]{:S(2)}, u32[]{:S(2)}) collective-permute-start(f32[4,16,256]{2,1,0:T(8,128)S(1)} %get-tuple-element.47.before), channel_id=1, source_target_pairs={{0,4},{4,8},{1,5},{5,9},{2,6},{6,10},{3,7},{7,11},{16,20},{20,24},... | collective-permute-start | bytes 196616 | tf_op jit(solution)/shard_map/ppermute | solution.py:547
  34.2 0.0 collective-permute-done.3.entering.refs_2_
  34.3 0.7 %collective-permute-start.4 = (f32[4,16,256]{2,1,0:T(8,128)S(1)}, f32[4,16,256]{2,1,0:T(8,128)S(1)}, u32[]{:S(2)}, u32[]{:S(2)}) collective-permute-start(f32[4,16,256]{2,1,0:T(8,128)S(1)} %answer.1), channel_id=1, source_target_pairs={{8,4},{9,5},{10,6},{11,7},{24,20},{25,21},{26,22},{27,23}} | collective-permute-start | bytes 196616 | tf_op jit(solution)/shard_map/ppermute | solution.py:525
  35.0 0.0 collective-permute-done.4.refs_3_
  35.1 1.3 %collective-permute-start.5 = (f32[4,16,256]{2,1,0:T(8,128)S(1)}, f32[4,16,256]{2,1,0:T(8,128)S(1)}, u32[]{:S(2)}, u32[]{:S(2)}) collective-permute-start(f32[4,16,256]{2,1,0:T(8,128)S(1)} %get-tuple-element.52.refs_4_.before), channel_id=1, source_target_pairs={{4,8},{8,12},{5,9},{9,13},{6,10},{10,14},{7,11},{11,15},{20,24},{2... | collective-permute-start | bytes 196616 | tf_op jit(solution)/shard_map/ppermute | solution.py:547
  36.4 0.0 collective-permute-done.6.refs_3_
  36.4 0.3 chunk.12
  36.7 8.1 %collective-permute-done.5.entering = f32[4,16,256]{2,1,0:T(8,128)S(1)} collective-permute-done((f32[4,16,256]{2,1,0:T(8,128)S(1)}, f32[4,16,256]{2,1,0:T(8,128)S(1)}, u32[]{:S(2)}, u32[]{:S(2)}) %collective-permute-start.5) | collective-permute-done | bytes 65568 | tf_op jit(solution)/shard_map/ppermute | solution.py:547
  44.7 1.3 %collective-permute-start.7 = (f32[4,16,256]{2,1,0:T(8,128)S(1)}, f32[4,16,256]{2,1,0:T(8,128)S(1)}, u32[]{:S(2)}, u32[]{:S(2)}) collective-permute-start(f32[4,16,256]{2,1,0:T(8,128)S(1)} %finish_leaving.3), channel_id=1, source_target_pairs={{8,12},{9,13},{10,14},{11,15},{24,28},{25,29},{26,30},{27,31}} | collective-permute-start | bytes 196616 | tf_op jit(solution)/shard_map/ppermute | solution.py:547
  46.0 1.4 %finish_state.6.refs_3_ = f32[8,16,256]{2,1,0:T(8,128)S(1)} custom-call(bf16[38,272,256]{2,1,0:T(8,128)(2,1)S(1)} %get-tuple-element.39.high, bf16[38,272,256]{2,1,0:T(8,128)(2,1)S(1)} %get-tuple-element.40.low, f32[4,16,256]{2,1,0:T(8,128)S(1)} %collective-permute-done.5.entering, f32[8,16,256]{2,1,0:T(8,128)S(1)} %finish_state.5.state), custom_call_target="tpu_custom_call" | custom-call | tf_op jit(solution)/shard_map/finish_state/pallas_call | solution.py:469
  47.5 4.8 %chunk.13 = (f32[8,16,256]{2,1,0:T(8,128)S(1)}, f32[4,16,256]{2,1,0:T(8,128)}) custom-call(bf16[8,1024,256]{2,1,0:T(8,128)(2,1)S(1)} %get-tuple-element.33.weight.refs_0_, f32[8,16,256]{2,1,0:T(8,128)S(1)} %get-tuple-element.34.base.refs_1_, f32[3,272,256]{2,1,0:T(8,128)S(1)} %collective-permute-done.soon.refs_2_, f32[8,16,256]{2,1,0:T(8,128)S(1)} %finish_state.6.refs_3_), custom_call_target="tpu_custom_call" | custom-call | tf_op jit(solution)/shard_map/chunk/pallas_call | solution.py:324
  52.3 0.2 collective-permute-done.7.entering
  52.5 2.1 %finish_state.7 = f32[8,16,256]{2,1,0:T(8,128)} custom-call(bf16[38,272,256]{2,1,0:T(8,128)(2,1)S(1)} %get-tuple-element.39.high, bf16[38,272,256]{2,1,0:T(8,128)(2,1)S(1)} %get-tuple-element.40.low, f32[4,16,256]{2,1,0:T(8,128)S(1)} %collective-permute-done.7.entering, f32[8,16,256]{2,1,0:T(8,128)S(1)} %get-tuple-element.56.state), custom_call_target="tpu_custom_call" | custom-call | tf_op jit(solution)/shard_map/finish_state/pallas_call | solution.py:469
  (10 shorter events, 0.2 us)
Async XLA Ops:
  3.9 7.7 %collective-permute-start = (f32[3,272,256]{2,1,0:T(8,128)S(1)}, f32[3,272,256]{2,1,0:T(8,128)S(1)}, u32[]{:S(2)}, u32[]{:S(2)}) collective-permute-start(f32[3,272,256]{2,1,0:T(8,128)S(1)} %get-tuple-element.35.soon), channel_id=1, source_target_pairs={{4,0},{8,4},{12,8},{5,1},{9,5},{13,9},{6,2},{10,6},{14,10},{7,3},{... | collective-permute-start | bytes 2506760 | tf_op jit(solution)/shard_map/ppermute | solution.py:512
  10.8 22.7 %collective-permute-start.1 = (f32[4,272,256]{2,1,0:T(8,128)S(1)}, f32[4,272,256]{2,1,0:T(8,128)S(1)}, u32[]{:S(2)}, u32[]{:S(2)}) collective-permute-start(f32[4,272,256]{2,1,0:T(8,128)S(1)} %respond.1), channel_id=1, source_target_pairs={{4,0},{5,1},{6,2},{7,3},{20,16},{21,17},{22,18},{23,19}} | collective-permute-start | bytes 3342344 | tf_op jit(solution)/shard_map/ppermute | solution.py:514
  25.7 10.7 %collective-permute-start.6 = (f32[4,272,256]{2,1,0:T(8,128)S(1)}, f32[4,272,256]{2,1,0:T(8,128)S(1)}, u32[]{:S(2)}, u32[]{:S(2)}) collective-permute-start(f32[4,272,256]{2,1,0:T(8,128)S(1)} %get-tuple-element.41.late), channel_id=1, source_target_pairs={{12,8},{13,9},{14,10},{15,11},{28,24},{29,25},{30,26},{31,27}} | collective-permute-start | bytes 3342344 | tf_op jit(solution)/shard_map/ppermute | solution.py:517
  32.8 0.7 %collective-permute-start.2 = (f32[4,16,256]{2,1,0:T(8,128)S(1)}, f32[4,16,256]{2,1,0:T(8,128)S(1)}, u32[]{:S(2)}, u32[]{:S(2)}) collective-permute-start(f32[4,16,256]{2,1,0:T(8,128)S(1)} %get-tuple-element.43.refs_5_.refs_4_), channel_id=1, source_target_pairs={{0,4},{1,5},{2,6},{3,7},{16,20},{17,21},{18,22},{19,23}} | collective-permute-start | bytes 196616 | tf_op jit(solution)/shard_map/ppermute | solution.py:547
  33.6 0.7 %collective-permute-start.3 = (f32[4,16,256]{2,1,0:T(8,128)S(1)}, f32[4,16,256]{2,1,0:T(8,128)S(1)}, u32[]{:S(2)}, u32[]{:S(2)}) collective-permute-start(f32[4,16,256]{2,1,0:T(8,128)S(1)} %get-tuple-element.47.before), channel_id=1, source_target_pairs={{0,4},{4,8},{1,5},{5,9},{2,6},{6,10},{3,7},{7,11},{16,20},{20,24},... | collective-permute-start | bytes 196616 | tf_op jit(solution)/shard_map/ppermute | solution.py:547
  34.3 0.7 %collective-permute-start.4 = (f32[4,16,256]{2,1,0:T(8,128)S(1)}, f32[4,16,256]{2,1,0:T(8,128)S(1)}, u32[]{:S(2)}, u32[]{:S(2)}) collective-permute-start(f32[4,16,256]{2,1,0:T(8,128)S(1)} %answer.1), channel_id=1, source_target_pairs={{8,4},{9,5},{10,6},{11,7},{24,20},{25,21},{26,22},{27,23}} | collective-permute-start | bytes 196616 | tf_op jit(solution)/shard_map/ppermute | solution.py:525
  35.1 9.7 %collective-permute-start.5 = (f32[4,16,256]{2,1,0:T(8,128)S(1)}, f32[4,16,256]{2,1,0:T(8,128)S(1)}, u32[]{:S(2)}, u32[]{:S(2)}) collective-permute-start(f32[4,16,256]{2,1,0:T(8,128)S(1)} %get-tuple-element.52.refs_4_.before), channel_id=1, source_target_pairs={{4,8},{8,12},{5,9},{9,13},{6,10},{10,14},{7,11},{11,15},{20,24},{2... | collective-permute-start | bytes 196616 | tf_op jit(solution)/shard_map/ppermute | solution.py:547
  44.7 7.7 %collective-permute-start.7 = (f32[4,16,256]{2,1,0:T(8,128)S(1)}, f32[4,16,256]{2,1,0:T(8,128)S(1)}, u32[]{:S(2)}, u32[]{:S(2)}) collective-permute-start(f32[4,16,256]{2,1,0:T(8,128)S(1)} %finish_leaving.3), channel_id=1, source_target_pairs={{8,12},{9,13},{10,14},{11,15},{24,28},{25,29},{26,30},{27,31}} | collective-permute-start | bytes 196616 | tf_op jit(solution)/shard_map/ppermute | solution.py:547

commit v8 on v7

--- a/solution.py
+++ b/solution.py
@@ -335,88 +335,130 @@
     return functools.reduce(jnp.logical_or, [lax.axis_index("lvl") == place for place in places])
 
 
+def is_open(levels, a, i):
+    return i + a < levels
+
+
 def slot_of(levels, a, i):
-    return a * levels + i if a < CHUNK else CHUNK * levels + sum(AHEAD - n for n in range(CHUNK, a)) + i
-
-
-def spread_kernel(places, weight, base, soon, high, low, kept, state, leaving, back_high, back_low, soon_high, soon_low):
+    if not is_open(levels, a, i):
+        return sum(range(1, a)) + i - (levels - a)
+    return sum(levels - n if n < CHUNK else AHEAD - n for n in range(a)) + i
+
+
+def get_answer(ways, levels, a, i, rows=slice(None)):
+    high, low = ways[0:2] if is_open(levels, a, i) else ways[2:4]
+    at = slot_of(levels, a, i)
+    return high[at, rows], low[at, rows]
+
+
+def spread_open_kernel(places, weight, base, high, low, kept):
+    levels, columns, phases = base.shape
+    rows = phases + columns
+
+    def step(at, i, terms, keep=None):
+        new = sum(dot_parts((high[x], low[x]), operator(weight, i, k)) for x, k in terms)
+        unit, run = new[0:phases], new[phases:rows] + base[i]
+        high[at, 0:phases], low[at, 0:phases] = split(unit)
+        high[at, phases:rows], low[at, phases:rows] = split(run)
+        if keep is not None:
+            kept[keep, 0:phases], kept[keep, phases:rows] = unit, run
+
+    @pl.when(among(places))
+    def _():
+        high[0, 0:phases], low[0, 0:phases] = operator(weight, 0, 0)
+        high[0, phases:rows], low[0, phases:rows] = split(base[0])
+
+        def up(i, _):
+            step(i, i, [(i - 1, 0)])
+            return 0
+
+        lax.fori_loop(1, levels, up, 0)
+        for a in range(1, AHEAD):
+            first, old = slot_of(levels, a, 0), slot_of(levels, a - 1, 0)
+            step(first, 0, [(old + 1, 1)], a - SOON if a >= SOON else None)
+
+            def both(i, _, first=first, old=old):
+                step(first + i, i, [(first + i - 1, 0), (old + i + 1, 1)])
+                return 0
+
+            lax.fori_loop(1, levels - a if a < CHUNK else AHEAD - a, both, 0)
+
+
+def spread_close_kernel(
+    places, weight, base, soon, open_high, open_low, before, high, low, state, leaving, feed_high, feed_low
+):
     levels, columns, phases = base.shape
     rows = phases + columns
     top = levels - 1
-
-    def step(a, i, terms, last=False):
-        new = sum(dot_parts(x, y) for x, y in terms)
-        unit, run = new[0:phases], new[phases:rows] + base[i]
-        at = slot_of(levels, a, i)
-        high[at, 0:phases], low[at, 0:phases] = split(unit)
-        high[at, phases:rows], low[at, phases:rows] = split(run)
-        if last and a >= SOON:
-            kept[a - SOON, 0:phases], kept[a - SOON, phases:rows] = unit, run
-        if a == CHUNK - 1:
-            state[i] = run
-        return run
-
-    def get(a, i):
-        at = slot_of(levels, a, i)
-        return high[at], low[at]
-
-    def below(a, i):
-        return get(a, i - 1), operator(weight, i, 0)
-
-    def above(a, i):
-        return get(a - 1, i + 1), operator(weight, i, 1)
+    ways = (open_high, open_low, high, low)
+
+    @pl.when(jnp.logical_not(among(places)))
+    def _():
+        state[...] = before[...]
 
     @pl.when(among(places))
     def _():
         for j in range(CHUNK - 1):
-            soon_high[j], soon_low[j] = split(soon[j, 0:phases])
-        high[0, 0:phases], low[0, 0:phases] = operator(weight, 0, 0)
-        high[0, phases:rows], low[0, phases:rows] = split(base[0])
-
-        def up(i, _):
-            step(0, i, [below(0, i)])
-            return 0
-
-        lax.fori_loop(1, levels, up, 0)
-        leaving[0] = get(0, top)[0][phases:rows].astype(F32) + get(0, top)[1][phases:rows].astype(F32)
-        for a in range(1, AHEAD):
-            step(a, 0, [above(a, 0)], True)
-
-            def both(i, _, a=a):
-                step(a, i, [below(a, i), above(a, i)])
-                return 0
-
-            lax.fori_loop(1, top if a < CHUNK else AHEAD - a, both, 0)
-            if a < CHUNK:
-                back = sum(dot_parts(get(a - 1 - j, top), (soon_high[j], soon_low[j])) for j in range(a))
-                back_high[0:phases], back_low[0:phases] = split(back[0:phases])
-                back_high[phases:rows], back_low[phases:rows] = split(back[phases:rows] + soon[a - 1, phases:rows])
-                terms = [below(a, top), ((back_high[...], back_low[...]), operator(weight, top, 1))]
-                leaving[a] = step(a, top, terms)
-
-
-def spread(places, weight, base, soon):
+            feed_high[j], feed_low[j] = split(soon[j, 0:phases])
+        for a in range(1, CHUNK):
+            for i in range(levels - a, levels):
+                new = dot_parts(get_answer(ways, levels, a, i - 1), operator(weight, i, 0))
+                if i < top:
+                    over = get_answer(ways, levels, a - 1, i + 1)
+                else:
+                    back = sum(
+                        dot_parts(get_answer(ways, levels, a - 1 - j, top), (feed_high[j], feed_low[j])) for j in range(a)
+                    )
+                    end = back[phases:rows] + soon[a - 1, phases:rows]
+                    over = split(jnp.concatenate([back[0:phases], end], axis=0))
+                new += dot_parts(over, operator(weight, i, 1))
+                at = slot_of(levels, a, i)
+                high[at, 0:phases], low[at, 0:phases] = split(new[0:phases])
+                high[at, phases:rows], low[at, phases:rows] = split(new[phases:rows] + base[i])
+
+        def run(a, i):
+            return sum(part.astype(F32) for part in get_answer(ways, levels, a, i, slice(phases, rows)))
+
+        for i in range(levels):
+            state[i] = run(CHUNK - 1, i)
+        for a in range(CHUNK):
+            leaving[a] = run(a, top)
+
+
+def spread_open(places, weight, base):
+    levels, columns, phases = base.shape
+    assert levels > AHEAD and levels >= 2 * CHUNK - 1
+    rows = phases + columns
+    slots = slot_of(levels, AHEAD, 0)
+    *ways, kept = pl.pallas_call(
+        functools.partial(spread_open_kernel, tuple(places)),
+        out_shape=[resident((slots, rows, phases), BF16)] * 2 + [resident((AHEAD - SOON, rows, phases), F32)],
+        in_specs=[VMEM] * 2,
+        out_specs=[VMEM] * 3,
+        compiler_params=pltpu.CompilerParams(vmem_limit_bytes=16 * 2**20),
+        name="spread_open",
+    )(*[pin(x) for x in (weight, base)])
+    return ways, kept
+
+
+def spread_close(places, weight, base, soon, ways, state):
     levels, columns, phases = base.shape
     rows = phases + columns
-    slots = slot_of(levels, AHEAD, 0)
-    *ways, kept, state, leaving = pl.pallas_call(
-        functools.partial(spread_kernel, tuple(places)),
-        out_shape=[resident((slots, rows, phases), BF16)] * 2
-        + [
-            resident((AHEAD - SOON, rows, phases), F32),
-            resident((levels, columns, phases), F32),
-            resident((CHUNK, columns, phases), F32),
-        ],
-        in_specs=[VMEM] * 3,
-        out_specs=[VMEM] * 5,
-        scratch_shapes=[pltpu.VMEM((rows, phases), BF16)] * 2 + [pltpu.VMEM((CHUNK - 1, phases, phases), BF16)] * 2,
+    *more, state, leaving = pl.pallas_call(
+        functools.partial(spread_close_kernel, tuple(places)),
+        out_shape=[resident((sum(range(CHUNK)), rows, phases), BF16)] * 2
+        + [resident((levels, columns, phases), F32), resident((CHUNK, columns, phases), F32)],
+        in_specs=[VMEM] * 6,
+        out_specs=[VMEM] * 4,
+        scratch_shapes=[pltpu.VMEM((CHUNK - 1, phases, phases), BF16)] * 2,
         compiler_params=pltpu.CompilerParams(vmem_limit_bytes=16 * 2**20),
-        name="spread",
-    )(*[pin(x) for x in (weight, base, soon)])
-    return ways, kept, state, leaving
-
-
-def finish_leaving_kernel(place, high, low, entering, leaving, before, new, *, levels):
+        name="spread_close",
+    )(*[pin(x) for x in (weight, base, soon, *ways, state)])
+    return [*ways, *more], state, leaving
+
+
+def finish_leaving_kernel(place, *refs, levels):
+    *ways, entering, leaving, before, new = refs
     columns, phases = entering.shape[1:]
 
     @pl.when(lax.axis_index("lvl") != place)
@@ -428,8 +470,7 @@
         values = [stack(entering[k]) for k in range(CHUNK)]
         total = [leaving[k] for k in range(CHUNK)]
         for a in range(CHUNK):
-            at = slot_of(levels, a, levels - 1)
-            pair = jnp.concatenate([high[at, 0:phases], low[at, 0:phases]], axis=0)
+            pair = jnp.concatenate(get_answer(ways, levels, a, levels - 1, slice(0, phases)), axis=0)
             for k, term in enumerate(apply_each(values[: CHUNK - a], pair, columns)):
                 total[a + k] += term
         for k in range(CHUNK):
@@ -440,14 +481,15 @@
     return pl.pallas_call(
         functools.partial(finish_leaving_kernel, place, levels=levels),
         out_shape=resident(leaving.shape, F32),
-        in_specs=[VMEM] * 5,
+        in_specs=[VMEM] * 7,
         out_specs=VMEM,
         compiler_params=pltpu.CompilerParams(vmem_limit_bytes=8 * 2**20),
         name="finish_leaving",
     )(*[pin(x) for x in (*ways, entering, leaving, before)])
 
 
-def finish_state_kernel(place, high, low, entering, state, new):
+def finish_state_kernel(place, *refs):
+    *ways, entering, state, new = refs
     levels, _, phases = state.shape
 
     @pl.when(lax.axis_index("lvl") != place)
@@ -460,8 +502,8 @@
         for i in range(levels):
             terms = []
             for a in range(CHUNK):
-                at = slot_of(levels, a, i)
-                terms.append((values[a], jnp.concatenate([high[at, 0:phases], low[at, 0:phases]], axis=0)))
+                pair = jnp.concatenate(get_answer(ways, levels, a, i, slice(0, phases)), axis=0)
+                terms.append((values[a], pair))
             new[i] = state[i] + apply(terms)
 
 
@@ -469,7 +511,7 @@
     return pl.pallas_call(
         functools.partial(finish_state_kernel, place),
         out_shape=(jax.ShapeDtypeStruct if last else resident)(state.shape, F32),
-        in_specs=[VMEM] * 4,
+        in_specs=[VMEM] * 6,
         out_specs=VMEM,
         compiler_params=pltpu.CompilerParams(vmem_limit_bytes=8 * 2**20),
         name="finish_state",
@@ -509,14 +551,13 @@
     weights, begun, soon_here = prepare(inverse_diag, down_block, up_block, reward)
     weight, base = weights
     late_odd = respond(odd, weights, begun) if odd else None
+    ways, late_here = spread_open(ready, weight, base)
     soon = lax.ppermute(soon_here, "lvl", [(d + 1, d) for d in range(top)])
-    if odd:
-        late = lax.ppermute(late_odd, "lvl", [(d, d - 1) for d in odd])
-        soon, late_odd = lax.optimization_barrier((soon, late_odd))
-    ways, late_here, state, parted_first = spread(ready, weight, base, soon)
+    late = lax.ppermute(late_odd, "lvl", [(d, d - 1) for d in odd]) if odd else None
+    soon, late_here, late_odd = lax.optimization_barrier((soon, late_here, late_odd))
     late_top = lax.ppermute(late_here, "lvl", [(top, top - 1)]) if top % 2 else None
     own = {"weight": weight, "base": base, "soon": soon}
-    leaving = entering = parted = None
+    state = leaving = entering = parted = None
     for step in range(count + 1):
         place = step - 1
         earlier = leaving
@@ -545,6 +586,11 @@
         if step < count:
             pairs = [(d, d + 1) for d in (place, step) if 0 <= d < top]
             entering = lax.ppermute(leaving, "lvl", pairs) if pairs else None
+        if step == 1:
+            ways_then, leaving = lax.optimization_barrier((ways, leaving))
+            ways, state, parted_first = spread_close(ready, weight, base, soon, ways_then, state)
+            if entering is not None:
+                entering, state = lax.optimization_barrier((entering, state))
         if place in ready:
             state = finish_state(place, ways, came, state, step == count)
         if step in ready:

time: 54.8 us -> 48 us (0.88)
  starting transfers between devices: 14.8 us -> 9.89 us
  waiting for transfers between devices: 8.29 us -> 5.88 us
  Pallas kernels: 31.2 us -> 31.8 us
    ppermute x1, starting transfers between devices: 6.88 us -> 1.95 us  [local(): lax.ppermute(late_here, 'lvl', [(top, top - 1)])]
    ppermute x4, waiting for transfers between devices: 8.28 us -> 5.87 us  [local(): entering = lax.ppermute(leaving, 'lvl', pairs) if pairs else None]
    pallas_call x1 -> x2, Pallas kernels: 14.1 us -> 14.6 us  [the longest x1 10.9 us: spread_open(): pl.pallas_call(functools.partial(spread_open_kernel, tuple(places)), out_...]
  transfers between devices with their start and end apart: 8 -> 8, of which waited for: 2 -> 2; matrix products, arithmetic and copies ran while one was open for 0% -> 0% of each run, Pallas kernels for 46% -> 54%
where the time goes in v8:
time: 48 us; the launch traced here: 47.8 us
  Pallas kernels  31.8 us (66%)
  starting transfers between devices  9.89 us (21%)
  waiting for transfers between devices  5.88 us (12%)
    pallas_call x1, Pallas kernels, spread_open(): pl.pallas_call(functools.partial(spread_open_kernel, tuple(places)), out_...  10.9 us
    ppermute x4, waiting for transfers between devices, local(): entering = lax.ppermute(leaving, 'lvl', pairs) if pairs else None  5.87 us
    pallas_call x7, Pallas kernels, run_chunk(): pl.pallas_call(functools.partial(chunk_kernel, chunk, tuple(places), part...  5.37 us
    pallas_call x1, Pallas kernels, prepare(): pl.pallas_call(prepare_rest_kernel, out_shape=operators(levels, columns,...  4.28 us
    ppermute x4, starting transfers between devices, local(): entering = lax.ppermute(leaving, 'lvl', pairs) if pairs else None  3.9 us
    pallas_call x1, Pallas kernels, prepare(): pl.pallas_call(prepare_kernel, out_shape=operators(SOON, columns, phases)...  3.88 us
    pallas_call x1, Pallas kernels, spread_close(): pl.pallas_call(functools.partial(spread_close_kernel, tuple(places)), out...  3.73 us
    pallas_call x4, Pallas kernels, finish_state(): pl.pallas_call(functools.partial(finish_state_kernel, place), out_shape=(...  3.57 us
  transfers between devices with their start and end apart: 8, of which 2 were waited for; matrix products, arithmetic and copies ran while one was open for 0% of the time, Pallas kernels for 54%

profile of v8, /device:TPU:11, one launch (start us, length us, event | category | flops | bytes accessed | tf_op | source)
XLA Modules:
  0.0 47.8 jit_solution(10998051433448875307)
XLA Ops:
  0.0 3.9 %prepare.1 = (bf16[3,1024,256]{2,1,0:T(8,128)(2,1)S(1)}, f32[3,16,256]{2,1,0:T(8,128)S(1)}, bf16[3,272,256]{2,1,0:T(8,128)(2,1)S(1)}, bf16[3,272,256]{2,1,0:T(8,128)(2,1)S(1)}, f32[3,272,256]{2,1,0:T(8,128)S(1)}) custom-call(f32[8,256,256]{2,1,0:T(8,128)} %inv.3, f32[8,256,256]{2,1,0:T(8,128)} %down.3, f32[8,256,256]{2,1,0:T(8,128)} %up.3, f32[8,16,256]{2,1,0:T(8,128)} %reward.3), custom_call_target="tpu_custom_call" | custom-call | tf_op jit(solution)/shard_map/prepare/pallas_call | solution.py:165
  3.9 2.6 %collective-permute-start = (f32[3,272,256]{2,1,0:T(8,128)S(1)}, f32[3,272,256]{2,1,0:T(8,128)S(1)}, u32[]{:S(2)}, u32[]{:S(2)}) collective-permute-start(f32[3,272,256]{2,1,0:T(8,128)S(1)} %get-tuple-element.45.soon), channel_id=1, source_target_pairs={{4,0},{8,4},{12,8},{5,1},{9,5},{13,9},{6,2},{10,6},{14,10},{7,3},{... | collective-permute-start | bytes 2506760 | tf_op jit(solution)/shard_map/ppermute | solution.py:555
  6.5 4.3 %prepare_rest.1 = (bf16[8,1024,256]{2,1,0:T(8,128)(2,1)S(1)}, f32[8,16,256]{2,1,0:T(8,128)S(1)}) custom-call(f32[8,256,256]{2,1,0:T(8,128)} %inv.3, f32[8,256,256]{2,1,0:T(8,128)} %down.3, f32[8,256,256]{2,1,0:T(8,128)} %up.3, f32[8,16,256]{2,1,0:T(8,128)} %reward.3, bf16[3,1024,256]{2,1,0:T(8,128)(2,1)S(1)} %get-tuple-element.39.weight_soon, ...), custom_call_target="tpu_custom_call" | custom-call | tf_op jit(solution)/shard_map/prepare_rest/pallas_call | solution.py:176
  10.8 0.7 %collective-permute-start.1 = (f32[4,272,256]{2,1,0:T(8,128)S(1)}, f32[4,272,256]{2,1,0:T(8,128)S(1)}, u32[]{:S(2)}, u32[]{:S(2)}) collective-permute-start(f32[4,272,256]{2,1,0:T(8,128)S(1)} %respond.1), channel_id=1, source_target_pairs={{4,0},{5,1},{6,2},{7,3},{20,16},{21,17},{22,18},{23,19}} | collective-permute-start | bytes 3342344 | tf_op jit(solution)/shard_map/ppermute | solution.py:556
  11.6 10.9 %spread_open.1 = (bf16[32,272,256]{2,1,0:T(8,128)(2,1)S(1)}, bf16[32,272,256]{2,1,0:T(8,128)(2,1)S(1)}, f32[4,272,256]{2,1,0:T(8,128)S(1)}) custom-call(bf16[8,1024,256]{2,1,0:T(8,128)(2,1)S(1)} %get-tuple-element.41.weight.refs_0_, f32[8,16,256]{2,1,0:T(8,128)S(1)} %get-tuple-element.42.base.refs_1_), custom_call_target="tpu_custom_call" | custom-call | tf_op jit(solution)/shard_map/spread_open/pallas_call | solution.py:433
  22.5 0.0 collective-permute-done.refs_2_.soon
  22.5 1.9 %collective-permute-start.6 = (f32[4,272,256]{2,1,0:T(8,128)S(1)}, f32[4,272,256]{2,1,0:T(8,128)S(1)}, u32[]{:S(2)}, u32[]{:S(2)}) collective-permute-start(f32[4,272,256]{2,1,0:T(8,128)S(1)} %get-tuple-element.60.late), channel_id=1, source_target_pairs={{12,8},{13,9},{14,10},{15,11},{28,24},{29,25},{30,26},{31,27}} | collective-permute-start | bytes 3342344 | tf_op jit(solution)/shard_map/ppermute | solution.py:558
  24.5 0.7 %collective-permute-start.2 = (f32[4,16,256]{2,1,0:T(8,128)S(1)}, f32[4,16,256]{2,1,0:T(8,128)S(1)}, u32[]{:S(2)}, u32[]{:S(2)}) collective-permute-start(f32[4,16,256]{2,1,0:T(8,128)S(1)} %get-tuple-element.50.refs_5_.refs_4_), channel_id=1, source_target_pairs={{0,4},{1,5},{2,6},{3,7},{16,20},{17,21},{18,22},{19,23}} | collective-permute-start | bytes 196616 | tf_op jit(solution)/shard_map/ppermute | solution.py:588
  25.1 0.0 collective-permute-done.2.refs_3_
  25.2 0.2 chunk.8
  25.4 0.0 collective-permute-done.1.refs_3_
  25.4 0.7 %collective-permute-start.3 = (f32[4,16,256]{2,1,0:T(8,128)S(1)}, f32[4,16,256]{2,1,0:T(8,128)S(1)}, u32[]{:S(2)}, u32[]{:S(2)}) collective-permute-start(f32[4,16,256]{2,1,0:T(8,128)S(1)} %get-tuple-element.67.refs_6_), channel_id=1, source_target_pairs={{0,4},{4,8},{1,5},{5,9},{2,6},{6,10},{3,7},{7,11},{16,20},{20,24},... | collective-permute-start | bytes 196616 | tf_op jit(solution)/shard_map/ppermute | solution.py:588
  26.1 3.7 %spread_close.1 = (bf16[6,272,256]{2,1,0:T(8,128)(2,1)S(1)}, bf16[6,272,256]{2,1,0:T(8,128)(2,1)S(1)}, f32[8,16,256]{2,1,0:T(8,128)S(1)}, f32[4,16,256]{2,1,0:T(8,128)S(1)}) custom-call(bf16[8,1024,256]{2,1,0:T(8,128)(2,1)S(1)} %get-tuple-element.41.weight.refs_0_, f32[8,16,256]{2,1,0:T(8,128)S(1)} %get-tuple-element.42.base.refs_1_, ...), custom_call_target="tpu_custom_call" | custom-call | tf_op jit(solution)/shard_map/spread_close/pallas_call | solution.py:447
  29.8 0.0 collective-permute-done.3.entering.refs_2_.refs_4_
  29.9 0.7 %collective-permute-start.4 = (f32[4,16,256]{2,1,0:T(8,128)S(1)}, f32[4,16,256]{2,1,0:T(8,128)S(1)}, u32[]{:S(2)}, u32[]{:S(2)}) collective-permute-start(f32[4,16,256]{2,1,0:T(8,128)S(1)} %answer.1), channel_id=1, source_target_pairs={{8,4},{9,5},{10,6},{11,7},{24,20},{25,21},{26,22},{27,23}} | collective-permute-start | bytes 196616 | tf_op jit(solution)/shard_map/ppermute | solution.py:566
  30.6 0.0 collective-permute-done.4.refs_3_
  30.7 1.3 %collective-permute-start.5 = (f32[4,16,256]{2,1,0:T(8,128)S(1)}, f32[4,16,256]{2,1,0:T(8,128)S(1)}, u32[]{:S(2)}, u32[]{:S(2)}) collective-permute-start(f32[4,16,256]{2,1,0:T(8,128)S(1)} %get-tuple-element.68.refs_4_.refs_6_), channel_id=1, source_target_pairs={{4,8},{8,12},{5,9},{9,13},{6,10},{10,14},{7,11},{11,15},{20,24},{2... | collective-permute-start | bytes 196616 | tf_op jit(solution)/shard_map/ppermute | solution.py:588
  32.0 0.0 collective-permute-done.6.refs_3_
  32.0 0.3 chunk.12
  32.3 5.7 %collective-permute-done.5.refs_4_ = f32[4,16,256]{2,1,0:T(8,128)S(1)} collective-permute-done((f32[4,16,256]{2,1,0:T(8,128)S(1)}, f32[4,16,256]{2,1,0:T(8,128)S(1)}, u32[]{:S(2)}, u32[]{:S(2)}) %collective-permute-start.5) | collective-permute-done | bytes 65568 | tf_op jit(solution)/shard_map/ppermute | solution.py:588
  37.9 1.3 %collective-permute-start.7 = (f32[4,16,256]{2,1,0:T(8,128)S(1)}, f32[4,16,256]{2,1,0:T(8,128)S(1)}, u32[]{:S(2)}, u32[]{:S(2)}) collective-permute-start(f32[4,16,256]{2,1,0:T(8,128)S(1)} %finish_leaving.3), channel_id=1, source_target_pairs={{8,12},{9,13},{10,14},{11,15},{24,28},{25,29},{26,30},{27,31}} | collective-permute-start | bytes 196616 | tf_op jit(solution)/shard_map/ppermute | solution.py:588
  39.2 1.4 %finish_state.6.refs_3_ = f32[8,16,256]{2,1,0:T(8,128)S(1)} custom-call(bf16[32,272,256]{2,1,0:T(8,128)(2,1)S(1)} %get-tuple-element.55.open_high.refs_0_, bf16[32,272,256]{2,1,0:T(8,128)(2,1)S(1)} %get-tuple-element.56.open_low.refs_1_, bf16[6,272,256]{2,1,0:T(8,128)(2,1)S(1)} %get-tuple-element.58.refs_2_, ...), custom_call_target="tpu_custom_call" | custom-call | tf_op jit(solution)/shard_map/finish_state/pallas_call | solution.py:511
  40.7 4.8 %chunk.13 = (f32[8,16,256]{2,1,0:T(8,128)S(1)}, f32[4,16,256]{2,1,0:T(8,128)}) custom-call(bf16[8,1024,256]{2,1,0:T(8,128)(2,1)S(1)} %get-tuple-element.41.weight.refs_0_, f32[8,16,256]{2,1,0:T(8,128)S(1)} %get-tuple-element.42.base.refs_1_, f32[3,272,256]{2,1,0:T(8,128)S(1)} %collective-permute-done.refs_2_.soon, f32[8,16,256]{2,1,0:T(8,128)S(1)} %finish_state.6.refs_3_), custom_call_target="tpu_custom_call" | custom-call | tf_op jit(solution)/shard_map/chunk/pallas_call | solution.py:324
  45.5 0.2 collective-permute-done.7.refs_4_
  45.7 2.1 %finish_state.7 = f32[8,16,256]{2,1,0:T(8,128)} custom-call(bf16[32,272,256]{2,1,0:T(8,128)(2,1)S(1)} %get-tuple-element.55.open_high.refs_0_, bf16[32,272,256]{2,1,0:T(8,128)(2,1)S(1)} %get-tuple-element.56.open_low.refs_1_, bf16[6,272,256]{2,1,0:T(8,128)(2,1)S(1)} %get-tuple-element.58.refs_2_, bf16[6,272,256]{2,1,0:T(8,128)(2,1)S(1)} %get-tuple-element.59.refs_3_, ...), custom_call_target="tpu_custom_call" | custom-call | tf_op jit(solution)/shard_map/finish_state/pallas_call | solution.py:511
  (10 shorter events, 0.2 us)
Async XLA Ops:
  3.9 18.6 %collective-permute-start = (f32[3,272,256]{2,1,0:T(8,128)S(1)}, f32[3,272,256]{2,1,0:T(8,128)S(1)}, u32[]{:S(2)}, u32[]{:S(2)}) collective-permute-start(f32[3,272,256]{2,1,0:T(8,128)S(1)} %get-tuple-element.45.soon), channel_id=1, source_target_pairs={{4,0},{8,4},{12,8},{5,1},{9,5},{13,9},{6,2},{10,6},{14,10},{7,3},{... | collective-permute-start | bytes 2506760 | tf_op jit(solution)/shard_map/ppermute | solution.py:555
  10.8 14.5 %collective-permute-start.1 = (f32[4,272,256]{2,1,0:T(8,128)S(1)}, f32[4,272,256]{2,1,0:T(8,128)S(1)}, u32[]{:S(2)}, u32[]{:S(2)}) collective-permute-start(f32[4,272,256]{2,1,0:T(8,128)S(1)} %respond.1), channel_id=1, source_target_pairs={{4,0},{5,1},{6,2},{7,3},{20,16},{21,17},{22,18},{23,19}} | collective-permute-start | bytes 3342344 | tf_op jit(solution)/shard_map/ppermute | solution.py:556
  22.5 9.5 %collective-permute-start.6 = (f32[4,272,256]{2,1,0:T(8,128)S(1)}, f32[4,272,256]{2,1,0:T(8,128)S(1)}, u32[]{:S(2)}, u32[]{:S(2)}) collective-permute-start(f32[4,272,256]{2,1,0:T(8,128)S(1)} %get-tuple-element.60.late), channel_id=1, source_target_pairs={{12,8},{13,9},{14,10},{15,11},{28,24},{29,25},{30,26},{31,27}} | collective-permute-start | bytes 3342344 | tf_op jit(solution)/shard_map/ppermute | solution.py:558
  24.5 0.7 %collective-permute-start.2 = (f32[4,16,256]{2,1,0:T(8,128)S(1)}, f32[4,16,256]{2,1,0:T(8,128)S(1)}, u32[]{:S(2)}, u32[]{:S(2)}) collective-permute-start(f32[4,16,256]{2,1,0:T(8,128)S(1)} %get-tuple-element.50.refs_5_.refs_4_), channel_id=1, source_target_pairs={{0,4},{1,5},{2,6},{3,7},{16,20},{17,21},{18,22},{19,23}} | collective-permute-start | bytes 196616 | tf_op jit(solution)/shard_map/ppermute | solution.py:588
  25.4 4.4 %collective-permute-start.3 = (f32[4,16,256]{2,1,0:T(8,128)S(1)}, f32[4,16,256]{2,1,0:T(8,128)S(1)}, u32[]{:S(2)}, u32[]{:S(2)}) collective-permute-start(f32[4,16,256]{2,1,0:T(8,128)S(1)} %get-tuple-element.67.refs_6_), channel_id=1, source_target_pairs={{0,4},{4,8},{1,5},{5,9},{2,6},{6,10},{3,7},{7,11},{16,20},{20,24},... | collective-permute-start | bytes 196616 | tf_op jit(solution)/shard_map/ppermute | solution.py:588
  29.9 0.7 %collective-permute-start.4 = (f32[4,16,256]{2,1,0:T(8,128)S(1)}, f32[4,16,256]{2,1,0:T(8,128)S(1)}, u32[]{:S(2)}, u32[]{:S(2)}) collective-permute-start(f32[4,16,256]{2,1,0:T(8,128)S(1)} %answer.1), channel_id=1, source_target_pairs={{8,4},{9,5},{10,6},{11,7},{24,20},{25,21},{26,22},{27,23}} | collective-permute-start | bytes 196616 | tf_op jit(solution)/shard_map/ppermute | solution.py:566
  30.7 7.3 %collective-permute-start.5 = (f32[4,16,256]{2,1,0:T(8,128)S(1)}, f32[4,16,256]{2,1,0:T(8,128)S(1)}, u32[]{:S(2)}, u32[]{:S(2)}) collective-permute-start(f32[4,16,256]{2,1,0:T(8,128)S(1)} %get-tuple-element.68.refs_4_.refs_6_), channel_id=1, source_target_pairs={{4,8},{8,12},{5,9},{9,13},{6,10},{10,14},{7,11},{11,15},{20,24},{2... | collective-permute-start | bytes 196616 | tf_op jit(solution)/shard_map/ppermute | solution.py:588
  37.9 7.7 %collective-permute-start.7 = (f32[4,16,256]{2,1,0:T(8,128)S(1)}, f32[4,16,256]{2,1,0:T(8,128)S(1)}, u32[]{:S(2)}, u32[]{:S(2)}) collective-permute-start(f32[4,16,256]{2,1,0:T(8,128)S(1)} %finish_leaving.3), channel_id=1, source_target_pairs={{8,12},{9,13},{10,14},{11,15},{24,28},{25,29},{26,30},{27,31}} | collective-permute-start | bytes 196616 | tf_op jit(solution)/shard_map/ppermute | solution.py:588

commit v9 on v8

--- a/solution.py
+++ b/solution.py
@@ -89,48 +89,46 @@
         kept[d - first, 0:phases], kept[d - first, phases:rows] = store(0, from_above(0))
 
 
-def products(wanted, given, weight, base, buffers, sems):
-    first = min(wanted)
-    names = {i: [0] + [n for n in (1, 2, 3) if n - 1 in wanted[i]] for i in wanted}
+def products(wanted, here_from, weight, base, inv, down, up, pay):
+    for i in wanted:
+        here_from(i)
+        here = split(inv[i])
+        for k, block in ((0, down), (1, up)):
+            if k in wanted[i]:
+                place_operator(weight, i, k, dot_parts(here, split(block[i])))
+        if 2 in wanted[i]:
+            base[i] = dot_parts(split(pay[i]), here, dot_nt)
+
+
+def prepare_kernel(inv_far, down_far, up_far, pay_far, weight, base, x_high, x_low, kept, inv, down, up, pay, sems):
+    levels = pay.shape[0]
 
     def copies(i):
-        return [
-            pltpu.make_async_copy(given[n].at[i], buffers[n].at[i - first], sems.at[n, i - first]) for n in names[i]
-        ]
-
-    for i in wanted:
+        pairs = ((inv_far, inv), (down_far, down), (pay_far, pay), (up_far, up))
+        return [pltpu.make_async_copy(far.at[i], near.at[i], sems.at[n, i]) for n, (far, near) in enumerate(pairs)]
+
+    def wait(i):
+        for copy in copies(i):
+            copy.wait()
+
+    for i in range(levels):
         for copy in copies(i):
             copy.start()
-
-    inv, down, up, pay = buffers
-    for i in wanted:
-        for copy in copies(i):
-            copy.wait()
-        at = i - first
-        here = split(inv[at])
-        for k, block in ((0, down), (1, up)):
-            if k in wanted[i]:
-                place_operator(weight, i, k, dot_parts(here, split(block[at])))
-        if 2 in wanted[i]:
-            base[i] = dot_parts(split(pay[at]), here, dot_nt)
-
-
-def prepare_kernel(inv, down, up, reward, weight, base, x_high, x_low, kept, *scratch):
-    *buffers, sems = scratch
     wanted = {i: (0, 1, 2) if i < SOON - 1 else (0, 2) for i in range(SOON)}
-    products(wanted, (inv, down, up, reward), weight, base, buffers, sems)
+    products(wanted, wait, weight, base, inv, down, up, pay)
     response(0, SOON, x_high, x_low, weight, base, kept)
-
-
-def prepare_rest_kernel(inv, down, up, reward, weight_soon, base_soon, weight, base, *scratch):
-    *buffers, sems = scratch
-    levels, phases = reward.shape[0], reward.shape[2]
+    for i in range(SOON, levels):
+        wait(i)
+
+
+def prepare_rest_kernel(weight_soon, base_soon, inv, down, up, pay, weight, base):
+    levels, _, phases = pay.shape
     for i in range(SOON):
         rows = (4 if i < SOON - 1 else 2) * phases
         weight[i, 0:rows] = weight_soon[i, 0:rows]
     base[0:SOON] = base_soon[...]
     wanted = {i: (0, 1, 2) if i >= SOON else (1,) for i in range(SOON - 1, levels)}
-    products(wanted, (inv, down, up, reward), weight, base, buffers, sems)
+    products(wanted, lambda i: None, weight, base, inv, down, up, pay)
 
 
 def respond_kernel(places, weight, base, x_high_soon, x_low_soon, kept, x_high, x_low):
@@ -149,40 +147,32 @@
     return [resident((levels, 4 * phases, phases), BF16), resident((levels, columns, phases), F32)]
 
 
-def buffers(levels, columns, phases):
-    return (
-        [pltpu.VMEM((levels, phases, phases), F32)] * 3
-        + [pltpu.VMEM((levels, columns, phases), F32)]
-        + [pltpu.SemaphoreType.DMA((4, levels))]
-    )
-
-
 def prepare(inverse_diag, down_block, up_block, reward):
     levels, columns, phases = reward.shape
-    assert levels >= AHEAD
     rows = phases + columns
-    given = [pin(x, pltpu.HBM) for x in (inverse_diag, down_block, up_block, reward)]
-    *soon, kept_soon = pl.pallas_call(
+    matrix = resident((levels, phases, phases), F32)
+    *soon, x_high, x_low, kept_soon, inv, down, up, pay = pl.pallas_call(
         prepare_kernel,
         out_shape=operators(SOON, columns, phases)
         + [resident((SOON, rows, phases), BF16)] * 2
-        + [resident((SOON, rows, phases), F32)],
+        + [resident((SOON, rows, phases), F32)]
+        + [matrix] * 3
+        + [resident((levels, columns, phases), F32)],
         in_specs=[HBM] * 4,
-        out_specs=[VMEM] * 5,
-        scratch_shapes=buffers(SOON, columns, phases),
+        out_specs=[VMEM] * 9,
+        scratch_shapes=[pltpu.SemaphoreType.DMA((4, levels))],
         compiler_params=pltpu.CompilerParams(vmem_limit_bytes=16 * 2**20),
         name="prepare",
-    )(*given)
+    )(*[pin(x, pltpu.HBM) for x in (inverse_diag, down_block, up_block, reward)])
     weights = pl.pallas_call(
         prepare_rest_kernel,
         out_shape=operators(levels, columns, phases),
-        in_specs=[HBM] * 4 + [VMEM] * 2,
+        in_specs=[VMEM] * 6,
         out_specs=[VMEM] * 2,
-        scratch_shapes=buffers(levels - SOON + 1, columns, phases),
         compiler_params=pltpu.CompilerParams(vmem_limit_bytes=16 * 2**20),
         name="prepare_rest",
-    )(*given, *[pin(x) for x in soon[:2]])
-    return weights, soon[2:], kept_soon
+    )(*[pin(x) for x in (*soon, inv, down, up, pay)])
+    return weights, (x_high, x_low), kept_soon
 
 
 def respond(places, weights, started):

time: 48 us -> 46.6 us (0.971)
  Pallas kernels: 31.8 us -> 29.7 us
  waiting for transfers between devices: 5.88 us -> 6.52 us
    pallas_call x1, Pallas kernels: 4.28 us -> 2.01 us  [prepare(): pl.pallas_call(prepare_rest_kernel, out_shape=operators(levels, columns,...]
    ppermute x4, waiting for transfers between devices: 5.87 us -> 6.5 us  [local(): entering = lax.ppermute(leaving, 'lvl', pairs) if pairs else None]
  transfers between devices with their start and end apart: 8 -> 8, of which waited for: 2 -> 2; matrix products, arithmetic and copies ran while one was open for 0% -> 0% of each run, Pallas kernels for 54% -> 51%
where the time goes in v9:
time: 46.6 us; the launch traced here: 46.3 us
  Pallas kernels  29.7 us (64%)
  starting transfers between devices  9.86 us (21%)
  waiting for transfers between devices  6.52 us (14%)
    pallas_call x1, Pallas kernels, spread_open(): pl.pallas_call(functools.partial(spread_open_kernel, tuple(places)), out_...  10.9 us
    ppermute x4, waiting for transfers between devices, local(): entering = lax.ppermute(leaving, 'lvl', pairs) if pairs else None  6.5 us
    pallas_call x7, Pallas kernels, run_chunk(): pl.pallas_call(functools.partial(chunk_kernel, chunk, tuple(places), part...  5.37 us
    pallas_call x1, Pallas kernels, prepare(): pl.pallas_call(prepare_kernel, out_shape=operators(SOON, columns, phases)...  4.11 us
    ppermute x4, starting transfers between devices, local(): entering = lax.ppermute(leaving, 'lvl', pairs) if pairs else None  3.9 us
    pallas_call x1, Pallas kernels, spread_close(): pl.pallas_call(functools.partial(spread_close_kernel, tuple(places)), out...  3.73 us
    pallas_call x4, Pallas kernels, finish_state(): pl.pallas_call(functools.partial(finish_state_kernel, place), out_shape=(...  3.57 us
    ppermute x1, starting transfers between devices, local(): soon = lax.ppermute(soon_here, 'lvl', [(d + 1, d) for d in range(top)])  2.63 us
  transfers between devices with their start and end apart: 8, of which 2 were waited for; matrix products, arithmetic and copies ran while one was open for 0% of the time, Pallas kernels for 51%

profile of v9, /device:TPU:11, one launch (start us, length us, event | category | flops | bytes accessed | tf_op | source)
XLA Modules:
  0.0 46.3 jit_solution(1084410176971386943)
XLA Ops:
  0.0 4.1 %prepare.1 = (bf16[3,1024,256]{2,1,0:T(8,128)(2,1)S(1)}, f32[3,16,256]{2,1,0:T(8,128)S(1)}, bf16[3,272,256]{2,1,0:T(8,128)(2,1)S(1)}, bf16[3,272,256]{2,1,0:T(8,...) custom-call(f32[8,256,256]{2,1,0:T(8,128)} %inv_far.1, ...), custom_call_target="tpu_custom_call" | custom-call | tf_op jit(solution)/shard_map/prepare/pallas_call | solution.py:154
  4.1 2.6 %collective-permute-start = (f32[3,272,256]{2,1,0:T(8,128)S(1)}, f32[3,272,256]{2,1,0:T(8,128)S(1)}, u32[]{:S(2)}, u32[]{:S(2)}) collective-permute-start(f32[3,272,256]{2,1,0:T(8,128)S(1)} %get-tuple-element.53.soon), channel_id=1, source_target_pairs={{4,0},{8,4},{12,8},{5,1},{9,5},{13,9},{6,2},{10,6},{14,10},{7,3},{... | collective-permute-start | bytes 2506760 | tf_op jit(solution)/shard_map/ppermute | solution.py:545
  6.8 2.0 %prepare_rest.1 = (bf16[8,1024,256]{2,1,0:T(8,128)(2,1)S(1)}, f32[8,16,256]{2,1,0:T(8,128)S(1)}) custom-call(bf16[3,1024,256]{2,1,0:T(8,128)(2,1)S(1)} %get-tuple-element.43.weight_soon, f32[3,16,256]{2,1,0:T(8,128)S(1)} %get-tuple-element.44.base_soon, f32[8,256,256]{2,1,0:T(8,128)S(1)} %get-tuple-element.45.inv, ...), custom_call_target="tpu_custom_call" | custom-call | tf_op jit(solution)/shard_map/prepare_rest/pallas_call | solution.py:167
  8.8 0.7 %collective-permute-start.1 = (f32[4,272,256]{2,1,0:T(8,128)S(1)}, f32[4,272,256]{2,1,0:T(8,128)S(1)}, u32[]{:S(2)}, u32[]{:S(2)}) collective-permute-start(f32[4,272,256]{2,1,0:T(8,128)S(1)} %respond.1), channel_id=1, source_target_pairs={{4,0},{5,1},{6,2},{7,3},{20,16},{21,17},{22,18},{23,19}} | collective-permute-start | bytes 3342344 | tf_op jit(solution)/shard_map/ppermute | solution.py:546
  9.5 10.9 %spread_open.1 = (bf16[32,272,256]{2,1,0:T(8,128)(2,1)S(1)}, bf16[32,272,256]{2,1,0:T(8,128)(2,1)S(1)}, f32[4,272,256]{2,1,0:T(8,128)S(1)}) custom-call(bf16[8,1024,256]{2,1,0:T(8,128)(2,1)S(1)} %get-tuple-element.49.weight.refs_0_, f32[8,16,256]{2,1,0:T(8,128)S(1)} %get-tuple-element.50.base.refs_1_), custom_call_target="tpu_custom_call" | custom-call | tf_op jit(solution)/shard_map/spread_open/pallas_call | solution.py:423
  20.4 0.0 collective-permute-done.refs_2_.soon
  20.4 1.9 %collective-permute-start.6 = (f32[4,272,256]{2,1,0:T(8,128)S(1)}, f32[4,272,256]{2,1,0:T(8,128)S(1)}, u32[]{:S(2)}, u32[]{:S(2)}) collective-permute-start(f32[4,272,256]{2,1,0:T(8,128)S(1)} %get-tuple-element.68.late), channel_id=1, source_target_pairs={{12,8},{13,9},{14,10},{15,11},{28,24},{29,25},{30,26},{31,27}} | collective-permute-start | bytes 3342344 | tf_op jit(solution)/shard_map/ppermute | solution.py:548
  22.4 0.7 %collective-permute-start.2 = (f32[4,16,256]{2,1,0:T(8,128)S(1)}, f32[4,16,256]{2,1,0:T(8,128)S(1)}, u32[]{:S(2)}, u32[]{:S(2)}) collective-permute-start(f32[4,16,256]{2,1,0:T(8,128)S(1)} %get-tuple-element.58.refs_5_.refs_4_), channel_id=1, source_target_pairs={{0,4},{1,5},{2,6},{3,7},{16,20},{17,21},{18,22},{19,23}} | collective-permute-start | bytes 196616 | tf_op jit(solution)/shard_map/ppermute | solution.py:578
  23.1 0.0 collective-permute-done.2.refs_3_
  23.1 0.2 chunk.8
  23.3 0.0 collective-permute-done.1.refs_3_
  23.4 0.7 %collective-permute-start.3 = (f32[4,16,256]{2,1,0:T(8,128)S(1)}, f32[4,16,256]{2,1,0:T(8,128)S(1)}, u32[]{:S(2)}, u32[]{:S(2)}) collective-permute-start(f32[4,16,256]{2,1,0:T(8,128)S(1)} %get-tuple-element.75.refs_6_), channel_id=1, source_target_pairs={{0,4},{4,8},{1,5},{5,9},{2,6},{6,10},{3,7},{7,11},{16,20},{20,24},... | collective-permute-start | bytes 196616 | tf_op jit(solution)/shard_map/ppermute | solution.py:578
  24.0 3.7 %spread_close.1 = (bf16[6,272,256]{2,1,0:T(8,128)(2,1)S(1)}, bf16[6,272,256]{2,1,0:T(8,128)(2,1)S(1)}, f32[8,16,256]{2,1,0:T(8,128)S(1)}, f32[4,16,256]{2,1,0:T(8,128)S(1)}) custom-call(bf16[8,1024,256]{2,1,0:T(8,128)(2,1)S(1)} %get-tuple-element.49.weight.refs_0_, f32[8,16,256]{2,1,0:T(8,128)S(1)} %get-tuple-element.50.base.refs_1_, ...), custom_call_target="tpu_custom_call" | custom-call | tf_op jit(solution)/shard_map/spread_close/pallas_call | solution.py:437
  27.8 0.0 collective-permute-done.3.entering.refs_2_.refs_4_
  27.8 0.7 %collective-permute-start.4 = (f32[4,16,256]{2,1,0:T(8,128)S(1)}, f32[4,16,256]{2,1,0:T(8,128)S(1)}, u32[]{:S(2)}, u32[]{:S(2)}) collective-permute-start(f32[4,16,256]{2,1,0:T(8,128)S(1)} %answer.1), channel_id=1, source_target_pairs={{8,4},{9,5},{10,6},{11,7},{24,20},{25,21},{26,22},{27,23}} | collective-permute-start | bytes 196616 | tf_op jit(solution)/shard_map/ppermute | solution.py:556
  28.6 0.0 collective-permute-done.4.refs_3_
  28.6 1.3 %collective-permute-start.5 = (f32[4,16,256]{2,1,0:T(8,128)S(1)}, f32[4,16,256]{2,1,0:T(8,128)S(1)}, u32[]{:S(2)}, u32[]{:S(2)}) collective-permute-start(f32[4,16,256]{2,1,0:T(8,128)S(1)} %get-tuple-element.76.refs_4_.refs_6_), channel_id=1, source_target_pairs={{4,8},{8,12},{5,9},{9,13},{6,10},{10,14},{7,11},{11,15},{20,24},{2... | collective-permute-start | bytes 196616 | tf_op jit(solution)/shard_map/ppermute | solution.py:578
  29.9 0.0 collective-permute-done.6.refs_3_
  30.0 0.3 chunk.12
  30.2 6.3 %collective-permute-done.5.refs_4_ = f32[4,16,256]{2,1,0:T(8,128)S(1)} collective-permute-done((f32[4,16,256]{2,1,0:T(8,128)S(1)}, f32[4,16,256]{2,1,0:T(8,128)S(1)}, u32[]{:S(2)}, u32[]{:S(2)}) %collective-permute-start.5) | collective-permute-done | bytes 65568 | tf_op jit(solution)/shard_map/ppermute | solution.py:578
  36.5 1.3 %collective-permute-start.7 = (f32[4,16,256]{2,1,0:T(8,128)S(1)}, f32[4,16,256]{2,1,0:T(8,128)S(1)}, u32[]{:S(2)}, u32[]{:S(2)}) collective-permute-start(f32[4,16,256]{2,1,0:T(8,128)S(1)} %finish_leaving.3), channel_id=1, source_target_pairs={{8,12},{9,13},{10,14},{11,15},{24,28},{25,29},{26,30},{27,31}} | collective-permute-start | bytes 196616 | tf_op jit(solution)/shard_map/ppermute | solution.py:578
  37.8 1.4 %finish_state.6.refs_3_ = f32[8,16,256]{2,1,0:T(8,128)S(1)} custom-call(bf16[32,272,256]{2,1,0:T(8,128)(2,1)S(1)} %get-tuple-element.63.open_high.refs_0_, bf16[32,272,256]{2,1,0:T(8,128)(2,1)S(1)} %get-tuple-element.64.open_low.refs_1_, bf16[6,272,256]{2,1,0:T(8,128)(2,1)S(1)} %get-tuple-element.66.refs_2_, ...), custom_call_target="tpu_custom_call" | custom-call | tf_op jit(solution)/shard_map/finish_state/pallas_call | solution.py:501
  39.3 4.8 %chunk.13 = (f32[8,16,256]{2,1,0:T(8,128)S(1)}, f32[4,16,256]{2,1,0:T(8,128)}) custom-call(bf16[8,1024,256]{2,1,0:T(8,128)(2,1)S(1)} %get-tuple-element.49.weight.refs_0_, f32[8,16,256]{2,1,0:T(8,128)S(1)} %get-tuple-element.50.base.refs_1_, f32[3,272,256]{2,1,0:T(8,128)S(1)} %collective-permute-done.refs_2_.soon, f32[8,16,256]{2,1,0:T(8,128)S(1)} %finish_state.6.refs_3_), custom_call_target="tpu_custom_call" | custom-call | tf_op jit(solution)/shard_map/chunk/pallas_call | solution.py:314
  44.0 0.2 collective-permute-done.7.refs_4_
  44.3 2.1 %finish_state.7 = f32[8,16,256]{2,1,0:T(8,128)} custom-call(bf16[32,272,256]{2,1,0:T(8,128)(2,1)S(1)} %get-tuple-element.63.open_high.refs_0_, bf16[32,272,256]{2,1,0:T(8,128)(2,1)S(1)} %get-tuple-element.64.open_low.refs_1_, bf16[6,272,256]{2,1,0:T(8,128)(2,1)S(1)} %get-tuple-element.66.refs_2_, bf16[6,272,256]{2,1,0:T(8,128)(2,1)S(1)} %get-tuple-element.67.refs_3_, ...), custom_call_target="tpu_custom_call" | custom-call | tf_op jit(solution)/shard_map/finish_state/pallas_call | solution.py:501
  (10 shorter events, 0.2 us)
Async XLA Ops:
  4.1 16.3 %collective-permute-start = (f32[3,272,256]{2,1,0:T(8,128)S(1)}, f32[3,272,256]{2,1,0:T(8,128)S(1)}, u32[]{:S(2)}, u32[]{:S(2)}) collective-permute-start(f32[3,272,256]{2,1,0:T(8,128)S(1)} %get-tuple-element.53.soon), channel_id=1, source_target_pairs={{4,0},{8,4},{12,8},{5,1},{9,5},{13,9},{6,2},{10,6},{14,10},{7,3},{... | collective-permute-start | bytes 2506760 | tf_op jit(solution)/shard_map/ppermute | solution.py:545
  8.8 14.5 %collective-permute-start.1 = (f32[4,272,256]{2,1,0:T(8,128)S(1)}, f32[4,272,256]{2,1,0:T(8,128)S(1)}, u32[]{:S(2)}, u32[]{:S(2)}) collective-permute-start(f32[4,272,256]{2,1,0:T(8,128)S(1)} %respond.1), channel_id=1, source_target_pairs={{4,0},{5,1},{6,2},{7,3},{20,16},{21,17},{22,18},{23,19}} | collective-permute-start | bytes 3342344 | tf_op jit(solution)/shard_map/ppermute | solution.py:546
  20.4 9.5 %collective-permute-start.6 = (f32[4,272,256]{2,1,0:T(8,128)S(1)}, f32[4,272,256]{2,1,0:T(8,128)S(1)}, u32[]{:S(2)}, u32[]{:S(2)}) collective-permute-start(f32[4,272,256]{2,1,0:T(8,128)S(1)} %get-tuple-element.68.late), channel_id=1, source_target_pairs={{12,8},{13,9},{14,10},{15,11},{28,24},{29,25},{30,26},{31,27}} | collective-permute-start | bytes 3342344 | tf_op jit(solution)/shard_map/ppermute | solution.py:548
  22.4 0.7 %collective-permute-start.2 = (f32[4,16,256]{2,1,0:T(8,128)S(1)}, f32[4,16,256]{2,1,0:T(8,128)S(1)}, u32[]{:S(2)}, u32[]{:S(2)}) collective-permute-start(f32[4,16,256]{2,1,0:T(8,128)S(1)} %get-tuple-element.58.refs_5_.refs_4_), channel_id=1, source_target_pairs={{0,4},{1,5},{2,6},{3,7},{16,20},{17,21},{18,22},{19,23}} | collective-permute-start | bytes 196616 | tf_op jit(solution)/shard_map/ppermute | solution.py:578
  23.4 4.4 %collective-permute-start.3 = (f32[4,16,256]{2,1,0:T(8,128)S(1)}, f32[4,16,256]{2,1,0:T(8,128)S(1)}, u32[]{:S(2)}, u32[]{:S(2)}) collective-permute-start(f32[4,16,256]{2,1,0:T(8,128)S(1)} %get-tuple-element.75.refs_6_), channel_id=1, source_target_pairs={{0,4},{4,8},{1,5},{5,9},{2,6},{6,10},{3,7},{7,11},{16,20},{20,24},... | collective-permute-start | bytes 196616 | tf_op jit(solution)/shard_map/ppermute | solution.py:578
  27.8 0.7 %collective-permute-start.4 = (f32[4,16,256]{2,1,0:T(8,128)S(1)}, f32[4,16,256]{2,1,0:T(8,128)S(1)}, u32[]{:S(2)}, u32[]{:S(2)}) collective-permute-start(f32[4,16,256]{2,1,0:T(8,128)S(1)} %answer.1), channel_id=1, source_target_pairs={{8,4},{9,5},{10,6},{11,7},{24,20},{25,21},{26,22},{27,23}} | collective-permute-start | bytes 196616 | tf_op jit(solution)/shard_map/ppermute | solution.py:556
  28.6 7.9 %collective-permute-start.5 = (f32[4,16,256]{2,1,0:T(8,128)S(1)}, f32[4,16,256]{2,1,0:T(8,128)S(1)}, u32[]{:S(2)}, u32[]{:S(2)}) collective-permute-start(f32[4,16,256]{2,1,0:T(8,128)S(1)} %get-tuple-element.76.refs_4_.refs_6_), channel_id=1, source_target_pairs={{4,8},{8,12},{5,9},{9,13},{6,10},{10,14},{7,11},{11,15},{20,24},{2... | collective-permute-start | bytes 196616 | tf_op jit(solution)/shard_map/ppermute | solution.py:578
  36.5 7.7 %collective-permute-start.7 = (f32[4,16,256]{2,1,0:T(8,128)S(1)}, f32[4,16,256]{2,1,0:T(8,128)S(1)}, u32[]{:S(2)}, u32[]{:S(2)}) collective-permute-start(f32[4,16,256]{2,1,0:T(8,128)S(1)} %finish_leaving.3), channel_id=1, source_target_pairs={{8,12},{9,13},{10,14},{11,15},{24,28},{25,29},{26,30},{27,31}} | collective-permute-start | bytes 196616 | tf_op jit(solution)/shard_map/ppermute | solution.py:578

commit v10 on v9

--- a/solution.py
+++ b/solution.py
@@ -542,10 +542,11 @@
     weight, base = weights
     late_odd = respond(odd, weights, begun) if odd else None
     ways, late_here = spread_open(ready, weight, base)
-    soon = lax.ppermute(soon_here, "lvl", [(d + 1, d) for d in range(top)])
+    soon_odd = lax.ppermute(soon_here, "lvl", [(d + 1, d) for d in range(1, top, 2)])
+    soon = lax.ppermute(soon_here, "lvl", [(d + 1, d) for d in range(0, top, 2)])
     late = lax.ppermute(late_odd, "lvl", [(d, d - 1) for d in odd]) if odd else None
     soon, late_here, late_odd = lax.optimization_barrier((soon, late_here, late_odd))
-    late_top = lax.ppermute(late_here, "lvl", [(top, top - 1)]) if top % 2 else None
+    late_top = None
     own = {"weight": weight, "base": base, "soon": soon}
     state = leaving = entering = parted = None
     for step in range(count + 1):
@@ -563,14 +564,16 @@
                 leaving = finish_leaving(step, ways, entering, parted_first, leaving, base.shape[0])
         elif step < count:
             state, leaving = run_chunk(
-                0, [step], {**own, "entering": entering, "state": state, "leaving": leaving}
+                0, [step], {**own, "soon": soon_odd if step % 2 else soon, "entering": entering, "state": state, "leaving": leaving}
             )
         if step == 1:
+            top_sent, leaving = lax.optimization_barrier((late_here, leaving))
+            late_top = lax.ppermute(top_sent, "lvl", [(top, top - 1)]) if top % 2 else None
             first_late = late if odd else late_top
             given_first = {**own, "late": first_late, "earlier": earlier, "state": state, "leaving": leaving}
             state, leaving = run_chunk(1, [0], given_first)
         if returned is not None:
-            given_rest = {**own, "returned": returned, "edge": edge, "state": state, "leaving": leaving}
+            given_rest = {**own, "soon": soon_odd, "returned": returned, "edge": edge, "state": state, "leaving": leaving}
             state, leaving = run_chunk(1, [place], given_rest, "late")
         came = entering
         if step < count:

time: 46.6 us -> 47.3 us (1.015)
  starting transfers between devices: 9.86 us -> 12.5 us
  waiting for transfers between devices: 6.52 us -> 4.59 us
    ppermute x2 -> x3, starting transfers between devices: 4.57 us -> 7.22 us  [the longest x1 3.87 us: local(): lax.ppermute(top_sent, 'lvl', [(top, top - 1)])]
    ppermute x4, waiting for transfers between devices: 6.5 us -> 4.58 us  [local(): entering = lax.ppermute(leaving, 'lvl', pairs) if pairs else None]
  transfers between devices with their start and end apart: 8 -> 9, of which waited for: 2 -> 2; matrix products, arithmetic and copies ran while one was open for 0% -> 0% of each run, Pallas kernels for 51% -> 50%
where the time goes in v10:
time: 47.3 us; the launch traced here: 47.1 us
  Pallas kernels  29.7 us (63%)
  starting transfers between devices  12.5 us (26%)
  waiting for transfers between devices  4.59 us (10%)
    pallas_call x1, Pallas kernels, spread_open(): pl.pallas_call(functools.partial(spread_open_kernel, tuple(places)), out_...  10.9 us
    pallas_call x7, Pallas kernels, run_chunk(): pl.pallas_call(functools.partial(chunk_kernel, chunk, tuple(places), part...  5.37 us
    ppermute x4, waiting for transfers between devices, local(): entering = lax.ppermute(leaving, 'lvl', pairs) if pairs else None  4.58 us
    pallas_call x1, Pallas kernels, prepare(): pl.pallas_call(prepare_kernel, out_shape=operators(SOON, columns, phases)...  4.11 us
    ppermute x4, starting transfers between devices, local(): entering = lax.ppermute(leaving, 'lvl', pairs) if pairs else None  3.9 us
    ppermute x1, starting transfers between devices, local(): lax.ppermute(top_sent, 'lvl', [(top, top - 1)])  3.87 us
    pallas_call x1, Pallas kernels, spread_close(): pl.pallas_call(functools.partial(spread_close_kernel, tuple(places)), out...  3.73 us
    pallas_call x4, Pallas kernels, finish_state(): pl.pallas_call(functools.partial(finish_state_kernel, place), out_shape=(...  3.57 us
  transfers between devices with their start and end apart: 9, of which 2 were waited for; matrix products, arithmetic and copies ran while one was open for 0% of the time, Pallas kernels for 50%

profile of v10, /device:TPU:11, one launch (start us, length us, event | category | flops | bytes accessed | tf_op | source)
XLA Modules:
  0.0 47.1 jit_solution(14469384870462301736)
XLA Ops:
  0.0 4.1 %prepare.1 = (bf16[3,1024,256]{2,1,0:T(8,128)(2,1)S(1)}, f32[3,16,256]{2,1,0:T(8,128)S(1)}, bf16[3,272,256]{2,1,0:T(8,128)(2,1)S(1)}, bf16[3,272,256]{2,1,0:T(8,...) custom-call(f32[8,256,256]{2,1,0:T(8,128)} %inv_far.1, ...), custom_call_target="tpu_custom_call" | custom-call | tf_op jit(solution)/shard_map/prepare/pallas_call | solution.py:154
  4.1 2.6 %collective-permute-start = (f32[3,272,256]{2,1,0:T(8,128)S(1)}, f32[3,272,256]{2,1,0:T(8,128)S(1)}, u32[]{:S(2)}, u32[]{:S(2)}) collective-permute-start(f32[3,272,256]{2,1,0:T(8,128)S(1)} %get-tuple-element.55.soon), channel_id=1, source_target_pairs={{4,0},{12,8},{5,1},{13,9},{6,2},{14,10},{7,3},{15,11},{20,16},{28,... | collective-permute-start | bytes 2506760 | tf_op jit(solution)/shard_map/ppermute | solution.py:546
  6.8 0.7 %collective-permute-start.2 = (f32[3,272,256]{2,1,0:T(8,128)S(1)}, f32[3,272,256]{2,1,0:T(8,128)S(1)}, u32[]{:S(2)}, u32[]{:S(2)}) collective-permute-start(f32[3,272,256]{2,1,0:T(8,128)S(1)} %get-tuple-element.55.soon), channel_id=1, source_target_pairs={{8,4},{9,5},{10,6},{11,7},{24,20},{25,21},{26,22},{27,23}} | collective-permute-start | bytes 2506760 | tf_op jit(solution)/shard_map/ppermute | solution.py:545
  7.5 2.0 %prepare_rest.1 = (bf16[8,1024,256]{2,1,0:T(8,128)(2,1)S(1)}, f32[8,16,256]{2,1,0:T(8,128)S(1)}) custom-call(bf16[3,1024,256]{2,1,0:T(8,128)(2,1)S(1)} %get-tuple-element.45.weight_soon, f32[3,16,256]{2,1,0:T(8,128)S(1)} %get-tuple-element.46.base_soon, f32[8,256,256]{2,1,0:T(8,128)S(1)} %get-tuple-element.47.inv, ...), custom_call_target="tpu_custom_call" | custom-call | tf_op jit(solution)/shard_map/prepare_rest/pallas_call | solution.py:167
  9.5 0.7 %collective-permute-start.1 = (f32[4,272,256]{2,1,0:T(8,128)S(1)}, f32[4,272,256]{2,1,0:T(8,128)S(1)}, u32[]{:S(2)}, u32[]{:S(2)}) collective-permute-start(f32[4,272,256]{2,1,0:T(8,128)S(1)} %respond.1), channel_id=1, source_target_pairs={{4,0},{5,1},{6,2},{7,3},{20,16},{21,17},{22,18},{23,19}} | collective-permute-start | bytes 3342344 | tf_op jit(solution)/shard_map/ppermute | solution.py:547
  10.3 10.9 %spread_open.1 = (bf16[32,272,256]{2,1,0:T(8,128)(2,1)S(1)}, bf16[32,272,256]{2,1,0:T(8,128)(2,1)S(1)}, f32[4,272,256]{2,1,0:T(8,128)S(1)}) custom-call(bf16[8,1024,256]{2,1,0:T(8,128)(2,1)S(1)} %get-tuple-element.51.weight.refs_0_, f32[8,16,256]{2,1,0:T(8,128)S(1)} %get-tuple-element.52.base.refs_1_), custom_call_target="tpu_custom_call" | custom-call | tf_op jit(solution)/shard_map/spread_open/pallas_call | solution.py:423
  21.2 0.0 collective-permute-done.refs_2_.soon
  21.2 0.7 %collective-permute-start.3 = (f32[4,16,256]{2,1,0:T(8,128)S(1)}, f32[4,16,256]{2,1,0:T(8,128)S(1)}, u32[]{:S(2)}, u32[]{:S(2)}) collective-permute-start(f32[4,16,256]{2,1,0:T(8,128)S(1)} %get-tuple-element.60.refs_5_.refs_4_), channel_id=1, source_target_pairs={{0,4},{1,5},{2,6},{3,7},{16,20},{17,21},{18,22},{19,23}} | collective-permute-start | bytes 196616 | tf_op jit(solution)/shard_map/ppermute | solution.py:581
  21.9 0.0 collective-permute-done.2.refs_2_
  21.9 0.0 collective-permute-done.3.refs_3_
  21.9 0.2 chunk.8
  22.1 3.9 %collective-permute-start.7 = (f32[4,272,256]{2,1,0:T(8,128)S(1)}, f32[4,272,256]{2,1,0:T(8,128)S(1)}, u32[]{:S(2)}, u32[]{:S(2)}) collective-permute-start(f32[4,272,256]{2,1,0:T(8,128)S(1)} %get-tuple-element.80.late), channel_id=1, source_target_pairs={{12,8},{13,9},{14,10},{15,11},{28,24},{29,25},{30,26},{31,27}} | collective-permute-start | bytes 3342344 | tf_op jit(solution)/shard_map/ppermute | solution.py:571
  26.0 0.0 collective-permute-done.1.refs_3_
  26.0 0.7 %collective-permute-start.4 = (f32[4,16,256]{2,1,0:T(8,128)S(1)}, f32[4,16,256]{2,1,0:T(8,128)S(1)}, u32[]{:S(2)}, u32[]{:S(2)}) collective-permute-start(f32[4,16,256]{2,1,0:T(8,128)S(1)} %get-tuple-element.78.refs_6_), channel_id=1, source_target_pairs={{0,4},{4,8},{1,5},{5,9},{2,6},{6,10},{3,7},{7,11},{16,20},{20,24},... | collective-permute-start | bytes 196616 | tf_op jit(solution)/shard_map/ppermute | solution.py:581
  26.7 3.7 %spread_close.1 = (bf16[6,272,256]{2,1,0:T(8,128)(2,1)S(1)}, bf16[6,272,256]{2,1,0:T(8,128)(2,1)S(1)}, f32[8,16,256]{2,1,0:T(8,128)S(1)}, f32[4,16,256]{2,1,0:T(8,128)S(1)}) custom-call(bf16[8,1024,256]{2,1,0:T(8,128)(2,1)S(1)} %get-tuple-element.51.weight.refs_0_, f32[8,16,256]{2,1,0:T(8,128)S(1)} %get-tuple-element.52.base.refs_1_, ...), custom_call_target="tpu_custom_call" | custom-call | tf_op jit(solution)/shard_map/spread_close/pallas_call | solution.py:437
  30.5 0.0 collective-permute-done.4.entering.refs_2_.refs_4_
  30.5 0.7 %collective-permute-start.5 = (f32[4,16,256]{2,1,0:T(8,128)S(1)}, f32[4,16,256]{2,1,0:T(8,128)S(1)}, u32[]{:S(2)}, u32[]{:S(2)}) collective-permute-start(f32[4,16,256]{2,1,0:T(8,128)S(1)} %answer.1), channel_id=1, source_target_pairs={{8,4},{9,5},{10,6},{11,7},{24,20},{25,21},{26,22},{27,23}} | collective-permute-start | bytes 196616 | tf_op jit(solution)/shard_map/ppermute | solution.py:557
  31.2 0.0 collective-permute-done.5.refs_3_
  31.3 1.3 %collective-permute-start.6 = (f32[4,16,256]{2,1,0:T(8,128)S(1)}, f32[4,16,256]{2,1,0:T(8,128)S(1)}, u32[]{:S(2)}, u32[]{:S(2)}) collective-permute-start(f32[4,16,256]{2,1,0:T(8,128)S(1)} %get-tuple-element.79.refs_4_.refs_6_), channel_id=1, source_target_pairs={{4,8},{8,12},{5,9},{9,13},{6,10},{10,14},{7,11},{11,15},{20,24},{2... | collective-permute-start | bytes 196616 | tf_op jit(solution)/shard_map/ppermute | solution.py:581
  32.6 0.0 collective-permute-done.7.refs_3_
  32.6 0.3 chunk.12
  32.9 4.4 %collective-permute-done.6.refs_4_ = f32[4,16,256]{2,1,0:T(8,128)S(1)} collective-permute-done((f32[4,16,256]{2,1,0:T(8,128)S(1)}, f32[4,16,256]{2,1,0:T(8,128)S(1)}, u32[]{:S(2)}, u32[]{:S(2)}) %collective-permute-start.6) | collective-permute-done | bytes 65568 | tf_op jit(solution)/shard_map/ppermute | solution.py:581
  37.2 1.3 %collective-permute-start.8 = (f32[4,16,256]{2,1,0:T(8,128)S(1)}, f32[4,16,256]{2,1,0:T(8,128)S(1)}, u32[]{:S(2)}, u32[]{:S(2)}) collective-permute-start(f32[4,16,256]{2,1,0:T(8,128)S(1)} %finish_leaving.3), channel_id=1, source_target_pairs={{8,12},{9,13},{10,14},{11,15},{24,28},{25,29},{26,30},{27,31}} | collective-permute-start | bytes 196616 | tf_op jit(solution)/shard_map/ppermute | solution.py:581
  38.6 1.4 %finish_state.6.refs_3_ = f32[8,16,256]{2,1,0:T(8,128)S(1)} custom-call(bf16[32,272,256]{2,1,0:T(8,128)(2,1)S(1)} %get-tuple-element.67.open_high.refs_0_, bf16[32,272,256]{2,1,0:T(8,128)(2,1)S(1)} %get-tuple-element.68.open_low.refs_1_, bf16[6,272,256]{2,1,0:T(8,128)(2,1)S(1)} %get-tuple-element.70.refs_2_, ...), custom_call_target="tpu_custom_call" | custom-call | tf_op jit(solution)/shard_map/finish_state/pallas_call | solution.py:501
  40.0 4.8 %chunk.13 = (f32[8,16,256]{2,1,0:T(8,128)S(1)}, f32[4,16,256]{2,1,0:T(8,128)}) custom-call(bf16[8,1024,256]{2,1,0:T(8,128)(2,1)S(1)} %get-tuple-element.51.weight.refs_0_, f32[8,16,256]{2,1,0:T(8,128)S(1)} %get-tuple-element.52.base.refs_1_, f32[3,272,256]{2,1,0:T(8,128)S(1)} %collective-permute-done.refs_2_.soon, f32[8,16,256]{2,1,0:T(8,128)S(1)} %finish_state.6.refs_3_), custom_call_target="tpu_custom_call" | custom-call | tf_op jit(solution)/shard_map/chunk/pallas_call | solution.py:314
  44.8 0.2 collective-permute-done.8.refs_4_
  45.0 2.1 %finish_state.7 = f32[8,16,256]{2,1,0:T(8,128)} custom-call(bf16[32,272,256]{2,1,0:T(8,128)(2,1)S(1)} %get-tuple-element.67.open_high.refs_0_, bf16[32,272,256]{2,1,0:T(8,128)(2,1)S(1)} %get-tuple-element.68.open_low.refs_1_, bf16[6,272,256]{2,1,0:T(8,128)(2,1)S(1)} %get-tuple-element.70.refs_2_, bf16[6,272,256]{2,1,0:T(8,128)(2,1)S(1)} %get-tuple-element.71.refs_3_, ...), custom_call_target="tpu_custom_call" | custom-call | tf_op jit(solution)/shard_map/finish_state/pallas_call | solution.py:501
  (10 shorter events, 0.2 us)
Async XLA Ops:
  4.1 17.0 %collective-permute-start = (f32[3,272,256]{2,1,0:T(8,128)S(1)}, f32[3,272,256]{2,1,0:T(8,128)S(1)}, u32[]{:S(2)}, u32[]{:S(2)}) collective-permute-start(f32[3,272,256]{2,1,0:T(8,128)S(1)} %get-tuple-element.55.soon), channel_id=1, source_target_pairs={{4,0},{12,8},{5,1},{13,9},{6,2},{14,10},{7,3},{15,11},{20,16},{28,... | collective-permute-start | bytes 2506760 | tf_op jit(solution)/shard_map/ppermute | solution.py:546
  6.8 15.1 %collective-permute-start.2 = (f32[3,272,256]{2,1,0:T(8,128)S(1)}, f32[3,272,256]{2,1,0:T(8,128)S(1)}, u32[]{:S(2)}, u32[]{:S(2)}) collective-permute-start(f32[3,272,256]{2,1,0:T(8,128)S(1)} %get-tuple-element.55.soon), channel_id=1, source_target_pairs={{8,4},{9,5},{10,6},{11,7},{24,20},{25,21},{26,22},{27,23}} | collective-permute-start | bytes 2506760 | tf_op jit(solution)/shard_map/ppermute | solution.py:545
  9.5 16.5 %collective-permute-start.1 = (f32[4,272,256]{2,1,0:T(8,128)S(1)}, f32[4,272,256]{2,1,0:T(8,128)S(1)}, u32[]{:S(2)}, u32[]{:S(2)}) collective-permute-start(f32[4,272,256]{2,1,0:T(8,128)S(1)} %respond.1), channel_id=1, source_target_pairs={{4,0},{5,1},{6,2},{7,3},{20,16},{21,17},{22,18},{23,19}} | collective-permute-start | bytes 3342344 | tf_op jit(solution)/shard_map/ppermute | solution.py:547
  21.2 0.7 %collective-permute-start.3 = (f32[4,16,256]{2,1,0:T(8,128)S(1)}, f32[4,16,256]{2,1,0:T(8,128)S(1)}, u32[]{:S(2)}, u32[]{:S(2)}) collective-permute-start(f32[4,16,256]{2,1,0:T(8,128)S(1)} %get-tuple-element.60.refs_5_.refs_4_), channel_id=1, source_target_pairs={{0,4},{1,5},{2,6},{3,7},{16,20},{17,21},{18,22},{19,23}} | collective-permute-start | bytes 196616 | tf_op jit(solution)/shard_map/ppermute | solution.py:581
  22.1 10.5 %collective-permute-start.7 = (f32[4,272,256]{2,1,0:T(8,128)S(1)}, f32[4,272,256]{2,1,0:T(8,128)S(1)}, u32[]{:S(2)}, u32[]{:S(2)}) collective-permute-start(f32[4,272,256]{2,1,0:T(8,128)S(1)} %get-tuple-element.80.late), channel_id=1, source_target_pairs={{12,8},{13,9},{14,10},{15,11},{28,24},{29,25},{30,26},{31,27}} | collective-permute-start | bytes 3342344 | tf_op jit(solution)/shard_map/ppermute | solution.py:571
  26.0 4.4 %collective-permute-start.4 = (f32[4,16,256]{2,1,0:T(8,128)S(1)}, f32[4,16,256]{2,1,0:T(8,128)S(1)}, u32[]{:S(2)}, u32[]{:S(2)}) collective-permute-start(f32[4,16,256]{2,1,0:T(8,128)S(1)} %get-tuple-element.78.refs_6_), channel_id=1, source_target_pairs={{0,4},{4,8},{1,5},{5,9},{2,6},{6,10},{3,7},{7,11},{16,20},{20,24},... | collective-permute-start | bytes 196616 | tf_op jit(solution)/shard_map/ppermute | solution.py:581
  30.5 0.7 %collective-permute-start.5 = (f32[4,16,256]{2,1,0:T(8,128)S(1)}, f32[4,16,256]{2,1,0:T(8,128)S(1)}, u32[]{:S(2)}, u32[]{:S(2)}) collective-permute-start(f32[4,16,256]{2,1,0:T(8,128)S(1)} %answer.1), channel_id=1, source_target_pairs={{8,4},{9,5},{10,6},{11,7},{24,20},{25,21},{26,22},{27,23}} | collective-permute-start | bytes 196616 | tf_op jit(solution)/shard_map/ppermute | solution.py:557
  31.3 6.0 %collective-permute-start.6 = (f32[4,16,256]{2,1,0:T(8,128)S(1)}, f32[4,16,256]{2,1,0:T(8,128)S(1)}, u32[]{:S(2)}, u32[]{:S(2)}) collective-permute-start(f32[4,16,256]{2,1,0:T(8,128)S(1)} %get-tuple-element.79.refs_4_.refs_6_), channel_id=1, source_target_pairs={{4,8},{8,12},{5,9},{9,13},{6,10},{10,14},{7,11},{11,15},{20,24},{2... | collective-permute-start | bytes 196616 | tf_op jit(solution)/shard_map/ppermute | solution.py:581
  37.2 7.7 %collective-permute-start.8 = (f32[4,16,256]{2,1,0:T(8,128)S(1)}, f32[4,16,256]{2,1,0:T(8,128)S(1)}, u32[]{:S(2)}, u32[]{:S(2)}) collective-permute-start(f32[4,16,256]{2,1,0:T(8,128)S(1)} %finish_leaving.3), channel_id=1, source_target_pairs={{8,12},{9,13},{10,14},{11,15},{24,28},{25,29},{26,30},{27,31}} | collective-permute-start | bytes 196616 | tf_op jit(solution)/shard_map/ppermute | solution.py:581

commit v11 on v10

--- a/solution.py
+++ b/solution.py
@@ -102,23 +102,30 @@
 
 def prepare_kernel(inv_far, down_far, up_far, pay_far, weight, base, x_high, x_low, kept, inv, down, up, pay, sems):
     levels = pay.shape[0]
-
-    def copies(i):
-        pairs = ((inv_far, inv), (down_far, down), (pay_far, pay), (up_far, up))
-        return [pltpu.make_async_copy(far.at[i], near.at[i], sems.at[n, i]) for n, (far, near) in enumerate(pairs)]
+    cuts = ((0, 1), (1, SOON), (SOON, levels))
+
+    def copies(part):
+        at, end = cuts[part]
+        pairs = [(inv_far, inv), (down_far, down), (up_far, up)]
+        found = [
+            pltpu.make_async_copy(far.at[at:end], near.at[at:end], sems.at[n, part])
+            for n, (far, near) in enumerate(pairs)
+        ]
+        return found + ([pltpu.make_async_copy(pay_far, pay, sems.at[3, 0])] if part == 0 else [])
 
     def wait(i):
-        for copy in copies(i):
-            copy.wait()
-
-    for i in range(levels):
-        for copy in copies(i):
+        for part, (at, _) in enumerate(cuts):
+            if i == at:
+                for copy in copies(part):
+                    copy.wait()
+
+    for part in range(len(cuts)):
+        for copy in copies(part):
             copy.start()
     wanted = {i: (0, 1, 2) if i < SOON - 1 else (0, 2) for i in range(SOON)}
     products(wanted, wait, weight, base, inv, down, up, pay)
     response(0, SOON, x_high, x_low, weight, base, kept)
-    for i in range(SOON, levels):
-        wait(i)
+    wait(SOON)
 
 
 def prepare_rest_kernel(weight_soon, base_soon, inv, down, up, pay, weight, base):
@@ -160,7 +167,7 @@
         + [resident((levels, columns, phases), F32)],
         in_specs=[HBM] * 4,
         out_specs=[VMEM] * 9,
-        scratch_shapes=[pltpu.SemaphoreType.DMA((4, levels))],
+        scratch_shapes=[pltpu.SemaphoreType.DMA((4, 3))],
         compiler_params=pltpu.CompilerParams(vmem_limit_bytes=16 * 2**20),
         name="prepare",
     )(*[pin(x, pltpu.HBM) for x in (inverse_diag, down_block, up_block, reward)])

time: 47.3 us -> 46.8 us (0.989)
  no operation moved by 1% of the time
where the time goes in v11:
time: 46.8 us; the launch traced here: 46.6 us
  Pallas kernels  29.3 us (63%)
  starting transfers between devices  12.5 us (27%)
  waiting for transfers between devices  4.58 us (10%)
    pallas_call x1, Pallas kernels, spread_open(): pl.pallas_call(functools.partial(spread_open_kernel, tuple(places)), out_...  10.9 us
    pallas_call x7, Pallas kernels, run_chunk(): pl.pallas_call(functools.partial(chunk_kernel, chunk, tuple(places), part...  5.37 us
    ppermute x4, waiting for transfers between devices, local(): entering = lax.ppermute(leaving, 'lvl', pairs) if pairs else None  4.57 us
    ppermute x4, starting transfers between devices, local(): entering = lax.ppermute(leaving, 'lvl', pairs) if pairs else None  3.9 us
    ppermute x1, starting transfers between devices, local(): lax.ppermute(top_sent, 'lvl', [(top, top - 1)])  3.88 us
    pallas_call x1, Pallas kernels, spread_close(): pl.pallas_call(functools.partial(spread_close_kernel, tuple(places)), out...  3.73 us
    pallas_call x1, Pallas kernels, prepare(): pl.pallas_call(prepare_kernel, out_shape=operators(SOON, columns, phases)...  3.65 us
    pallas_call x4, Pallas kernels, finish_state(): pl.pallas_call(functools.partial(finish_state_kernel, place), out_shape=(...  3.57 us
  transfers between devices with their start and end apart: 9, of which 2 were waited for; matrix products, arithmetic and copies ran while one was open for 0% of the time, Pallas kernels for 50%

profile of v11, /device:TPU:11, one launch (start us, length us, event | category | flops | bytes accessed | tf_op | source)
XLA Modules:
  0.0 46.6 jit_solution(13487676871357924793)
XLA Ops:
  0.0 3.7 %prepare.1 = (bf16[3,1024,256]{2,1,0:T(8,128)(2,1)S(1)}, f32[3,16,256]{2,1,0:T(8,128)S(1)}, bf16[3,272,256]{2,1,0:T(8,128)(2,1)S(1)}, bf16[3,272,256]{2,1,0:T(8,...) custom-call(f32[8,256,256]{2,1,0:T(8,128)} %inv_far.1, ...), custom_call_target="tpu_custom_call" | custom-call | tf_op jit(solution)/shard_map/prepare/pallas_call | solution.py:161
  3.7 2.6 %collective-permute-start = (f32[3,272,256]{2,1,0:T(8,128)S(1)}, f32[3,272,256]{2,1,0:T(8,128)S(1)}, u32[]{:S(2)}, u32[]{:S(2)}) collective-permute-start(f32[3,272,256]{2,1,0:T(8,128)S(1)} %get-tuple-element.55.soon), channel_id=1, source_target_pairs={{4,0},{12,8},{5,1},{13,9},{6,2},{14,10},{7,3},{15,11},{20,16},{28,... | collective-permute-start | bytes 2506760 | tf_op jit(solution)/shard_map/ppermute | solution.py:553
  6.3 0.7 %collective-permute-start.2 = (f32[3,272,256]{2,1,0:T(8,128)S(1)}, f32[3,272,256]{2,1,0:T(8,128)S(1)}, u32[]{:S(2)}, u32[]{:S(2)}) collective-permute-start(f32[3,272,256]{2,1,0:T(8,128)S(1)} %get-tuple-element.55.soon), channel_id=1, source_target_pairs={{8,4},{9,5},{10,6},{11,7},{24,20},{25,21},{26,22},{27,23}} | collective-permute-start | bytes 2506760 | tf_op jit(solution)/shard_map/ppermute | solution.py:552
  7.0 2.0 %prepare_rest.1 = (bf16[8,1024,256]{2,1,0:T(8,128)(2,1)S(1)}, f32[8,16,256]{2,1,0:T(8,128)S(1)}) custom-call(bf16[3,1024,256]{2,1,0:T(8,128)(2,1)S(1)} %get-tuple-element.45.weight_soon, f32[3,16,256]{2,1,0:T(8,128)S(1)} %get-tuple-element.46.base_soon, f32[8,256,256]{2,1,0:T(8,128)S(1)} %get-tuple-element.47.inv, ...), custom_call_target="tpu_custom_call" | custom-call | tf_op jit(solution)/shard_map/prepare_rest/pallas_call | solution.py:174
  9.1 0.7 %collective-permute-start.1 = (f32[4,272,256]{2,1,0:T(8,128)S(1)}, f32[4,272,256]{2,1,0:T(8,128)S(1)}, u32[]{:S(2)}, u32[]{:S(2)}) collective-permute-start(f32[4,272,256]{2,1,0:T(8,128)S(1)} %respond.1), channel_id=1, source_target_pairs={{4,0},{5,1},{6,2},{7,3},{20,16},{21,17},{22,18},{23,19}} | collective-permute-start | bytes 3342344 | tf_op jit(solution)/shard_map/ppermute | solution.py:554
  9.8 10.9 %spread_open.1 = (bf16[32,272,256]{2,1,0:T(8,128)(2,1)S(1)}, bf16[32,272,256]{2,1,0:T(8,128)(2,1)S(1)}, f32[4,272,256]{2,1,0:T(8,128)S(1)}) custom-call(bf16[8,1024,256]{2,1,0:T(8,128)(2,1)S(1)} %get-tuple-element.51.weight.refs_0_, f32[8,16,256]{2,1,0:T(8,128)S(1)} %get-tuple-element.52.base.refs_1_), custom_call_target="tpu_custom_call" | custom-call | tf_op jit(solution)/shard_map/spread_open/pallas_call | solution.py:430
  20.7 0.0 collective-permute-done.refs_2_.soon
  20.7 0.7 %collective-permute-start.3 = (f32[4,16,256]{2,1,0:T(8,128)S(1)}, f32[4,16,256]{2,1,0:T(8,128)S(1)}, u32[]{:S(2)}, u32[]{:S(2)}) collective-permute-start(f32[4,16,256]{2,1,0:T(8,128)S(1)} %get-tuple-element.60.refs_5_.refs_4_), channel_id=1, source_target_pairs={{0,4},{1,5},{2,6},{3,7},{16,20},{17,21},{18,22},{19,23}} | collective-permute-start | bytes 196616 | tf_op jit(solution)/shard_map/ppermute | solution.py:588
  21.4 0.0 collective-permute-done.2.refs_2_
  21.4 0.0 collective-permute-done.3.refs_3_
  21.4 0.2 chunk.8
  21.6 3.9 %collective-permute-start.7 = (f32[4,272,256]{2,1,0:T(8,128)S(1)}, f32[4,272,256]{2,1,0:T(8,128)S(1)}, u32[]{:S(2)}, u32[]{:S(2)}) collective-permute-start(f32[4,272,256]{2,1,0:T(8,128)S(1)} %get-tuple-element.80.late), channel_id=1, source_target_pairs={{12,8},{13,9},{14,10},{15,11},{28,24},{29,25},{30,26},{31,27}} | collective-permute-start | bytes 3342344 | tf_op jit(solution)/shard_map/ppermute | solution.py:578
  25.5 0.0 collective-permute-done.1.refs_3_
  25.6 0.7 %collective-permute-start.4 = (f32[4,16,256]{2,1,0:T(8,128)S(1)}, f32[4,16,256]{2,1,0:T(8,128)S(1)}, u32[]{:S(2)}, u32[]{:S(2)}) collective-permute-start(f32[4,16,256]{2,1,0:T(8,128)S(1)} %get-tuple-element.78.refs_6_), channel_id=1, source_target_pairs={{0,4},{4,8},{1,5},{5,9},{2,6},{6,10},{3,7},{7,11},{16,20},{20,24},... | collective-permute-start | bytes 196616 | tf_op jit(solution)/shard_map/ppermute | solution.py:588
  26.3 3.7 %spread_close.1 = (bf16[6,272,256]{2,1,0:T(8,128)(2,1)S(1)}, bf16[6,272,256]{2,1,0:T(8,128)(2,1)S(1)}, f32[8,16,256]{2,1,0:T(8,128)S(1)}, f32[4,16,256]{2,1,0:T(8,128)S(1)}) custom-call(bf16[8,1024,256]{2,1,0:T(8,128)(2,1)S(1)} %get-tuple-element.51.weight.refs_0_, f32[8,16,256]{2,1,0:T(8,128)S(1)} %get-tuple-element.52.base.refs_1_, ...), custom_call_target="tpu_custom_call" | custom-call | tf_op jit(solution)/shard_map/spread_close/pallas_call | solution.py:444
  30.0 0.0 collective-permute-done.4.entering.refs_2_.refs_4_
  30.0 0.7 %collective-permute-start.5 = (f32[4,16,256]{2,1,0:T(8,128)S(1)}, f32[4,16,256]{2,1,0:T(8,128)S(1)}, u32[]{:S(2)}, u32[]{:S(2)}) collective-permute-start(f32[4,16,256]{2,1,0:T(8,128)S(1)} %answer.1), channel_id=1, source_target_pairs={{8,4},{9,5},{10,6},{11,7},{24,20},{25,21},{26,22},{27,23}} | collective-permute-start | bytes 196616 | tf_op jit(solution)/shard_map/ppermute | solution.py:564
  30.8 0.0 collective-permute-done.5.refs_3_
  30.8 1.3 %collective-permute-start.6 = (f32[4,16,256]{2,1,0:T(8,128)S(1)}, f32[4,16,256]{2,1,0:T(8,128)S(1)}, u32[]{:S(2)}, u32[]{:S(2)}) collective-permute-start(f32[4,16,256]{2,1,0:T(8,128)S(1)} %get-tuple-element.79.refs_4_.refs_6_), channel_id=1, source_target_pairs={{4,8},{8,12},{5,9},{9,13},{6,10},{10,14},{7,11},{11,15},{20,24},{2... | collective-permute-start | bytes 196616 | tf_op jit(solution)/shard_map/ppermute | solution.py:588
  32.2 0.0 collective-permute-done.7.refs_3_
  32.2 0.3 chunk.12
  32.4 4.3 %collective-permute-done.6.refs_4_ = f32[4,16,256]{2,1,0:T(8,128)S(1)} collective-permute-done((f32[4,16,256]{2,1,0:T(8,128)S(1)}, f32[4,16,256]{2,1,0:T(8,128)S(1)}, u32[]{:S(2)}, u32[]{:S(2)}) %collective-permute-start.6) | collective-permute-done | bytes 65568 | tf_op jit(solution)/shard_map/ppermute | solution.py:588
  36.8 1.3 %collective-permute-start.8 = (f32[4,16,256]{2,1,0:T(8,128)S(1)}, f32[4,16,256]{2,1,0:T(8,128)S(1)}, u32[]{:S(2)}, u32[]{:S(2)}) collective-permute-start(f32[4,16,256]{2,1,0:T(8,128)S(1)} %finish_leaving.3), channel_id=1, source_target_pairs={{8,12},{9,13},{10,14},{11,15},{24,28},{25,29},{26,30},{27,31}} | collective-permute-start | bytes 196616 | tf_op jit(solution)/shard_map/ppermute | solution.py:588
  38.1 1.4 %finish_state.6.refs_3_ = f32[8,16,256]{2,1,0:T(8,128)S(1)} custom-call(bf16[32,272,256]{2,1,0:T(8,128)(2,1)S(1)} %get-tuple-element.67.open_high.refs_0_, bf16[32,272,256]{2,1,0:T(8,128)(2,1)S(1)} %get-tuple-element.68.open_low.refs_1_, bf16[6,272,256]{2,1,0:T(8,128)(2,1)S(1)} %get-tuple-element.70.refs_2_, ...), custom_call_target="tpu_custom_call" | custom-call | tf_op jit(solution)/shard_map/finish_state/pallas_call | solution.py:508
  39.5 4.8 %chunk.13 = (f32[8,16,256]{2,1,0:T(8,128)S(1)}, f32[4,16,256]{2,1,0:T(8,128)}) custom-call(bf16[8,1024,256]{2,1,0:T(8,128)(2,1)S(1)} %get-tuple-element.51.weight.refs_0_, f32[8,16,256]{2,1,0:T(8,128)S(1)} %get-tuple-element.52.base.refs_1_, f32[3,272,256]{2,1,0:T(8,128)S(1)} %collective-permute-done.refs_2_.soon, f32[8,16,256]{2,1,0:T(8,128)S(1)} %finish_state.6.refs_3_), custom_call_target="tpu_custom_call" | custom-call | tf_op jit(solution)/shard_map/chunk/pallas_call | solution.py:321
  44.3 0.2 collective-permute-done.8.refs_4_
  44.5 2.1 %finish_state.7 = f32[8,16,256]{2,1,0:T(8,128)} custom-call(bf16[32,272,256]{2,1,0:T(8,128)(2,1)S(1)} %get-tuple-element.67.open_high.refs_0_, bf16[32,272,256]{2,1,0:T(8,128)(2,1)S(1)} %get-tuple-element.68.open_low.refs_1_, bf16[6,272,256]{2,1,0:T(8,128)(2,1)S(1)} %get-tuple-element.70.refs_2_, bf16[6,272,256]{2,1,0:T(8,128)(2,1)S(1)} %get-tuple-element.71.refs_3_, ...), custom_call_target="tpu_custom_call" | custom-call | tf_op jit(solution)/shard_map/finish_state/pallas_call | solution.py:508
  (10 shorter events, 0.2 us)
Async XLA Ops:
  3.7 17.0 %collective-permute-start = (f32[3,272,256]{2,1,0:T(8,128)S(1)}, f32[3,272,256]{2,1,0:T(8,128)S(1)}, u32[]{:S(2)}, u32[]{:S(2)}) collective-permute-start(f32[3,272,256]{2,1,0:T(8,128)S(1)} %get-tuple-element.55.soon), channel_id=1, source_target_pairs={{4,0},{12,8},{5,1},{13,9},{6,2},{14,10},{7,3},{15,11},{20,16},{28,... | collective-permute-start | bytes 2506760 | tf_op jit(solution)/shard_map/ppermute | solution.py:553
  6.3 15.1 %collective-permute-start.2 = (f32[3,272,256]{2,1,0:T(8,128)S(1)}, f32[3,272,256]{2,1,0:T(8,128)S(1)}, u32[]{:S(2)}, u32[]{:S(2)}) collective-permute-start(f32[3,272,256]{2,1,0:T(8,128)S(1)} %get-tuple-element.55.soon), channel_id=1, source_target_pairs={{8,4},{9,5},{10,6},{11,7},{24,20},{25,21},{26,22},{27,23}} | collective-permute-start | bytes 2506760 | tf_op jit(solution)/shard_map/ppermute | solution.py:552
  9.1 16.5 %collective-permute-start.1 = (f32[4,272,256]{2,1,0:T(8,128)S(1)}, f32[4,272,256]{2,1,0:T(8,128)S(1)}, u32[]{:S(2)}, u32[]{:S(2)}) collective-permute-start(f32[4,272,256]{2,1,0:T(8,128)S(1)} %respond.1), channel_id=1, source_target_pairs={{4,0},{5,1},{6,2},{7,3},{20,16},{21,17},{22,18},{23,19}} | collective-permute-start | bytes 3342344 | tf_op jit(solution)/shard_map/ppermute | solution.py:554
  20.7 0.7 %collective-permute-start.3 = (f32[4,16,256]{2,1,0:T(8,128)S(1)}, f32[4,16,256]{2,1,0:T(8,128)S(1)}, u32[]{:S(2)}, u32[]{:S(2)}) collective-permute-start(f32[4,16,256]{2,1,0:T(8,128)S(1)} %get-tuple-element.60.refs_5_.refs_4_), channel_id=1, source_target_pairs={{0,4},{1,5},{2,6},{3,7},{16,20},{17,21},{18,22},{19,23}} | collective-permute-start | bytes 196616 | tf_op jit(solution)/shard_map/ppermute | solution.py:588
  21.6 10.5 %collective-permute-start.7 = (f32[4,272,256]{2,1,0:T(8,128)S(1)}, f32[4,272,256]{2,1,0:T(8,128)S(1)}, u32[]{:S(2)}, u32[]{:S(2)}) collective-permute-start(f32[4,272,256]{2,1,0:T(8,128)S(1)} %get-tuple-element.80.late), channel_id=1, source_target_pairs={{12,8},{13,9},{14,10},{15,11},{28,24},{29,25},{30,26},{31,27}} | collective-permute-start | bytes 3342344 | tf_op jit(solution)/shard_map/ppermute | solution.py:578
  25.6 4.4 %collective-permute-start.4 = (f32[4,16,256]{2,1,0:T(8,128)S(1)}, f32[4,16,256]{2,1,0:T(8,128)S(1)}, u32[]{:S(2)}, u32[]{:S(2)}) collective-permute-start(f32[4,16,256]{2,1,0:T(8,128)S(1)} %get-tuple-element.78.refs_6_), channel_id=1, source_target_pairs={{0,4},{4,8},{1,5},{5,9},{2,6},{6,10},{3,7},{7,11},{16,20},{20,24},... | collective-permute-start | bytes 196616 | tf_op jit(solution)/shard_map/ppermute | solution.py:588
  30.0 0.7 %collective-permute-start.5 = (f32[4,16,256]{2,1,0:T(8,128)S(1)}, f32[4,16,256]{2,1,0:T(8,128)S(1)}, u32[]{:S(2)}, u32[]{:S(2)}) collective-permute-start(f32[4,16,256]{2,1,0:T(8,128)S(1)} %answer.1), channel_id=1, source_target_pairs={{8,4},{9,5},{10,6},{11,7},{24,20},{25,21},{26,22},{27,23}} | collective-permute-start | bytes 196616 | tf_op jit(solution)/shard_map/ppermute | solution.py:564
  30.8 6.0 %collective-permute-start.6 = (f32[4,16,256]{2,1,0:T(8,128)S(1)}, f32[4,16,256]{2,1,0:T(8,128)S(1)}, u32[]{:S(2)}, u32[]{:S(2)}) collective-permute-start(f32[4,16,256]{2,1,0:T(8,128)S(1)} %get-tuple-element.79.refs_4_.refs_6_), channel_id=1, source_target_pairs={{4,8},{8,12},{5,9},{9,13},{6,10},{10,14},{7,11},{11,15},{20,24},{2... | collective-permute-start | bytes 196616 | tf_op jit(solution)/shard_map/ppermute | solution.py:588
  36.8 7.7 %collective-permute-start.8 = (f32[4,16,256]{2,1,0:T(8,128)S(1)}, f32[4,16,256]{2,1,0:T(8,128)S(1)}, u32[]{:S(2)}, u32[]{:S(2)}) collective-permute-start(f32[4,16,256]{2,1,0:T(8,128)S(1)} %finish_leaving.3), channel_id=1, source_target_pairs={{8,12},{9,13},{10,14},{11,15},{24,28},{25,29},{26,30},{27,31}} | collective-permute-start | bytes 196616 | tf_op jit(solution)/shard_map/ppermute | solution.py:588

commit v12 on v11

--- a/solution.py
+++ b/solution.py
@@ -225,20 +225,29 @@
     return soon[j] if j < SOON else late[j - SOON]
 
 
+def carry_terms(soon, late, past, first, last):
+    phases = soon.shape[2]
+    columns = soon.shape[1] - phases
+    above = {n: kept_at(soon, late, n - 1)[phases:] for n in range(max(first, 1), last + 1)}
+
+    def add(j):
+        pairs = [(n, n - j) for n in above if n - j in past]
+        held = whole(kept_at(soon, late, j)[0:phases])
+        for (n, _), term in zip(pairs, apply_each([past[m] for _, m in pairs], held, columns)):
+            above[n] += term
+        return held
+
+    return above, [functools.partial(add, j) for j in range(last)]
+
+
 def carried(soon, late, past, first, last):
-    phases = soon.shape[2]
-    above = {n: kept_at(soon, late, n - 1)[phases:] for n in range(max(first, 1), last + 1)}
-    columns = soon.shape[1] - phases
-    for j in range(last) if past else ():
-        pairs = [(n, n - j) for n in above if n - j in past]
-        if pairs:
-            terms = [past[m] for _, m in pairs]
-            for (n, _), term in zip(pairs, apply_each(terms, whole(kept_at(soon, late, j)[0:phases]), columns)):
-                above[n] += term
+    above, calls = carry_terms(soon, late, past, first, last)
+    for call in calls:
+        call()
     return above
 
 
-def wave(first, weight, base, now, above, feedback, due, emit):
+def wave(first, weight, base, now, above, feedback, due, emit, chores):
     levels, _, phases = base.shape
     for turn in range(levels + 2 * (CHUNK - 1)):
         for k in range(CHUNK):
@@ -258,6 +267,8 @@
             if i == levels - 1:
                 for later in range(n, first + CHUNK):
                     above[later] += apply([(now[i, n], feedback[later - n])])
+        if chores and levels - 2 - turn < len(chores):
+            chores.pop(0)()
 
 
 def edge_level(levels, k):
@@ -279,17 +290,25 @@
     @pl.when(among(places))
     def _():
         zero = jnp.zeros((columns, phases), F32)
-        above, feedback = {first + k: zero for k in range(CHUNK)}, []
+        above, feedback, chores = {first + k: zero for k in range(CHUNK)}, {}, []
         if part != "early":
             soon = given["soon"]
-            feedback = [whole(soon[j, 0:phases]) for j in range(SOON)]
-            if not first:
-                above = carried(soon, None, {}, first, first + CHUNK - 1)
-            elif "late" in given:
+
+            def hold(j, call):
+                feedback[j] = call()
+
+            if first and "late" in given:
                 past = {n + 1: stack(given["earlier"][n]) for n in range(first)}
-                above = carried(soon, given["late"], past, first, first + CHUNK - 1)
-            elif "returned" in given:
-                above = {first + k: given["returned"][k] for k in range(CHUNK)}
+                above, calls = carry_terms(soon, given["late"], past, first, first + CHUNK - 1)
+            else:
+                if not first:
+                    above, _ = carry_terms(soon, None, {}, first, first + CHUNK - 1)
+                elif "returned" in given:
+                    above = {first + k: given["returned"][k] for k in range(CHUNK)}
+                calls = [lambda j=j: whole(soon[j, 0:phases]) for j in range(SOON)]
+            chores = [functools.partial(hold, j, call) for j, call in enumerate(calls)]
+            while part == "late" and chores:
+                chores.pop(0)()
 
         now = {}
         if part == "late":
@@ -312,7 +331,7 @@
             if i == (edge_level(levels, k) if part == "early" else levels - 1):
                 leaving[k] = value
 
-        wave(first, weight, base, now, above, feedback, due, emit)
+        wave(first, weight, base, now, above, feedback, due, emit, chores)
 
 
 def run_chunk(chunk, places, given, part="all"):
@@ -579,6 +598,8 @@
             first_late = late if odd else late_top
             given_first = {**own, "late": first_late, "earlier": earlier, "state": state, "leaving": leaving}
             state, leaving = run_chunk(1, [0], given_first)
+        if step in ready and step > 1:
+            state = finish_state(step, ways, entering, state, False)
         if returned is not None:
             given_rest = {**own, "soon": soon_odd, "returned": returned, "edge": edge, "state": state, "leaving": leaving}
             state, leaving = run_chunk(1, [place], given_rest, "late")
@@ -594,7 +615,8 @@
         if place in ready:
             state = finish_state(place, ways, came, state, step == count)
         if step in ready:
-            state = finish_state(step, ways, came, state, False)
+            if step == 1:
+                state = finish_state(step, ways, came, state, False)
             extra = {} if step == top else {"late": late_top if step == top - 1 else late, "earlier": leaving}
             state, parted = run_chunk(1, [step], {**own, **extra, "state": state})
     return state[:, :given] if columns != given else state

time: 46.8 us -> 46.6 us (level)
  transfers between devices with their start and end apart: 9 -> 9, of which waited for: 2 -> 1; matrix products, arithmetic and copies ran while one was open for 0% -> 0% of each run, Pallas kernels for 50% -> 51%
where the time goes in v12:
time: 46.6 us; the launch traced here: 46.4 us
  Pallas kernels  29.3 us (63%)
  starting transfers between devices  12.5 us (27%)
  waiting for transfers between devices  4.37 us (9%)
    pallas_call x1, Pallas kernels, spread_open(): pl.pallas_call(functools.partial(spread_open_kernel, tuple(places)), out_...  10.9 us
    pallas_call x7, Pallas kernels, run_chunk(): pl.pallas_call(functools.partial(chunk_kernel, chunk, tuple(places), part...  5.37 us
    ppermute x4, waiting for transfers between devices, local(): entering = lax.ppermute(leaving, 'lvl', pairs) if pairs else None  4.36 us
    ppermute x4, starting transfers between devices, local(): entering = lax.ppermute(leaving, 'lvl', pairs) if pairs else None  3.9 us
    ppermute x1, starting transfers between devices, local(): lax.ppermute(top_sent, 'lvl', [(top, top - 1)])  3.88 us
    pallas_call x1, Pallas kernels, spread_close(): pl.pallas_call(functools.partial(spread_close_kernel, tuple(places)), out...  3.73 us
    pallas_call x1, Pallas kernels, prepare(): pl.pallas_call(prepare_kernel, out_shape=operators(SOON, columns, phases)...  3.65 us
    pallas_call x4, Pallas kernels, finish_state(): pl.pallas_call(functools.partial(finish_state_kernel, place), out_shape=(...  3.57 us
  transfers between devices with their start and end apart: 9, of which 1 were waited for; matrix products, arithmetic and copies ran while one was open for 0% of the time, Pallas kernels for 51%

profile of v12, /device:TPU:11, one launch (start us, length us, event | category | flops | bytes accessed | tf_op | source)
XLA Modules:
  0.0 46.4 jit_solution(1427123966405830254)
XLA Ops:
  0.0 3.7 %prepare.1 = (bf16[3,1024,256]{2,1,0:T(8,128)(2,1)S(1)}, f32[3,16,256]{2,1,0:T(8,128)S(1)}, bf16[3,272,256]{2,1,0:T(8,128)(2,1)S(1)}, bf16[3,272,256]{2,1,0:T(8,...) custom-call(f32[8,256,256]{2,1,0:T(8,128)} %inv_far.1, ...), custom_call_target="tpu_custom_call" | custom-call | tf_op jit(solution)/shard_map/prepare/pallas_call | solution.py:161
  3.7 2.6 %collective-permute-start = (f32[3,272,256]{2,1,0:T(8,128)S(1)}, f32[3,272,256]{2,1,0:T(8,128)S(1)}, u32[]{:S(2)}, u32[]{:S(2)}) collective-permute-start(f32[3,272,256]{2,1,0:T(8,128)S(1)} %get-tuple-element.55.soon), channel_id=1, source_target_pairs={{4,0},{12,8},{5,1},{13,9},{6,2},{14,10},{7,3},{15,11},{20,16},{28,... | collective-permute-start | bytes 2506760 | tf_op jit(solution)/shard_map/ppermute | solution.py:572
  6.3 0.7 %collective-permute-start.2 = (f32[3,272,256]{2,1,0:T(8,128)S(1)}, f32[3,272,256]{2,1,0:T(8,128)S(1)}, u32[]{:S(2)}, u32[]{:S(2)}) collective-permute-start(f32[3,272,256]{2,1,0:T(8,128)S(1)} %get-tuple-element.55.soon), channel_id=1, source_target_pairs={{8,4},{9,5},{10,6},{11,7},{24,20},{25,21},{26,22},{27,23}} | collective-permute-start | bytes 2506760 | tf_op jit(solution)/shard_map/ppermute | solution.py:571
  7.0 2.0 %prepare_rest.1 = (bf16[8,1024,256]{2,1,0:T(8,128)(2,1)S(1)}, f32[8,16,256]{2,1,0:T(8,128)S(1)}) custom-call(bf16[3,1024,256]{2,1,0:T(8,128)(2,1)S(1)} %get-tuple-element.45.weight_soon, f32[3,16,256]{2,1,0:T(8,128)S(1)} %get-tuple-element.46.base_soon, f32[8,256,256]{2,1,0:T(8,128)S(1)} %get-tuple-element.47.inv, ...), custom_call_target="tpu_custom_call" | custom-call | tf_op jit(solution)/shard_map/prepare_rest/pallas_call | solution.py:174
  9.1 0.7 %collective-permute-start.1 = (f32[4,272,256]{2,1,0:T(8,128)S(1)}, f32[4,272,256]{2,1,0:T(8,128)S(1)}, u32[]{:S(2)}, u32[]{:S(2)}) collective-permute-start(f32[4,272,256]{2,1,0:T(8,128)S(1)} %respond.1), channel_id=1, source_target_pairs={{4,0},{5,1},{6,2},{7,3},{20,16},{21,17},{22,18},{23,19}} | collective-permute-start | bytes 3342344 | tf_op jit(solution)/shard_map/ppermute | solution.py:573
  9.8 10.9 %spread_open.1 = (bf16[32,272,256]{2,1,0:T(8,128)(2,1)S(1)}, bf16[32,272,256]{2,1,0:T(8,128)(2,1)S(1)}, f32[4,272,256]{2,1,0:T(8,128)S(1)}) custom-call(bf16[8,1024,256]{2,1,0:T(8,128)(2,1)S(1)} %get-tuple-element.51.weight.refs_0_, f32[8,16,256]{2,1,0:T(8,128)S(1)} %get-tuple-element.52.base.refs_1_), custom_call_target="tpu_custom_call" | custom-call | tf_op jit(solution)/shard_map/spread_open/pallas_call | solution.py:449
  20.7 0.0 collective-permute-done.refs_2_.soon
  20.7 0.7 %collective-permute-start.3 = (f32[4,16,256]{2,1,0:T(8,128)S(1)}, f32[4,16,256]{2,1,0:T(8,128)S(1)}, u32[]{:S(2)}, u32[]{:S(2)}) collective-permute-start(f32[4,16,256]{2,1,0:T(8,128)S(1)} %get-tuple-element.60.refs_5_.refs_4_), channel_id=1, source_target_pairs={{0,4},{1,5},{2,6},{3,7},{16,20},{17,21},{18,22},{19,23}} | collective-permute-start | bytes 196616 | tf_op jit(solution)/shard_map/ppermute | solution.py:609
  21.4 0.0 collective-permute-done.2.refs_2_
  21.4 0.0 collective-permute-done.3.refs_3_
  21.4 0.2 chunk.8
  21.6 3.9 %collective-permute-start.7 = (f32[4,272,256]{2,1,0:T(8,128)S(1)}, f32[4,272,256]{2,1,0:T(8,128)S(1)}, u32[]{:S(2)}, u32[]{:S(2)}) collective-permute-start(f32[4,272,256]{2,1,0:T(8,128)S(1)} %get-tuple-element.80.late), channel_id=1, source_target_pairs={{12,8},{13,9},{14,10},{15,11},{28,24},{29,25},{30,26},{31,27}} | collective-permute-start | bytes 3342344 | tf_op jit(solution)/shard_map/ppermute | solution.py:597
  25.5 0.0 collective-permute-done.1.refs_3_
  25.6 0.7 %collective-permute-start.4 = (f32[4,16,256]{2,1,0:T(8,128)S(1)}, f32[4,16,256]{2,1,0:T(8,128)S(1)}, u32[]{:S(2)}, u32[]{:S(2)}) collective-permute-start(f32[4,16,256]{2,1,0:T(8,128)S(1)} %get-tuple-element.78.refs_6_), channel_id=1, source_target_pairs={{0,4},{4,8},{1,5},{5,9},{2,6},{6,10},{3,7},{7,11},{16,20},{20,24},... | collective-permute-start | bytes 196616 | tf_op jit(solution)/shard_map/ppermute | solution.py:609
  26.3 3.7 %spread_close.1 = (bf16[6,272,256]{2,1,0:T(8,128)(2,1)S(1)}, bf16[6,272,256]{2,1,0:T(8,128)(2,1)S(1)}, f32[8,16,256]{2,1,0:T(8,128)S(1)}, f32[4,16,256]{2,1,0:T(8,128)S(1)}) custom-call(bf16[8,1024,256]{2,1,0:T(8,128)(2,1)S(1)} %get-tuple-element.51.weight.refs_0_, f32[8,16,256]{2,1,0:T(8,128)S(1)} %get-tuple-element.52.base.refs_1_, ...), custom_call_target="tpu_custom_call" | custom-call | tf_op jit(solution)/shard_map/spread_close/pallas_call | solution.py:463
  30.0 0.0 collective-permute-done.4.entering.refs_2_.refs_4_
  30.0 0.7 %collective-permute-start.5 = (f32[4,16,256]{2,1,0:T(8,128)S(1)}, f32[4,16,256]{2,1,0:T(8,128)S(1)}, u32[]{:S(2)}, u32[]{:S(2)}) collective-permute-start(f32[4,16,256]{2,1,0:T(8,128)S(1)} %answer.1), channel_id=1, source_target_pairs={{8,4},{9,5},{10,6},{11,7},{24,20},{25,21},{26,22},{27,23}} | collective-permute-start | bytes 196616 | tf_op jit(solution)/shard_map/ppermute | solution.py:583
  30.8 0.0 collective-permute-done.5.refs_3_
  30.9 1.3 %collective-permute-start.6 = (f32[4,16,256]{2,1,0:T(8,128)S(1)}, f32[4,16,256]{2,1,0:T(8,128)S(1)}, u32[]{:S(2)}, u32[]{:S(2)}) collective-permute-start(f32[4,16,256]{2,1,0:T(8,128)S(1)} %get-tuple-element.79.refs_4_.refs_6_), channel_id=1, source_target_pairs={{4,8},{8,12},{5,9},{9,13},{6,10},{10,14},{7,11},{11,15},{20,24},{2... | collective-permute-start | bytes 196616 | tf_op jit(solution)/shard_map/ppermute | solution.py:609
  32.2 0.0 collective-permute-done.7.refs_3_
  32.2 0.3 chunk.12
  32.4 4.3 %collective-permute-done.6.refs_4_ = f32[4,16,256]{2,1,0:T(8,128)S(1)} collective-permute-done((f32[4,16,256]{2,1,0:T(8,128)S(1)}, f32[4,16,256]{2,1,0:T(8,128)S(1)}, u32[]{:S(2)}, u32[]{:S(2)}) %collective-permute-start.6) | collective-permute-done | bytes 65568 | tf_op jit(solution)/shard_map/ppermute | solution.py:609
  36.8 1.3 %collective-permute-start.8 = (f32[4,16,256]{2,1,0:T(8,128)S(1)}, f32[4,16,256]{2,1,0:T(8,128)S(1)}, u32[]{:S(2)}, u32[]{:S(2)}) collective-permute-start(f32[4,16,256]{2,1,0:T(8,128)S(1)} %finish_leaving.3), channel_id=1, source_target_pairs={{8,12},{9,13},{10,14},{11,15},{24,28},{25,29},{26,30},{27,31}} | collective-permute-start | bytes 196616 | tf_op jit(solution)/shard_map/ppermute | solution.py:609
  38.1 1.4 %finish_state.5.refs_5_ = f32[8,16,256]{2,1,0:T(8,128)S(1)} custom-call(bf16[32,272,256]{2,1,0:T(8,128)(2,1)S(1)} %get-tuple-element.67.open_high.refs_0_, bf16[32,272,256]{2,1,0:T(8,128)(2,1)S(1)} %get-tuple-element.68.open_low.refs_1_, bf16[6,272,256]{2,1,0:T(8,128)(2,1)S(1)} %get-tuple-element.70.refs_2_, ...), custom_call_target="tpu_custom_call" | custom-call | tf_op jit(solution)/shard_map/finish_state/pallas_call | solution.py:527
  39.5 4.8 %chunk.13 = (f32[8,16,256]{2,1,0:T(8,128)S(1)}, f32[4,16,256]{2,1,0:T(8,128)}) custom-call(bf16[8,1024,256]{2,1,0:T(8,128)(2,1)S(1)} %get-tuple-element.51.weight.refs_0_, f32[8,16,256]{2,1,0:T(8,128)S(1)} %get-tuple-element.52.base.refs_1_, f32[3,272,256]{2,1,0:T(8,128)S(1)} %collective-permute-done.refs_2_.soon, f32[8,16,256]{2,1,0:T(8,128)S(1)} %finish_state.6.refs_3_), custom_call_target="tpu_custom_call" | custom-call | tf_op jit(solution)/shard_map/chunk/pallas_call | solution.py:340
  44.3 0.0 collective-permute-done.8.refs_4_
  44.3 2.1 %finish_state.7 = f32[8,16,256]{2,1,0:T(8,128)} custom-call(bf16[32,272,256]{2,1,0:T(8,128)(2,1)S(1)} %get-tuple-element.67.open_high.refs_0_, bf16[32,272,256]{2,1,0:T(8,128)(2,1)S(1)} %get-tuple-element.68.open_low.refs_1_, bf16[6,272,256]{2,1,0:T(8,128)(2,1)S(1)} %get-tuple-element.70.refs_2_, bf16[6,272,256]{2,1,0:T(8,128)(2,1)S(1)} %get-tuple-element.71.refs_3_, ...), custom_call_target="tpu_custom_call" | custom-call | tf_op jit(solution)/shard_map/finish_state/pallas_call | solution.py:527
  (10 shorter events, 0.2 us)
Async XLA Ops:
  3.7 17.0 %collective-permute-start = (f32[3,272,256]{2,1,0:T(8,128)S(1)}, f32[3,272,256]{2,1,0:T(8,128)S(1)}, u32[]{:S(2)}, u32[]{:S(2)}) collective-permute-start(f32[3,272,256]{2,1,0:T(8,128)S(1)} %get-tuple-element.55.soon), channel_id=1, source_target_pairs={{4,0},{12,8},{5,1},{13,9},{6,2},{14,10},{7,3},{15,11},{20,16},{28,... | collective-permute-start | bytes 2506760 | tf_op jit(solution)/shard_map/ppermute | solution.py:572
  6.3 15.1 %collective-permute-start.2 = (f32[3,272,256]{2,1,0:T(8,128)S(1)}, f32[3,272,256]{2,1,0:T(8,128)S(1)}, u32[]{:S(2)}, u32[]{:S(2)}) collective-permute-start(f32[3,272,256]{2,1,0:T(8,128)S(1)} %get-tuple-element.55.soon), channel_id=1, source_target_pairs={{8,4},{9,5},{10,6},{11,7},{24,20},{25,21},{26,22},{27,23}} | collective-permute-start | bytes 2506760 | tf_op jit(solution)/shard_map/ppermute | solution.py:571
  9.1 16.5 %collective-permute-start.1 = (f32[4,272,256]{2,1,0:T(8,128)S(1)}, f32[4,272,256]{2,1,0:T(8,128)S(1)}, u32[]{:S(2)}, u32[]{:S(2)}) collective-permute-start(f32[4,272,256]{2,1,0:T(8,128)S(1)} %respond.1), channel_id=1, source_target_pairs={{4,0},{5,1},{6,2},{7,3},{20,16},{21,17},{22,18},{23,19}} | collective-permute-start | bytes 3342344 | tf_op jit(solution)/shard_map/ppermute | solution.py:573
  20.7 0.7 %collective-permute-start.3 = (f32[4,16,256]{2,1,0:T(8,128)S(1)}, f32[4,16,256]{2,1,0:T(8,128)S(1)}, u32[]{:S(2)}, u32[]{:S(2)}) collective-permute-start(f32[4,16,256]{2,1,0:T(8,128)S(1)} %get-tuple-element.60.refs_5_.refs_4_), channel_id=1, source_target_pairs={{0,4},{1,5},{2,6},{3,7},{16,20},{17,21},{18,22},{19,23}} | collective-permute-start | bytes 196616 | tf_op jit(solution)/shard_map/ppermute | solution.py:609
  21.6 10.5 %collective-permute-start.7 = (f32[4,272,256]{2,1,0:T(8,128)S(1)}, f32[4,272,256]{2,1,0:T(8,128)S(1)}, u32[]{:S(2)}, u32[]{:S(2)}) collective-permute-start(f32[4,272,256]{2,1,0:T(8,128)S(1)} %get-tuple-element.80.late), channel_id=1, source_target_pairs={{12,8},{13,9},{14,10},{15,11},{28,24},{29,25},{30,26},{31,27}} | collective-permute-start | bytes 3342344 | tf_op jit(solution)/shard_map/ppermute | solution.py:597
  25.6 4.4 %collective-permute-start.4 = (f32[4,16,256]{2,1,0:T(8,128)S(1)}, f32[4,16,256]{2,1,0:T(8,128)S(1)}, u32[]{:S(2)}, u32[]{:S(2)}) collective-permute-start(f32[4,16,256]{2,1,0:T(8,128)S(1)} %get-tuple-element.78.refs_6_), channel_id=1, source_target_pairs={{0,4},{4,8},{1,5},{5,9},{2,6},{6,10},{3,7},{7,11},{16,20},{20,24},... | collective-permute-start | bytes 196616 | tf_op jit(solution)/shard_map/ppermute | solution.py:609
  30.0 0.8 %collective-permute-start.5 = (f32[4,16,256]{2,1,0:T(8,128)S(1)}, f32[4,16,256]{2,1,0:T(8,128)S(1)}, u32[]{:S(2)}, u32[]{:S(2)}) collective-permute-start(f32[4,16,256]{2,1,0:T(8,128)S(1)} %answer.1), channel_id=1, source_target_pairs={{8,4},{9,5},{10,6},{11,7},{24,20},{25,21},{26,22},{27,23}} | collective-permute-start | bytes 196616 | tf_op jit(solution)/shard_map/ppermute | solution.py:583
  30.9 5.9 %collective-permute-start.6 = (f32[4,16,256]{2,1,0:T(8,128)S(1)}, f32[4,16,256]{2,1,0:T(8,128)S(1)}, u32[]{:S(2)}, u32[]{:S(2)}) collective-permute-start(f32[4,16,256]{2,1,0:T(8,128)S(1)} %get-tuple-element.79.refs_4_.refs_6_), channel_id=1, source_target_pairs={{4,8},{8,12},{5,9},{9,13},{6,10},{10,14},{7,11},{11,15},{20,24},{2... | collective-permute-start | bytes 196616 | tf_op jit(solution)/shard_map/ppermute | solution.py:609
  36.8 7.5 %collective-permute-start.8 = (f32[4,16,256]{2,1,0:T(8,128)S(1)}, f32[4,16,256]{2,1,0:T(8,128)S(1)}, u32[]{:S(2)}, u32[]{:S(2)}) collective-permute-start(f32[4,16,256]{2,1,0:T(8,128)S(1)} %finish_leaving.3), channel_id=1, source_target_pairs={{8,12},{9,13},{10,14},{11,15},{24,28},{25,29},{26,30},{27,31}} | collective-permute-start | bytes 196616 | tf_op jit(solution)/shard_map/ppermute | solution.py:609

commit v13 on v12

--- a/solution.py
+++ b/solution.py
@@ -80,12 +80,8 @@
             continue
         store(d, from_below(d))
 
-        def level(k, _, d=d):
-            i = d - k
+        for i in range(d - 1, 0, -1):
             store(i, from_below(i) + from_above(i))
-            return 0
-
-        lax.fori_loop(1, d, level, 0)
         kept[d - first, 0:phases], kept[d - first, phases:rows] = store(0, from_above(0))
 
 
@@ -258,13 +254,13 @@
             terms = []
             if (i - 1, n) in now:
                 terms.append((now[i - 1, n], weight[i, 0 : 2 * phases]))
-            if n > 1:
+            if n > 1 and not (i == levels - 1 and above is None):
                 over = stack(above[n - 1]) if i == levels - 1 else now[i + 1, n - 1]
                 terms.append((over, weight[i, 2 * phases : 4 * phases]))
             value = base[i] + apply(terms) if terms else base[i]
             now[i, n] = stack(value)
             emit(i, k, value)
-            if i == levels - 1:
+            if i == levels - 1 and above is not None:
                 for later in range(n, first + CHUNK):
                     above[later] += apply([(now[i, n], feedback[later - n])])
         if chores and levels - 2 - turn < len(chores):
@@ -277,7 +273,8 @@
 
 def chunk_kernel(chunk, places, part, names, *refs):
     given = dict(zip(names, refs))
-    new_state, leaving = refs[len(names) :]
+    new_state, *leaving = refs[len(names) :]
+    leaving = leaving[0] if leaving else None
     weight, base = given["weight"], given["base"]
     levels, columns, phases = base.shape
     first = chunk * CHUNK
@@ -285,13 +282,16 @@
     @pl.when(jnp.logical_not(among(places)))
     def _():
         for name, target in (("state", new_state), ("leaving", leaving)):
-            target[...] = given[name][...] if name in given else jnp.zeros_like(target)
+            if target is not None:
+                target[...] = given[name][...] if name in given else jnp.zeros_like(target)
 
     @pl.when(among(places))
     def _():
         zero = jnp.zeros((columns, phases), F32)
         above, feedback, chores = {first + k: zero for k in range(CHUNK)}, {}, []
-        if part != "early":
+        if "soon" not in given and part != "early":
+            above = None
+        elif part != "early":
             soon = given["soon"]
 
             def hold(j, call):
@@ -328,20 +328,20 @@
         def emit(i, k, value):
             if k == CHUNK - 1:
                 new_state[i] = value
-            if i == (edge_level(levels, k) if part == "early" else levels - 1):
+            if leaving is not None and i == (edge_level(levels, k) if part == "early" else levels - 1):
                 leaving[k] = value
 
         wave(first, weight, base, now, above, feedback, due, emit, chores)
 
 
-def run_chunk(chunk, places, given, part="all"):
+def run_chunk(chunk, places, given, part="all", sends=True):
     given = {name: x for name, x in given.items() if x is not None}
     levels, columns, phases = given["base"].shape
     return pl.pallas_call(
         functools.partial(chunk_kernel, chunk, tuple(places), part, tuple(given)),
-        out_shape=[resident((levels, columns, phases), F32), resident((CHUNK, columns, phases), F32)],
+        out_shape=[resident((levels, columns, phases), F32)] + [resident((CHUNK, columns, phases), F32)] * sends,
         in_specs=[VMEM] * len(given),
-        out_specs=[VMEM] * 2,
+        out_specs=[VMEM] * (1 + sends),
         compiler_params=pltpu.CompilerParams(vmem_limit_bytes=16 * 2**20),
         name="chunk",
     )(*[pin(x) for x in given.values()])
@@ -384,20 +384,14 @@
         high[0, 0:phases], low[0, 0:phases] = operator(weight, 0, 0)
         high[0, phases:rows], low[0, phases:rows] = split(base[0])
 
-        def up(i, _):
+        for i in range(1, levels):
             step(i, i, [(i - 1, 0)])
-            return 0
-
-        lax.fori_loop(1, levels, up, 0)
         for a in range(1, AHEAD):
             first, old = slot_of(levels, a, 0), slot_of(levels, a - 1, 0)
             step(first, 0, [(old + 1, 1)], a - SOON if a >= SOON else None)
 
-            def both(i, _, first=first, old=old):
+            for i in range(1, levels - a if a < CHUNK else AHEAD - a):
                 step(first + i, i, [(first + i - 1, 0), (old + i + 1, 1)])
-                return 0
-
-            lax.fori_loop(1, levels - a if a < CHUNK else AHEAD - a, both, 0)
 
 
 def spread_close_kernel(
@@ -617,8 +611,11 @@
         if step in ready:
             if step == 1:
                 state = finish_state(step, ways, came, state, False)
-            extra = {} if step == top else {"late": late_top if step == top - 1 else late, "earlier": leaving}
-            state, parted = run_chunk(1, [step], {**own, **extra, "state": state})
+            if step == top:
+                (state,) = run_chunk(1, [step], {"weight": weight, "base": base, "state": state}, sends=False)
+            else:
+                extra = {"late": late_top if step == top - 1 else late, "earlier": leaving}
+                state, parted = run_chunk(1, [step], {**own, **extra, "state": state})
     return state[:, :given] if columns != given else state
 
 

time: 46.6 us -> 45.7 us (0.981)
  Pallas kernels: 29.3 us -> 27.7 us
  waiting for transfers between devices: 4.37 us -> 5.04 us
    pallas_call x7, Pallas kernels: 5.37 us -> 3.74 us  [run_chunk(): pl.pallas_call(functools.partial(chunk_kernel, chunk, tuple(places), part...]
    ppermute x4, waiting for transfers between devices: 4.36 us -> 5.03 us  [local(): entering = lax.ppermute(leaving, 'lvl', pairs) if pairs else None]
  transfers between devices with their start and end apart: 9 -> 9, of which waited for: 1 -> 2; matrix products, arithmetic and copies ran while one was open for 0% -> 0% of each run, Pallas kernels for 51% -> 48%
where the time goes in v13:
time: 45.7 us; the launch traced here: 45.5 us
  Pallas kernels  27.7 us (61%)
  starting transfers between devices  12.5 us (27%)
  waiting for transfers between devices  5.04 us (11%)
    pallas_call x1, Pallas kernels, spread_open(): pl.pallas_call(functools.partial(spread_open_kernel, tuple(places)), out_...  10.7 us
    ppermute x4, waiting for transfers between devices, local(): entering = lax.ppermute(leaving, 'lvl', pairs) if pairs else None  5.03 us
    ppermute x4, starting transfers between devices, local(): entering = lax.ppermute(leaving, 'lvl', pairs) if pairs else None  3.9 us
    ppermute x1, starting transfers between devices, local(): lax.ppermute(top_sent, 'lvl', [(top, top - 1)])  3.88 us
    pallas_call x4, Pallas kernels, finish_state(): pl.pallas_call(functools.partial(finish_state_kernel, place), out_shape=(...  3.83 us
    pallas_call x7, Pallas kernels, run_chunk(): pl.pallas_call(functools.partial(chunk_kernel, chunk, tuple(places), part...  3.74 us
    pallas_call x1, Pallas kernels, spread_close(): pl.pallas_call(functools.partial(spread_close_kernel, tuple(places)), out...  3.73 us
    pallas_call x1, Pallas kernels, prepare(): pl.pallas_call(prepare_kernel, out_shape=operators(SOON, columns, phases)...  3.65 us
  transfers between devices with their start and end apart: 9, of which 2 were waited for; matrix products, arithmetic and copies ran while one was open for 0% of the time, Pallas kernels for 48%

profile of v13, /device:TPU:11, one launch (start us, length us, event | category | flops | bytes accessed | tf_op | source)
XLA Modules:
  0.0 45.5 jit_solution(8821829023300993933)
XLA Ops:
  0.0 3.7 %prepare.1 = (bf16[3,1024,256]{2,1,0:T(8,128)(2,1)S(1)}, f32[3,16,256]{2,1,0:T(8,128)S(1)}, bf16[3,272,256]{2,1,0:T(8,128)(2,1)S(1)}, bf16[3,272,256]{2,1,0:T(8,...) custom-call(f32[8,256,256]{2,1,0:T(8,128)} %inv_far.1, ...), custom_call_target="tpu_custom_call" | custom-call | tf_op jit(solution)/shard_map/prepare/pallas_call | solution.py:157
  3.7 2.6 %collective-permute-start = (f32[3,272,256]{2,1,0:T(8,128)S(1)}, f32[3,272,256]{2,1,0:T(8,128)S(1)}, u32[]{:S(2)}, u32[]{:S(2)}) collective-permute-start(f32[3,272,256]{2,1,0:T(8,128)S(1)} %get-tuple-element.54.soon), channel_id=1, source_target_pairs={{4,0},{12,8},{5,1},{13,9},{6,2},{14,10},{7,3},{15,11},{20,16},{28,... | collective-permute-start | bytes 2506760 | tf_op jit(solution)/shard_map/ppermute | solution.py:566
  6.3 0.7 %collective-permute-start.2 = (f32[3,272,256]{2,1,0:T(8,128)S(1)}, f32[3,272,256]{2,1,0:T(8,128)S(1)}, u32[]{:S(2)}, u32[]{:S(2)}) collective-permute-start(f32[3,272,256]{2,1,0:T(8,128)S(1)} %get-tuple-element.54.soon), channel_id=1, source_target_pairs={{8,4},{9,5},{10,6},{11,7},{24,20},{25,21},{26,22},{27,23}} | collective-permute-start | bytes 2506760 | tf_op jit(solution)/shard_map/ppermute | solution.py:565
  7.0 2.0 %prepare_rest.1 = (bf16[8,1024,256]{2,1,0:T(8,128)(2,1)S(1)}, f32[8,16,256]{2,1,0:T(8,128)S(1)}) custom-call(bf16[3,1024,256]{2,1,0:T(8,128)(2,1)S(1)} %get-tuple-element.44.weight_soon, f32[3,16,256]{2,1,0:T(8,128)S(1)} %get-tuple-element.45.base_soon, f32[8,256,256]{2,1,0:T(8,128)S(1)} %get-tuple-element.46.inv, ...), custom_call_target="tpu_custom_call" | custom-call | tf_op jit(solution)/shard_map/prepare_rest/pallas_call | solution.py:170
  9.1 0.7 %collective-permute-start.1 = (f32[4,272,256]{2,1,0:T(8,128)S(1)}, f32[4,272,256]{2,1,0:T(8,128)S(1)}, u32[]{:S(2)}, u32[]{:S(2)}) collective-permute-start(f32[4,272,256]{2,1,0:T(8,128)S(1)} %respond.1), channel_id=1, source_target_pairs={{4,0},{5,1},{6,2},{7,3},{20,16},{21,17},{22,18},{23,19}} | collective-permute-start | bytes 3342344 | tf_op jit(solution)/shard_map/ppermute | solution.py:567
  9.8 10.7 %spread_open.1 = (bf16[32,272,256]{2,1,0:T(8,128)(2,1)S(1)}, bf16[32,272,256]{2,1,0:T(8,128)(2,1)S(1)}, f32[4,272,256]{2,1,0:T(8,128)S(1)}) custom-call(bf16[8,1024,256]{2,1,0:T(8,128)(2,1)S(1)} %get-tuple-element.50.weight.refs_0_, f32[8,16,256]{2,1,0:T(8,128)S(1)} %get-tuple-element.51.base.refs_1_), custom_call_target="tpu_custom_call" | custom-call | tf_op jit(solution)/shard_map/spread_open/pallas_call | solution.py:443
  20.5 0.0 collective-permute-done.refs_2_.soon
  20.5 0.7 %collective-permute-start.3 = (f32[4,16,256]{2,1,0:T(8,128)S(1)}, f32[4,16,256]{2,1,0:T(8,128)S(1)}, u32[]{:S(2)}, u32[]{:S(2)}) collective-permute-start(f32[4,16,256]{2,1,0:T(8,128)S(1)} %get-tuple-element.59.refs_5_.refs_4_), channel_id=1, source_target_pairs={{0,4},{1,5},{2,6},{3,7},{16,20},{17,21},{18,22},{19,23}} | collective-permute-start | bytes 196616 | tf_op jit(solution)/shard_map/ppermute | solution.py:603
  21.2 0.0 collective-permute-done.2.refs_2_
  21.2 0.0 collective-permute-done.3.refs_3_
  21.2 3.9 %collective-permute-start.7 = (f32[4,272,256]{2,1,0:T(8,128)S(1)}, f32[4,272,256]{2,1,0:T(8,128)S(1)}, u32[]{:S(2)}, u32[]{:S(2)}) collective-permute-start(f32[4,272,256]{2,1,0:T(8,128)S(1)} %get-tuple-element.79.late), channel_id=1, source_target_pairs={{12,8},{13,9},{14,10},{15,11},{28,24},{29,25},{30,26},{31,27}} | collective-permute-start | bytes 3342344 | tf_op jit(solution)/shard_map/ppermute | solution.py:591
  25.1 0.0 collective-permute-done.1.refs_3_
  25.1 0.3 chunk.9
  25.4 0.7 %collective-permute-start.4 = (f32[4,16,256]{2,1,0:T(8,128)S(1)}, f32[4,16,256]{2,1,0:T(8,128)S(1)}, u32[]{:S(2)}, u32[]{:S(2)}) collective-permute-start(f32[4,16,256]{2,1,0:T(8,128)S(1)} %get-tuple-element.77.refs_6_), channel_id=1, source_target_pairs={{0,4},{4,8},{1,5},{5,9},{2,6},{6,10},{3,7},{7,11},{16,20},{20,24},... | collective-permute-start | bytes 196616 | tf_op jit(solution)/shard_map/ppermute | solution.py:603
  26.1 3.7 %spread_close.1 = (bf16[6,272,256]{2,1,0:T(8,128)(2,1)S(1)}, bf16[6,272,256]{2,1,0:T(8,128)(2,1)S(1)}, f32[8,16,256]{2,1,0:T(8,128)S(1)}, f32[4,16,256]{2,1,0:T(8,128)S(1)}) custom-call(bf16[8,1024,256]{2,1,0:T(8,128)(2,1)S(1)} %get-tuple-element.50.weight.refs_0_, f32[8,16,256]{2,1,0:T(8,128)S(1)} %get-tuple-element.51.base.refs_1_, ...), custom_call_target="tpu_custom_call" | custom-call | tf_op jit(solution)/shard_map/spread_close/pallas_call | solution.py:457
  29.8 0.0 collective-permute-done.4.entering.refs_2_.refs_4_
  29.8 0.7 %collective-permute-start.5 = (f32[4,16,256]{2,1,0:T(8,128)S(1)}, f32[4,16,256]{2,1,0:T(8,128)S(1)}, u32[]{:S(2)}, u32[]{:S(2)}) collective-permute-start(f32[4,16,256]{2,1,0:T(8,128)S(1)} %answer.1), channel_id=1, source_target_pairs={{8,4},{9,5},{10,6},{11,7},{24,20},{25,21},{26,22},{27,23}} | collective-permute-start | bytes 196616 | tf_op jit(solution)/shard_map/ppermute | solution.py:577
  30.6 0.0 collective-permute-done.5.refs_3_
  30.7 1.3 %collective-permute-start.6 = (f32[4,16,256]{2,1,0:T(8,128)S(1)}, f32[4,16,256]{2,1,0:T(8,128)S(1)}, u32[]{:S(2)}, u32[]{:S(2)}) collective-permute-start(f32[4,16,256]{2,1,0:T(8,128)S(1)} %get-tuple-element.78.refs_4_.refs_6_), channel_id=1, source_target_pairs={{4,8},{8,12},{5,9},{9,13},{6,10},{10,14},{7,11},{11,15},{20,24},{2... | collective-permute-start | bytes 196616 | tf_op jit(solution)/shard_map/ppermute | solution.py:603
  32.0 0.0 collective-permute-done.7.refs_3_
  32.0 4.5 %collective-permute-done.6.refs_4_ = f32[4,16,256]{2,1,0:T(8,128)S(1)} collective-permute-done((f32[4,16,256]{2,1,0:T(8,128)S(1)}, f32[4,16,256]{2,1,0:T(8,128)S(1)}, u32[]{:S(2)}, u32[]{:S(2)}) %collective-permute-start.6) | collective-permute-done | bytes 65568 | tf_op jit(solution)/shard_map/ppermute | solution.py:603
  36.6 1.3 %collective-permute-start.8 = (f32[4,16,256]{2,1,0:T(8,128)S(1)}, f32[4,16,256]{2,1,0:T(8,128)S(1)}, u32[]{:S(2)}, u32[]{:S(2)}) collective-permute-start(f32[4,16,256]{2,1,0:T(8,128)S(1)} %finish_leaving.3), channel_id=1, source_target_pairs={{8,12},{9,13},{10,14},{11,15},{24,28},{25,29},{26,30},{27,31}} | collective-permute-start | bytes 196616 | tf_op jit(solution)/shard_map/ppermute | solution.py:603
  37.9 1.7 %finish_state.5.refs_5_ = f32[8,16,256]{2,1,0:T(8,128)S(1)} custom-call(bf16[32,272,256]{2,1,0:T(8,128)(2,1)S(1)} %get-tuple-element.66.open_high.refs_0_, bf16[32,272,256]{2,1,0:T(8,128)(2,1)S(1)} %get-tuple-element.67.open_low.refs_1_, bf16[6,272,256]{2,1,0:T(8,128)(2,1)S(1)} %get-tuple-element.69.refs_2_, ...), custom_call_target="tpu_custom_call" | custom-call | tf_op jit(solution)/shard_map/finish_state/pallas_call | solution.py:521
  39.6 3.3 %chunk.13.refs_5_ = f32[8,16,256]{2,1,0:T(8,128)S(1)} custom-call(bf16[8,1024,256]{2,1,0:T(8,128)(2,1)S(1)} %get-tuple-element.50.weight.refs_0_, f32[8,16,256]{2,1,0:T(8,128)S(1)} %get-tuple-element.51.base.refs_1_, f32[8,16,256]{2,1,0:T(8,128)S(1)} %finish_state.6.refs_2_), custom_call_target="tpu_custom_call" | custom-call | tf_op jit(solution)/shard_map/chunk/pallas_call | solution.py:340
  42.9 0.5 %collective-permute-done.8.refs_4_ = f32[4,16,256]{2,1,0:T(8,128)S(1)} collective-permute-done((f32[4,16,256]{2,1,0:T(8,128)S(1)}, f32[4,16,256]{2,1,0:T(8,128)S(1)}, u32[]{:S(2)}, u32[]{:S(2)}) %collective-permute-start.8) | collective-permute-done | bytes 65568 | tf_op jit(solution)/shard_map/ppermute | solution.py:603
  43.4 2.1 %finish_state.7 = f32[8,16,256]{2,1,0:T(8,128)} custom-call(bf16[32,272,256]{2,1,0:T(8,128)(2,1)S(1)} %get-tuple-element.66.open_high.refs_0_, bf16[32,272,256]{2,1,0:T(8,128)(2,1)S(1)} %get-tuple-element.67.open_low.refs_1_, bf16[6,272,256]{2,1,0:T(8,128)(2,1)S(1)} %get-tuple-element.69.refs_2_, bf16[6,272,256]{2,1,0:T(8,128)(2,1)S(1)} %get-tuple-element.70.refs_3_, ...), custom_call_target="tpu_custom_call" | custom-call | tf_op jit(solution)/shard_map/finish_state/pallas_call | solution.py:521
  (11 shorter events, 0.3 us)
Async XLA Ops:
  3.7 16.8 %collective-permute-start = (f32[3,272,256]{2,1,0:T(8,128)S(1)}, f32[3,272,256]{2,1,0:T(8,128)S(1)}, u32[]{:S(2)}, u32[]{:S(2)}) collective-permute-start(f32[3,272,256]{2,1,0:T(8,128)S(1)} %get-tuple-element.54.soon), channel_id=1, source_target_pairs={{4,0},{12,8},{5,1},{13,9},{6,2},{14,10},{7,3},{15,11},{20,16},{28,... | collective-permute-start | bytes 2506760 | tf_op jit(solution)/shard_map/ppermute | solution.py:566
  6.3 14.9 %collective-permute-start.2 = (f32[3,272,256]{2,1,0:T(8,128)S(1)}, f32[3,272,256]{2,1,0:T(8,128)S(1)}, u32[]{:S(2)}, u32[]{:S(2)}) collective-permute-start(f32[3,272,256]{2,1,0:T(8,128)S(1)} %get-tuple-element.54.soon), channel_id=1, source_target_pairs={{8,4},{9,5},{10,6},{11,7},{24,20},{25,21},{26,22},{27,23}} | collective-permute-start | bytes 2506760 | tf_op jit(solution)/shard_map/ppermute | solution.py:565
  9.1 16.1 %collective-permute-start.1 = (f32[4,272,256]{2,1,0:T(8,128)S(1)}, f32[4,272,256]{2,1,0:T(8,128)S(1)}, u32[]{:S(2)}, u32[]{:S(2)}) collective-permute-start(f32[4,272,256]{2,1,0:T(8,128)S(1)} %respond.1), channel_id=1, source_target_pairs={{4,0},{5,1},{6,2},{7,3},{20,16},{21,17},{22,18},{23,19}} | collective-permute-start | bytes 3342344 | tf_op jit(solution)/shard_map/ppermute | solution.py:567
  20.5 0.7 %collective-permute-start.3 = (f32[4,16,256]{2,1,0:T(8,128)S(1)}, f32[4,16,256]{2,1,0:T(8,128)S(1)}, u32[]{:S(2)}, u32[]{:S(2)}) collective-permute-start(f32[4,16,256]{2,1,0:T(8,128)S(1)} %get-tuple-element.59.refs_5_.refs_4_), channel_id=1, source_target_pairs={{0,4},{1,5},{2,6},{3,7},{16,20},{17,21},{18,22},{19,23}} | collective-permute-start | bytes 196616 | tf_op jit(solution)/shard_map/ppermute | solution.py:603
  21.2 10.7 %collective-permute-start.7 = (f32[4,272,256]{2,1,0:T(8,128)S(1)}, f32[4,272,256]{2,1,0:T(8,128)S(1)}, u32[]{:S(2)}, u32[]{:S(2)}) collective-permute-start(f32[4,272,256]{2,1,0:T(8,128)S(1)} %get-tuple-element.79.late), channel_id=1, source_target_pairs={{12,8},{13,9},{14,10},{15,11},{28,24},{29,25},{30,26},{31,27}} | collective-permute-start | bytes 3342344 | tf_op jit(solution)/shard_map/ppermute | solution.py:591
  25.4 4.4 %collective-permute-start.4 = (f32[4,16,256]{2,1,0:T(8,128)S(1)}, f32[4,16,256]{2,1,0:T(8,128)S(1)}, u32[]{:S(2)}, u32[]{:S(2)}) collective-permute-start(f32[4,16,256]{2,1,0:T(8,128)S(1)} %get-tuple-element.77.refs_6_), channel_id=1, source_target_pairs={{0,4},{4,8},{1,5},{5,9},{2,6},{6,10},{3,7},{7,11},{16,20},{20,24},... | collective-permute-start | bytes 196616 | tf_op jit(solution)/shard_map/ppermute | solution.py:603
  29.8 0.8 %collective-permute-start.5 = (f32[4,16,256]{2,1,0:T(8,128)S(1)}, f32[4,16,256]{2,1,0:T(8,128)S(1)}, u32[]{:S(2)}, u32[]{:S(2)}) collective-permute-start(f32[4,16,256]{2,1,0:T(8,128)S(1)} %answer.1), channel_id=1, source_target_pairs={{8,4},{9,5},{10,6},{11,7},{24,20},{25,21},{26,22},{27,23}} | collective-permute-start | bytes 196616 | tf_op jit(solution)/shard_map/ppermute | solution.py:577
  30.7 5.9 %collective-permute-start.6 = (f32[4,16,256]{2,1,0:T(8,128)S(1)}, f32[4,16,256]{2,1,0:T(8,128)S(1)}, u32[]{:S(2)}, u32[]{:S(2)}) collective-permute-start(f32[4,16,256]{2,1,0:T(8,128)S(1)} %get-tuple-element.78.refs_4_.refs_6_), channel_id=1, source_target_pairs={{4,8},{8,12},{5,9},{9,13},{6,10},{10,14},{7,11},{11,15},{20,24},{2... | collective-permute-start | bytes 196616 | tf_op jit(solution)/shard_map/ppermute | solution.py:603
  36.6 6.8 %collective-permute-start.8 = (f32[4,16,256]{2,1,0:T(8,128)S(1)}, f32[4,16,256]{2,1,0:T(8,128)S(1)}, u32[]{:S(2)}, u32[]{:S(2)}) collective-permute-start(f32[4,16,256]{2,1,0:T(8,128)S(1)} %finish_leaving.3), channel_id=1, source_target_pairs={{8,12},{9,13},{10,14},{11,15},{24,28},{25,29},{26,30},{27,31}} | collective-permute-start | bytes 196616 | tf_op jit(solution)/shard_map/ppermute | solution.py:603

commit v14 on v13

--- a/solution.py
+++ b/solution.py
@@ -70,19 +70,20 @@
     def from_above(i):
         return dot_parts((x_high[i + 1], x_low[i + 1]), operator(weight, i, 1))
 
-    for d in range(first, last):
-        if d == 0:
-            high, low = weight[0, 0:phases], weight[0, phases : 2 * phases]
-            x_high[0, 0:phases], x_low[0, 0:phases] = high, low
-            x_high[0, phases:rows], x_low[0, phases:rows] = split(base[0])
-            kept[0, 0:phases] = high.astype(F32) + low.astype(F32)
-            kept[0, phases:rows] = base[0]
-            continue
-        store(d, from_below(d))
-
-        for i in range(d - 1, 0, -1):
+    if first == 0:
+        high, low = operator(weight, 0, 0)
+        x_high[0, 0:phases], x_low[0, 0:phases] = high, low
+        x_high[0, phases:rows], x_low[0, phases:rows] = split(base[0])
+        kept[0, 0:phases] = high.astype(F32) + low.astype(F32)
+        kept[0, phases:rows] = base[0]
+    units = [(a, d - a) for d in range(max(first, 1), last) for a in range(d + 1)]
+    for a, i in sorted(units, key=lambda unit: (unit[1] + 2 * unit[0], unit)):
+        if a == 0:
+            store(i, from_below(i))
+        elif i > 0:
             store(i, from_below(i) + from_above(i))
-        kept[d - first, 0:phases], kept[d - first, phases:rows] = store(0, from_above(0))
+        else:
+            kept[a - first, 0:phases], kept[a - first, phases:rows] = store(0, from_above(0))
 
 
 def products(wanted, here_from, weight, base, inv, down, up, pay):
@@ -384,14 +385,14 @@
         high[0, 0:phases], low[0, 0:phases] = operator(weight, 0, 0)
         high[0, phases:rows], low[0, phases:rows] = split(base[0])
 
-        for i in range(1, levels):
-            step(i, i, [(i - 1, 0)])
-        for a in range(1, AHEAD):
-            first, old = slot_of(levels, a, 0), slot_of(levels, a - 1, 0)
-            step(first, 0, [(old + 1, 1)], a - SOON if a >= SOON else None)
-
-            for i in range(1, levels - a if a < CHUNK else AHEAD - a):
-                step(first + i, i, [(first + i - 1, 0), (old + i + 1, 1)])
+        units = [(a, i) for a in range(AHEAD) for i in range(levels - a if a < CHUNK else AHEAD - a) if a + i]
+        for a, i in sorted(units, key=lambda unit: (unit[1] + 2 * unit[0], unit)):
+            terms = []
+            if i > 0:
+                terms.append((slot_of(levels, a, i - 1), 0))
+            if a > 0:
+                terms.append((slot_of(levels, a - 1, i + 1), 1))
+            step(slot_of(levels, a, i), i, terms, a - SOON if i == 0 and a >= SOON else None)
 
 
 def spread_close_kernel(
@@ -410,21 +411,21 @@
     def _():
         for j in range(CHUNK - 1):
             feed_high[j], feed_low[j] = split(soon[j, 0:phases])
-        for a in range(1, CHUNK):
-            for i in range(levels - a, levels):
-                new = dot_parts(get_answer(ways, levels, a, i - 1), operator(weight, i, 0))
-                if i < top:
-                    over = get_answer(ways, levels, a - 1, i + 1)
-                else:
-                    back = sum(
-                        dot_parts(get_answer(ways, levels, a - 1 - j, top), (feed_high[j], feed_low[j])) for j in range(a)
-                    )
-                    end = back[phases:rows] + soon[a - 1, phases:rows]
-                    over = split(jnp.concatenate([back[0:phases], end], axis=0))
-                new += dot_parts(over, operator(weight, i, 1))
-                at = slot_of(levels, a, i)
-                high[at, 0:phases], low[at, 0:phases] = split(new[0:phases])
-                high[at, phases:rows], low[at, phases:rows] = split(new[phases:rows] + base[i])
+        units = [(a, i) for a in range(1, CHUNK) for i in range(levels - a, levels)]
+        for a, i in sorted(units, key=lambda unit: (unit[1] + 2 * unit[0], unit[1])):
+            new = dot_parts(get_answer(ways, levels, a, i - 1), operator(weight, i, 0))
+            if i < top:
+                over = get_answer(ways, levels, a - 1, i + 1)
+            else:
+                back = sum(
+                    dot_parts(get_answer(ways, levels, a - 1 - j, top), (feed_high[j], feed_low[j])) for j in range(a)
+                )
+                end = back[phases:rows] + soon[a - 1, phases:rows]
+                over = split(jnp.concatenate([back[0:phases], end], axis=0))
+            new += dot_parts(over, operator(weight, i, 1))
+            at = slot_of(levels, a, i)
+            high[at, 0:phases], low[at, 0:phases] = split(new[0:phases])
+            high[at, phases:rows], low[at, phases:rows] = split(new[phases:rows] + base[i])
 
         def run(a, i):
             return sum(part.astype(F32) for part in get_answer(ways, levels, a, i, slice(phases, rows)))

time: 45.7 us -> 44.7 us (0.978)
  Pallas kernels: 27.7 us -> 23.6 us
  waiting for transfers between devices: 5.04 us -> 8.03 us
    pallas_call x1, Pallas kernels: 10.7 us -> 6.4 us  [spread_open(): pl.pallas_call(functools.partial(spread_open_kernel, tuple(places)), out_...]
    ppermute x4, waiting for transfers between devices: 5.03 us -> 8.02 us  [local(): entering = lax.ppermute(leaving, 'lvl', pairs) if pairs else None]
  transfers between devices with their start and end apart: 9 -> 9, of which waited for: 2 -> 2; matrix products, arithmetic and copies ran while one was open for 0% -> 0% of each run, Pallas kernels for 48% -> 40%
where the time goes in v14:
time: 44.7 us; the launch traced here: 44.4 us
  Pallas kernels  23.6 us (53%)
  starting transfers between devices  12.5 us (28%)
  waiting for transfers between devices  8.03 us (18%)
    ppermute x4, waiting for transfers between devices, local(): entering = lax.ppermute(leaving, 'lvl', pairs) if pairs else None  8.02 us
    pallas_call x1, Pallas kernels, spread_open(): pl.pallas_call(functools.partial(spread_open_kernel, tuple(places)), out_...  6.4 us
    pallas_call x1, Pallas kernels, spread_close(): pl.pallas_call(functools.partial(spread_close_kernel, tuple(places)), out...  4.13 us
    ppermute x4, starting transfers between devices, local(): entering = lax.ppermute(leaving, 'lvl', pairs) if pairs else None  3.9 us
    ppermute x1, starting transfers between devices, local(): lax.ppermute(top_sent, 'lvl', [(top, top - 1)])  3.9 us
    pallas_call x7, Pallas kernels, run_chunk(): pl.pallas_call(functools.partial(chunk_kernel, chunk, tuple(places), part...  3.78 us
    pallas_call x1, Pallas kernels, prepare(): pl.pallas_call(prepare_kernel, out_shape=operators(SOON, columns, phases)...  3.65 us
    pallas_call x4, Pallas kernels, finish_state(): pl.pallas_call(functools.partial(finish_state_kernel, place), out_shape=(...  3.57 us
  transfers between devices with their start and end apart: 9, of which 2 were waited for; matrix products, arithmetic and copies ran while one was open for 0% of the time, Pallas kernels for 40%

profile of v14, /device:TPU:11, one launch (start us, length us, event | category | flops | bytes accessed | tf_op | source)
XLA Modules:
  0.0 44.4 jit_solution(17205187939748943269)
XLA Ops:
  0.0 3.7 %prepare.1 = (bf16[3,1024,256]{2,1,0:T(8,128)(2,1)S(1)}, f32[3,16,256]{2,1,0:T(8,128)S(1)}, bf16[3,272,256]{2,1,0:T(8,128)(2,1)S(1)}, bf16[3,272,256]{2,1,0:T(8,...) custom-call(f32[8,256,256]{2,1,0:T(8,128)} %inv_far.1, ...), custom_call_target="tpu_custom_call" | custom-call | tf_op jit(solution)/shard_map/prepare/pallas_call | solution.py:158
  3.7 2.6 %collective-permute-start = (f32[3,272,256]{2,1,0:T(8,128)S(1)}, f32[3,272,256]{2,1,0:T(8,128)S(1)}, u32[]{:S(2)}, u32[]{:S(2)}) collective-permute-start(f32[3,272,256]{2,1,0:T(8,128)S(1)} %get-tuple-element.54.soon), channel_id=1, source_target_pairs={{4,0},{12,8},{5,1},{13,9},{6,2},{14,10},{7,3},{15,11},{20,16},{28,... | collective-permute-start | bytes 2506760 | tf_op jit(solution)/shard_map/ppermute | solution.py:567
  6.3 0.7 %collective-permute-start.2 = (f32[3,272,256]{2,1,0:T(8,128)S(1)}, f32[3,272,256]{2,1,0:T(8,128)S(1)}, u32[]{:S(2)}, u32[]{:S(2)}) collective-permute-start(f32[3,272,256]{2,1,0:T(8,128)S(1)} %get-tuple-element.54.soon), channel_id=1, source_target_pairs={{8,4},{9,5},{10,6},{11,7},{24,20},{25,21},{26,22},{27,23}} | collective-permute-start | bytes 2506760 | tf_op jit(solution)/shard_map/ppermute | solution.py:566
  7.0 2.0 %prepare_rest.1 = (bf16[8,1024,256]{2,1,0:T(8,128)(2,1)S(1)}, f32[8,16,256]{2,1,0:T(8,128)S(1)}) custom-call(bf16[3,1024,256]{2,1,0:T(8,128)(2,1)S(1)} %get-tuple-element.44.weight_soon, f32[3,16,256]{2,1,0:T(8,128)S(1)} %get-tuple-element.45.base_soon, f32[8,256,256]{2,1,0:T(8,128)S(1)} %get-tuple-element.46.inv, ...), custom_call_target="tpu_custom_call" | custom-call | tf_op jit(solution)/shard_map/prepare_rest/pallas_call | solution.py:171
  9.1 0.7 %collective-permute-start.1 = (f32[4,272,256]{2,1,0:T(8,128)S(1)}, f32[4,272,256]{2,1,0:T(8,128)S(1)}, u32[]{:S(2)}, u32[]{:S(2)}) collective-permute-start(f32[4,272,256]{2,1,0:T(8,128)S(1)} %respond.1), channel_id=1, source_target_pairs={{4,0},{5,1},{6,2},{7,3},{20,16},{21,17},{22,18},{23,19}} | collective-permute-start | bytes 3342344 | tf_op jit(solution)/shard_map/ppermute | solution.py:568
  9.8 6.4 %spread_open.1 = (bf16[32,272,256]{2,1,0:T(8,128)(2,1)S(1)}, bf16[32,272,256]{2,1,0:T(8,128)(2,1)S(1)}, f32[4,272,256]{2,1,0:T(8,128)S(1)}) custom-call(bf16[8,1024,256]{2,1,0:T(8,128)(2,1)S(1)} %get-tuple-element.50.weight.refs_0_, f32[8,16,256]{2,1,0:T(8,128)S(1)} %get-tuple-element.51.base.refs_1_), custom_call_target="tpu_custom_call" | custom-call | tf_op jit(solution)/shard_map/spread_open/pallas_call | solution.py:444
  16.2 0.0 collective-permute-done.refs_2_.soon
  16.3 0.7 %collective-permute-start.3 = (f32[4,16,256]{2,1,0:T(8,128)S(1)}, f32[4,16,256]{2,1,0:T(8,128)S(1)}, u32[]{:S(2)}, u32[]{:S(2)}) collective-permute-start(f32[4,16,256]{2,1,0:T(8,128)S(1)} %get-tuple-element.59.refs_5_.refs_4_), channel_id=1, source_target_pairs={{0,4},{1,5},{2,6},{3,7},{16,20},{17,21},{18,22},{19,23}} | collective-permute-start | bytes 196616 | tf_op jit(solution)/shard_map/ppermute | solution.py:604
  16.9 0.0 collective-permute-done.2.refs_2_
  16.9 0.0 collective-permute-done.3.refs_3_
  17.0 3.9 %collective-permute-start.7 = (f32[4,272,256]{2,1,0:T(8,128)S(1)}, f32[4,272,256]{2,1,0:T(8,128)S(1)}, u32[]{:S(2)}, u32[]{:S(2)}) collective-permute-start(f32[4,272,256]{2,1,0:T(8,128)S(1)} %get-tuple-element.79.late), channel_id=1, source_target_pairs={{12,8},{13,9},{14,10},{15,11},{28,24},{29,25},{30,26},{31,27}} | collective-permute-start | bytes 3342344 | tf_op jit(solution)/shard_map/ppermute | solution.py:592
  20.9 0.0 collective-permute-done.1.refs_3_
  20.9 0.7 %collective-permute-start.4 = (f32[4,16,256]{2,1,0:T(8,128)S(1)}, f32[4,16,256]{2,1,0:T(8,128)S(1)}, u32[]{:S(2)}, u32[]{:S(2)}) collective-permute-start(f32[4,16,256]{2,1,0:T(8,128)S(1)} %get-tuple-element.77.refs_6_), channel_id=1, source_target_pairs={{0,4},{4,8},{1,5},{5,9},{2,6},{6,10},{3,7},{7,11},{16,20},{20,24},... | collective-permute-start | bytes 196616 | tf_op jit(solution)/shard_map/ppermute | solution.py:604
  21.6 4.1 %spread_close.1 = (bf16[6,272,256]{2,1,0:T(8,128)(2,1)S(1)}, bf16[6,272,256]{2,1,0:T(8,128)(2,1)S(1)}, f32[8,16,256]{2,1,0:T(8,128)S(1)}, f32[4,16,256]{2,1,0:T(8,128)S(1)}) custom-call(bf16[8,1024,256]{2,1,0:T(8,128)(2,1)S(1)} %get-tuple-element.50.weight.refs_0_, f32[8,16,256]{2,1,0:T(8,128)S(1)} %get-tuple-element.51.base.refs_1_, ...), custom_call_target="tpu_custom_call" | custom-call | tf_op jit(solution)/shard_map/spread_close/pallas_call | solution.py:458
  25.7 0.0 collective-permute-done.4.entering.refs_2_.refs_4_
  25.8 0.7 %collective-permute-start.5 = (f32[4,16,256]{2,1,0:T(8,128)S(1)}, f32[4,16,256]{2,1,0:T(8,128)S(1)}, u32[]{:S(2)}, u32[]{:S(2)}) collective-permute-start(f32[4,16,256]{2,1,0:T(8,128)S(1)} %answer.1), channel_id=1, source_target_pairs={{8,4},{9,5},{10,6},{11,7},{24,20},{25,21},{26,22},{27,23}} | collective-permute-start | bytes 196616 | tf_op jit(solution)/shard_map/ppermute | solution.py:578
  26.6 0.0 collective-permute-done.5.refs_3_
  26.6 1.3 %collective-permute-start.6 = (f32[4,16,256]{2,1,0:T(8,128)S(1)}, f32[4,16,256]{2,1,0:T(8,128)S(1)}, u32[]{:S(2)}, u32[]{:S(2)}) collective-permute-start(f32[4,16,256]{2,1,0:T(8,128)S(1)} %get-tuple-element.78.refs_4_.refs_6_), channel_id=1, source_target_pairs={{4,8},{8,12},{5,9},{9,13},{6,10},{10,14},{7,11},{11,15},{20,24},{2... | collective-permute-start | bytes 196616 | tf_op jit(solution)/shard_map/ppermute | solution.py:604
  27.9 0.0 collective-permute-done.7.refs_3_
  28.0 7.5 %collective-permute-done.6.refs_4_ = f32[4,16,256]{2,1,0:T(8,128)S(1)} collective-permute-done((f32[4,16,256]{2,1,0:T(8,128)S(1)}, f32[4,16,256]{2,1,0:T(8,128)S(1)}, u32[]{:S(2)}, u32[]{:S(2)}) %collective-permute-start.6) | collective-permute-done | bytes 65568 | tf_op jit(solution)/shard_map/ppermute | solution.py:604
  35.5 1.3 %collective-permute-start.8 = (f32[4,16,256]{2,1,0:T(8,128)S(1)}, f32[4,16,256]{2,1,0:T(8,128)S(1)}, u32[]{:S(2)}, u32[]{:S(2)}) collective-permute-start(f32[4,16,256]{2,1,0:T(8,128)S(1)} %finish_leaving.3), channel_id=1, source_target_pairs={{8,12},{9,13},{10,14},{11,15},{24,28},{25,29},{26,30},{27,31}} | collective-permute-start | bytes 196616 | tf_op jit(solution)/shard_map/ppermute | solution.py:604
  36.8 1.4 %finish_state.5.refs_5_ = f32[8,16,256]{2,1,0:T(8,128)S(1)} custom-call(bf16[32,272,256]{2,1,0:T(8,128)(2,1)S(1)} %get-tuple-element.66.open_high.refs_0_, bf16[32,272,256]{2,1,0:T(8,128)(2,1)S(1)} %get-tuple-element.67.open_low.refs_1_, bf16[6,272,256]{2,1,0:T(8,128)(2,1)S(1)} %get-tuple-element.69.refs_2_, ...), custom_call_target="tpu_custom_call" | custom-call | tf_op jit(solution)/shard_map/finish_state/pallas_call | solution.py:522
  38.2 3.6 %chunk.13.refs_5_ = f32[8,16,256]{2,1,0:T(8,128)S(1)} custom-call(bf16[8,1024,256]{2,1,0:T(8,128)(2,1)S(1)} %get-tuple-element.50.weight.refs_0_, f32[8,16,256]{2,1,0:T(8,128)S(1)} %get-tuple-element.51.base.refs_1_, f32[8,16,256]{2,1,0:T(8,128)S(1)} %finish_state.6.refs_2_), custom_call_target="tpu_custom_call" | custom-call | tf_op jit(solution)/shard_map/chunk/pallas_call | solution.py:341
  41.8 0.5 %collective-permute-done.8.refs_4_ = f32[4,16,256]{2,1,0:T(8,128)S(1)} collective-permute-done((f32[4,16,256]{2,1,0:T(8,128)S(1)}, f32[4,16,256]{2,1,0:T(8,128)S(1)}, u32[]{:S(2)}, u32[]{:S(2)}) %collective-permute-start.8) | collective-permute-done | bytes 65568 | tf_op jit(solution)/shard_map/ppermute | solution.py:604
  42.3 2.1 %finish_state.7 = f32[8,16,256]{2,1,0:T(8,128)} custom-call(bf16[32,272,256]{2,1,0:T(8,128)(2,1)S(1)} %get-tuple-element.66.open_high.refs_0_, bf16[32,272,256]{2,1,0:T(8,128)(2,1)S(1)} %get-tuple-element.67.open_low.refs_1_, bf16[6,272,256]{2,1,0:T(8,128)(2,1)S(1)} %get-tuple-element.69.refs_2_, bf16[6,272,256]{2,1,0:T(8,128)(2,1)S(1)} %get-tuple-element.70.refs_3_, ...), custom_call_target="tpu_custom_call" | custom-call | tf_op jit(solution)/shard_map/finish_state/pallas_call | solution.py:522
  (12 shorter events, 0.3 us)
Async XLA Ops:
  3.7 12.5 %collective-permute-start = (f32[3,272,256]{2,1,0:T(8,128)S(1)}, f32[3,272,256]{2,1,0:T(8,128)S(1)}, u32[]{:S(2)}, u32[]{:S(2)}) collective-permute-start(f32[3,272,256]{2,1,0:T(8,128)S(1)} %get-tuple-element.54.soon), channel_id=1, source_target_pairs={{4,0},{12,8},{5,1},{13,9},{6,2},{14,10},{7,3},{15,11},{20,16},{28,... | collective-permute-start | bytes 2506760 | tf_op jit(solution)/shard_map/ppermute | solution.py:567
  6.3 10.6 %collective-permute-start.2 = (f32[3,272,256]{2,1,0:T(8,128)S(1)}, f32[3,272,256]{2,1,0:T(8,128)S(1)}, u32[]{:S(2)}, u32[]{:S(2)}) collective-permute-start(f32[3,272,256]{2,1,0:T(8,128)S(1)} %get-tuple-element.54.soon), channel_id=1, source_target_pairs={{8,4},{9,5},{10,6},{11,7},{24,20},{25,21},{26,22},{27,23}} | collective-permute-start | bytes 2506760 | tf_op jit(solution)/shard_map/ppermute | solution.py:566
  9.1 11.8 %collective-permute-start.1 = (f32[4,272,256]{2,1,0:T(8,128)S(1)}, f32[4,272,256]{2,1,0:T(8,128)S(1)}, u32[]{:S(2)}, u32[]{:S(2)}) collective-permute-start(f32[4,272,256]{2,1,0:T(8,128)S(1)} %respond.1), channel_id=1, source_target_pairs={{4,0},{5,1},{6,2},{7,3},{20,16},{21,17},{22,18},{23,19}} | collective-permute-start | bytes 3342344 | tf_op jit(solution)/shard_map/ppermute | solution.py:568
  16.3 0.7 %collective-permute-start.3 = (f32[4,16,256]{2,1,0:T(8,128)S(1)}, f32[4,16,256]{2,1,0:T(8,128)S(1)}, u32[]{:S(2)}, u32[]{:S(2)}) collective-permute-start(f32[4,16,256]{2,1,0:T(8,128)S(1)} %get-tuple-element.59.refs_5_.refs_4_), channel_id=1, source_target_pairs={{0,4},{1,5},{2,6},{3,7},{16,20},{17,21},{18,22},{19,23}} | collective-permute-start | bytes 196616 | tf_op jit(solution)/shard_map/ppermute | solution.py:604
  17.0 10.9 %collective-permute-start.7 = (f32[4,272,256]{2,1,0:T(8,128)S(1)}, f32[4,272,256]{2,1,0:T(8,128)S(1)}, u32[]{:S(2)}, u32[]{:S(2)}) collective-permute-start(f32[4,272,256]{2,1,0:T(8,128)S(1)} %get-tuple-element.79.late), channel_id=1, source_target_pairs={{12,8},{13,9},{14,10},{15,11},{28,24},{29,25},{30,26},{31,27}} | collective-permute-start | bytes 3342344 | tf_op jit(solution)/shard_map/ppermute | solution.py:592
  20.9 4.8 %collective-permute-start.4 = (f32[4,16,256]{2,1,0:T(8,128)S(1)}, f32[4,16,256]{2,1,0:T(8,128)S(1)}, u32[]{:S(2)}, u32[]{:S(2)}) collective-permute-start(f32[4,16,256]{2,1,0:T(8,128)S(1)} %get-tuple-element.77.refs_6_), channel_id=1, source_target_pairs={{0,4},{4,8},{1,5},{5,9},{2,6},{6,10},{3,7},{7,11},{16,20},{20,24},... | collective-permute-start | bytes 196616 | tf_op jit(solution)/shard_map/ppermute | solution.py:604
  25.8 0.8 %collective-permute-start.5 = (f32[4,16,256]{2,1,0:T(8,128)S(1)}, f32[4,16,256]{2,1,0:T(8,128)S(1)}, u32[]{:S(2)}, u32[]{:S(2)}) collective-permute-start(f32[4,16,256]{2,1,0:T(8,128)S(1)} %answer.1), channel_id=1, source_target_pairs={{8,4},{9,5},{10,6},{11,7},{24,20},{25,21},{26,22},{27,23}} | collective-permute-start | bytes 196616 | tf_op jit(solution)/shard_map/ppermute | solution.py:578
  26.6 8.9 %collective-permute-start.6 = (f32[4,16,256]{2,1,0:T(8,128)S(1)}, f32[4,16,256]{2,1,0:T(8,128)S(1)}, u32[]{:S(2)}, u32[]{:S(2)}) collective-permute-start(f32[4,16,256]{2,1,0:T(8,128)S(1)} %get-tuple-element.78.refs_4_.refs_6_), channel_id=1, source_target_pairs={{4,8},{8,12},{5,9},{9,13},{6,10},{10,14},{7,11},{11,15},{20,24},{2... | collective-permute-start | bytes 196616 | tf_op jit(solution)/shard_map/ppermute | solution.py:604
  35.5 6.8 %collective-permute-start.8 = (f32[4,16,256]{2,1,0:T(8,128)S(1)}, f32[4,16,256]{2,1,0:T(8,128)S(1)}, u32[]{:S(2)}, u32[]{:S(2)}) collective-permute-start(f32[4,16,256]{2,1,0:T(8,128)S(1)} %finish_leaving.3), channel_id=1, source_target_pairs={{8,12},{9,13},{10,14},{11,15},{24,28},{25,29},{26,30},{27,31}} | collective-permute-start | bytes 196616 | tf_op jit(solution)/shard_map/ppermute | solution.py:604

commit v15 on v14

--- a/solution.py
+++ b/solution.py
@@ -53,7 +53,7 @@
     return weight[i, at : at + phases], weight[i, at + phases : at + 2 * phases]
 
 
-def response(first, last, x_high, x_low, weight, base, kept):
+def response(first, last, x_high, x_low, weight, base, kept, before=None):
     _, columns, phases = base.shape
     rows = phases + columns
 
@@ -78,6 +78,8 @@
         kept[0, phases:rows] = base[0]
     units = [(a, d - a) for d in range(max(first, 1), last) for a in range(d + 1)]
     for a, i in sorted(units, key=lambda unit: (unit[1] + 2 * unit[0], unit)):
+        if before is not None:
+            before(a, i)
         if a == 0:
             store(i, from_below(i))
         elif i > 0:
@@ -86,9 +88,8 @@
             kept[a - first, 0:phases], kept[a - first, phases:rows] = store(0, from_above(0))
 
 
-def products(wanted, here_from, weight, base, inv, down, up, pay):
+def products(wanted, weight, base, inv, down, up, pay):
     for i in wanted:
-        here_from(i)
         here = split(inv[i])
         for k, block in ((0, down), (1, up)):
             if k in wanted[i]:
@@ -119,9 +120,18 @@
     for part in range(len(cuts)):
         for copy in copies(part):
             copy.start()
-    wanted = {i: (0, 1, 2) if i < SOON - 1 else (0, 2) for i in range(SOON)}
-    products(wanted, wait, weight, base, inv, down, up, pay)
-    response(0, SOON, x_high, x_low, weight, base, kept)
+    need = functools.partial(products, weight=weight, base=base, inv=inv, down=down, up=up, pay=pay)
+    wait(0)
+    need({0: (0, 1, 2)})
+    ahead = {(0, 1): {1: (0, 2)}, (0, 2): {2: (0, 2)}, (1, 0): {1: (1,)}}
+    assert SOON == 3
+
+    def before(a, i):
+        if (a, i) == (0, 1):
+            wait(1)
+        need(ahead.get((a, i), {}))
+
+    response(0, SOON, x_high, x_low, weight, base, kept, before)
     wait(SOON)
 
 
@@ -132,7 +142,7 @@
         weight[i, 0:rows] = weight_soon[i, 0:rows]
     base[0:SOON] = base_soon[...]
     wanted = {i: (0, 1, 2) if i >= SOON else (1,) for i in range(SOON - 1, levels)}
-    products(wanted, lambda i: None, weight, base, inv, down, up, pay)
+    products(wanted, weight, base, inv, down, up, pay)
 
 
 def respond_kernel(places, weight, base, x_high_soon, x_low_soon, kept, x_high, x_low):

time: 44.7 us -> 44.8 us (level)
  no operation moved by 1% of the time
where the time goes in v15:
time: 44.8 us; the launch traced here: 44.6 us
  Pallas kernels  23.8 us (53%)
  starting transfers between devices  12.5 us (28%)
  waiting for transfers between devices  8.03 us (18%)
    ppermute x4, waiting for transfers between devices, local(): entering = lax.ppermute(leaving, 'lvl', pairs) if pairs else None  8.02 us
    pallas_call x1, Pallas kernels, spread_open(): pl.pallas_call(functools.partial(spread_open_kernel, tuple(places)), out_...  6.41 us
    pallas_call x1, Pallas kernels, spread_close(): pl.pallas_call(functools.partial(spread_close_kernel, tuple(places)), out...  4.13 us
    ppermute x4, starting transfers between devices, local(): entering = lax.ppermute(leaving, 'lvl', pairs) if pairs else None  3.9 us
    ppermute x1, starting transfers between devices, local(): lax.ppermute(top_sent, 'lvl', [(top, top - 1)])  3.88 us
    pallas_call x1, Pallas kernels, prepare(): pl.pallas_call(prepare_kernel, out_shape=operators(SOON, columns, phases)...  3.81 us
    pallas_call x7, Pallas kernels, run_chunk(): pl.pallas_call(functools.partial(chunk_kernel, chunk, tuple(places), part...  3.78 us
    pallas_call x4, Pallas kernels, finish_state(): pl.pallas_call(functools.partial(finish_state_kernel, place), out_shape=(...  3.57 us
  transfers between devices with their start and end apart: 9, of which 2 were waited for; matrix products, arithmetic and copies ran while one was open for 0% of the time, Pallas kernels for 40%

profile of v15, /device:TPU:11, one launch (start us, length us, event | category | flops | bytes accessed | tf_op | source)
XLA Modules:
  0.0 44.6 jit_solution(8832799815277819605)
XLA Ops:
  0.0 3.8 %prepare.1 = (bf16[3,1024,256]{2,1,0:T(8,128)(2,1)S(1)}, f32[3,16,256]{2,1,0:T(8,128)S(1)}, bf16[3,272,256]{2,1,0:T(8,128)(2,1)S(1)}, bf16[3,272,256]{2,1,0:T(8,...) custom-call(f32[8,256,256]{2,1,0:T(8,128)} %inv_far.1, ...), custom_call_target="tpu_custom_call" | custom-call | tf_op jit(solution)/shard_map/prepare/pallas_call | solution.py:168
  3.8 2.6 %collective-permute-start = (f32[3,272,256]{2,1,0:T(8,128)S(1)}, f32[3,272,256]{2,1,0:T(8,128)S(1)}, u32[]{:S(2)}, u32[]{:S(2)}) collective-permute-start(f32[3,272,256]{2,1,0:T(8,128)S(1)} %get-tuple-element.54.soon), channel_id=1, source_target_pairs={{4,0},{12,8},{5,1},{13,9},{6,2},{14,10},{7,3},{15,11},{20,16},{28,... | collective-permute-start | bytes 2506760 | tf_op jit(solution)/shard_map/ppermute | solution.py:577
  6.5 0.7 %collective-permute-start.2 = (f32[3,272,256]{2,1,0:T(8,128)S(1)}, f32[3,272,256]{2,1,0:T(8,128)S(1)}, u32[]{:S(2)}, u32[]{:S(2)}) collective-permute-start(f32[3,272,256]{2,1,0:T(8,128)S(1)} %get-tuple-element.54.soon), channel_id=1, source_target_pairs={{8,4},{9,5},{10,6},{11,7},{24,20},{25,21},{26,22},{27,23}} | collective-permute-start | bytes 2506760 | tf_op jit(solution)/shard_map/ppermute | solution.py:576
  7.2 2.0 %prepare_rest.1 = (bf16[8,1024,256]{2,1,0:T(8,128)(2,1)S(1)}, f32[8,16,256]{2,1,0:T(8,128)S(1)}) custom-call(bf16[3,1024,256]{2,1,0:T(8,128)(2,1)S(1)} %get-tuple-element.44.weight_soon, f32[3,16,256]{2,1,0:T(8,128)S(1)} %get-tuple-element.45.base_soon, f32[8,256,256]{2,1,0:T(8,128)S(1)} %get-tuple-element.46.inv, ...), custom_call_target="tpu_custom_call" | custom-call | tf_op jit(solution)/shard_map/prepare_rest/pallas_call | solution.py:181
  9.2 0.7 %collective-permute-start.1 = (f32[4,272,256]{2,1,0:T(8,128)S(1)}, f32[4,272,256]{2,1,0:T(8,128)S(1)}, u32[]{:S(2)}, u32[]{:S(2)}) collective-permute-start(f32[4,272,256]{2,1,0:T(8,128)S(1)} %respond.1), channel_id=1, source_target_pairs={{4,0},{5,1},{6,2},{7,3},{20,16},{21,17},{22,18},{23,19}} | collective-permute-start | bytes 3342344 | tf_op jit(solution)/shard_map/ppermute | solution.py:578
  10.0 6.4 %spread_open.1 = (bf16[32,272,256]{2,1,0:T(8,128)(2,1)S(1)}, bf16[32,272,256]{2,1,0:T(8,128)(2,1)S(1)}, f32[4,272,256]{2,1,0:T(8,128)S(1)}) custom-call(bf16[8,1024,256]{2,1,0:T(8,128)(2,1)S(1)} %get-tuple-element.50.weight.refs_0_, f32[8,16,256]{2,1,0:T(8,128)S(1)} %get-tuple-element.51.base.refs_1_), custom_call_target="tpu_custom_call" | custom-call | tf_op jit(solution)/shard_map/spread_open/pallas_call | solution.py:454
  16.4 0.0 collective-permute-done.refs_2_.soon
  16.4 0.7 %collective-permute-start.3 = (f32[4,16,256]{2,1,0:T(8,128)S(1)}, f32[4,16,256]{2,1,0:T(8,128)S(1)}, u32[]{:S(2)}, u32[]{:S(2)}) collective-permute-start(f32[4,16,256]{2,1,0:T(8,128)S(1)} %get-tuple-element.59.refs_5_.refs_4_), channel_id=1, source_target_pairs={{0,4},{1,5},{2,6},{3,7},{16,20},{17,21},{18,22},{19,23}} | collective-permute-start | bytes 196616 | tf_op jit(solution)/shard_map/ppermute | solution.py:614
  17.1 0.0 collective-permute-done.2.refs_2_
  17.1 0.0 collective-permute-done.3.refs_3_
  17.2 3.9 %collective-permute-start.7 = (f32[4,272,256]{2,1,0:T(8,128)S(1)}, f32[4,272,256]{2,1,0:T(8,128)S(1)}, u32[]{:S(2)}, u32[]{:S(2)}) collective-permute-start(f32[4,272,256]{2,1,0:T(8,128)S(1)} %get-tuple-element.79.late), channel_id=1, source_target_pairs={{12,8},{13,9},{14,10},{15,11},{28,24},{29,25},{30,26},{31,27}} | collective-permute-start | bytes 3342344 | tf_op jit(solution)/shard_map/ppermute | solution.py:602
  21.0 0.0 collective-permute-done.1.refs_3_
  21.1 0.7 %collective-permute-start.4 = (f32[4,16,256]{2,1,0:T(8,128)S(1)}, f32[4,16,256]{2,1,0:T(8,128)S(1)}, u32[]{:S(2)}, u32[]{:S(2)}) collective-permute-start(f32[4,16,256]{2,1,0:T(8,128)S(1)} %get-tuple-element.77.refs_6_), channel_id=1, source_target_pairs={{0,4},{4,8},{1,5},{5,9},{2,6},{6,10},{3,7},{7,11},{16,20},{20,24},... | collective-permute-start | bytes 196616 | tf_op jit(solution)/shard_map/ppermute | solution.py:614
  21.8 4.1 %spread_close.1 = (bf16[6,272,256]{2,1,0:T(8,128)(2,1)S(1)}, bf16[6,272,256]{2,1,0:T(8,128)(2,1)S(1)}, f32[8,16,256]{2,1,0:T(8,128)S(1)}, f32[4,16,256]{2,1,0:T(8,128)S(1)}) custom-call(bf16[8,1024,256]{2,1,0:T(8,128)(2,1)S(1)} %get-tuple-element.50.weight.refs_0_, f32[8,16,256]{2,1,0:T(8,128)S(1)} %get-tuple-element.51.base.refs_1_, ...), custom_call_target="tpu_custom_call" | custom-call | tf_op jit(solution)/shard_map/spread_close/pallas_call | solution.py:468
  25.9 0.0 collective-permute-done.4.entering.refs_2_.refs_4_
  25.9 0.7 %collective-permute-start.5 = (f32[4,16,256]{2,1,0:T(8,128)S(1)}, f32[4,16,256]{2,1,0:T(8,128)S(1)}, u32[]{:S(2)}, u32[]{:S(2)}) collective-permute-start(f32[4,16,256]{2,1,0:T(8,128)S(1)} %answer.1), channel_id=1, source_target_pairs={{8,4},{9,5},{10,6},{11,7},{24,20},{25,21},{26,22},{27,23}} | collective-permute-start | bytes 196616 | tf_op jit(solution)/shard_map/ppermute | solution.py:588
  26.7 0.0 collective-permute-done.5.refs_3_
  26.8 1.3 %collective-permute-start.6 = (f32[4,16,256]{2,1,0:T(8,128)S(1)}, f32[4,16,256]{2,1,0:T(8,128)S(1)}, u32[]{:S(2)}, u32[]{:S(2)}) collective-permute-start(f32[4,16,256]{2,1,0:T(8,128)S(1)} %get-tuple-element.78.refs_4_.refs_6_), channel_id=1, source_target_pairs={{4,8},{8,12},{5,9},{9,13},{6,10},{10,14},{7,11},{11,15},{20,24},{2... | collective-permute-start | bytes 196616 | tf_op jit(solution)/shard_map/ppermute | solution.py:614
  28.1 0.0 collective-permute-done.7.refs_3_
  28.1 7.5 %collective-permute-done.6.refs_4_ = f32[4,16,256]{2,1,0:T(8,128)S(1)} collective-permute-done((f32[4,16,256]{2,1,0:T(8,128)S(1)}, f32[4,16,256]{2,1,0:T(8,128)S(1)}, u32[]{:S(2)}, u32[]{:S(2)}) %collective-permute-start.6) | collective-permute-done | bytes 65568 | tf_op jit(solution)/shard_map/ppermute | solution.py:614
  35.7 1.3 %collective-permute-start.8 = (f32[4,16,256]{2,1,0:T(8,128)S(1)}, f32[4,16,256]{2,1,0:T(8,128)S(1)}, u32[]{:S(2)}, u32[]{:S(2)}) collective-permute-start(f32[4,16,256]{2,1,0:T(8,128)S(1)} %finish_leaving.3), channel_id=1, source_target_pairs={{8,12},{9,13},{10,14},{11,15},{24,28},{25,29},{26,30},{27,31}} | collective-permute-start | bytes 196616 | tf_op jit(solution)/shard_map/ppermute | solution.py:614
  36.9 1.4 %finish_state.5.refs_5_ = f32[8,16,256]{2,1,0:T(8,128)S(1)} custom-call(bf16[32,272,256]{2,1,0:T(8,128)(2,1)S(1)} %get-tuple-element.66.open_high.refs_0_, bf16[32,272,256]{2,1,0:T(8,128)(2,1)S(1)} %get-tuple-element.67.open_low.refs_1_, bf16[6,272,256]{2,1,0:T(8,128)(2,1)S(1)} %get-tuple-element.69.refs_2_, ...), custom_call_target="tpu_custom_call" | custom-call | tf_op jit(solution)/shard_map/finish_state/pallas_call | solution.py:532
  38.4 3.6 %chunk.13.refs_5_ = f32[8,16,256]{2,1,0:T(8,128)S(1)} custom-call(bf16[8,1024,256]{2,1,0:T(8,128)(2,1)S(1)} %get-tuple-element.50.weight.refs_0_, f32[8,16,256]{2,1,0:T(8,128)S(1)} %get-tuple-element.51.base.refs_1_, f32[8,16,256]{2,1,0:T(8,128)S(1)} %finish_state.6.refs_2_), custom_call_target="tpu_custom_call" | custom-call | tf_op jit(solution)/shard_map/chunk/pallas_call | solution.py:351
  42.0 0.5 %collective-permute-done.8.refs_4_ = f32[4,16,256]{2,1,0:T(8,128)S(1)} collective-permute-done((f32[4,16,256]{2,1,0:T(8,128)S(1)}, f32[4,16,256]{2,1,0:T(8,128)S(1)}, u32[]{:S(2)}, u32[]{:S(2)}) %collective-permute-start.8) | collective-permute-done | bytes 65568 | tf_op jit(solution)/shard_map/ppermute | solution.py:614
  42.5 2.1 %finish_state.7 = f32[8,16,256]{2,1,0:T(8,128)} custom-call(bf16[32,272,256]{2,1,0:T(8,128)(2,1)S(1)} %get-tuple-element.66.open_high.refs_0_, bf16[32,272,256]{2,1,0:T(8,128)(2,1)S(1)} %get-tuple-element.67.open_low.refs_1_, bf16[6,272,256]{2,1,0:T(8,128)(2,1)S(1)} %get-tuple-element.69.refs_2_, bf16[6,272,256]{2,1,0:T(8,128)(2,1)S(1)} %get-tuple-element.70.refs_3_, ...), custom_call_target="tpu_custom_call" | custom-call | tf_op jit(solution)/shard_map/finish_state/pallas_call | solution.py:532
  (12 shorter events, 0.3 us)
Async XLA Ops:
  3.8 12.6 %collective-permute-start = (f32[3,272,256]{2,1,0:T(8,128)S(1)}, f32[3,272,256]{2,1,0:T(8,128)S(1)}, u32[]{:S(2)}, u32[]{:S(2)}) collective-permute-start(f32[3,272,256]{2,1,0:T(8,128)S(1)} %get-tuple-element.54.soon), channel_id=1, source_target_pairs={{4,0},{12,8},{5,1},{13,9},{6,2},{14,10},{7,3},{15,11},{20,16},{28,... | collective-permute-start | bytes 2506760 | tf_op jit(solution)/shard_map/ppermute | solution.py:577
  6.5 10.6 %collective-permute-start.2 = (f32[3,272,256]{2,1,0:T(8,128)S(1)}, f32[3,272,256]{2,1,0:T(8,128)S(1)}, u32[]{:S(2)}, u32[]{:S(2)}) collective-permute-start(f32[3,272,256]{2,1,0:T(8,128)S(1)} %get-tuple-element.54.soon), channel_id=1, source_target_pairs={{8,4},{9,5},{10,6},{11,7},{24,20},{25,21},{26,22},{27,23}} | collective-permute-start | bytes 2506760 | tf_op jit(solution)/shard_map/ppermute | solution.py:576
  9.2 11.8 %collective-permute-start.1 = (f32[4,272,256]{2,1,0:T(8,128)S(1)}, f32[4,272,256]{2,1,0:T(8,128)S(1)}, u32[]{:S(2)}, u32[]{:S(2)}) collective-permute-start(f32[4,272,256]{2,1,0:T(8,128)S(1)} %respond.1), channel_id=1, source_target_pairs={{4,0},{5,1},{6,2},{7,3},{20,16},{21,17},{22,18},{23,19}} | collective-permute-start | bytes 3342344 | tf_op jit(solution)/shard_map/ppermute | solution.py:578
  16.4 0.7 %collective-permute-start.3 = (f32[4,16,256]{2,1,0:T(8,128)S(1)}, f32[4,16,256]{2,1,0:T(8,128)S(1)}, u32[]{:S(2)}, u32[]{:S(2)}) collective-permute-start(f32[4,16,256]{2,1,0:T(8,128)S(1)} %get-tuple-element.59.refs_5_.refs_4_), channel_id=1, source_target_pairs={{0,4},{1,5},{2,6},{3,7},{16,20},{17,21},{18,22},{19,23}} | collective-permute-start | bytes 196616 | tf_op jit(solution)/shard_map/ppermute | solution.py:614
  17.2 10.9 %collective-permute-start.7 = (f32[4,272,256]{2,1,0:T(8,128)S(1)}, f32[4,272,256]{2,1,0:T(8,128)S(1)}, u32[]{:S(2)}, u32[]{:S(2)}) collective-permute-start(f32[4,272,256]{2,1,0:T(8,128)S(1)} %get-tuple-element.79.late), channel_id=1, source_target_pairs={{12,8},{13,9},{14,10},{15,11},{28,24},{29,25},{30,26},{31,27}} | collective-permute-start | bytes 3342344 | tf_op jit(solution)/shard_map/ppermute | solution.py:602
  21.1 4.8 %collective-permute-start.4 = (f32[4,16,256]{2,1,0:T(8,128)S(1)}, f32[4,16,256]{2,1,0:T(8,128)S(1)}, u32[]{:S(2)}, u32[]{:S(2)}) collective-permute-start(f32[4,16,256]{2,1,0:T(8,128)S(1)} %get-tuple-element.77.refs_6_), channel_id=1, source_target_pairs={{0,4},{4,8},{1,5},{5,9},{2,6},{6,10},{3,7},{7,11},{16,20},{20,24},... | collective-permute-start | bytes 196616 | tf_op jit(solution)/shard_map/ppermute | solution.py:614
  25.9 0.8 %collective-permute-start.5 = (f32[4,16,256]{2,1,0:T(8,128)S(1)}, f32[4,16,256]{2,1,0:T(8,128)S(1)}, u32[]{:S(2)}, u32[]{:S(2)}) collective-permute-start(f32[4,16,256]{2,1,0:T(8,128)S(1)} %answer.1), channel_id=1, source_target_pairs={{8,4},{9,5},{10,6},{11,7},{24,20},{25,21},{26,22},{27,23}} | collective-permute-start | bytes 196616 | tf_op jit(solution)/shard_map/ppermute | solution.py:588
  26.8 8.9 %collective-permute-start.6 = (f32[4,16,256]{2,1,0:T(8,128)S(1)}, f32[4,16,256]{2,1,0:T(8,128)S(1)}, u32[]{:S(2)}, u32[]{:S(2)}) collective-permute-start(f32[4,16,256]{2,1,0:T(8,128)S(1)} %get-tuple-element.78.refs_4_.refs_6_), channel_id=1, source_target_pairs={{4,8},{8,12},{5,9},{9,13},{6,10},{10,14},{7,11},{11,15},{20,24},{2... | collective-permute-start | bytes 196616 | tf_op jit(solution)/shard_map/ppermute | solution.py:614
  35.7 6.8 %collective-permute-start.8 = (f32[4,16,256]{2,1,0:T(8,128)S(1)}, f32[4,16,256]{2,1,0:T(8,128)S(1)}, u32[]{:S(2)}, u32[]{:S(2)}) collective-permute-start(f32[4,16,256]{2,1,0:T(8,128)S(1)} %finish_leaving.3), channel_id=1, source_target_pairs={{8,12},{9,13},{10,14},{11,15},{24,28},{25,29},{26,30},{27,31}} | collective-permute-start | bytes 196616 | tf_op jit(solution)/shard_map/ppermute | solution.py:614

commit v16 on v14

--- a/solution.py
+++ b/solution.py
@@ -518,14 +518,51 @@
             new[i] = state[i] + apply(terms)
 
 
-def finish_state(place, ways, entering, state, last):
+def finish_state(place, ways, entering, state):
     return pl.pallas_call(
         functools.partial(finish_state_kernel, place),
-        out_shape=(jax.ShapeDtypeStruct if last else resident)(state.shape, F32),
+        out_shape=resident(state.shape, F32),
         in_specs=[VMEM] * 6,
         out_specs=VMEM,
         compiler_params=pltpu.CompilerParams(vmem_limit_bytes=8 * 2**20),
         name="finish_state",
+    )(*[pin(x) for x in (*ways, entering, state)])
+
+
+def finish_last_kernel(place, *refs):
+    *ways, entering, state, far, near, sems = refs
+    levels, _, phases = state.shape
+
+    @pl.when(lax.axis_index("lvl") != place)
+    def _():
+        copy = pltpu.make_async_copy(state, far, sems.at[levels])
+        copy.start()
+        copy.wait()
+
+    @pl.when(lax.axis_index("lvl") == place)
+    def _():
+        copies = [pltpu.make_async_copy(near.at[i], far.at[i], sems.at[i]) for i in range(levels)]
+        values = [stack(entering[CHUNK - 1 - a]) for a in range(CHUNK)]
+        for i in range(levels):
+            terms = []
+            for a in range(CHUNK):
+                pair = jnp.concatenate(get_answer(ways, levels, a, i, slice(0, phases)), axis=0)
+                terms.append((values[a], pair))
+            near[i] = state[i] + apply(terms)
+            copies[i].start()
+        for copy in copies:
+            copy.wait()
+
+
+def finish_last(place, ways, entering, state):
+    return pl.pallas_call(
+        functools.partial(finish_last_kernel, place),
+        out_shape=jax.ShapeDtypeStruct(state.shape, F32),
+        in_specs=[VMEM] * 6,
+        out_specs=HBM,
+        scratch_shapes=[pltpu.VMEM(state.shape, F32), pltpu.SemaphoreType.DMA((state.shape[0] + 1,))],
+        compiler_params=pltpu.CompilerParams(vmem_limit_bytes=8 * 2**20),
+        name="finish_last",
     )(*[pin(x) for x in (*ways, entering, state)])
 
 
@@ -563,8 +600,8 @@
     weight, base = weights
     late_odd = respond(odd, weights, begun) if odd else None
     ways, late_here = spread_open(ready, weight, base)
-    soon_odd = lax.ppermute(soon_here, "lvl", [(d + 1, d) for d in range(1, top, 2)])
-    soon = lax.ppermute(soon_here, "lvl", [(d + 1, d) for d in range(0, top, 2)])
+    soon = lax.ppermute(soon_here, "lvl", [(1, 0)])
+    soon_far = lax.ppermute(soon_here, "lvl", [(d + 1, d) for d in range(1, top)]) if top > 1 else soon
     late = lax.ppermute(late_odd, "lvl", [(d, d - 1) for d in odd]) if odd else None
     soon, late_here, late_odd = lax.optimization_barrier((soon, late_here, late_odd))
     late_top = None
@@ -585,7 +622,7 @@
                 leaving = finish_leaving(step, ways, entering, parted_first, leaving, base.shape[0])
         elif step < count:
             state, leaving = run_chunk(
-                0, [step], {**own, "soon": soon_odd if step % 2 else soon, "entering": entering, "state": state, "leaving": leaving}
+                0, [step], {**own, "soon": soon_far if step else soon, "entering": entering, "state": state, "leaving": leaving}
             )
         if step == 1:
             top_sent, leaving = lax.optimization_barrier((late_here, leaving))
@@ -594,9 +631,9 @@
             given_first = {**own, "late": first_late, "earlier": earlier, "state": state, "leaving": leaving}
             state, leaving = run_chunk(1, [0], given_first)
         if step in ready and step > 1:
-            state = finish_state(step, ways, entering, state, False)
+            state = finish_state(step, ways, entering, state)
         if returned is not None:
-            given_rest = {**own, "soon": soon_odd, "returned": returned, "edge": edge, "state": state, "leaving": leaving}
+            given_rest = {**own, "soon": soon_far, "returned": returned, "edge": edge, "state": state, "leaving": leaving}
             state, leaving = run_chunk(1, [place], given_rest, "late")
         came = entering
         if step < count:
@@ -604,19 +641,19 @@
             entering = lax.ppermute(leaving, "lvl", pairs) if pairs else None
         if step == 1:
             ways_then, leaving = lax.optimization_barrier((ways, leaving))
-            ways, state, parted_first = spread_close(ready, weight, base, soon, ways_then, state)
+            ways, state, parted_first = spread_close(ready, weight, base, soon_far, ways_then, state)
             if entering is not None:
                 entering, state = lax.optimization_barrier((entering, state))
         if place in ready:
-            state = finish_state(place, ways, came, state, step == count)
+            state = (finish_last if step == count else finish_state)(place, ways, came, state)
         if step in ready:
             if step == 1:
-                state = finish_state(step, ways, came, state, False)
+                state = finish_state(step, ways, came, state)
             if step == top:
                 (state,) = run_chunk(1, [step], {"weight": weight, "base": base, "state": state}, sends=False)
             else:
                 extra = {"late": late_top if step == top - 1 else late, "earlier": leaving}
-                state, parted = run_chunk(1, [step], {**own, **extra, "state": state})
+                state, parted = run_chunk(1, [step], {**own, "soon": soon_far, **extra, "state": state})
     return state[:, :given] if columns != given else state
 
 

time: 44.7 us -> 44.9 us (level)
  no operation moved by 1% of the time
where the time goes in v16:
time: 44.9 us; the launch traced here: 44.7 us
  Pallas kernels  23.7 us (53%)
  starting transfers between devices  12.5 us (28%)
  waiting for transfers between devices  8.03 us (18%)
  between operations  0.45 us (1%)
    ppermute x4, waiting for transfers between devices, local(): entering = lax.ppermute(leaving, 'lvl', pairs) if pairs else None  8.02 us
    pallas_call x1, Pallas kernels, spread_open(): pl.pallas_call(functools.partial(spread_open_kernel, tuple(places)), out_...  6.4 us
    pallas_call x1, Pallas kernels, spread_close(): pl.pallas_call(functools.partial(spread_close_kernel, tuple(places)), out...  4.13 us
    ppermute x4, starting transfers between devices, local(): entering = lax.ppermute(leaving, 'lvl', pairs) if pairs else None  3.9 us
    ppermute x1, starting transfers between devices, local(): lax.ppermute(top_sent, 'lvl', [(top, top - 1)])  3.9 us
    pallas_call x7, Pallas kernels, run_chunk(): pl.pallas_call(functools.partial(chunk_kernel, chunk, tuple(places), part...  3.78 us
    pallas_call x1, Pallas kernels, prepare(): pl.pallas_call(prepare_kernel, out_shape=operators(SOON, columns, phases)...  3.65 us
    ppermute x1, starting transfers between devices, local(): lax.ppermute(soon_here, 'lvl', [(d + 1, d) for d in range(1, top)])  2.62 us
  transfers between devices with their start and end apart: 9, of which 2 were waited for; matrix products, arithmetic and copies ran while one was open for 0% of the time, Pallas kernels for 40%

profile of v16, /device:TPU:11, one launch (start us, length us, event | category | flops | bytes accessed | tf_op | source)
XLA Modules:
  0.0 44.7 jit_solution(3956325753806087110)
XLA Ops:
  0.0 3.7 %prepare.1 = (bf16[3,1024,256]{2,1,0:T(8,128)(2,1)S(1)}, f32[3,16,256]{2,1,0:T(8,128)S(1)}, bf16[3,272,256]{2,1,0:T(8,128)(2,1)S(1)}, bf16[3,272,256]{2,1,0:T(8,...) custom-call(f32[8,256,256]{2,1,0:T(8,128)} %inv_far.1, ...), custom_call_target="tpu_custom_call" | custom-call | tf_op jit(solution)/shard_map/prepare/pallas_call | solution.py:158
  3.7 0.7 %collective-permute-start = (f32[3,272,256]{2,1,0:T(8,128)S(1)}, f32[3,272,256]{2,1,0:T(8,128)S(1)}, u32[]{:S(2)}, u32[]{:S(2)}) collective-permute-start(f32[3,272,256]{2,1,0:T(8,128)S(1)} %get-tuple-element.54.soon), channel_id=1, source_target_pairs={{4,0},{5,1},{6,2},{7,3},{20,16},{21,17},{22,18},{23,19}} | collective-permute-start | bytes 2506760 | tf_op jit(solution)/shard_map/ppermute | solution.py:603
  4.4 2.6 %collective-permute-start.2 = (f32[3,272,256]{2,1,0:T(8,128)S(1)}, f32[3,272,256]{2,1,0:T(8,128)S(1)}, u32[]{:S(2)}, u32[]{:S(2)}) collective-permute-start(f32[3,272,256]{2,1,0:T(8,128)S(1)} %get-tuple-element.54.soon), channel_id=1, source_target_pairs={{8,4},{12,8},{9,5},{13,9},{10,6},{14,10},{11,7},{15,11},{24,20},{2... | collective-permute-start | bytes 2506760 | tf_op jit(solution)/shard_map/ppermute | solution.py:604
  7.0 2.0 %prepare_rest.1 = (bf16[8,1024,256]{2,1,0:T(8,128)(2,1)S(1)}, f32[8,16,256]{2,1,0:T(8,128)S(1)}) custom-call(bf16[3,1024,256]{2,1,0:T(8,128)(2,1)S(1)} %get-tuple-element.44.weight_soon, f32[3,16,256]{2,1,0:T(8,128)S(1)} %get-tuple-element.45.base_soon, f32[8,256,256]{2,1,0:T(8,128)S(1)} %get-tuple-element.46.inv, ...), custom_call_target="tpu_custom_call" | custom-call | tf_op jit(solution)/shard_map/prepare_rest/pallas_call | solution.py:171
  9.1 0.7 %collective-permute-start.1 = (f32[4,272,256]{2,1,0:T(8,128)S(1)}, f32[4,272,256]{2,1,0:T(8,128)S(1)}, u32[]{:S(2)}, u32[]{:S(2)}) collective-permute-start(f32[4,272,256]{2,1,0:T(8,128)S(1)} %respond.1), channel_id=1, source_target_pairs={{4,0},{5,1},{6,2},{7,3},{20,16},{21,17},{22,18},{23,19}} | collective-permute-start | bytes 3342344 | tf_op jit(solution)/shard_map/ppermute | solution.py:605
  9.8 6.4 %spread_open.1 = (bf16[32,272,256]{2,1,0:T(8,128)(2,1)S(1)}, bf16[32,272,256]{2,1,0:T(8,128)(2,1)S(1)}, f32[4,272,256]{2,1,0:T(8,128)S(1)}) custom-call(bf16[8,1024,256]{2,1,0:T(8,128)(2,1)S(1)} %get-tuple-element.50.weight.refs_0_, f32[8,16,256]{2,1,0:T(8,128)S(1)} %get-tuple-element.51.base.refs_1_), custom_call_target="tpu_custom_call" | custom-call | tf_op jit(solution)/shard_map/spread_open/pallas_call | solution.py:444
  16.2 0.0 collective-permute-done.refs_2_
  16.3 0.7 %collective-permute-start.3 = (f32[4,16,256]{2,1,0:T(8,128)S(1)}, f32[4,16,256]{2,1,0:T(8,128)S(1)}, u32[]{:S(2)}, u32[]{:S(2)}) collective-permute-start(f32[4,16,256]{2,1,0:T(8,128)S(1)} %get-tuple-element.59.refs_5_.refs_4_), channel_id=1, source_target_pairs={{0,4},{1,5},{2,6},{3,7},{16,20},{17,21},{18,22},{19,23}} | collective-permute-start | bytes 196616 | tf_op jit(solution)/shard_map/ppermute | solution.py:641
  16.9 0.0 collective-permute-done.2.refs_2_.soon
  16.9 0.0 collective-permute-done.3.refs_3_
  17.0 3.9 %collective-permute-start.7 = (f32[4,272,256]{2,1,0:T(8,128)S(1)}, f32[4,272,256]{2,1,0:T(8,128)S(1)}, u32[]{:S(2)}, u32[]{:S(2)}) collective-permute-start(f32[4,272,256]{2,1,0:T(8,128)S(1)} %get-tuple-element.79.late), channel_id=1, source_target_pairs={{12,8},{13,9},{14,10},{15,11},{28,24},{29,25},{30,26},{31,27}} | collective-permute-start | bytes 3342344 | tf_op jit(solution)/shard_map/ppermute | solution.py:629
  20.9 0.0 collective-permute-done.1.refs_3_
  20.9 0.7 %collective-permute-start.4 = (f32[4,16,256]{2,1,0:T(8,128)S(1)}, f32[4,16,256]{2,1,0:T(8,128)S(1)}, u32[]{:S(2)}, u32[]{:S(2)}) collective-permute-start(f32[4,16,256]{2,1,0:T(8,128)S(1)} %get-tuple-element.77.refs_6_), channel_id=1, source_target_pairs={{0,4},{4,8},{1,5},{5,9},{2,6},{6,10},{3,7},{7,11},{16,20},{20,24},... | collective-permute-start | bytes 196616 | tf_op jit(solution)/shard_map/ppermute | solution.py:641
  21.6 4.1 %spread_close.1 = (bf16[6,272,256]{2,1,0:T(8,128)(2,1)S(1)}, bf16[6,272,256]{2,1,0:T(8,128)(2,1)S(1)}, f32[8,16,256]{2,1,0:T(8,128)S(1)}, f32[4,16,256]{2,1,0:T(8,128)S(1)}) custom-call(bf16[8,1024,256]{2,1,0:T(8,128)(2,1)S(1)} %get-tuple-element.50.weight.refs_0_, f32[8,16,256]{2,1,0:T(8,128)S(1)} %get-tuple-element.51.base.refs_1_, ...), custom_call_target="tpu_custom_call" | custom-call | tf_op jit(solution)/shard_map/spread_close/pallas_call | solution.py:458
  25.7 0.0 collective-permute-done.4.entering.refs_2_.refs_4_
  25.8 0.7 %collective-permute-start.5 = (f32[4,16,256]{2,1,0:T(8,128)S(1)}, f32[4,16,256]{2,1,0:T(8,128)S(1)}, u32[]{:S(2)}, u32[]{:S(2)}) collective-permute-start(f32[4,16,256]{2,1,0:T(8,128)S(1)} %answer.1), channel_id=1, source_target_pairs={{8,4},{9,5},{10,6},{11,7},{24,20},{25,21},{26,22},{27,23}} | collective-permute-start | bytes 196616 | tf_op jit(solution)/shard_map/ppermute | solution.py:615
  26.6 0.0 collective-permute-done.5.refs_3_
  26.6 1.3 %collective-permute-start.6 = (f32[4,16,256]{2,1,0:T(8,128)S(1)}, f32[4,16,256]{2,1,0:T(8,128)S(1)}, u32[]{:S(2)}, u32[]{:S(2)}) collective-permute-start(f32[4,16,256]{2,1,0:T(8,128)S(1)} %get-tuple-element.78.refs_4_.refs_6_), channel_id=1, source_target_pairs={{4,8},{8,12},{5,9},{9,13},{6,10},{10,14},{7,11},{11,15},{20,24},{2... | collective-permute-start | bytes 196616 | tf_op jit(solution)/shard_map/ppermute | solution.py:641
  27.9 0.0 collective-permute-done.7.refs_3_
  28.0 7.5 %collective-permute-done.6.refs_4_ = f32[4,16,256]{2,1,0:T(8,128)S(1)} collective-permute-done((f32[4,16,256]{2,1,0:T(8,128)S(1)}, f32[4,16,256]{2,1,0:T(8,128)S(1)}, u32[]{:S(2)}, u32[]{:S(2)}) %collective-permute-start.6) | collective-permute-done | bytes 65568 | tf_op jit(solution)/shard_map/ppermute | solution.py:641
  35.5 1.3 %collective-permute-start.8 = (f32[4,16,256]{2,1,0:T(8,128)S(1)}, f32[4,16,256]{2,1,0:T(8,128)S(1)}, u32[]{:S(2)}, u32[]{:S(2)}) collective-permute-start(f32[4,16,256]{2,1,0:T(8,128)S(1)} %finish_leaving.3), channel_id=1, source_target_pairs={{8,12},{9,13},{10,14},{11,15},{24,28},{25,29},{26,30},{27,31}} | collective-permute-start | bytes 196616 | tf_op jit(solution)/shard_map/ppermute | solution.py:641
  36.8 1.4 %finish_state.4.refs_5_ = f32[8,16,256]{2,1,0:T(8,128)S(1)} custom-call(bf16[32,272,256]{2,1,0:T(8,128)(2,1)S(1)} %get-tuple-element.66.open_high.refs_0_, bf16[32,272,256]{2,1,0:T(8,128)(2,1)S(1)} %get-tuple-element.67.open_low.refs_1_, bf16[6,272,256]{2,1,0:T(8,128)(2,1)S(1)} %get-tuple-element.69.refs_2_, ...), custom_call_target="tpu_custom_call" | custom-call | tf_op jit(solution)/shard_map/finish_state/pallas_call | solution.py:522
  38.2 3.6 %chunk.13.refs_5_ = f32[8,16,256]{2,1,0:T(8,128)S(1)} custom-call(bf16[8,1024,256]{2,1,0:T(8,128)(2,1)S(1)} %get-tuple-element.50.weight.refs_0_, f32[8,16,256]{2,1,0:T(8,128)S(1)} %get-tuple-element.51.base.refs_1_, f32[8,16,256]{2,1,0:T(8,128)S(1)} %finish_state.5.refs_2_), custom_call_target="tpu_custom_call" | custom-call | tf_op jit(solution)/shard_map/chunk/pallas_call | solution.py:341
  41.8 0.5 %collective-permute-done.8.refs_4_ = f32[4,16,256]{2,1,0:T(8,128)S(1)} collective-permute-done((f32[4,16,256]{2,1,0:T(8,128)S(1)}, f32[4,16,256]{2,1,0:T(8,128)S(1)}, u32[]{:S(2)}, u32[]{:S(2)}) %collective-permute-start.8) | collective-permute-done | bytes 65568 | tf_op jit(solution)/shard_map/ppermute | solution.py:641
  42.3 2.1 %finish_last.1 = f32[8,16,256]{2,1,0:T(8,128)} custom-call(bf16[32,272,256]{2,1,0:T(8,128)(2,1)S(1)} %get-tuple-element.66.open_high.refs_0_, bf16[32,272,256]{2,1,0:T(8,128)(2,1)S(1)} %get-tuple-element.67.open_low.refs_1_, bf16[6,272,256]{2,1,0:T(8,128)(2,1)S(1)} %get-tuple-element.69.refs_2_, bf16[6,272,256]{2,1,0:T(8,128)(2,1)S(1)} %get-tuple-element.70.refs_3_, ...), custom_call_target="tpu_custom_call" | custom-call | tf_op jit(solution)/shard_map/finish_last/pallas_call | solution.py:558
  (12 shorter events, 0.3 us)
Async XLA Ops:
  3.7 12.5 %collective-permute-start = (f32[3,272,256]{2,1,0:T(8,128)S(1)}, f32[3,272,256]{2,1,0:T(8,128)S(1)}, u32[]{:S(2)}, u32[]{:S(2)}) collective-permute-start(f32[3,272,256]{2,1,0:T(8,128)S(1)} %get-tuple-element.54.soon), channel_id=1, source_target_pairs={{4,0},{5,1},{6,2},{7,3},{20,16},{21,17},{22,18},{23,19}} | collective-permute-start | bytes 2506760 | tf_op jit(solution)/shard_map/ppermute | solution.py:603
  4.4 12.5 %collective-permute-start.2 = (f32[3,272,256]{2,1,0:T(8,128)S(1)}, f32[3,272,256]{2,1,0:T(8,128)S(1)}, u32[]{:S(2)}, u32[]{:S(2)}) collective-permute-start(f32[3,272,256]{2,1,0:T(8,128)S(1)} %get-tuple-element.54.soon), channel_id=1, source_target_pairs={{8,4},{12,8},{9,5},{13,9},{10,6},{14,10},{11,7},{15,11},{24,20},{2... | collective-permute-start | bytes 2506760 | tf_op jit(solution)/shard_map/ppermute | solution.py:604
  9.1 11.8 %collective-permute-start.1 = (f32[4,272,256]{2,1,0:T(8,128)S(1)}, f32[4,272,256]{2,1,0:T(8,128)S(1)}, u32[]{:S(2)}, u32[]{:S(2)}) collective-permute-start(f32[4,272,256]{2,1,0:T(8,128)S(1)} %respond.1), channel_id=1, source_target_pairs={{4,0},{5,1},{6,2},{7,3},{20,16},{21,17},{22,18},{23,19}} | collective-permute-start | bytes 3342344 | tf_op jit(solution)/shard_map/ppermute | solution.py:605
  16.3 0.7 %collective-permute-start.3 = (f32[4,16,256]{2,1,0:T(8,128)S(1)}, f32[4,16,256]{2,1,0:T(8,128)S(1)}, u32[]{:S(2)}, u32[]{:S(2)}) collective-permute-start(f32[4,16,256]{2,1,0:T(8,128)S(1)} %get-tuple-element.59.refs_5_.refs_4_), channel_id=1, source_target_pairs={{0,4},{1,5},{2,6},{3,7},{16,20},{17,21},{18,22},{19,23}} | collective-permute-start | bytes 196616 | tf_op jit(solution)/shard_map/ppermute | solution.py:641
  17.0 10.9 %collective-permute-start.7 = (f32[4,272,256]{2,1,0:T(8,128)S(1)}, f32[4,272,256]{2,1,0:T(8,128)S(1)}, u32[]{:S(2)}, u32[]{:S(2)}) collective-permute-start(f32[4,272,256]{2,1,0:T(8,128)S(1)} %get-tuple-element.79.late), channel_id=1, source_target_pairs={{12,8},{13,9},{14,10},{15,11},{28,24},{29,25},{30,26},{31,27}} | collective-permute-start | bytes 3342344 | tf_op jit(solution)/shard_map/ppermute | solution.py:629
  20.9 4.8 %collective-permute-start.4 = (f32[4,16,256]{2,1,0:T(8,128)S(1)}, f32[4,16,256]{2,1,0:T(8,128)S(1)}, u32[]{:S(2)}, u32[]{:S(2)}) collective-permute-start(f32[4,16,256]{2,1,0:T(8,128)S(1)} %get-tuple-element.77.refs_6_), channel_id=1, source_target_pairs={{0,4},{4,8},{1,5},{5,9},{2,6},{6,10},{3,7},{7,11},{16,20},{20,24},... | collective-permute-start | bytes 196616 | tf_op jit(solution)/shard_map/ppermute | solution.py:641
  25.8 0.8 %collective-permute-start.5 = (f32[4,16,256]{2,1,0:T(8,128)S(1)}, f32[4,16,256]{2,1,0:T(8,128)S(1)}, u32[]{:S(2)}, u32[]{:S(2)}) collective-permute-start(f32[4,16,256]{2,1,0:T(8,128)S(1)} %answer.1), channel_id=1, source_target_pairs={{8,4},{9,5},{10,6},{11,7},{24,20},{25,21},{26,22},{27,23}} | collective-permute-start | bytes 196616 | tf_op jit(solution)/shard_map/ppermute | solution.py:615
  26.6 8.9 %collective-permute-start.6 = (f32[4,16,256]{2,1,0:T(8,128)S(1)}, f32[4,16,256]{2,1,0:T(8,128)S(1)}, u32[]{:S(2)}, u32[]{:S(2)}) collective-permute-start(f32[4,16,256]{2,1,0:T(8,128)S(1)} %get-tuple-element.78.refs_4_.refs_6_), channel_id=1, source_target_pairs={{4,8},{8,12},{5,9},{9,13},{6,10},{10,14},{7,11},{11,15},{20,24},{2... | collective-permute-start | bytes 196616 | tf_op jit(solution)/shard_map/ppermute | solution.py:641
  35.5 6.8 %collective-permute-start.8 = (f32[4,16,256]{2,1,0:T(8,128)S(1)}, f32[4,16,256]{2,1,0:T(8,128)S(1)}, u32[]{:S(2)}, u32[]{:S(2)}) collective-permute-start(f32[4,16,256]{2,1,0:T(8,128)S(1)} %finish_leaving.3), channel_id=1, source_target_pairs={{8,12},{9,13},{10,14},{11,15},{24,28},{25,29},{26,30},{27,31}} | collective-permute-start | bytes 196616 | tf_op jit(solution)/shard_map/ppermute | solution.py:641

commit v17 on v14

--- a/solution.py
+++ b/solution.py
@@ -576,7 +576,7 @@
         returned = edge = None
         if step % 2 == 0 and 0 < step < count:
             returned = lax.ppermute(answer(step, soon_here, late_here, entering), "lvl", [(step, place)])
-            given_early = {"weight": weight, "base": base, "entering": entering, "state": state}
+            given_early = {"weight": weight, "base": base, "entering": entering_next, "state": state}
             state, edge = run_chunk(1, [place], given_early, "early")
         if place in ready and place < top:
             leaving = finish_leaving(place, ways, entering, parted, leaving, base.shape[0])
@@ -587,6 +587,8 @@
             state, leaving = run_chunk(
                 0, [step], {**own, "soon": soon_odd if step % 2 else soon, "entering": entering, "state": state, "leaving": leaving}
             )
+        if step == 1 and top > 1:
+            sent_first = lax.ppermute(leaving, "lvl", [(1, 2)])
         if step == 1:
             top_sent, leaving = lax.optimization_barrier((late_here, leaving))
             late_top = lax.ppermute(top_sent, "lvl", [(top, top - 1)]) if top % 2 else None
@@ -601,7 +603,11 @@
         came = entering
         if step < count:
             pairs = [(d, d + 1) for d in (place, step) if 0 <= d < top]
-            entering = lax.ppermute(leaving, "lvl", pairs) if pairs else None
+            if step == 1 and top > 1:
+                entering_next = lax.ppermute(leaving, "lvl", [(0, 1)])
+                entering = sent_first
+            else:
+                entering = entering_next = lax.ppermute(leaving, "lvl", pairs) if pairs else None
         if step == 1:
             ways_then, leaving = lax.optimization_barrier((ways, leaving))
             ways, state, parted_first = spread_close(ready, weight, base, soon, ways_then, state)

time: 44.7 us -> 44 us (0.984)
  waiting for transfers between devices: 8.03 us -> 6.67 us
  starting transfers between devices: 12.5 us -> 13.2 us
    ppermute x4 -> x5, waiting for transfers between devices: 8.02 us -> 6.65 us  [the longest x3 6.65 us: local(): lax.ppermute(leaving, 'lvl', pairs)]
    ppermute x4 -> x5, starting transfers between devices: 3.9 us -> 4.57 us  [the longest x3 3.24 us: local(): lax.ppermute(leaving, 'lvl', pairs)]
  transfers between devices with their start and end apart: 9 -> 10, of which waited for: 2 -> 2; matrix products, arithmetic and copies ran while one was open for 0% -> 0% of each run, Pallas kernels for 40% -> 41%
where the time goes in v17:
time: 44 us; the launch traced here: 43.7 us
  Pallas kernels  23.6 us (54%)
  starting transfers between devices  13.2 us (30%)
  waiting for transfers between devices  6.67 us (15%)
    ppermute x3, waiting for transfers between devices, local(): lax.ppermute(leaving, 'lvl', pairs)  6.65 us
    pallas_call x1, Pallas kernels, spread_open(): pl.pallas_call(functools.partial(spread_open_kernel, tuple(places)), out_...  6.4 us
    pallas_call x1, Pallas kernels, spread_close(): pl.pallas_call(functools.partial(spread_close_kernel, tuple(places)), out...  4.13 us
    ppermute x1, starting transfers between devices, local(): lax.ppermute(top_sent, 'lvl', [(top, top - 1)])  3.9 us
    pallas_call x7, Pallas kernels, run_chunk(): pl.pallas_call(functools.partial(chunk_kernel, chunk, tuple(places), part...  3.78 us
    pallas_call x1, Pallas kernels, prepare(): pl.pallas_call(prepare_kernel, out_shape=operators(SOON, columns, phases)...  3.65 us
    pallas_call x4, Pallas kernels, finish_state(): pl.pallas_call(functools.partial(finish_state_kernel, place), out_shape=(...  3.57 us
    ppermute x3, starting transfers between devices, local(): lax.ppermute(leaving, 'lvl', pairs)  3.24 us
  transfers between devices with their start and end apart: 10, of which 2 were waited for; matrix products, arithmetic and copies ran while one was open for 0% of the time, Pallas kernels for 41%

profile of v17, /device:TPU:11, one launch (start us, length us, event | category | flops | bytes accessed | tf_op | source)
XLA Modules:
  0.0 43.7 jit_solution(17754022236438710737)
XLA Ops:
  0.0 3.7 %prepare.1 = (bf16[3,1024,256]{2,1,0:T(8,128)(2,1)S(1)}, f32[3,16,256]{2,1,0:T(8,128)S(1)}, bf16[3,272,256]{2,1,0:T(8,128)(2,1)S(1)}, bf16[3,272,256]{2,1,0:T(8,...) custom-call(f32[8,256,256]{2,1,0:T(8,128)} %inv_far.1, ...), custom_call_target="tpu_custom_call" | custom-call | tf_op jit(solution)/shard_map/prepare/pallas_call | solution.py:158
  3.7 2.6 %collective-permute-start = (f32[3,272,256]{2,1,0:T(8,128)S(1)}, f32[3,272,256]{2,1,0:T(8,128)S(1)}, u32[]{:S(2)}, u32[]{:S(2)}) collective-permute-start(f32[3,272,256]{2,1,0:T(8,128)S(1)} %get-tuple-element.54.soon), channel_id=1, source_target_pairs={{4,0},{12,8},{5,1},{13,9},{6,2},{14,10},{7,3},{15,11},{20,16},{28,... | collective-permute-start | bytes 2506760 | tf_op jit(solution)/shard_map/ppermute | solution.py:567
  6.3 0.7 %collective-permute-start.2 = (f32[3,272,256]{2,1,0:T(8,128)S(1)}, f32[3,272,256]{2,1,0:T(8,128)S(1)}, u32[]{:S(2)}, u32[]{:S(2)}) collective-permute-start(f32[3,272,256]{2,1,0:T(8,128)S(1)} %get-tuple-element.54.soon), channel_id=1, source_target_pairs={{8,4},{9,5},{10,6},{11,7},{24,20},{25,21},{26,22},{27,23}} | collective-permute-start | bytes 2506760 | tf_op jit(solution)/shard_map/ppermute | solution.py:566
  7.0 2.0 %prepare_rest.1 = (bf16[8,1024,256]{2,1,0:T(8,128)(2,1)S(1)}, f32[8,16,256]{2,1,0:T(8,128)S(1)}) custom-call(bf16[3,1024,256]{2,1,0:T(8,128)(2,1)S(1)} %get-tuple-element.44.weight_soon, f32[3,16,256]{2,1,0:T(8,128)S(1)} %get-tuple-element.45.base_soon, f32[8,256,256]{2,1,0:T(8,128)S(1)} %get-tuple-element.46.inv, ...), custom_call_target="tpu_custom_call" | custom-call | tf_op jit(solution)/shard_map/prepare_rest/pallas_call | solution.py:171
  9.1 0.7 %collective-permute-start.1 = (f32[4,272,256]{2,1,0:T(8,128)S(1)}, f32[4,272,256]{2,1,0:T(8,128)S(1)}, u32[]{:S(2)}, u32[]{:S(2)}) collective-permute-start(f32[4,272,256]{2,1,0:T(8,128)S(1)} %respond.1), channel_id=1, source_target_pairs={{4,0},{5,1},{6,2},{7,3},{20,16},{21,17},{22,18},{23,19}} | collective-permute-start | bytes 3342344 | tf_op jit(solution)/shard_map/ppermute | solution.py:568
  9.8 6.4 %spread_open.1 = (bf16[32,272,256]{2,1,0:T(8,128)(2,1)S(1)}, bf16[32,272,256]{2,1,0:T(8,128)(2,1)S(1)}, f32[4,272,256]{2,1,0:T(8,128)S(1)}) custom-call(bf16[8,1024,256]{2,1,0:T(8,128)(2,1)S(1)} %get-tuple-element.50.weight.refs_0_, f32[8,16,256]{2,1,0:T(8,128)S(1)} %get-tuple-element.51.base.refs_1_), custom_call_target="tpu_custom_call" | custom-call | tf_op jit(solution)/shard_map/spread_open/pallas_call | solution.py:444
  16.2 0.0 collective-permute-done.refs_2_.soon
  16.3 0.7 %collective-permute-start.3 = (f32[4,16,256]{2,1,0:T(8,128)S(1)}, f32[4,16,256]{2,1,0:T(8,128)S(1)}, u32[]{:S(2)}, u32[]{:S(2)}) collective-permute-start(f32[4,16,256]{2,1,0:T(8,128)S(1)} %get-tuple-element.59.refs_5_.refs_4_), channel_id=1, source_target_pairs={{0,4},{1,5},{2,6},{3,7},{16,20},{17,21},{18,22},{19,23}} | collective-permute-start | bytes 196616 | tf_op jit(solution)/shard_map/ppermute | solution.py:610
  16.9 0.0 collective-permute-done.2.refs_2_
  16.9 0.0 collective-permute-done.3.refs_3_
  17.0 3.9 %collective-permute-start.8 = (f32[4,272,256]{2,1,0:T(8,128)S(1)}, f32[4,272,256]{2,1,0:T(8,128)S(1)}, u32[]{:S(2)}, u32[]{:S(2)}) collective-permute-start(f32[4,272,256]{2,1,0:T(8,128)S(1)} %get-tuple-element.79.late), channel_id=1, source_target_pairs={{12,8},{13,9},{14,10},{15,11},{28,24},{29,25},{30,26},{31,27}} | collective-permute-start | bytes 3342344 | tf_op jit(solution)/shard_map/ppermute | solution.py:594
  20.9 0.7 %collective-permute-start.4 = (f32[4,16,256]{2,1,0:T(8,128)S(1)}, f32[4,16,256]{2,1,0:T(8,128)S(1)}, u32[]{:S(2)}, u32[]{:S(2)}) collective-permute-start(f32[4,16,256]{2,1,0:T(8,128)S(1)} %get-tuple-element.64.refs_6_), channel_id=1, source_target_pairs={{4,8},{5,9},{6,10},{7,11},{20,24},{21,25},{22,26},{23,27}} | collective-permute-start | bytes 196616 | tf_op jit(solution)/shard_map/ppermute | solution.py:591
  21.6 0.0 collective-permute-done.1.refs_3_
  21.6 0.7 %collective-permute-start.6 = (f32[4,16,256]{2,1,0:T(8,128)S(1)}, f32[4,16,256]{2,1,0:T(8,128)S(1)}, u32[]{:S(2)}, u32[]{:S(2)}) collective-permute-start(f32[4,16,256]{2,1,0:T(8,128)S(1)} %get-tuple-element.77.refs_6_), channel_id=1, source_target_pairs={{0,4},{1,5},{2,6},{3,7},{16,20},{17,21},{18,22},{19,23}} | collective-permute-start | bytes 196616 | tf_op jit(solution)/shard_map/ppermute | solution.py:607
  22.3 4.1 %spread_close.1 = (bf16[6,272,256]{2,1,0:T(8,128)(2,1)S(1)}, bf16[6,272,256]{2,1,0:T(8,128)(2,1)S(1)}, f32[8,16,256]{2,1,0:T(8,128)S(1)}, f32[4,16,256]{2,1,0:T(8,128)S(1)}) custom-call(bf16[8,1024,256]{2,1,0:T(8,128)(2,1)S(1)} %get-tuple-element.50.weight.refs_0_, f32[8,16,256]{2,1,0:T(8,128)S(1)} %get-tuple-element.51.base.refs_1_, ...), custom_call_target="tpu_custom_call" | custom-call | tf_op jit(solution)/shard_map/spread_close/pallas_call | solution.py:458
  26.4 0.0 collective-permute-done.4.entering.refs_4_
  26.5 0.7 %collective-permute-start.5 = (f32[4,16,256]{2,1,0:T(8,128)S(1)}, f32[4,16,256]{2,1,0:T(8,128)S(1)}, u32[]{:S(2)}, u32[]{:S(2)}) collective-permute-start(f32[4,16,256]{2,1,0:T(8,128)S(1)} %answer.1), channel_id=1, source_target_pairs={{8,4},{9,5},{10,6},{11,7},{24,20},{25,21},{26,22},{27,23}} | collective-permute-start | bytes 196616 | tf_op jit(solution)/shard_map/ppermute | solution.py:578
  27.2 0.0 collective-permute-done.6.refs_2_
  27.2 0.0 collective-permute-done.5.refs_3_
  27.3 1.3 %collective-permute-start.7 = (f32[4,16,256]{2,1,0:T(8,128)S(1)}, f32[4,16,256]{2,1,0:T(8,128)S(1)}, u32[]{:S(2)}, u32[]{:S(2)}) collective-permute-start(f32[4,16,256]{2,1,0:T(8,128)S(1)} %get-tuple-element.78.refs_4_.refs_6_), channel_id=1, source_target_pairs={{4,8},{8,12},{5,9},{9,13},{6,10},{10,14},{7,11},{11,15},{20,24},{2... | collective-permute-start | bytes 196616 | tf_op jit(solution)/shard_map/ppermute | solution.py:610
  28.6 0.0 collective-permute-done.8.refs_3_
  28.6 6.2 %collective-permute-done.7.refs_4_ = f32[4,16,256]{2,1,0:T(8,128)S(1)} collective-permute-done((f32[4,16,256]{2,1,0:T(8,128)S(1)}, f32[4,16,256]{2,1,0:T(8,128)S(1)}, u32[]{:S(2)}, u32[]{:S(2)}) %collective-permute-start.7) | collective-permute-done | bytes 65568 | tf_op jit(solution)/shard_map/ppermute | solution.py:610
  34.8 1.3 %collective-permute-start.9 = (f32[4,16,256]{2,1,0:T(8,128)S(1)}, f32[4,16,256]{2,1,0:T(8,128)S(1)}, u32[]{:S(2)}, u32[]{:S(2)}) collective-permute-start(f32[4,16,256]{2,1,0:T(8,128)S(1)} %finish_leaving.3), channel_id=1, source_target_pairs={{8,12},{9,13},{10,14},{11,15},{24,28},{25,29},{26,30},{27,31}} | collective-permute-start | bytes 196616 | tf_op jit(solution)/shard_map/ppermute | solution.py:610
  36.1 1.4 %finish_state.5.refs_5_ = f32[8,16,256]{2,1,0:T(8,128)S(1)} custom-call(bf16[32,272,256]{2,1,0:T(8,128)(2,1)S(1)} %get-tuple-element.66.open_high.refs_0_, bf16[32,272,256]{2,1,0:T(8,128)(2,1)S(1)} %get-tuple-element.67.open_low.refs_1_, bf16[6,272,256]{2,1,0:T(8,128)(2,1)S(1)} %get-tuple-element.69.refs_2_, ...), custom_call_target="tpu_custom_call" | custom-call | tf_op jit(solution)/shard_map/finish_state/pallas_call | solution.py:522
  37.6 3.6 %chunk.13.refs_5_ = f32[8,16,256]{2,1,0:T(8,128)S(1)} custom-call(bf16[8,1024,256]{2,1,0:T(8,128)(2,1)S(1)} %get-tuple-element.50.weight.refs_0_, f32[8,16,256]{2,1,0:T(8,128)S(1)} %get-tuple-element.51.base.refs_1_, f32[8,16,256]{2,1,0:T(8,128)S(1)} %finish_state.6.refs_2_), custom_call_target="tpu_custom_call" | custom-call | tf_op jit(solution)/shard_map/chunk/pallas_call | solution.py:341
  41.2 0.5 %collective-permute-done.9.refs_4_ = f32[4,16,256]{2,1,0:T(8,128)S(1)} collective-permute-done((f32[4,16,256]{2,1,0:T(8,128)S(1)}, f32[4,16,256]{2,1,0:T(8,128)S(1)}, u32[]{:S(2)}, u32[]{:S(2)}) %collective-permute-start.9) | collective-permute-done | bytes 65568 | tf_op jit(solution)/shard_map/ppermute | solution.py:610
  41.6 2.1 %finish_state.7 = f32[8,16,256]{2,1,0:T(8,128)} custom-call(bf16[32,272,256]{2,1,0:T(8,128)(2,1)S(1)} %get-tuple-element.66.open_high.refs_0_, bf16[32,272,256]{2,1,0:T(8,128)(2,1)S(1)} %get-tuple-element.67.open_low.refs_1_, bf16[6,272,256]{2,1,0:T(8,128)(2,1)S(1)} %get-tuple-element.69.refs_2_, bf16[6,272,256]{2,1,0:T(8,128)(2,1)S(1)} %get-tuple-element.70.refs_3_, ...), custom_call_target="tpu_custom_call" | custom-call | tf_op jit(solution)/shard_map/finish_state/pallas_call | solution.py:522
  (12 shorter events, 0.3 us)
Async XLA Ops:
  3.7 12.5 %collective-permute-start = (f32[3,272,256]{2,1,0:T(8,128)S(1)}, f32[3,272,256]{2,1,0:T(8,128)S(1)}, u32[]{:S(2)}, u32[]{:S(2)}) collective-permute-start(f32[3,272,256]{2,1,0:T(8,128)S(1)} %get-tuple-element.54.soon), channel_id=1, source_target_pairs={{4,0},{12,8},{5,1},{13,9},{6,2},{14,10},{7,3},{15,11},{20,16},{28,... | collective-permute-start | bytes 2506760 | tf_op jit(solution)/shard_map/ppermute | solution.py:567
  6.3 10.6 %collective-permute-start.2 = (f32[3,272,256]{2,1,0:T(8,128)S(1)}, f32[3,272,256]{2,1,0:T(8,128)S(1)}, u32[]{:S(2)}, u32[]{:S(2)}) collective-permute-start(f32[3,272,256]{2,1,0:T(8,128)S(1)} %get-tuple-element.54.soon), channel_id=1, source_target_pairs={{8,4},{9,5},{10,6},{11,7},{24,20},{25,21},{26,22},{27,23}} | collective-permute-start | bytes 2506760 | tf_op jit(solution)/shard_map/ppermute | solution.py:566
  9.1 12.5 %collective-permute-start.1 = (f32[4,272,256]{2,1,0:T(8,128)S(1)}, f32[4,272,256]{2,1,0:T(8,128)S(1)}, u32[]{:S(2)}, u32[]{:S(2)}) collective-permute-start(f32[4,272,256]{2,1,0:T(8,128)S(1)} %respond.1), channel_id=1, source_target_pairs={{4,0},{5,1},{6,2},{7,3},{20,16},{21,17},{22,18},{23,19}} | collective-permute-start | bytes 3342344 | tf_op jit(solution)/shard_map/ppermute | solution.py:568
  16.3 0.7 %collective-permute-start.3 = (f32[4,16,256]{2,1,0:T(8,128)S(1)}, f32[4,16,256]{2,1,0:T(8,128)S(1)}, u32[]{:S(2)}, u32[]{:S(2)}) collective-permute-start(f32[4,16,256]{2,1,0:T(8,128)S(1)} %get-tuple-element.59.refs_5_.refs_4_), channel_id=1, source_target_pairs={{0,4},{1,5},{2,6},{3,7},{16,20},{17,21},{18,22},{19,23}} | collective-permute-start | bytes 196616 | tf_op jit(solution)/shard_map/ppermute | solution.py:610
  17.0 11.6 %collective-permute-start.8 = (f32[4,272,256]{2,1,0:T(8,128)S(1)}, f32[4,272,256]{2,1,0:T(8,128)S(1)}, u32[]{:S(2)}, u32[]{:S(2)}) collective-permute-start(f32[4,272,256]{2,1,0:T(8,128)S(1)} %get-tuple-element.79.late), channel_id=1, source_target_pairs={{12,8},{13,9},{14,10},{15,11},{28,24},{29,25},{30,26},{31,27}} | collective-permute-start | bytes 3342344 | tf_op jit(solution)/shard_map/ppermute | solution.py:594
  20.9 5.5 %collective-permute-start.4 = (f32[4,16,256]{2,1,0:T(8,128)S(1)}, f32[4,16,256]{2,1,0:T(8,128)S(1)}, u32[]{:S(2)}, u32[]{:S(2)}) collective-permute-start(f32[4,16,256]{2,1,0:T(8,128)S(1)} %get-tuple-element.64.refs_6_), channel_id=1, source_target_pairs={{4,8},{5,9},{6,10},{7,11},{20,24},{21,25},{22,26},{23,27}} | collective-permute-start | bytes 196616 | tf_op jit(solution)/shard_map/ppermute | solution.py:591
  21.6 5.6 %collective-permute-start.6 = (f32[4,16,256]{2,1,0:T(8,128)S(1)}, f32[4,16,256]{2,1,0:T(8,128)S(1)}, u32[]{:S(2)}, u32[]{:S(2)}) collective-permute-start(f32[4,16,256]{2,1,0:T(8,128)S(1)} %get-tuple-element.77.refs_6_), channel_id=1, source_target_pairs={{0,4},{1,5},{2,6},{3,7},{16,20},{17,21},{18,22},{19,23}} | collective-permute-start | bytes 196616 | tf_op jit(solution)/shard_map/ppermute | solution.py:607
  26.5 0.8 %collective-permute-start.5 = (f32[4,16,256]{2,1,0:T(8,128)S(1)}, f32[4,16,256]{2,1,0:T(8,128)S(1)}, u32[]{:S(2)}, u32[]{:S(2)}) collective-permute-start(f32[4,16,256]{2,1,0:T(8,128)S(1)} %answer.1), channel_id=1, source_target_pairs={{8,4},{9,5},{10,6},{11,7},{24,20},{25,21},{26,22},{27,23}} | collective-permute-start | bytes 196616 | tf_op jit(solution)/shard_map/ppermute | solution.py:578
  27.3 7.5 %collective-permute-start.7 = (f32[4,16,256]{2,1,0:T(8,128)S(1)}, f32[4,16,256]{2,1,0:T(8,128)S(1)}, u32[]{:S(2)}, u32[]{:S(2)}) collective-permute-start(f32[4,16,256]{2,1,0:T(8,128)S(1)} %get-tuple-element.78.refs_4_.refs_6_), channel_id=1, source_target_pairs={{4,8},{8,12},{5,9},{9,13},{6,10},{10,14},{7,11},{11,15},{20,24},{2... | collective-permute-start | bytes 196616 | tf_op jit(solution)/shard_map/ppermute | solution.py:610
  34.8 6.8 %collective-permute-start.9 = (f32[4,16,256]{2,1,0:T(8,128)S(1)}, f32[4,16,256]{2,1,0:T(8,128)S(1)}, u32[]{:S(2)}, u32[]{:S(2)}) collective-permute-start(f32[4,16,256]{2,1,0:T(8,128)S(1)} %finish_leaving.3), channel_id=1, source_target_pairs={{8,12},{9,13},{10,14},{11,15},{24,28},{25,29},{26,30},{27,31}} | collective-permute-start | bytes 196616 | tf_op jit(solution)/shard_map/ppermute | solution.py:610

commit v18 on v17

--- a/solution.py
+++ b/solution.py
@@ -203,8 +203,7 @@
 
 
 def apply(terms):
-    values = jnp.concatenate([x for x, _ in terms for _ in range(2)], axis=1)
-    return fold(dot(values, jnp.concatenate([operator for _, operator in terms], axis=0)))
+    return fold(sum(dot(jnp.concatenate([x, x], axis=1), operator) for x, operator in terms))
 
 
 def apply_each(values, operator, columns):

time: 44 us -> 43.5 us (0.989)
  Pallas kernels: 23.6 us -> 22.8 us
    pallas_call x7, Pallas kernels: 3.78 us -> 2.93 us  [run_chunk(): pl.pallas_call(functools.partial(chunk_kernel, chunk, tuple(places), part...]
  transfers between devices with their start and end apart: 10 -> 10, of which waited for: 2 -> 2; matrix products, arithmetic and copies ran while one was open for 0% -> 0% of each run, Pallas kernels for 41% -> 39%
where the time goes in v18:
time: 43.5 us; the launch traced here: 43.2 us
  Pallas kernels  22.8 us (52%)
  starting transfers between devices  13.2 us (30%)
  waiting for transfers between devices  7.02 us (16%)
    ppermute x3, waiting for transfers between devices, local(): lax.ppermute(leaving, 'lvl', pairs)  7 us
    pallas_call x1, Pallas kernels, spread_open(): pl.pallas_call(functools.partial(spread_open_kernel, tuple(places)), out_...  6.4 us
    pallas_call x1, Pallas kernels, spread_close(): pl.pallas_call(functools.partial(spread_close_kernel, tuple(places)), out...  4.13 us
    ppermute x1, starting transfers between devices, local(): lax.ppermute(top_sent, 'lvl', [(top, top - 1)])  3.9 us
    pallas_call x1, Pallas kernels, prepare(): pl.pallas_call(prepare_kernel, out_shape=operators(SOON, columns, phases)...  3.65 us
    pallas_call x4, Pallas kernels, finish_state(): pl.pallas_call(functools.partial(finish_state_kernel, place), out_shape=(...  3.57 us
    ppermute x3, starting transfers between devices, local(): lax.ppermute(leaving, 'lvl', pairs)  3.24 us
    pallas_call x7, Pallas kernels, run_chunk(): pl.pallas_call(functools.partial(chunk_kernel, chunk, tuple(places), part...  2.93 us
  transfers between devices with their start and end apart: 10, of which 2 were waited for; matrix products, arithmetic and copies ran while one was open for 0% of the time, Pallas kernels for 39%

profile of v18, /device:TPU:11, one launch (start us, length us, event | category | flops | bytes accessed | tf_op | source)
XLA Modules:
  0.0 43.2 jit_solution(14890833126754029740)
XLA Ops:
  0.0 3.7 %prepare.1 = (bf16[3,1024,256]{2,1,0:T(8,128)(2,1)S(1)}, f32[3,16,256]{2,1,0:T(8,128)S(1)}, bf16[3,272,256]{2,1,0:T(8,128)(2,1)S(1)}, bf16[3,272,256]{2,1,0:T(8,...) custom-call(f32[8,256,256]{2,1,0:T(8,128)} %inv_far.1, ...), custom_call_target="tpu_custom_call" | custom-call | tf_op jit(solution)/shard_map/prepare/pallas_call | solution.py:158
  3.7 2.6 %collective-permute-start = (f32[3,272,256]{2,1,0:T(8,128)S(1)}, f32[3,272,256]{2,1,0:T(8,128)S(1)}, u32[]{:S(2)}, u32[]{:S(2)}) collective-permute-start(f32[3,272,256]{2,1,0:T(8,128)S(1)} %get-tuple-element.54.soon), channel_id=1, source_target_pairs={{4,0},{12,8},{5,1},{13,9},{6,2},{14,10},{7,3},{15,11},{20,16},{28,... | collective-permute-start | bytes 2506760 | tf_op jit(solution)/shard_map/ppermute | solution.py:566
  6.3 0.7 %collective-permute-start.2 = (f32[3,272,256]{2,1,0:T(8,128)S(1)}, f32[3,272,256]{2,1,0:T(8,128)S(1)}, u32[]{:S(2)}, u32[]{:S(2)}) collective-permute-start(f32[3,272,256]{2,1,0:T(8,128)S(1)} %get-tuple-element.54.soon), channel_id=1, source_target_pairs={{8,4},{9,5},{10,6},{11,7},{24,20},{25,21},{26,22},{27,23}} | collective-permute-start | bytes 2506760 | tf_op jit(solution)/shard_map/ppermute | solution.py:565
  7.0 2.0 %prepare_rest.1 = (bf16[8,1024,256]{2,1,0:T(8,128)(2,1)S(1)}, f32[8,16,256]{2,1,0:T(8,128)S(1)}) custom-call(bf16[3,1024,256]{2,1,0:T(8,128)(2,1)S(1)} %get-tuple-element.44.weight_soon, f32[3,16,256]{2,1,0:T(8,128)S(1)} %get-tuple-element.45.base_soon, f32[8,256,256]{2,1,0:T(8,128)S(1)} %get-tuple-element.46.inv, ...), custom_call_target="tpu_custom_call" | custom-call | tf_op jit(solution)/shard_map/prepare_rest/pallas_call | solution.py:171
  9.1 0.7 %collective-permute-start.1 = (f32[4,272,256]{2,1,0:T(8,128)S(1)}, f32[4,272,256]{2,1,0:T(8,128)S(1)}, u32[]{:S(2)}, u32[]{:S(2)}) collective-permute-start(f32[4,272,256]{2,1,0:T(8,128)S(1)} %respond.1), channel_id=1, source_target_pairs={{4,0},{5,1},{6,2},{7,3},{20,16},{21,17},{22,18},{23,19}} | collective-permute-start | bytes 3342344 | tf_op jit(solution)/shard_map/ppermute | solution.py:567
  9.8 6.4 %spread_open.1 = (bf16[32,272,256]{2,1,0:T(8,128)(2,1)S(1)}, bf16[32,272,256]{2,1,0:T(8,128)(2,1)S(1)}, f32[4,272,256]{2,1,0:T(8,128)S(1)}) custom-call(bf16[8,1024,256]{2,1,0:T(8,128)(2,1)S(1)} %get-tuple-element.50.weight.refs_0_, f32[8,16,256]{2,1,0:T(8,128)S(1)} %get-tuple-element.51.base.refs_1_), custom_call_target="tpu_custom_call" | custom-call | tf_op jit(solution)/shard_map/spread_open/pallas_call | solution.py:443
  16.2 0.0 collective-permute-done.refs_2_.soon
  16.3 0.7 %collective-permute-start.3 = (f32[4,16,256]{2,1,0:T(8,128)S(1)}, f32[4,16,256]{2,1,0:T(8,128)S(1)}, u32[]{:S(2)}, u32[]{:S(2)}) collective-permute-start(f32[4,16,256]{2,1,0:T(8,128)S(1)} %get-tuple-element.59.refs_5_.refs_4_), channel_id=1, source_target_pairs={{0,4},{1,5},{2,6},{3,7},{16,20},{17,21},{18,22},{19,23}} | collective-permute-start | bytes 196616 | tf_op jit(solution)/shard_map/ppermute | solution.py:609
  16.9 0.0 collective-permute-done.2.refs_2_
  16.9 0.0 collective-permute-done.3.refs_3_
  17.0 3.9 %collective-permute-start.8 = (f32[4,272,256]{2,1,0:T(8,128)S(1)}, f32[4,272,256]{2,1,0:T(8,128)S(1)}, u32[]{:S(2)}, u32[]{:S(2)}) collective-permute-start(f32[4,272,256]{2,1,0:T(8,128)S(1)} %get-tuple-element.79.late), channel_id=1, source_target_pairs={{12,8},{13,9},{14,10},{15,11},{28,24},{29,25},{30,26},{31,27}} | collective-permute-start | bytes 3342344 | tf_op jit(solution)/shard_map/ppermute | solution.py:593
  20.9 0.7 %collective-permute-start.4 = (f32[4,16,256]{2,1,0:T(8,128)S(1)}, f32[4,16,256]{2,1,0:T(8,128)S(1)}, u32[]{:S(2)}, u32[]{:S(2)}) collective-permute-start(f32[4,16,256]{2,1,0:T(8,128)S(1)} %get-tuple-element.64.refs_6_), channel_id=1, source_target_pairs={{4,8},{5,9},{6,10},{7,11},{20,24},{21,25},{22,26},{23,27}} | collective-permute-start | bytes 196616 | tf_op jit(solution)/shard_map/ppermute | solution.py:590
  21.6 0.0 collective-permute-done.1.refs_3_
  21.6 0.7 %collective-permute-start.6 = (f32[4,16,256]{2,1,0:T(8,128)S(1)}, f32[4,16,256]{2,1,0:T(8,128)S(1)}, u32[]{:S(2)}, u32[]{:S(2)}) collective-permute-start(f32[4,16,256]{2,1,0:T(8,128)S(1)} %get-tuple-element.77.refs_6_), channel_id=1, source_target_pairs={{0,4},{1,5},{2,6},{3,7},{16,20},{17,21},{18,22},{19,23}} | collective-permute-start | bytes 196616 | tf_op jit(solution)/shard_map/ppermute | solution.py:606
  22.3 4.1 %spread_close.1 = (bf16[6,272,256]{2,1,0:T(8,128)(2,1)S(1)}, bf16[6,272,256]{2,1,0:T(8,128)(2,1)S(1)}, f32[8,16,256]{2,1,0:T(8,128)S(1)}, f32[4,16,256]{2,1,0:T(8,128)S(1)}) custom-call(bf16[8,1024,256]{2,1,0:T(8,128)(2,1)S(1)} %get-tuple-element.50.weight.refs_0_, f32[8,16,256]{2,1,0:T(8,128)S(1)} %get-tuple-element.51.base.refs_1_, ...), custom_call_target="tpu_custom_call" | custom-call | tf_op jit(solution)/shard_map/spread_close/pallas_call | solution.py:457
  26.4 0.0 collective-permute-done.4.entering.refs_4_
  26.5 0.7 %collective-permute-start.5 = (f32[4,16,256]{2,1,0:T(8,128)S(1)}, f32[4,16,256]{2,1,0:T(8,128)S(1)}, u32[]{:S(2)}, u32[]{:S(2)}) collective-permute-start(f32[4,16,256]{2,1,0:T(8,128)S(1)} %answer.1), channel_id=1, source_target_pairs={{8,4},{9,5},{10,6},{11,7},{24,20},{25,21},{26,22},{27,23}} | collective-permute-start | bytes 196616 | tf_op jit(solution)/shard_map/ppermute | solution.py:577
  27.2 0.0 collective-permute-done.6.refs_2_
  27.2 0.0 collective-permute-done.5.refs_3_
  27.3 1.3 %collective-permute-start.7 = (f32[4,16,256]{2,1,0:T(8,128)S(1)}, f32[4,16,256]{2,1,0:T(8,128)S(1)}, u32[]{:S(2)}, u32[]{:S(2)}) collective-permute-start(f32[4,16,256]{2,1,0:T(8,128)S(1)} %get-tuple-element.78.refs_4_.refs_6_), channel_id=1, source_target_pairs={{4,8},{8,12},{5,9},{9,13},{6,10},{10,14},{7,11},{11,15},{20,24},{2... | collective-permute-start | bytes 196616 | tf_op jit(solution)/shard_map/ppermute | solution.py:609
  28.6 0.0 collective-permute-done.8.refs_3_
  28.6 5.9 %collective-permute-done.7.refs_4_ = f32[4,16,256]{2,1,0:T(8,128)S(1)} collective-permute-done((f32[4,16,256]{2,1,0:T(8,128)S(1)}, f32[4,16,256]{2,1,0:T(8,128)S(1)}, u32[]{:S(2)}, u32[]{:S(2)}) %collective-permute-start.7) | collective-permute-done | bytes 65568 | tf_op jit(solution)/shard_map/ppermute | solution.py:609
  34.6 1.3 %collective-permute-start.9 = (f32[4,16,256]{2,1,0:T(8,128)S(1)}, f32[4,16,256]{2,1,0:T(8,128)S(1)}, u32[]{:S(2)}, u32[]{:S(2)}) collective-permute-start(f32[4,16,256]{2,1,0:T(8,128)S(1)} %finish_leaving.3), channel_id=1, source_target_pairs={{8,12},{9,13},{10,14},{11,15},{24,28},{25,29},{26,30},{27,31}} | collective-permute-start | bytes 196616 | tf_op jit(solution)/shard_map/ppermute | solution.py:609
  35.9 1.4 %finish_state.5.refs_5_ = f32[8,16,256]{2,1,0:T(8,128)S(1)} custom-call(bf16[32,272,256]{2,1,0:T(8,128)(2,1)S(1)} %get-tuple-element.66.open_high.refs_0_, bf16[32,272,256]{2,1,0:T(8,128)(2,1)S(1)} %get-tuple-element.67.open_low.refs_1_, bf16[6,272,256]{2,1,0:T(8,128)(2,1)S(1)} %get-tuple-element.69.refs_2_, ...), custom_call_target="tpu_custom_call" | custom-call | tf_op jit(solution)/shard_map/finish_state/pallas_call | solution.py:521
  37.3 2.7 %chunk.13.refs_5_ = f32[8,16,256]{2,1,0:T(8,128)S(1)} custom-call(bf16[8,1024,256]{2,1,0:T(8,128)(2,1)S(1)} %get-tuple-element.50.weight.refs_0_, f32[8,16,256]{2,1,0:T(8,128)S(1)} %get-tuple-element.51.base.refs_1_, f32[8,16,256]{2,1,0:T(8,128)S(1)} %finish_state.6.refs_2_), custom_call_target="tpu_custom_call" | custom-call | tf_op jit(solution)/shard_map/chunk/pallas_call | solution.py:340
  40.1 1.1 %collective-permute-done.9.refs_4_ = f32[4,16,256]{2,1,0:T(8,128)S(1)} collective-permute-done((f32[4,16,256]{2,1,0:T(8,128)S(1)}, f32[4,16,256]{2,1,0:T(8,128)S(1)}, u32[]{:S(2)}, u32[]{:S(2)}) %collective-permute-start.9) | collective-permute-done | bytes 65568 | tf_op jit(solution)/shard_map/ppermute | solution.py:609
  41.1 2.1 %finish_state.7 = f32[8,16,256]{2,1,0:T(8,128)} custom-call(bf16[32,272,256]{2,1,0:T(8,128)(2,1)S(1)} %get-tuple-element.66.open_high.refs_0_, bf16[32,272,256]{2,1,0:T(8,128)(2,1)S(1)} %get-tuple-element.67.open_low.refs_1_, bf16[6,272,256]{2,1,0:T(8,128)(2,1)S(1)} %get-tuple-element.69.refs_2_, bf16[6,272,256]{2,1,0:T(8,128)(2,1)S(1)} %get-tuple-element.70.refs_3_, ...), custom_call_target="tpu_custom_call" | custom-call | tf_op jit(solution)/shard_map/finish_state/pallas_call | solution.py:521
  (12 shorter events, 0.3 us)
Async XLA Ops:
  3.7 12.5 %collective-permute-start = (f32[3,272,256]{2,1,0:T(8,128)S(1)}, f32[3,272,256]{2,1,0:T(8,128)S(1)}, u32[]{:S(2)}, u32[]{:S(2)}) collective-permute-start(f32[3,272,256]{2,1,0:T(8,128)S(1)} %get-tuple-element.54.soon), channel_id=1, source_target_pairs={{4,0},{12,8},{5,1},{13,9},{6,2},{14,10},{7,3},{15,11},{20,16},{28,... | collective-permute-start | bytes 2506760 | tf_op jit(solution)/shard_map/ppermute | solution.py:566
  6.3 10.6 %collective-permute-start.2 = (f32[3,272,256]{2,1,0:T(8,128)S(1)}, f32[3,272,256]{2,1,0:T(8,128)S(1)}, u32[]{:S(2)}, u32[]{:S(2)}) collective-permute-start(f32[3,272,256]{2,1,0:T(8,128)S(1)} %get-tuple-element.54.soon), channel_id=1, source_target_pairs={{8,4},{9,5},{10,6},{11,7},{24,20},{25,21},{26,22},{27,23}} | collective-permute-start | bytes 2506760 | tf_op jit(solution)/shard_map/ppermute | solution.py:565
  9.1 12.5 %collective-permute-start.1 = (f32[4,272,256]{2,1,0:T(8,128)S(1)}, f32[4,272,256]{2,1,0:T(8,128)S(1)}, u32[]{:S(2)}, u32[]{:S(2)}) collective-permute-start(f32[4,272,256]{2,1,0:T(8,128)S(1)} %respond.1), channel_id=1, source_target_pairs={{4,0},{5,1},{6,2},{7,3},{20,16},{21,17},{22,18},{23,19}} | collective-permute-start | bytes 3342344 | tf_op jit(solution)/shard_map/ppermute | solution.py:567
  16.3 0.7 %collective-permute-start.3 = (f32[4,16,256]{2,1,0:T(8,128)S(1)}, f32[4,16,256]{2,1,0:T(8,128)S(1)}, u32[]{:S(2)}, u32[]{:S(2)}) collective-permute-start(f32[4,16,256]{2,1,0:T(8,128)S(1)} %get-tuple-element.59.refs_5_.refs_4_), channel_id=1, source_target_pairs={{0,4},{1,5},{2,6},{3,7},{16,20},{17,21},{18,22},{19,23}} | collective-permute-start | bytes 196616 | tf_op jit(solution)/shard_map/ppermute | solution.py:609
  17.0 11.6 %collective-permute-start.8 = (f32[4,272,256]{2,1,0:T(8,128)S(1)}, f32[4,272,256]{2,1,0:T(8,128)S(1)}, u32[]{:S(2)}, u32[]{:S(2)}) collective-permute-start(f32[4,272,256]{2,1,0:T(8,128)S(1)} %get-tuple-element.79.late), channel_id=1, source_target_pairs={{12,8},{13,9},{14,10},{15,11},{28,24},{29,25},{30,26},{31,27}} | collective-permute-start | bytes 3342344 | tf_op jit(solution)/shard_map/ppermute | solution.py:593
  20.9 5.5 %collective-permute-start.4 = (f32[4,16,256]{2,1,0:T(8,128)S(1)}, f32[4,16,256]{2,1,0:T(8,128)S(1)}, u32[]{:S(2)}, u32[]{:S(2)}) collective-permute-start(f32[4,16,256]{2,1,0:T(8,128)S(1)} %get-tuple-element.64.refs_6_), channel_id=1, source_target_pairs={{4,8},{5,9},{6,10},{7,11},{20,24},{21,25},{22,26},{23,27}} | collective-permute-start | bytes 196616 | tf_op jit(solution)/shard_map/ppermute | solution.py:590
  21.6 5.6 %collective-permute-start.6 = (f32[4,16,256]{2,1,0:T(8,128)S(1)}, f32[4,16,256]{2,1,0:T(8,128)S(1)}, u32[]{:S(2)}, u32[]{:S(2)}) collective-permute-start(f32[4,16,256]{2,1,0:T(8,128)S(1)} %get-tuple-element.77.refs_6_), channel_id=1, source_target_pairs={{0,4},{1,5},{2,6},{3,7},{16,20},{17,21},{18,22},{19,23}} | collective-permute-start | bytes 196616 | tf_op jit(solution)/shard_map/ppermute | solution.py:606
  26.5 0.8 %collective-permute-start.5 = (f32[4,16,256]{2,1,0:T(8,128)S(1)}, f32[4,16,256]{2,1,0:T(8,128)S(1)}, u32[]{:S(2)}, u32[]{:S(2)}) collective-permute-start(f32[4,16,256]{2,1,0:T(8,128)S(1)} %answer.1), channel_id=1, source_target_pairs={{8,4},{9,5},{10,6},{11,7},{24,20},{25,21},{26,22},{27,23}} | collective-permute-start | bytes 196616 | tf_op jit(solution)/shard_map/ppermute | solution.py:577
  27.3 7.3 %collective-permute-start.7 = (f32[4,16,256]{2,1,0:T(8,128)S(1)}, f32[4,16,256]{2,1,0:T(8,128)S(1)}, u32[]{:S(2)}, u32[]{:S(2)}) collective-permute-start(f32[4,16,256]{2,1,0:T(8,128)S(1)} %get-tuple-element.78.refs_4_.refs_6_), channel_id=1, source_target_pairs={{4,8},{8,12},{5,9},{9,13},{6,10},{10,14},{7,11},{11,15},{20,24},{2... | collective-permute-start | bytes 196616 | tf_op jit(solution)/shard_map/ppermute | solution.py:609
  34.6 6.6 %collective-permute-start.9 = (f32[4,16,256]{2,1,0:T(8,128)S(1)}, f32[4,16,256]{2,1,0:T(8,128)S(1)}, u32[]{:S(2)}, u32[]{:S(2)}) collective-permute-start(f32[4,16,256]{2,1,0:T(8,128)S(1)} %finish_leaving.3), channel_id=1, source_target_pairs={{8,12},{9,13},{10,14},{11,15},{24,28},{25,29},{26,30},{27,31}} | collective-permute-start | bytes 196616 | tf_op jit(solution)/shard_map/ppermute | solution.py:609
